TPU v7x, 256 devices: a whole 4x4x8 slice. The times are simulated.
256 devices in a mesh: dp: 64 (over z, y, x_hi), tensor: 4 (over x_lo, core).
Axes of the slice: x: 4 (x_hi: 2, x_lo: 2; x = x_hi * 2 + x_lo), y: 4, z: 8, core: 2. Of those that a mesh axis runs over, the one named last changes fastest.
Arguments:
- target_queries: bfloat16 [32768, 8192], P('dp', 'tensor'), may hold values from -6 to 6
- target_keys: bfloat16 [32768, 1024], P('dp', 'tensor'), may hold values from -4 to 4
- target_values: bfloat16 [32768, 1024], P('dp', 'tensor'), may hold values from -6 to 6
- low_feature: bfloat16 [32768, 8192], P(('dp', 'tensor')), may hold values from -24 to 24
- mid_feature: bfloat16 [32768, 8192], P(('dp', 'tensor')), may hold values from -6 to 6
- merging_gain: float32 [3, 8192], replicated, may hold values from 0.25 to 4
- draft_gain: float32 [8192], replicated, may hold values from 0.5 to 2
- draft_weight: bfloat16 [8192, 512], P(('dp', 'tensor')), may hold values from -0.0625 to 0.0625
- cotangent: bfloat16 [3, 32768, 512], P(None, ('dp', 'tensor')), may hold values from -6 to 6
- doc_lengths: int32 [64, 8], P('dp'), may hold values from 1 to 256, 512 in all within a row
- step_offsets: int32 [3], replicated, may hold values from 1 to 32, as said below
Outputs:
- draft_values: bfloat16 [3, 32768, 512], P(None, ('dp', 'tensor'))
- weight_grad: float32 [8192, 512], P(('dp', 'tensor'))
- gain_grad: float32 [8192], P(('dp', 'tensor'))
Inputs may be any that keep to these rules, and one draw needn't show every extreme that they name: `step_offsets`: each offset lies in 1 to 32; one of them equals 32.
All inputs are finite; a program needn't handle non-finite values.
Results may differ from a plain program's by a relative error of at most 0.0062.
Values may be sent and summed in bfloat16 or wider, within the bound.
No kernel may reach another device: no remote copies, remote signals or barrier semaphores. Data moves between devices by JAX's collectives and lax.ppermute only.
A program may use at most 128 MiB of HBM per device.

v0:
```python
import jax
import jax.numpy as jnp
from jax import lax
from jax.sharding import PartitionSpec as P

HD = 128
STEPS = 3


EPSILON = 1e-05


def passed_along(value, axis, steps):
    count = lax.axis_size(axis)
    first, last = (max(0, -steps), min(count, count - steps))
    return lax.ppermute(value, axis, [(source, source + steps) for source in range(first, last)])


def row_norm(values):
    values = values.astype(jnp.float32)
    return values * lax.rsqrt(jnp.mean(values * values, axis=-1, keepdims=True) + EPSILON)


def body(
    target_queries,
    target_keys,
    target_values,
    low_feature,
    mid_feature,
    merging_gain,
    draft_gain,
    draft_weight,
    cotangent,
    doc_lengths,
    step_offsets,
):
    tensor_place = lax.axis_index("tensor")
    pack_size = target_queries.shape[0]
    local_rows = low_feature.shape[0]
    ends = jnp.cumsum(doc_lengths[0])

    def segment_of(places):
        return jnp.sum((places[:, None] >= ends[None, :]).astype(jnp.int32), axis=-1)

    segment = segment_of(jnp.arange(pack_size, dtype=jnp.int32))
    kv_local = target_keys.shape[1] // HD
    query_local = target_queries.shape[1] // HD
    group_size = query_local // kv_local
    block = min(512, pack_size)
    blocks = pack_size // block
    query_blocks = target_queries.reshape(blocks, block, kv_local, group_size, HD)
    key_three = target_keys.reshape(pack_size, kv_local, HD)
    value_three = target_values.reshape(pack_size, kv_local, HD)
    key_places = jnp.arange(pack_size, dtype=jnp.int32)

    def attend_block(operands):
        query_block, block_index = operands
        query_places = block_index * block + jnp.arange(block, dtype=jnp.int32)
        scores = jnp.einsum(
            "qgrh,kgh->grqk", query_block, key_three, preferred_element_type=jnp.float32
        ) / jnp.sqrt(jnp.float32(HD))
        allowed = (key_places[None, :] <= query_places[:, None]) & (
            segment[None, :] == segment[:, None]
        )
        scores = jnp.where(allowed, scores, -1e30)
        highest = jnp.max(scores, axis=-1, keepdims=True)
        expo = jnp.where(allowed, jnp.exp(scores - highest), 0.0)
        weights = (expo / jnp.sum(expo, axis=-1, keepdims=True)).astype(jnp.bfloat16)
        mixed = jnp.einsum(
            "grqk,kgh->qgrh", weights, value_three, preferred_element_type=jnp.float32
        )
        return mixed.astype(jnp.bfloat16).reshape(block, query_local * HD)

    heads_out = lax.map(attend_block, (query_blocks, jnp.arange(blocks, dtype=jnp.int32)))
    heads_out = heads_out.reshape(pack_size, query_local * HD)
    high = lax.all_to_all(heads_out, "tensor", split_axis=0, concat_axis=1, tiled=True)
    merged = (
        row_norm(low_feature) * merging_gain[0]
        + row_norm(mid_feature) * merging_gain[1]
        + row_norm(high) * merging_gain[2]
    ).astype(jnp.bfloat16)
    prior = passed_along(merged, "tensor", 1)
    joined = jnp.concatenate([prior, merged], axis=0)
    lead = prior.shape[0]
    row_places = tensor_place * local_rows + jnp.arange(local_rows, dtype=jnp.int32)
    row_segment = segment_of(row_places)
    hidden_parts = []
    normed_parts = []
    for step_index in range(STEPS):
        offset = step_offsets[step_index]
        source_places = row_places - offset
        valid = (source_places >= 0) & (segment_of(source_places) == row_segment)
        shifted = lax.dynamic_slice_in_dim(joined, lead - offset, local_rows, 0)
        shifted = jnp.where(valid[:, None], shifted, jnp.zeros((), jnp.bfloat16))
        normed = row_norm(shifted)
        normed_parts.append(normed)
        hidden_parts.append((normed * draft_gain).astype(jnp.bfloat16))
    normed_all = jnp.concatenate(normed_parts, axis=0)
    hidden_all = jnp.concatenate(hidden_parts, axis=0)
    grads_in = cotangent.reshape(STEPS * local_rows, cotangent.shape[2])
    value_width = draft_weight.shape[1]
    piece = lax.all_gather(draft_weight, ("dp", "tensor"), axis=0, tiled=True)
    values_acc = jnp.dot(hidden_all, piece, preferred_element_type=jnp.float32)
    back = lax.dot_general(
        grads_in, piece, (((1,), (1,)), ((), ())), preferred_element_type=jnp.float32
    )
    gain_acc = jnp.sum(back * normed_all, axis=0)
    values_acc, gain_part = (values_acc, gain_acc)
    draft_values = values_acc.astype(jnp.bfloat16).reshape(STEPS, local_rows, value_width)
    term = lax.dot_general(
        hidden_all, grads_in, (((0,), (0,)), ((), ())), preferred_element_type=jnp.float32
    )
    weight_grad, gain_grad = (
        lax.psum_scatter(term, ("dp", "tensor"), scatter_dimension=0, tiled=True),
        lax.psum_scatter(gain_part, ("dp", "tensor"), scatter_dimension=0, tiled=True),
    )
    return (draft_values, weight_grad, gain_grad)


def solution(mesh):
    placed = (
        P("dp", "tensor"),
        P("dp", "tensor"),
        P("dp", "tensor"),
        P(("dp", "tensor"), None),
        P(("dp", "tensor"), None),
        P(),
        P(),
        P(("dp", "tensor"), None),
        P(None, ("dp", "tensor"), None),
        P("dp", None),
        P(),
    )
    return jax.shard_map(
        body,
        mesh=mesh,
        in_specs=placed,
        out_specs=(P(None, ("dp", "tensor"), None), P(("dp", "tensor"), None), P(("dp", "tensor"))),
        check_vma=False,
    )
```

profile of v0, /device:TPU:1, one launch (start us, length us, event | category | flops | bytes accessed | tf_op | source)
XLA Modules:
  0.0 1432.8 jit_solution(4247422951291664510)
XLA Ops:
  7.2 0.0 copy-start
  7.2 0.0 all-gather.2.cloned.1.call-start
  7.2 0.7 all-gather.2.cloned.1.call-update
  7.9 0.8 reduce-window.8
  8.7 0.1 convert_reduce_fusion
  8.8 0.2 fusion.36
  9.1 1.0 reshape.151
  10.1 1.0 reshape.152
  11.1 2.2 copy.44
  13.3 10.6 fusion.51
  23.9 10.7 convert_bitcast_fusion.1
  34.6 2.9 copy.34
  37.5 2.3 all_to_all.10
  39.9 6.9 all-to-all-start
  46.8 0.0 reduce-scatter.2.cloned.1.call-start
  46.8 2.1 fusion.9
  48.9 2.1 fusion.14
  51.0 0.0 copy-done.6
  51.0 0.1 fusion.49
  51.1 21.7 %all-to-all-done = bf16[4,128,2048]{2,1,0:T(8,128)(2,1)S(1)} async-done(((bf16[4,128,2048]{2,1,0:T(8,128)(2,1)}), bf16[4,128,2048]{2,1,0:T(8,128)(2,1)S(1)}, u32[]{:S(2)}, u32[]{:S(2)}) %all-to-all-start) | async-done | bytes 2097184 | tf_op jit(solution)/shard_map/all_to_all | solution.py:76
  72.8 0.5 convert_bitcast_fusion
  73.3 0.0 copy-start.1
  73.3 0.0 copy-start.2
  73.3 0.3 copy.43
  73.6 0.5 fusion.19
  74.1 0.8 copy-done.1
  74.9 0.6 copy-done.2
  75.6 1.9 fusion.13
  77.4 3.2 collective-permute-start
  80.7 0.6 fusion.50
  85.2 1.3 broadcast_subtract_fusion.1
  86.5 0.7 iota_add_fusion
  87.1 0.1 convert_reduce_fusion.4
  87.2 20.1 %collective-permute-done = bf16[128,8192]{1,0:T(8,128)(2,1)} collective-permute-done((bf16[128,8192]{1,0:T(8,128)(2,1)S(1)}, bf16[128,8192]{1,0:T(8,128)(2,1)}, u32[]{:S(2)}, u32[]{:S(2)}) %collective-permute-start) | collective-permute-done | bytes 2097184 | tf_op jit(solution)/shard_map/ppermute | solution.py:16
  107.3 7.5 fusion.16
  114.8 2.7 convert_multiply_fusion.1
  117.5 2.6 convert_multiply_fusion.3
  120.2 2.7 convert_multiply_fusion.5
  122.9 0.0 copy-done
  122.9 1.3 copy-done.4
  124.2 8.1 fusion.20
  132.3 0.0 reduce-scatter.2.cloned.1.call-update
  132.4 1.6 all-gather.2.cloned.1.call-done
  134.0 8.9 fusion.4
  142.9 79.0 %all-reduce = f32[8192]{0:T(1024)S(1)} all-reduce(f32[8192]{0:T(1024)S(1)} %fusion.4), channel_id=3, replica_groups=mesh['dp'=64,'tensor'=4] {'dp','tensor'}, use_global_device_ids=true, to_apply=%region_16.17.clone | all-reduce | flops 8192 | bytes 65536
  221.9 0.6 dynamic-slice
  222.5 8.8 fusion.35
  231.3 1194.7 %reduce-scatter.2.cloned.1.call-done = f32[32,512]{1,0:T(8,128)} async-done(((f32[8192,512]{1,0:T(8,128)}), f32[32,512]{1,0:T(8,128)}) %reduce-scatter.2.cloned.1.call-update) | async-done | bytes 65552 | tf_op jit(solution)/shard_map/reduce_scatter | solution.py:114
  (14 shorter events, 0.1 us)
Async XLA Ops:
  7.2 115.8 %copy-start = (bf16[3,128,512]{2,1,0:T(8,128)(2,1)S(1)}, bf16[3,128,512]{2,1,0:T(8,128)(2,1)}, u32[]{:S(2)}) copy-start(bf16[3,128,512]{2,1,0:T(8,128)(2,1)} %param.19) | copy-start | bytes 1179652
  7.2 126.8 %all-gather.2.cloned.1.call-start = ((), (), s32[]{:S(2)}) async-start(), calls=%async_computation.2 | async-start | bytes 8421376 | tf_op jit(solution)/shard_map/all_gather | solution.py:102
  39.9 11.1 copy-start.6
  39.9 32.9 %all-to-all-start = ((bf16[4,128,2048]{2,1,0:T(8,128)(2,1)}), bf16[4,128,2048]{2,1,0:T(8,128)(2,1)S(1)}, u32[]{:S(2)}, u32[]{:S(2)}) async-start(bf16[4,128,2048]{2,1,0:T(8,128)(2,1)} %all_to_all.10), calls=%async_computation | async-start | bytes 4194304 | tf_op jit(solution)/shard_map/all_to_all | solution.py:76
  46.8 1379.1 %reduce-scatter.2.cloned.1.call-start = ((), (), s32[]{:S(2)}) async-start(), calls=%async_computation.3 | async-start | bytes 16842752 | tf_op jit(solution)/shard_map/reduce_scatter | solution.py:114
  73.3 1.6 copy-start.1
  73.3 2.2 copy-start.2
  75.6 5.1 copy-start.7
  77.4 29.9 %collective-permute-start = (bf16[128,8192]{1,0:T(8,128)(2,1)S(1)}, bf16[128,8192]{1,0:T(8,128)(2,1)}, u32[]{:S(2)}, u32[]{:S(2)}) collective-permute-start(bf16[128,8192]{1,0:T(8,128)(2,1)S(1)} %fusion.13), channel_id=1, source_target_pairs={{0,1},{1,2},{2,3},{4,5},{5,6},{6,7},{8,9},{9,10},{10,11},{12,13},{... | collective-permute-start | bytes 6291464 | tf_op jit(solution)/shard_map/ppermute | solution.py:16
  107.3 7.5 copy-start.5
  120.2 2.8 copy-start.3
  122.9 1.3 copy-start.4
Sparse Core Ops, SparseCore 0:
  11.6 122.3 all-gather.1
  137.1 1288.8 reduce-scatter.1
where the time goes:
time: 1440 us; the launch traced here: 1430 us
  waiting for transfers between devices  1240 us (86%)
  blocking collectives  79 us (5%)
  matrix products  47.1 us (3%)
  other arithmetic  25.8 us (2%)
  between operations  18.1 us (1%)
    reduce_scatter x1, waiting for transfers between devices, body(): lax.psum_scatter(term, ('dp', 'tensor'), scatter_dimension=0, tiled=True)  1190 us
    unnamed x1, blocking collectives  79 us
  transfers between devices with their start and end apart: 4, of which 4 were waited for; matrix products, arithmetic and copies ran while one was open for 6% of the time, Pallas kernels for 0%

commit v1 on v0

v1 whole, which is shorter than its diff:
```python
import functools
import math

import jax
import jax.numpy as jnp
from jax import lax
from jax.experimental import pallas as pl
from jax.experimental.pallas import tpu as pltpu
from jax.sharding import PartitionSpec as P

HD = 128
STEPS = 3
OFFMAX = 32
EPSILON = 1e-05
VMEM_LIMIT = 48 * 1024 * 1024

VMEM = pl.BlockSpec(memory_space=pltpu.VMEM)
SMEM = pl.BlockSpec(memory_space=pltpu.SMEM)
F32 = jnp.float32
BF16 = jnp.bfloat16


def segment_start(places, lengths_ref):
    end = jnp.int32(0)
    start = jnp.zeros_like(places)
    for s in range(lengths_ref.shape[1]):
        end = end + lengths_ref[0, s]
        start = jnp.where(places >= end, end, start)
    return start


def column(row):
    n = row.shape[-1]
    eye = lax.broadcasted_iota(jnp.int32, (n, n), 0) == lax.broadcasted_iota(jnp.int32, (n, n), 1)
    return jnp.sum(jnp.where(eye, row, 0.0), axis=1, keepdims=True)


def lane_sums(values):
    return lax.dot_general(
        jnp.ones((8, values.shape[1]), F32), values, (((1,), (1,)), ((), ())),
        precision=lax.Precision.HIGHEST, preferred_element_type=F32)


def folded_square_sum(values):
    total = None
    for c in range(0, values.shape[1], 128):
        piece = values[:, c:c + 128]
        total = piece * piece if total is None else total + piece * piece
    return total


def features_kernel(tn, place_ref, low_ref, mid_ref, gain_ref, *outs):
    j = place_ref[0]
    width = low_ref.shape[1]
    piece = width // tn
    step = 1024

    def rms_scale(ref):
        total = None
        for c in range(0, width, step):
            part = folded_square_sum(ref[:, c:c + step].astype(F32))
            total = part if total is None else total + part
        return lax.rsqrt(jnp.sum(total, axis=1, keepdims=True) / width + EPSILON)

    low_scale = rms_scale(low_ref)
    mid_scale = rms_scale(mid_ref)
    for s, out in enumerate(outs):
        first = pl.multiple_of((j ^ s) * piece, piece)
        for c in range(0, piece, 512):
            at = pl.ds(first + c, 512)
            value = (low_ref[:, at].astype(F32) * low_scale * gain_ref[0:1, at]
                     + mid_ref[:, at].astype(F32) * mid_scale * gain_ref[1:2, at])
            out[:, c:c + 512] = value.astype(BF16)


def features(place, low, mid, gain, tn):
    rows, width = low.shape
    block = 32
    piece = width // tn
    return pl.pallas_call(
        functools.partial(features_kernel, tn),
        grid=(rows // block,),
        in_specs=[
            SMEM,
            pl.BlockSpec((block, width), lambda b: (b, 0)),
            pl.BlockSpec((block, width), lambda b: (b, 0)),
            pl.BlockSpec(gain.shape, lambda b: (0, 0)),
        ],
        out_specs=[pl.BlockSpec((block, piece), lambda b: (b, 0))] * tn,
        out_shape=[jax.ShapeDtypeStruct((rows, piece), BF16)] * tn,
        compiler_params=pltpu.CompilerParams(vmem_limit_bytes=VMEM_LIMIT),
        cost_estimate=pl.CostEstimate(flops=10 * rows * width, bytes_accessed=6 * rows * width, transcendentals=0),
        name="features",
    )(place, low, mid, gain)


def attend_kernel(window, lengths_ref, query_ref, key_ref, value_ref, high_ref, square_ref):
    block = query_ref.shape[0]
    pack = key_ref.shape[0]
    b = pl.program_id(0)
    first = pl.multiple_of(jnp.clip(b * block - (window - block), 0, pack - window), block)
    query_places = b * block + lax.broadcasted_iota(jnp.int32, (block, window), 0)
    key_places = first + lax.broadcasted_iota(jnp.int32, (block, window), 1)
    allowed = (key_places <= query_places) & (key_places >= segment_start(query_places, lengths_ref))
    bias = jnp.where(allowed, 0.0, -1e30).astype(F32)
    group = (query_ref.shape[1] // HD) // (key_ref.shape[1] // HD)
    squares = jnp.zeros((block, HD), F32)
    ones = jnp.ones((window, HD), BF16)
    scale = math.log2(math.e) / math.sqrt(HD)
    for g in range(key_ref.shape[1] // HD):
        key = key_ref[pl.ds(first, window), g * HD:(g + 1) * HD]
        value = jnp.concatenate([value_ref[pl.ds(first, window), g * HD:(g + 1) * HD], ones], axis=1)
        for r in range(group):
            at = slice((g * group + r) * HD, (g * group + r + 1) * HD)
            scores = lax.dot_general(query_ref[:, at], key, (((1,), (1,)), ((), ())), preferred_element_type=F32)
            scores = scores * scale + bias
            highest = jnp.max(scores, axis=1, keepdims=True)
            expo = jnp.exp2(scores - highest).astype(BF16)
            mixed = jnp.dot(expo, value, preferred_element_type=F32)
            out = (mixed[:, :HD] / mixed[:, HD:]).astype(BF16)
            high_ref[:, at] = out
            out = out.astype(F32)
            squares = squares + out * out
    square_ref[0] = lane_sums(squares)


def attend(lengths, queries, keys, values):
    pack, width = queries.shape
    block = 128
    window = min(pack, 256 + block)
    return pl.pallas_call(
        functools.partial(attend_kernel, window),
        grid=(pack // block,),
        in_specs=[
            SMEM,
            pl.BlockSpec((block, width), lambda b: (b, 0)),
            pl.BlockSpec(keys.shape, lambda b: (0, 0)),
            pl.BlockSpec(values.shape, lambda b: (0, 0)),
        ],
        out_specs=[
            pl.BlockSpec((block, width), lambda b: (b, 0)),
            pl.BlockSpec((1, 8, block), lambda b: (b, 0, 0)),
        ],
        out_shape=[
            jax.ShapeDtypeStruct((pack, width), BF16),
            jax.ShapeDtypeStruct((pack // block, 8, block), F32),
        ],
        compiler_params=pltpu.CompilerParams(vmem_limit_bytes=VMEM_LIMIT),
        cost_estimate=pl.CostEstimate(
            flops=4 * pack * window * width, bytes_accessed=4 * pack * width,
            transcendentals=pack * window * width // HD),
        name="attend",
    )(lengths, queries, keys, values)


def chosen(place_ref, lengths_ref, offset, rows, lead):
    target = place_ref[0] * rows + lax.broadcasted_iota(jnp.int32, (rows, rows + lead), 0)
    source = place_ref[0] * rows - lead + lax.broadcasted_iota(jnp.int32, (rows, rows + lead), 1)
    hit = (source == target - offset) & (source >= segment_start(target, lengths_ref))
    return jnp.where(hit, 1.0, 0.0).astype(BF16)


def fold_kernel(place_ref, lengths_ref, offsets_ref, cotangent_ref, out_ref):
    steps, rows, width = cotangent_ref.shape
    total = None
    for s in range(steps):
        pick = chosen(place_ref, lengths_ref, offsets_ref[s], rows, OFFMAX)
        part = lax.dot_general(pick, cotangent_ref[s], (((0,), (0,)), ((), ())), preferred_element_type=F32)
        total = part if total is None else total + part
    out_ref[...] = total.astype(BF16)


def fold(place, lengths, offsets, cotangent):
    steps, rows, width = cotangent.shape
    return pl.pallas_call(
        fold_kernel,
        in_specs=[SMEM, SMEM, SMEM, VMEM],
        out_specs=VMEM,
        out_shape=jax.ShapeDtypeStruct((rows + OFFMAX, width), BF16),
        compiler_params=pltpu.CompilerParams(vmem_limit_bytes=VMEM_LIMIT),
        cost_estimate=pl.CostEstimate(flops=2 * steps * rows * 160 * width, bytes_accessed=2 * steps * rows * width, transcendentals=0),
        name="fold",
    )(place, lengths, offsets, cotangent)


def merge_kernel(width, place_ref, square_ref, gain_ref, high_ref, *refs):
    tn = len(refs) - 2
    parts, out_ref, out_square_ref = refs[:tn], refs[tn], refs[tn + 1]
    j = place_ref[0]
    rows = parts[0].shape[0]
    for s in range(tn):
        b = j ^ s
        at = pl.ds(pl.multiple_of(b * rows, rows), rows)
        scale = lax.rsqrt(column(square_ref[pl.ds(b, 1), :]) / width + EPSILON)
        total = jnp.zeros((rows, 128), F32)
        for c in range(0, high_ref.shape[1], 128):
            cols = slice(c, c + 128)
            merged = (parts[s][:, cols].astype(F32)
                      + high_ref[at, cols].astype(F32) * scale * gain_ref[:, cols]).astype(BF16)
            out_ref[at, cols] = merged
            merged = merged.astype(F32)
            total = total + merged * merged
        out_square_ref[b] = lane_sums(total)


def merge(place, squares, gain, high, parts, width):
    pack, piece = high.shape
    return pl.pallas_call(
        functools.partial(merge_kernel, width),
        in_specs=[SMEM, VMEM, VMEM, VMEM] + [VMEM] * len(parts),
        out_specs=[VMEM, VMEM],
        out_shape=[
            jax.ShapeDtypeStruct((pack, piece), BF16),
            jax.ShapeDtypeStruct((len(parts), 8, pack // len(parts)), F32),
        ],
        compiler_params=pltpu.CompilerParams(vmem_limit_bytes=VMEM_LIMIT),
        cost_estimate=pl.CostEstimate(flops=8 * pack * piece, bytes_accessed=6 * pack * piece, transcendentals=0),
        name="merge",
    )(place, squares, gain, high, *parts)


def project(place, squares, gain, merged, weight, folds, width):
    pack, piece = merged.shape
    tn = len(folds)
    rows = pack // tn
    vw = weight.shape[1]

    def kernel(place_ref, square_ref, gain_ref, merged_ref, weight_ref, *refs):
        fold_refs = refs[:tn]
        grad_ref = refs[tn]
        value_refs = refs[tn + 1:2 * tn + 1]
        hidden_ref, fold_ref, total_ref = refs[2 * tn + 1:]
        j = place_ref[0]
        for b in range(tn):
            at = slice(b * rows, (b + 1) * rows)
            scale = lax.rsqrt(column(square_ref[b:b + 1, :]) / width + EPSILON)
            for c in range(0, piece, 128):
                cols = slice(c, c + 128)
                hidden_ref[at, cols] = (merged_ref[at, cols].astype(F32) * scale * gain_ref[:, cols]).astype(BF16)
        fold_ref[...] = jnp.zeros_like(fold_ref)
        for s in range(tn):
            at = pl.ds(pl.multiple_of((j ^ s) * rows, rows), rows + OFFMAX)
            fold_ref[at, :] = fold_ref[at, :] + fold_refs[s][...].astype(F32)
        folded = fold_ref[OFFMAX:, :].astype(BF16)
        total_ref[0:OFFMAX, :] = jnp.zeros((OFFMAX, vw), F32)
        for c in range(0, piece, 256):
            grad_ref[c:c + 256, :] = lax.dot_general(
                hidden_ref[:, c:c + 256], folded, (((0,), (0,)), ((), ())), preferred_element_type=F32)
        for c in range(0, pack, 256):
            total_ref[OFFMAX + c:OFFMAX + c + 256, :] = jnp.dot(
                hidden_ref[c:c + 256, :], weight_ref[...], preferred_element_type=F32)
        for s in range(tn):
            at = pl.ds(pl.multiple_of((j ^ s) * rows, rows), rows + OFFMAX)
            value_refs[s][...] = total_ref[at, :].astype(value_refs[s].dtype)

    return pl.pallas_call(
        kernel,
        in_specs=[SMEM] + [VMEM] * (4 + tn),
        out_specs=[VMEM] * (1 + tn),
        out_shape=[jax.ShapeDtypeStruct((piece, vw), F32)]
        + [jax.ShapeDtypeStruct((rows + OFFMAX, vw), F32 if s == 0 else BF16) for s in range(tn)],
        scratch_shapes=[
            pltpu.VMEM((pack, piece), BF16),
            pltpu.VMEM((pack + OFFMAX, vw), F32),
            pltpu.VMEM((pack + OFFMAX, vw), F32),
        ],
        compiler_params=pltpu.CompilerParams(vmem_limit_bytes=VMEM_LIMIT),
        cost_estimate=pl.CostEstimate(flops=4 * pack * piece * vw, bytes_accessed=12 * pack * piece, transcendentals=0),
        name="project",
    )(place, squares, gain, merged, weight, *folds)


def spread(place, lengths, offsets, parts):
    rows, vw = parts[0].shape[0] - OFFMAX, parts[0].shape[1]

    def kernel(place_ref, lengths_ref, offsets_ref, *refs):
        parts_refs, out_ref = refs[:-1], refs[-1]
        total = None
        for ref in parts_refs:
            part = ref[...].astype(F32)
            total = part if total is None else total + part
        total = total.astype(BF16)
        for s in range(STEPS):
            pick = chosen(place_ref, lengths_ref, offsets_ref[s], rows, OFFMAX)
            out_ref[s] = jnp.dot(pick, total, preferred_element_type=F32).astype(BF16)

    return pl.pallas_call(
        kernel,
        in_specs=[SMEM] * 3 + [VMEM] * len(parts),
        out_specs=VMEM,
        out_shape=jax.ShapeDtypeStruct((STEPS, rows, vw), BF16),
        compiler_params=pltpu.CompilerParams(vmem_limit_bytes=VMEM_LIMIT),
        cost_estimate=pl.CostEstimate(flops=2 * STEPS * rows * 160 * vw, bytes_accessed=8 * STEPS * rows * vw, transcendentals=0),
        name="spread",
    )(place, lengths, offsets, *parts)


def body(
    target_queries,
    target_keys,
    target_values,
    low_feature,
    mid_feature,
    merging_gain,
    draft_gain,
    draft_weight,
    cotangent,
    doc_lengths,
    step_offsets,
):
    n = lax.axis_size("dp")
    tn = lax.axis_size("tensor")
    j = lax.axis_index("tensor")
    flat = lax.axis_index("dp") * tn + j
    place = j.reshape(1).astype(jnp.int32)
    width = low_feature.shape[1]
    piece = width // tn
    pack = target_queries.shape[0]
    both = ("dp", "tensor")

    def swapped(values, s):
        return lax.ppermute(values, "tensor", [(a, a ^ s) for a in range(tn)])

    moved = lax.ppermute(draft_weight, both, [(r, (r % n) * tn + r // n) for r in range(n * tn)])
    weight = lax.all_gather(moved, "dp", axis=0, tiled=True)

    folded = fold(place, doc_lengths, step_offsets, cotangent)
    folds = [folded] + [swapped(folded, s) for s in range(1, tn)]
    sent = features(place, low_feature, mid_feature, merging_gain, tn)
    parts = [sent[0]] + [swapped(sent[s], s) for s in range(1, tn)]

    high, high_squares = attend(doc_lengths, target_queries, target_keys, target_values)

    def summed(squares):
        squares = squares[:, 0, :]
        total = squares
        for s in range(1, tn):
            total = total + swapped(squares, s)
        return total

    own_gain = lax.dynamic_slice(merging_gain, (2, j * piece), (1, piece))
    merged, squares = merge(place, summed(high_squares), own_gain, high, parts, width)
    own_gain = lax.dynamic_slice(draft_gain, (j * piece,), (piece,)).reshape(1, piece)
    grad, *values = project(place, summed(squares), own_gain, merged, weight, folds, width)
    values = [values[0]] + [swapped(values[s], s) for s in range(1, tn)]
    draft_values = spread(place, doc_lengths, step_offsets, values)

    grad = lax.psum_scatter(grad, "dp", scatter_dimension=0, tiled=True)
    weight_grad = lax.ppermute(grad, both, [((r % n) * tn + r // n, r) for r in range(n * tn)])
    rows = weight_grad.shape[0]
    gain = lax.dynamic_slice(draft_gain, (flat * rows,), (rows,))
    gain_grad = jnp.sum(weight_grad * draft_weight.astype(F32), axis=1) / gain
    return (draft_values, weight_grad, gain_grad)


def solution(mesh):
    placed = (
        P("dp", "tensor"),
        P("dp", "tensor"),
        P("dp", "tensor"),
        P(("dp", "tensor"), None),
        P(("dp", "tensor"), None),
        P(),
        P(),
        P(("dp", "tensor"), None),
        P(None, ("dp", "tensor"), None),
        P("dp", None),
        P(),
    )
    return jax.shard_map(
        body,
        mesh=mesh,
        in_specs=placed,
        out_specs=(P(None, ("dp", "tensor"), None), P(("dp", "tensor"), None), P(("dp", "tensor"))),
        check_vma=False,
    )
```

time: 1440 us -> 534 us (0.37)
  waiting for transfers between devices: 1240 us -> 423 us
  blocking collectives: 79 us -> 0 us
  matrix products: 47.1 us -> 0 us
  starting transfers between devices: 10.2 us -> 53.6 us
  other arithmetic: 25.8 us -> 1.41 us
  Pallas kernels: 0 us -> 23.3 us
    reduce_scatter x1, waiting for transfers between devices: 1190 us -> 313 us  [body(): grad = lax.psum_scatter(grad, 'dp', scatter_dimension=0, tiled=True)]
    unnamed x1 -> x0, blocking collectives: 79 us -> none
    all_gather x1, waiting for transfers between devices: 1.6 us -> 67.8 us  [body(): weight = lax.all_gather(moved, 'dp', axis=0, tiled=True)]
    ppermute x1 -> x17, starting transfers between devices: 3.23 us -> 53.5 us  [the longest x1 28.9 us: body(): lax.ppermute(grad, both, [(r % n * tn + r // n, r) for r in range(n * tn)])]
    dot_general x4 -> x0, matrix products: 36.5 us -> none  [the longest x1 10.7 us: attend_block(): jnp.einsum('grqk,kgh->qgrh', weights, value_three, preferred_element_type...]
    pallas_call x0 -> x6, Pallas kernels: none -> 23.3 us  [the longest x1 8.17 us: attend(): pl.pallas_call(functools.partial(attend_kernel, window), grid=(pack // bl...]
    all_to_all x1 -> x0, waiting for transfers between devices: 21.7 us -> none  [body(): lax.all_to_all(heads_out, 'tensor', split_axis=0, concat_axis=1, tiled=True)]
    ppermute x1 -> x17, waiting for transfers between devices: 20.1 us -> 41.6 us  [the longest x1 20.6 us: body(): lax.ppermute(grad, both, [(r % n * tn + r // n, r) for r in range(n * tn)])]
  transfers between devices with their start and end apart: 4 -> 19, of which waited for: 4 -> 7; matrix products, arithmetic and copies ran while one was open for 6% -> 0% of each run, Pallas kernels for 0% -> 4%
where the time goes in v1:
time: 534 us; the launch traced here: 527 us
  waiting for transfers between devices  423 us (79%)
  starting transfers between devices  53.6 us (10%)
  Pallas kernels  23.3 us (4%)
  between operations  14.2 us (3%)
  local copies, waits for them, and re-layouts  11.2 us (2%)
    reduce_scatter x1, waiting for transfers between devices, body(): grad = lax.psum_scatter(grad, 'dp', scatter_dimension=0, tiled=True)  313 us
    all_gather x1, waiting for transfers between devices, body(): weight = lax.all_gather(moved, 'dp', axis=0, tiled=True)  67.8 us
    ppermute x1, starting transfers between devices, body(): lax.ppermute(grad, both, [(r % n * tn + r // n, r) for r in range(n * tn)])  28.9 us
    ppermute x1, waiting for transfers between devices, body(): lax.ppermute(grad, both, [(r % n * tn + r // n, r) for r in range(n * tn)])  20.6 us
    ppermute x15, waiting for transfers between devices, swapped(): return lax.ppermute(values, 'tensor', [(a, a ^ s) for a in range(tn)])  19 us
    ppermute x15, starting transfers between devices, swapped(): return lax.ppermute(values, 'tensor', [(a, a ^ s) for a in range(tn)])  18.6 us
  transfers between devices with their start and end apart: 19, of which 7 were waited for; matrix products, arithmetic and copies ran while one was open for 0% of the time, Pallas kernels for 4%

profile of v1, /device:TPU:1, one launch (start us, length us, event | category | flops | bytes accessed | tf_op | source)
XLA Modules:
  0.0 526.5 jit_solution(13969887548983571530)
XLA Ops:
  7.2 0.0 all-gather.2.cloned.1.call-start
  7.2 6.0 %collective-permute-start.9 = (bf16[32,512]{1,0:T(8,128)(2,1)}, bf16[32,512]{1,0:T(8,128)(2,1)S(1)}, u32[]{:S(2)}, u32[]{:S(2)}) collective-permute-start(bf16[32,512]{1,0:T(8,128)(2,1)} %param.18), channel_id=1, source_target_pairs={{0,0},{1,4},{2,8},{3,12},{4,16},{5,20},{6,24},{7,28},{8,32},{9,36}... | collective-permute-start | bytes 98312 | tf_op jit(solution)/shard_map/ppermute | solution.py:324
  13.3 2.0 collective-permute-done.9
  15.3 0.6 copy-done.13
  15.9 0.0 all-gather.2.cloned.1.call-update
  15.9 0.0 reduce-scatter.2.cloned.1.call-start
  16.0 1.6 copy-done
  17.6 0.9 copy-done.3
  18.5 4.4 features.1
  22.9 5.8 %collective-permute-start.4 = (bf16[128,2048]{1,0:T(8,128)(2,1)S(1)}, bf16[128,2048]{1,0:T(8,128)(2,1)S(1)}, u32[]{:S(2)}, u32[]{:S(2)}) collective-permute-start(bf16[128,2048]{1,0:T(8,128)(2,1)S(1)} %get-tuple-element.20), channel_id=1, source_target_pairs={{0,2},{1,3},{2,0},{3,1},{4,6},{5,7},{6,4},{7,5},{8,10},{9,11},{10,... | collective-permute-start | bytes 1572872 | tf_op jit(solution)/shard_map/ppermute | solution.py:322
  28.7 0.0 collective-permute-start.5
  28.7 8.2 %attend.1 = (bf16[512,2048]{1,0:T(8,128)(2,1)S(1)}, f32[4,8,128]{2,1,0:T(8,128)S(1)}) custom-call(s32[1,8]{1,0:T(1,128)S(1)} %copy-done.4, bf16[512,2048]{1,0:T(8,128)(2,1)S(1)} %copy-done.6, bf16[512,256]{1,0:T(8,128)(2,1)S(1)} %copy-done.10, bf16[512,256]{1,0:T(8,128)(2,1)S(1)} %copy-done.11), custom_call_target="tpu_custom_call" | custom-call | flops 1610612736 | bytes 4194304 | tf_op jit(solution)/shard_map/attend/pallas_call | solution.py:131
  36.9 1.4 copy-done.1
  38.3 1.6 collective-permute-start.1
  39.9 0.4 collective-permute-start.2
  40.3 12.3 %collective-permute-done.1 = f32[4,128]{1,0:T(4,128)S(1)} collective-permute-done((f32[4,128]{1,0:T(4,128)S(1)}, f32[4,128]{1,0:T(4,128)S(1)}, u32[]{:S(2)}, u32[]{:S(2)}) %collective-permute-start.1) | collective-permute-done | bytes 2080 | tf_op jit(solution)/shard_map/ppermute | solution.py:322
  52.6 0.6 collective-permute-start
  53.1 0.8 constant_dynamic-slice_fusion.gain_ref
  54.0 0.0 collective-permute-done.2
  54.0 0.0 collective-permute-done.5.refs_3_
  54.0 0.0 copy-start.2
  54.0 0.0 copy-start.5
  54.0 3.4 merge.1
  57.4 1.4 copy-done.8
  58.8 1.5 collective-permute-start.7
  60.3 0.4 collective-permute-start.8
  60.7 0.1 collective-permute-start.6
  60.8 0.9 fold.1.refs_0_
  61.7 1.9 collective-permute-start.12
  63.6 0.7 dynamic_slice.10
  64.3 0.5 collective-permute-start.10
  64.8 3.5 collective-permute-done.12.refs_3_
  68.3 3.2 collective-permute-done.11.refs_2_
  71.5 67.8 %all-gather.2.cloned.1.call-done.weight_ref = bf16[2048,512]{1,0:T(8,128)(2,1)} async-done(((bf16[32,512]{1,0:T(8,128)(2,1)}), bf16[2048,512]{1,0:T(8,128)(2,1)}) %all-gather.2.cloned.1.call-update) | async-done | bytes 2097168 | tf_op jit(solution)/shard_map/all_gather | solution.py:325
  139.3 1.6 copy-done.7
  140.9 1.6 copy-done.9
  142.5 4.8 project.1
  147.3 0.0 reduce-scatter.2.cloned.1.call-update
  147.3 4.1 collective-permute-start.13
  151.4 0.3 collective-permute-start.14
  151.7 1.4 collective-permute-start.15
  153.1 313.4 %reduce-scatter.2.cloned.1.call-done = f32[32,512]{1,0:T(8,128)} async-done(((f32[2048,512]{1,0:T(8,128)}), f32[32,512]{1,0:T(8,128)}) %reduce-scatter.2.cloned.1.call-update) | async-done | bytes 65552 | tf_op jit(solution)/shard_map/reduce_scatter | solution.py:348
  466.5 28.9 %collective-permute-start.16 = (f32[32,512]{1,0:T(8,128)}, f32[32,512]{1,0:T(8,128)S(1)}, u32[]{:S(2)}, u32[]{:S(2)}) collective-permute-start(f32[32,512]{1,0:T(8,128)} %reduce-scatter.2.cloned.1.call-done), channel_id=1, source_target_pairs={{0,0},{4,1},{8,2},{12,3},{16,4},{20,5},{24,6},{28,7},{32,8},{36,9}... | collective-permute-start | bytes 196616 | tf_op jit(solution)/shard_map/ppermute | solution.py:349
  495.4 1.6 spread.1
  497.1 20.6 %collective-permute-done.16 = f32[32,512]{1,0:T(8,128)S(1)} collective-permute-done((f32[32,512]{1,0:T(8,128)}, f32[32,512]{1,0:T(8,128)S(1)}, u32[]{:S(2)}, u32[]{:S(2)}) %collective-permute-start.16) | collective-permute-done | bytes 65568 | tf_op jit(solution)/shard_map/ppermute | solution.py:349
  517.7 0.1 multiply_reduce_fusion
  517.8 1.3 dynamic-slice_divide_fusion
  519.1 0.6 copy.17
  (37 shorter events, 0.1 us)
Async XLA Ops:
  7.2 132.2 %all-gather.2.cloned.1.call-start = ((), (), s32[]{:S(2)}) async-start(), calls=%async_computation.1 | async-start | bytes 2129920 | tf_op jit(solution)/shard_map/all_gather | solution.py:325
  7.2 8.1 %collective-permute-start.9 = (bf16[32,512]{1,0:T(8,128)(2,1)}, bf16[32,512]{1,0:T(8,128)(2,1)S(1)}, u32[]{:S(2)}, u32[]{:S(2)}) collective-permute-start(bf16[32,512]{1,0:T(8,128)(2,1)} %param.18), channel_id=1, source_target_pairs={{0,0},{1,4},{2,8},{3,12},{4,16},{5,20},{6,24},{7,28},{8,32},{9,36}... | collective-permute-start | bytes 98312 | tf_op jit(solution)/shard_map/ppermute | solution.py:324
  15.3 0.6 copy-start.13
  15.9 450.6 %reduce-scatter.2.cloned.1.call-start = ((), (), s32[]{:S(2)}) async-start(), calls=%async_computation.2 | async-start | bytes 4259840 | tf_op jit(solution)/shard_map/reduce_scatter | solution.py:348
  16.0 1.6 copy-start
  17.6 0.9 copy-start.3
  18.5 10.2 %copy-start.4 = (s32[1,8]{1,0:T(1,128)S(1)}, s32[1,8]{1,0:T(1,128)}, u32[]{:S(2)}) copy-start(s32[1,8]{1,0:T(1,128)} %lengths_ref.5) | copy-start | bytes 100
  18.5 10.2 %copy-start.6 = (bf16[512,2048]{1,0:T(8,128)(2,1)S(1)}, bf16[512,2048]{1,0:T(8,128)(2,1)}, u32[]{:S(2)}) copy-start(bf16[512,2048]{1,0:T(8,128)(2,1)} %query_ref.1) | copy-start | bytes 6291460
  18.5 10.2 %copy-start.10 = (bf16[512,256]{1,0:T(8,128)(2,1)S(1)}, bf16[512,256]{1,0:T(8,128)(2,1)}, u32[]{:S(2)}) copy-start(bf16[512,256]{1,0:T(8,128)(2,1)} %key_ref.1) | copy-start | bytes 786436
  18.5 10.2 %copy-start.11 = (bf16[512,256]{1,0:T(8,128)(2,1)S(1)}, bf16[512,256]{1,0:T(8,128)(2,1)}, u32[]{:S(2)}) copy-start(bf16[512,256]{1,0:T(8,128)(2,1)} %value_ref.1) | copy-start | bytes 786436
  22.9 31.1 %collective-permute-start.3 = (bf16[128,2048]{1,0:T(8,128)(2,1)}, bf16[128,2048]{1,0:T(8,128)(2,1)S(1)}, u32[]{:S(2)}, u32[]{:S(2)}) collective-permute-start(bf16[128,2048]{1,0:T(8,128)(2,1)} %get-tuple-element.19), channel_id=1, source_target_pairs={{0,1},{1,0},{2,3},{3,2},{4,5},{5,4},{6,7},{7,6},{8,9},{9,8},{10,11... | collective-permute-start | bytes 1572872 | tf_op jit(solution)/shard_map/ppermute | solution.py:322
  22.9 31.1 %collective-permute-start.4 = (bf16[128,2048]{1,0:T(8,128)(2,1)S(1)}, bf16[128,2048]{1,0:T(8,128)(2,1)S(1)}, u32[]{:S(2)}, u32[]{:S(2)}) collective-permute-start(bf16[128,2048]{1,0:T(8,128)(2,1)S(1)} %get-tuple-element.20), channel_id=1, source_target_pairs={{0,2},{1,3},{2,0},{3,1},{4,6},{5,7},{6,4},{7,5},{8,10},{9,11},{10,... | collective-permute-start | bytes 1572872 | tf_op jit(solution)/shard_map/ppermute | solution.py:322
  28.7 25.3 %collective-permute-start.5 = (bf16[128,2048]{1,0:T(8,128)(2,1)S(1)}, bf16[128,2048]{1,0:T(8,128)(2,1)S(1)}, u32[]{:S(2)}, u32[]{:S(2)}) collective-permute-start(bf16[128,2048]{1,0:T(8,128)(2,1)S(1)} %get-tuple-element.21), channel_id=1, source_target_pairs={{0,3},{1,2},{2,1},{3,0},{4,7},{5,6},{6,5},{7,4},{8,11},{9,10},{10,... | collective-permute-start | bytes 1572872 | tf_op jit(solution)/shard_map/ppermute | solution.py:322
  36.9 1.4 copy-start.1
  38.3 14.3 %collective-permute-start.1 = (f32[4,128]{1,0:T(4,128)S(1)}, f32[4,128]{1,0:T(4,128)S(1)}, u32[]{:S(2)}, u32[]{:S(2)}) collective-permute-start(f32[4,128]{1,0:T(4,128)S(1)} %slice_bitcast_fusion.1), channel_id=1, source_target_pairs={{0,2},{1,3},{2,0},{3,1},{4,6},{5,7},{6,4},{7,5},{8,10},{9,11},{10,... | collective-permute-start | bytes 6152 | tf_op jit(solution)/shard_map/ppermute | solution.py:322
  39.9 14.1 %collective-permute-start.2 = (f32[4,128]{1,0:T(4,128)S(1)}, f32[4,128]{1,0:T(4,128)S(1)}, u32[]{:S(2)}, u32[]{:S(2)}) collective-permute-start(f32[4,128]{1,0:T(4,128)S(1)} %slice_bitcast_fusion.1), channel_id=1, source_target_pairs={{0,3},{1,2},{2,1},{3,0},{4,7},{5,6},{6,5},{7,4},{8,11},{9,10},{10,... | collective-permute-start | bytes 6152 | tf_op jit(solution)/shard_map/ppermute | solution.py:322
  52.6 1.4 collective-permute-start
  54.0 6.8 %copy-start.2 = (bf16[3,128,512]{2,1,0:T(8,128)(2,1)S(1)}, bf16[3,128,512]{2,1,0:T(8,128)(2,1)}, u32[]{:S(2)}) copy-start(bf16[3,128,512]{2,1,0:T(8,128)(2,1)} %cotangent_ref.1) | copy-start | bytes 1179652
  54.0 6.8 %copy-start.5 = (s32[3]{0:T(128)S(1)}, s32[3]{0:T(128)}, u32[]{:S(2)}) copy-start(s32[3]{0:T(128)} %offsets_ref.3) | copy-start | bytes 40
  57.4 1.4 copy-start.8
  58.8 5.5 %collective-permute-start.7 = (f32[4,128]{1,0:T(4,128)S(1)}, f32[4,128]{1,0:T(4,128)S(1)}, u32[]{:S(2)}, u32[]{:S(2)}) collective-permute-start(f32[4,128]{1,0:T(4,128)S(1)} %slice_bitcast_fusion), channel_id=1, source_target_pairs={{0,2},{1,3},{2,0},{3,1},{4,6},{5,7},{6,4},{7,5},{8,10},{9,11},{10,... | collective-permute-start | bytes 6152 | tf_op jit(solution)/shard_map/ppermute | solution.py:322
  60.3 4.5 collective-permute-start.8
  60.7 4.1 collective-permute-start.6
  61.7 6.6 %collective-permute-start.12 = (bf16[160,512]{1,0:T(8,128)(2,1)S(1)}, bf16[160,512]{1,0:T(8,128)(2,1)S(1)}, u32[]{:S(2)}, u32[]{:S(2)}) collective-permute-start(bf16[160,512]{1,0:T(8,128)(2,1)S(1)} %fold.1.refs_0_), channel_id=1, source_target_pairs={{0,3},{1,2},{2,1},{3,0},{4,7},{5,6},{6,5},{7,4},{8,11},{9,10},{10,... | collective-permute-start | bytes 491528 | tf_op jit(solution)/shard_map/ppermute | solution.py:322
  63.6 7.9 %collective-permute-start.11 = (bf16[160,512]{1,0:T(8,128)(2,1)S(1)}, bf16[160,512]{1,0:T(8,128)(2,1)S(1)}, u32[]{:S(2)}, u32[]{:S(2)}) collective-permute-start(bf16[160,512]{1,0:T(8,128)(2,1)S(1)} %fold.1.refs_0_), channel_id=1, source_target_pairs={{0,2},{1,3},{2,0},{3,1},{4,6},{5,7},{6,4},{7,5},{8,10},{9,11},{10,... | collective-permute-start | bytes 491528 | tf_op jit(solution)/shard_map/ppermute | solution.py:322
  64.3 7.2 %collective-permute-start.10 = (bf16[160,512]{1,0:T(8,128)(2,1)S(1)}, bf16[160,512]{1,0:T(8,128)(2,1)S(1)}, u32[]{:S(2)}, u32[]{:S(2)}) collective-permute-start(bf16[160,512]{1,0:T(8,128)(2,1)S(1)} %fold.1.refs_0_), channel_id=1, source_target_pairs={{0,1},{1,0},{2,3},{3,2},{4,5},{5,4},{6,7},{7,6},{8,9},{9,8},{10,11... | collective-permute-start | bytes 491528 | tf_op jit(solution)/shard_map/ppermute | solution.py:322
  139.3 1.6 copy-start.7
  140.9 1.6 copy-start.9
  147.3 370.4 %copy-start.12 = (bf16[32,512]{1,0:T(8,128)(2,1)S(1)}, bf16[32,512]{1,0:T(8,128)(2,1)}, u32[]{:S(2)}) copy-start(bf16[32,512]{1,0:T(8,128)(2,1)} %param.18) | copy-start | bytes 98308
  147.3 348.1 %collective-permute-start.13 = (bf16[160,512]{1,0:T(8,128)(2,1)S(1)}, bf16[160,512]{1,0:T(8,128)(2,1)S(1)}, u32[]{:S(2)}, u32[]{:S(2)}) collective-permute-start(bf16[160,512]{1,0:T(8,128)(2,1)S(1)} %get-tuple-element.25), channel_id=1, source_target_pairs={{0,1},{1,0},{2,3},{3,2},{4,5},{5,4},{6,7},{7,6},{8,9},{9,8},{10,11... | collective-permute-start | bytes 491528 | tf_op jit(solution)/shard_map/ppermute | solution.py:322
  151.4 344.0 %collective-permute-start.14 = (bf16[160,512]{1,0:T(8,128)(2,1)S(1)}, bf16[160,512]{1,0:T(8,128)(2,1)S(1)}, u32[]{:S(2)}, u32[]{:S(2)}) collective-permute-start(bf16[160,512]{1,0:T(8,128)(2,1)S(1)} %get-tuple-element.26), channel_id=1, source_target_pairs={{0,2},{1,3},{2,0},{3,1},{4,6},{5,7},{6,4},{7,5},{8,10},{9,11},{10,... | collective-permute-start | bytes 491528 | tf_op jit(solution)/shard_map/ppermute | solution.py:322
  151.7 343.7 %collective-permute-start.15 = (bf16[160,512]{1,0:T(8,128)(2,1)S(1)}, bf16[160,512]{1,0:T(8,128)(2,1)S(1)}, u32[]{:S(2)}, u32[]{:S(2)}) collective-permute-start(bf16[160,512]{1,0:T(8,128)(2,1)S(1)} %get-tuple-element.27), channel_id=1, source_target_pairs={{0,3},{1,2},{2,1},{3,0},{4,7},{5,6},{6,5},{7,4},{8,11},{9,10},{10,... | collective-permute-start | bytes 491528 | tf_op jit(solution)/shard_map/ppermute | solution.py:322
  466.5 51.1 %collective-permute-start.16 = (f32[32,512]{1,0:T(8,128)}, f32[32,512]{1,0:T(8,128)S(1)}, u32[]{:S(2)}, u32[]{:S(2)}) collective-permute-start(f32[32,512]{1,0:T(8,128)} %reduce-scatter.2.cloned.1.call-done), channel_id=1, source_target_pairs={{0,0},{4,1},{8,2},{12,3},{16,4},{20,5},{24,6},{28,7},{32,8},{36,9}... | collective-permute-start | bytes 196616 | tf_op jit(solution)/shard_map/ppermute | solution.py:349
Sparse Core Ops, SparseCore 0:
  16.1 123.2 all-gather.1
  147.4 319.0 reduce-scatter.1

commit v2 on v1

--- a/solution.py
+++ b/solution.py
@@ -3,6 +3,7 @@
 
 import jax
 import jax.numpy as jnp
+import numpy as np
 from jax import lax
 from jax.experimental import pallas as pl
 from jax.experimental.pallas import tpu as pltpu
@@ -12,12 +13,84 @@
 STEPS = 3
 OFFMAX = 32
 EPSILON = 1e-05
-VMEM_LIMIT = 48 * 1024 * 1024
+VMEM_LIMIT = 20 * 1024 * 1024
 
 VMEM = pl.BlockSpec(memory_space=pltpu.VMEM)
 SMEM = pl.BlockSpec(memory_space=pltpu.SMEM)
 F32 = jnp.float32
 BF16 = jnp.bfloat16
+
+
+SIDES = {64: (8, 4, 2)}
+
+
+def sides_of(n):
+    return SIDES.get(n, (1, 1, n))
+
+
+def groups_along(n, *sides):
+    sizes = sides_of(n)
+    where = np.moveaxis(np.arange(n).reshape(sizes), sides, range(-len(sides), 0))
+    return where.reshape(-1, math.prod(sizes[side] for side in sides)).tolist()
+
+
+def block_order(n, tn):
+    nz, ny, nx = sides_of(n)
+    order = np.arange(n).reshape(ny, nz, nx)
+    if nz == 2 * tn and n == ny * nx * tn * 2:
+        for y in range(ny):
+            for z in range(nz):
+                for x in range(nx):
+                    order[y, z, x] = (((z // tn) * ny + y) * nx + x) * tn + z % tn
+    return order
+
+
+def place_weight(weight):
+    n, tn = lax.axis_size("dp"), lax.axis_size("tensor")
+    nz, ny, nx = sides_of(n)
+    pairs = []
+    for j in range(tn):
+        for q in range(n):
+            y, z, x = q // (nz * nx), q // nx % nz, q % nx
+            pairs.append((j * n + q, ((z * ny + y) * nx + x) * tn + j))
+    return lax.ppermute(weight, ("dp", "tensor"), pairs)
+
+
+def gather_weight(weight, sides):
+    groups = groups_along(lax.axis_size("dp"), *sides)
+    if len(groups[0]) > 1:
+        weight = lax.all_gather(weight, "dp", axis=0, tiled=True, axis_index_groups=groups)
+    return weight
+
+
+def reduce_grad(grad):
+    n, tn = lax.axis_size("dp"), lax.axis_size("tensor")
+    nz, ny, nx = sides_of(n)
+    columns = grad.shape[1]
+    for side in (1, 0):
+        count = sides_of(n)[side]
+        if count > 1:
+            if grad.dtype != BF16:
+                grad = grad.astype(BF16)
+            grad = lax.all_to_all(grad, "dp", 0, 0, tiled=True, axis_index_groups=groups_along(n, side))
+            grad = jnp.sum(grad.reshape(count, -1, columns).astype(F32), axis=0)
+    grad = grad.astype(F32)
+    rows = grad.shape[0] // nx
+    order = block_order(n, tn)
+    x = lax.axis_index("dp") % nx
+    total = None
+    for turn in range(nx):
+        pairs = []
+        for z in range(nz):
+            for y in range(ny):
+                for x0 in range(nx):
+                    for j in range(tn):
+                        block = j * n + int(order[y, z, (x0 + turn) % nx])
+                        pairs.append((((z * ny + y) * nx + x0) * tn + j, block))
+        part = lax.dynamic_slice(grad, ((x + turn) % nx * rows, 0), (rows, columns))
+        part = lax.ppermute(part, ("dp", "tensor"), pairs)
+        total = part if total is None else total + part
+    return total
 
 
 def segment_start(places, lengths_ref):
@@ -121,7 +194,7 @@
             high_ref[:, at] = out
             out = out.astype(F32)
             squares = squares + out * out
-    square_ref[0] = lane_sums(squares)
+    square_ref[...] = lane_sums(squares)
 
 
 def attend(lengths, queries, keys, values):
@@ -139,11 +212,11 @@
         ],
         out_specs=[
             pl.BlockSpec((block, width), lambda b: (b, 0)),
-            pl.BlockSpec((1, 8, block), lambda b: (b, 0, 0)),
+            pl.BlockSpec((8, block), lambda b: (0, b)),
         ],
         out_shape=[
             jax.ShapeDtypeStruct((pack, width), BF16),
-            jax.ShapeDtypeStruct((pack // block, 8, block), F32),
+            jax.ShapeDtypeStruct((8, pack), F32),
         ],
         compiler_params=pltpu.CompilerParams(vmem_limit_bytes=VMEM_LIMIT),
         cost_estimate=pl.CostEstimate(
@@ -183,69 +256,105 @@
     )(place, lengths, offsets, cotangent)
 
 
-def merge_kernel(width, place_ref, square_ref, gain_ref, high_ref, *refs):
-    tn = len(refs) - 2
-    parts, out_ref, out_square_ref = refs[:tn], refs[tn], refs[tn + 1]
+def merge_kernel(width, tn, place_ref, gain_ref, high_ref, *refs):
+    parts, square_refs, out_ref, out_square_ref = refs[:tn], refs[tn:2 * tn], refs[2 * tn], refs[2 * tn + 1]
     j = place_ref[0]
     rows = parts[0].shape[0]
+    piece = high_ref.shape[1]
+    squares = square_refs[0][...]
+    for s in range(1, tn):
+        squares = squares + square_refs[s][...]
+    scales = lax.rsqrt(squares / width + EPSILON)
+    for b in range(tn):
+        out_square_ref[:, b * rows:(b + 1) * rows] = scales[:, b * rows:(b + 1) * rows]
     for s in range(tn):
-        b = j ^ s
-        at = pl.ds(pl.multiple_of(b * rows, rows), rows)
-        scale = lax.rsqrt(column(square_ref[pl.ds(b, 1), :]) / width + EPSILON)
+        first = pl.multiple_of((j ^ s) * rows, rows)
+        at = pl.ds(first, rows)
+        scale = column(out_square_ref[0:1, at])
         total = jnp.zeros((rows, 128), F32)
-        for c in range(0, high_ref.shape[1], 128):
+        for c in range(0, piece, 128):
             cols = slice(c, c + 128)
-            merged = (parts[s][:, cols].astype(F32)
-                      + high_ref[at, cols].astype(F32) * scale * gain_ref[:, cols]).astype(BF16)
+            gain = gain_ref[2:3, pl.ds(pl.multiple_of(j * piece + c, 128), 128)]
+            merged = (parts[s][:, cols].astype(F32) + high_ref[at, cols].astype(F32) * scale * gain).astype(BF16)
             out_ref[at, cols] = merged
             merged = merged.astype(F32)
             total = total + merged * merged
-        out_square_ref[b] = lane_sums(total)
-
-
-def merge(place, squares, gain, high, parts, width):
+        out_square_ref[:, at] = lane_sums(total)
+
+
+def merge(place, gain, high, parts, squares, width):
     pack, piece = high.shape
-    return pl.pallas_call(
-        functools.partial(merge_kernel, width),
-        in_specs=[SMEM, VMEM, VMEM, VMEM] + [VMEM] * len(parts),
+    tn = len(parts)
+    return pl.pallas_call(
+        functools.partial(merge_kernel, width, tn),
+        in_specs=[SMEM] + [VMEM] * (2 + 2 * tn),
         out_specs=[VMEM, VMEM],
         out_shape=[
             jax.ShapeDtypeStruct((pack, piece), BF16),
-            jax.ShapeDtypeStruct((len(parts), 8, pack // len(parts)), F32),
+            jax.ShapeDtypeStruct((8, pack), F32),
         ],
         compiler_params=pltpu.CompilerParams(vmem_limit_bytes=VMEM_LIMIT),
         cost_estimate=pl.CostEstimate(flops=8 * pack * piece, bytes_accessed=6 * pack * piece, transcendentals=0),
         name="merge",
-    )(place, squares, gain, high, *parts)
-
-
-def project(place, squares, gain, merged, weight, folds, width):
+    )(place, gain, high, *parts, *squares)
+
+
+def grads(place, gain, merged, folds, squares, width, order):
     pack, piece = merged.shape
-    tn = len(folds)
+    tn = len(squares)
     rows = pack // tn
-    vw = weight.shape[1]
-
-    def kernel(place_ref, square_ref, gain_ref, merged_ref, weight_ref, *refs):
-        fold_refs = refs[:tn]
-        grad_ref = refs[tn]
-        value_refs = refs[tn + 1:2 * tn + 1]
-        hidden_ref, fold_ref, total_ref = refs[2 * tn + 1:]
+    vw = folds[0].shape[1]
+    blocks = order.reshape(-1)
+    size = piece // blocks.size
+
+    def kernel(place_ref, gain_ref, merged_ref, *refs):
+        fold_refs, square_refs, (grad_ref, hidden_ref, fold_ref) = refs[:tn], refs[tn:2 * tn], refs[2 * tn:]
         j = place_ref[0]
+        squares = square_refs[0][...]
+        for s in range(1, tn):
+            squares = squares + square_refs[s][...]
+        scales = lax.rsqrt(squares / width + EPSILON)
         for b in range(tn):
             at = slice(b * rows, (b + 1) * rows)
-            scale = lax.rsqrt(column(square_ref[b:b + 1, :]) / width + EPSILON)
+            scale = column(scales[0:1, at])
             for c in range(0, piece, 128):
                 cols = slice(c, c + 128)
-                hidden_ref[at, cols] = (merged_ref[at, cols].astype(F32) * scale * gain_ref[:, cols]).astype(BF16)
+                gain = gain_ref[:, pl.ds(pl.multiple_of(j * piece + c, 128), 128)]
+                hidden_ref[at, cols] = (merged_ref[at, cols].astype(F32) * scale * gain).astype(BF16)
         fold_ref[...] = jnp.zeros_like(fold_ref)
         for s in range(tn):
             at = pl.ds(pl.multiple_of((j ^ s) * rows, rows), rows + OFFMAX)
             fold_ref[at, :] = fold_ref[at, :] + fold_refs[s][...].astype(F32)
         folded = fold_ref[OFFMAX:, :].astype(BF16)
+        chunk = max(256, size)
+        for c in range(0, piece, chunk):
+            part = lax.dot_general(
+                hidden_ref[:, c:c + chunk], folded, (((0,), (0,)), ((), ())), preferred_element_type=F32).astype(BF16)
+            for q in range(c // size, (c + chunk) // size):
+                to = int(np.argmax(blocks == q)) * size
+                grad_ref[to:to + size, :] = part[q * size - c:(q + 1) * size - c, :]
+
+    return pl.pallas_call(
+        kernel,
+        in_specs=[SMEM] + [VMEM] * (2 + 2 * tn),
+        out_specs=[VMEM] * 2,
+        out_shape=[jax.ShapeDtypeStruct((piece, vw), BF16), jax.ShapeDtypeStruct((pack, piece), BF16)],
+        scratch_shapes=[pltpu.VMEM((pack + OFFMAX, vw), F32)],
+        compiler_params=pltpu.CompilerParams(vmem_limit_bytes=VMEM_LIMIT),
+        cost_estimate=pl.CostEstimate(flops=2 * pack * piece * vw, bytes_accessed=8 * pack * piece, transcendentals=0),
+        name="grads",
+    )(place, gain, merged, *folds, *squares)
+
+
+def project(place, hidden, weight, tn):
+    pack, piece = hidden.shape
+    rows = pack // tn
+    vw = weight.shape[1]
+
+    def kernel(place_ref, hidden_ref, weight_ref, *refs):
+        value_refs, total_ref = refs[:tn], refs[tn]
+        j = place_ref[0]
         total_ref[0:OFFMAX, :] = jnp.zeros((OFFMAX, vw), F32)
-        for c in range(0, piece, 256):
-            grad_ref[c:c + 256, :] = lax.dot_general(
-                hidden_ref[:, c:c + 256], folded, (((0,), (0,)), ((), ())), preferred_element_type=F32)
         for c in range(0, pack, 256):
             total_ref[OFFMAX + c:OFFMAX + c + 256, :] = jnp.dot(
                 hidden_ref[c:c + 256, :], weight_ref[...], preferred_element_type=F32)
@@ -255,19 +364,14 @@
 
     return pl.pallas_call(
         kernel,
-        in_specs=[SMEM] + [VMEM] * (4 + tn),
-        out_specs=[VMEM] * (1 + tn),
-        out_shape=[jax.ShapeDtypeStruct((piece, vw), F32)]
-        + [jax.ShapeDtypeStruct((rows + OFFMAX, vw), F32 if s == 0 else BF16) for s in range(tn)],
-        scratch_shapes=[
-            pltpu.VMEM((pack, piece), BF16),
-            pltpu.VMEM((pack + OFFMAX, vw), F32),
-            pltpu.VMEM((pack + OFFMAX, vw), F32),
-        ],
-        compiler_params=pltpu.CompilerParams(vmem_limit_bytes=VMEM_LIMIT),
-        cost_estimate=pl.CostEstimate(flops=4 * pack * piece * vw, bytes_accessed=12 * pack * piece, transcendentals=0),
+        in_specs=[SMEM] + [VMEM] * 2,
+        out_specs=[VMEM] * tn,
+        out_shape=[jax.ShapeDtypeStruct((rows + OFFMAX, vw), F32 if s == 0 else BF16) for s in range(tn)],
+        scratch_shapes=[pltpu.VMEM((pack + OFFMAX, vw), F32)],
+        compiler_params=pltpu.CompilerParams(vmem_limit_bytes=VMEM_LIMIT),
+        cost_estimate=pl.CostEstimate(flops=2 * pack * piece * vw, bytes_accessed=4 * pack * piece, transcendentals=0),
         name="project",
-    )(place, squares, gain, merged, weight, *folds)
+    )(place, hidden, weight)
 
 
 def spread(place, lengths, offsets, parts):
@@ -321,32 +425,30 @@
     def swapped(values, s):
         return lax.ppermute(values, "tensor", [(a, a ^ s) for a in range(tn)])
 
-    moved = lax.ppermute(draft_weight, both, [(r, (r % n) * tn + r // n) for r in range(n * tn)])
-    weight = lax.all_gather(moved, "dp", axis=0, tiled=True)
-
+    own_weight = place_weight(draft_weight)
+    low_feature, _ = lax.optimization_barrier((low_feature, own_weight))
+    sent = features(place, low_feature, mid_feature, merging_gain, tn)
+    parts = [sent[0]] + [swapped(sent[s], s) for s in range(1, tn)]
+    some_weight = gather_weight(own_weight, (0, 2))
+
+    high, squares = attend(doc_lengths, target_queries, target_keys, target_values)
+    squares = [squares] + [swapped(squares, s) for s in range(1, tn)]
+    cotangent, _ = lax.optimization_barrier((cotangent, high))
     folded = fold(place, doc_lengths, step_offsets, cotangent)
     folds = [folded] + [swapped(folded, s) for s in range(1, tn)]
-    sent = features(place, low_feature, mid_feature, merging_gain, tn)
-    parts = [sent[0]] + [swapped(sent[s], s) for s in range(1, tn)]
-
-    high, high_squares = attend(doc_lengths, target_queries, target_keys, target_values)
-
-    def summed(squares):
-        squares = squares[:, 0, :]
-        total = squares
-        for s in range(1, tn):
-            total = total + swapped(squares, s)
-        return total
-
-    own_gain = lax.dynamic_slice(merging_gain, (2, j * piece), (1, piece))
-    merged, squares = merge(place, summed(high_squares), own_gain, high, parts, width)
-    own_gain = lax.dynamic_slice(draft_gain, (j * piece,), (piece,)).reshape(1, piece)
-    grad, *values = project(place, summed(squares), own_gain, merged, weight, folds, width)
+    gain, _ = lax.optimization_barrier((merging_gain, folds[1]))
+    merged, squares = merge(place, gain, high, parts, squares, width)
+    some_weight, _ = lax.optimization_barrier((some_weight, merged))
+    weight = gather_weight(some_weight, (1,))
+    squares = [squares] + [swapped(squares, s) for s in range(1, tn)]
+    grad, hidden = grads(
+        place, draft_gain.reshape(1, width), merged, folds, squares, width, block_order(n, tn))
+    weight_grad = reduce_grad(grad)
+
+    values = project(place, hidden, weight, tn)
     values = [values[0]] + [swapped(values[s], s) for s in range(1, tn)]
     draft_values = spread(place, doc_lengths, step_offsets, values)
 
-    grad = lax.psum_scatter(grad, "dp", scatter_dimension=0, tiled=True)
-    weight_grad = lax.ppermute(grad, both, [((r % n) * tn + r // n, r) for r in range(n * tn)])
     rows = weight_grad.shape[0]
     gain = lax.dynamic_slice(draft_gain, (flat * rows,), (rows,))
     gain_grad = jnp.sum(weight_grad * draft_weight.astype(F32), axis=1) / gain

time: 534 us -> 207 us (0.39); the launches traced: 527 us -> 206 us
  waiting for transfers between devices: 423 us -> 36.2 us
  blocking collectives: 0 us -> 71 us
    reduce_scatter x1 -> x0, waiting for transfers between devices: 313 us -> none  [body(): grad = lax.psum_scatter(grad, 'dp', scatter_dimension=0, tiled=True)]
    all_gather x1, waiting for transfers between devices: 67.8 us -> 0.02 us  [gather_weight(): lax.all_gather(weight, 'dp', axis=0, tiled=True, axis_index_groups=groups)]
    all_gather x0 -> x1, blocking collectives: none -> 40.7 us  [gather_weight(): lax.all_gather(weight, 'dp', axis=0, tiled=True, axis_index_groups=groups)]
    all_to_all x0 -> x1, blocking collectives: none -> 30.3 us  [reduce_grad(): lax.all_to_all(grad, 'dp', 0, 0, tiled=True, axis_index_groups=groups_alo...]
    ppermute x2 -> x3, waiting for transfers between devices: 22.6 us -> 5.28 us  [the longest x2 3.24 us: reduce_grad(): part = lax.ppermute(part, ('dp', 'tensor'), pairs)]
    all_to_all x0 -> x1, waiting for transfers between devices: none -> 12.1 us  [reduce_grad(): lax.all_to_all(grad, 'dp', 0, 0, tiled=True, axis_index_groups=groups_alo...]
    ppermute x2 -> x3, starting transfers between devices: 34.9 us -> 32.7 us  [the longest x2 26.6 us: reduce_grad(): part = lax.ppermute(part, ('dp', 'tensor'), pairs)]
  transfers between devices with their start and end apart: 19 -> 20, of which waited for: 7 -> 7; matrix products, arithmetic and copies ran while one was open for 0% -> 2% of each run, Pallas kernels for 4% -> 7%
where the time goes in v2:
time: 207 us; the launch traced here: 206 us
  blocking collectives  71 us (34%)
  starting transfers between devices  52.5 us (25%)
  waiting for transfers between devices  36.2 us (17%)
  Pallas kernels  19 us (9%)
  between operations  14.2 us (7%)
  local copies, waits for them, and re-layouts  8.67 us (4%)
  other arithmetic  4.28 us (2%)
    all_gather x1, blocking collectives, gather_weight(): lax.all_gather(weight, 'dp', axis=0, tiled=True, axis_index_groups=groups)  40.7 us
    all_to_all x1, blocking collectives, reduce_grad(): lax.all_to_all(grad, 'dp', 0, 0, tiled=True, axis_index_groups=groups_alo...  30.3 us
    ppermute x2, starting transfers between devices, reduce_grad(): part = lax.ppermute(part, ('dp', 'tensor'), pairs)  26.6 us
    ppermute x15, waiting for transfers between devices, swapped(): return lax.ppermute(values, 'tensor', [(a, a ^ s) for a in range(tn)])  18.8 us
    ppermute x15, starting transfers between devices, swapped(): return lax.ppermute(values, 'tensor', [(a, a ^ s) for a in range(tn)])  15.9 us
    all_to_all x1, waiting for transfers between devices, reduce_grad(): lax.all_to_all(grad, 'dp', 0, 0, tiled=True, axis_index_groups=groups_alo...  12.1 us
    unnamed x28, local copies, waits for them, and re-layouts  8.65 us
    pallas_call x1, Pallas kernels, attend(): pl.pallas_call(functools.partial(attend_kernel, window), grid=(pack // bl...  8.53 us
  transfers between devices with their start and end apart: 20, of which 7 were waited for; matrix products, arithmetic and copies ran while one was open for 2% of the time, Pallas kernels for 7%

profile of v2, /device:TPU:1, one launch (start us, length us, event | category | flops | bytes accessed | tf_op | source)
XLA Modules:
  0.0 205.8 jit_solution(9460969781558285078)
XLA Ops:
  7.2 0.0 all-gather.2.cloned.1.call-start
  7.2 6.0 %collective-permute-start.1 = (bf16[32,512]{1,0:T(8,128)(2,1)}, bf16[32,512]{1,0:T(8,128)(2,1)S(1)}, u32[]{:S(2)}, u32[]{:S(2)}) collective-permute-start(bf16[32,512]{1,0:T(8,128)(2,1)} %param.18), channel_id=1, source_target_pairs={{0,0},{1,4},{2,32},{3,36},{4,64},{5,68},{6,96},{7,100},{8,128},{9,... | collective-permute-start | bytes 98312 | tf_op jit(solution)/shard_map/ppermute | solution.py:56
  13.3 2.0 collective-permute-done.1
  15.3 1.6 copy-done
  16.9 1.6 copy-done.1
  18.5 0.9 copy-done.3
  19.4 2.0 features.1
  21.4 0.1 collective-permute-start.2
  21.5 5.9 %collective-permute-start.3 = (bf16[128,2048]{1,0:T(8,128)(2,1)S(1)}, bf16[128,2048]{1,0:T(8,128)(2,1)S(1)}, u32[]{:S(2)}, u32[]{:S(2)}) collective-permute-start(bf16[128,2048]{1,0:T(8,128)(2,1)S(1)} %get-tuple-element.27), channel_id=1, source_target_pairs={{0,2},{1,3},{2,0},{3,1},{4,6},{5,7},{6,4},{7,5},{8,10},{9,11},{10,... | collective-permute-start | bytes 1572872 | tf_op jit(solution)/shard_map/ppermute | solution.py:426
  27.4 0.1 collective-permute-start.4
  27.5 8.5 %attend.1 = (bf16[512,2048]{1,0:T(8,128)(2,1)S(1)}, f32[8,512]{1,0:T(8,128)S(1)}) custom-call(s32[1,8]{1,0:T(1,128)S(1)} %copy-done.5, bf16[512,2048]{1,0:T(8,128)(2,1)S(1)} %copy-done.8, bf16[512,256]{1,0:T(8,128)(2,1)S(1)} %copy-done.11, bf16[512,256]{1,0:T(8,128)(2,1)S(1)} %copy-done.12), custom_call_target="tpu_custom_call" | custom-call | flops 1610612736 | bytes 4194304 | tf_op jit(solution)/shard_map/attend/pallas_call | solution.py:204
  36.0 0.9 fold.1.refs_0_
  36.9 0.4 collective-permute-start
  37.3 0.2 collective-permute-start.5
  37.5 1.0 collective-permute-done.5.refs_5_
  38.5 1.5 collective-permute-start.6
  40.1 0.3 collective-permute-start.7
  40.4 10.4 %collective-permute-done.6.refs_6_ = f32[8,512]{1,0:T(8,128)S(1)} collective-permute-done((f32[8,512]{1,0:T(8,128)S(1)}, f32[8,512]{1,0:T(8,128)S(1)}, u32[]{:S(2)}, u32[]{:S(2)}) %collective-permute-start.6) | collective-permute-done | bytes 16416 | tf_op jit(solution)/shard_map/ppermute | solution.py:426
  50.8 1.3 collective-permute-start.8
  52.1 1.5 collective-permute-start.9
  53.6 2.6 %merge.1 = (bf16[512,2048]{1,0:T(8,128)(2,1)S(1)}, f32[8,512]{1,0:T(8,128)S(1)}) custom-call(s32[1]{0:T(128)} %bitcast.place_ref, f32[3,8192]{1,0:T(4,128)S(1)} %copy-done.3, bf16[512,2048]{1,0:T(8,128)(2,1)S(1)} %get-tuple-element.21.high_ref, bf16[128,2048]{1,0:T(8,128)(2,1)S(1)} %get-tuple-element.25.refs_0_, ...), custom_call_target="tpu_custom_call" | custom-call | flops 8388608 | bytes 6291456 | tf_op jit(solution)/shard_map/merge/pallas_call | solution.py:288
  56.2 1.4 copy-done.9
  57.6 0.1 collective-permute-start.10
  57.8 1.3 collective-permute-start.11
  59.1 0.7 collective-permute-start.12
  59.7 40.7 %all_gather.6 = bf16[512,512]{1,0:T(8,128)(2,1)} all-gather(bf16[32,512]{1,0:T(8,128)(2,1)S(1)} %collective-permute-done.1), channel_id=1, replica_groups={{0,4,32,36,64,68,96,100,128,132,160,164,192,196,224,228},{8,12,40,44,72..., dimensions={0}, use_global_device_ids=true | all-gather | bytes 557056 | tf_op jit(solution)/shard_map/all_gather | solution.py:62
  100.4 0.0 all-gather.2.cloned.1.call-update
  100.5 1.6 copy-done.10
  102.1 2.0 grads.1
  104.1 30.3 %all_to_all.18 = bf16[4,512,512]{2,1,0:T(8,128)(2,1)} all-to-all(bf16[4,512,512]{2,1,0:T(8,128)(2,1)S(1)} %bitcast.4), channel_id=1, replica_groups={{0,8,16,24},{4,12,20,28},{32,40,48,56},{36,44,52,60},{64,72,80,88},{68,..., dimensions={0} | all-to-all | bytes 4194304 | tf_op jit(solution)/shard_map/all_to_all | solution.py:75
  134.4 2.9 %reduce_sum.30 = bf16[512,512]{1,0:T(8,128)(2,1)} reduce(bf16[4,512,512]{2,1,0:T(8,128)(2,1)} %all_to_all.18, bf16[]{:T(256)} %constant.33.clone.1), dimensions={0}, to_apply=%region_0.0 | reduce | flops 786432 | bytes 2621442 | tf_op jit(solution)/shard_map/reduce_sum | solution.py:76
  137.3 3.9 %all-to-all-start.1 = ((bf16[8,64,512]{2,1,0:T(8,128)(2,1)}), bf16[8,64,512]{2,1,0:T(8,128)(2,1)S(1)}, u32[]{:S(2)}, u32[]{:S(2)}) async-start(bf16[8,64,512]{2,1,0:T(8,128)(2,1)} %bitcast.3), calls=%async_computation.1 | async-start | bytes 1048576 | tf_op jit(solution)/shard_map/all_to_all | solution.py:75
  141.1 12.1 %all-to-all-done.1 = bf16[8,64,512]{2,1,0:T(8,128)(2,1)S(1)} async-done(((bf16[8,64,512]{2,1,0:T(8,128)(2,1)}), bf16[8,64,512]{2,1,0:T(8,128)(2,1)S(1)}, u32[]{:S(2)}, u32[]{:S(2)}) %all-to-all-start.1) | async-done | bytes 524320 | tf_op jit(solution)/shard_map/all_to_all | solution.py:75
  153.3 0.1 convert_reduce_fusion
  153.4 23.1 %collective-permute-start.16 = (f32[32,512]{1,0:T(8,128)S(1)}, f32[32,512]{1,0:T(8,128)S(1)}, u32[]{:S(2)}, u32[]{:S(2)}) collective-permute-start(f32[32,512]{1,0:T(8,128)S(1)} %get-tuple-element.42), channel_id=1, source_target_pairs={{0,0},{1,64},{2,128},{3,192},{4,4},{5,68},{6,132},{7,196},{8,8},{9... | collective-permute-start | bytes 196616 | tf_op jit(solution)/shard_map/ppermute | solution.py:91
  176.5 3.5 %collective-permute-start.17 = (f32[32,512]{1,0:T(8,128)S(1)}, f32[32,512]{1,0:T(8,128)S(1)}, u32[]{:S(2)}, u32[]{:S(2)}) collective-permute-start(f32[32,512]{1,0:T(8,128)S(1)} %get-tuple-element.41), channel_id=1, source_target_pairs={{0,4},{1,68},{2,132},{3,196},{4,0},{5,64},{6,128},{7,192},{8,12},{... | collective-permute-start | bytes 196616 | tf_op jit(solution)/shard_map/ppermute | solution.py:91
  180.0 3.2 %collective-permute-done.17 = f32[32,512]{1,0:T(8,128)S(1)} collective-permute-done((f32[32,512]{1,0:T(8,128)S(1)}, f32[32,512]{1,0:T(8,128)S(1)}, u32[]{:S(2)}, u32[]{:S(2)}) %collective-permute-start.17) | collective-permute-done | bytes 65568 | tf_op jit(solution)/shard_map/ppermute | solution.py:91
  183.3 0.7 multiply_reduce_fusion
  184.0 0.0 all-gather.2.cloned.1.call-done.weight_ref
  184.1 1.6 copy-done.2
  185.7 1.3 project.1
  187.0 0.1 collective-permute-start.13
  187.1 2.3 %collective-permute-start.14 = (bf16[160,512]{1,0:T(8,128)(2,1)S(1)}, bf16[160,512]{1,0:T(8,128)(2,1)S(1)}, u32[]{:S(2)}, u32[]{:S(2)}) collective-permute-start(bf16[160,512]{1,0:T(8,128)(2,1)S(1)} %get-tuple-element.36), channel_id=1, source_target_pairs={{0,2},{1,3},{2,0},{3,1},{4,6},{5,7},{6,4},{7,5},{8,10},{9,11},{10,... | collective-permute-start | bytes 491528 | tf_op jit(solution)/shard_map/ppermute | solution.py:426
  189.4 0.1 collective-permute-start.15
  189.5 0.6 dynamic-slice_divide_fusion
  190.1 3.8 %collective-permute-done.14.refs_2_ = bf16[160,512]{1,0:T(8,128)(2,1)S(1)} collective-permute-done((bf16[160,512]{1,0:T(8,128)(2,1)S(1)}, bf16[160,512]{1,0:T(8,128)(2,1)S(1)}, u32[]{:S(2)}, u32[]{:S(2)}) %collective-permute-start.14) | collective-permute-done | bytes 163872 | tf_op jit(solution)/shard_map/ppermute | solution.py:426
  193.9 3.5 %collective-permute-done.15.refs_3_ = bf16[160,512]{1,0:T(8,128)(2,1)S(1)} collective-permute-done((bf16[160,512]{1,0:T(8,128)(2,1)S(1)}, bf16[160,512]{1,0:T(8,128)(2,1)S(1)}, u32[]{:S(2)}, u32[]{:S(2)}) %collective-permute-start.15) | collective-permute-done | bytes 163872 | tf_op jit(solution)/shard_map/ppermute | solution.py:426
  197.4 1.6 spread.1
  (35 shorter events, 0.1 us)
Async XLA Ops:
  7.2 176.9 %all-gather.2.cloned.1.call-start = ((), (), s32[]{:S(2)}) async-start(), calls=%async_computation.2 | async-start | bytes 2621440 | tf_op jit(solution)/shard_map/all_gather | solution.py:62
  7.2 8.1 %collective-permute-start.1 = (bf16[32,512]{1,0:T(8,128)(2,1)}, bf16[32,512]{1,0:T(8,128)(2,1)S(1)}, u32[]{:S(2)}, u32[]{:S(2)}) collective-permute-start(bf16[32,512]{1,0:T(8,128)(2,1)} %param.18), channel_id=1, source_target_pairs={{0,0},{1,4},{2,32},{3,36},{4,64},{5,68},{6,96},{7,100},{8,128},{9,... | collective-permute-start | bytes 98312 | tf_op jit(solution)/shard_map/ppermute | solution.py:56
  15.3 1.6 copy-start
  16.9 1.6 copy-start.1
  18.5 0.9 copy-start.3
  19.4 8.1 %copy-start.5 = (s32[1,8]{1,0:T(1,128)S(1)}, s32[1,8]{1,0:T(1,128)}, u32[]{:S(2)}) copy-start(s32[1,8]{1,0:T(1,128)} %lengths_ref.5) | copy-start | bytes 100
  19.4 8.1 %copy-start.8 = (bf16[512,2048]{1,0:T(8,128)(2,1)S(1)}, bf16[512,2048]{1,0:T(8,128)(2,1)}, u32[]{:S(2)}) copy-start(bf16[512,2048]{1,0:T(8,128)(2,1)} %query_ref.1) | copy-start | bytes 6291460
  19.4 8.1 %copy-start.11 = (bf16[512,256]{1,0:T(8,128)(2,1)S(1)}, bf16[512,256]{1,0:T(8,128)(2,1)}, u32[]{:S(2)}) copy-start(bf16[512,256]{1,0:T(8,128)(2,1)} %key_ref.1) | copy-start | bytes 786436
  19.4 8.1 %copy-start.12 = (bf16[512,256]{1,0:T(8,128)(2,1)S(1)}, bf16[512,256]{1,0:T(8,128)(2,1)}, u32[]{:S(2)}) copy-start(bf16[512,256]{1,0:T(8,128)(2,1)} %value_ref.1) | copy-start | bytes 786436
  21.4 32.2 %collective-permute-start.2 = (bf16[128,2048]{1,0:T(8,128)(2,1)S(1)}, bf16[128,2048]{1,0:T(8,128)(2,1)S(1)}, u32[]{:S(2)}, u32[]{:S(2)}) collective-permute-start(bf16[128,2048]{1,0:T(8,128)(2,1)S(1)} %get-tuple-element.26), channel_id=1, source_target_pairs={{0,1},{1,0},{2,3},{3,2},{4,5},{5,4},{6,7},{7,6},{8,9},{9,8},{10,11... | collective-permute-start | bytes 1572872 | tf_op jit(solution)/shard_map/ppermute | solution.py:426
  21.5 32.1 %collective-permute-start.3 = (bf16[128,2048]{1,0:T(8,128)(2,1)S(1)}, bf16[128,2048]{1,0:T(8,128)(2,1)S(1)}, u32[]{:S(2)}, u32[]{:S(2)}) collective-permute-start(bf16[128,2048]{1,0:T(8,128)(2,1)S(1)} %get-tuple-element.27), channel_id=1, source_target_pairs={{0,2},{1,3},{2,0},{3,1},{4,6},{5,7},{6,4},{7,5},{8,10},{9,11},{10,... | collective-permute-start | bytes 1572872 | tf_op jit(solution)/shard_map/ppermute | solution.py:426
  27.4 8.6 %copy-start.4 = (bf16[3,128,512]{2,1,0:T(8,128)(2,1)S(1)}, bf16[3,128,512]{2,1,0:T(8,128)(2,1)}, u32[]{:S(2)}) copy-start(bf16[3,128,512]{2,1,0:T(8,128)(2,1)} %cotangent_ref) | copy-start | bytes 1179652
  27.4 8.6 %copy-start.6 = (s32[3]{0:T(128)S(1)}, s32[3]{0:T(128)}, u32[]{:S(2)}) copy-start(s32[3]{0:T(128)} %offsets_ref.3) | copy-start | bytes 40
  27.4 26.3 %collective-permute-start.4 = (bf16[128,2048]{1,0:T(8,128)(2,1)S(1)}, bf16[128,2048]{1,0:T(8,128)(2,1)S(1)}, u32[]{:S(2)}, u32[]{:S(2)}) collective-permute-start(bf16[128,2048]{1,0:T(8,128)(2,1)S(1)} %get-tuple-element.28), channel_id=1, source_target_pairs={{0,3},{1,2},{2,1},{3,0},{4,7},{5,6},{6,5},{7,4},{8,11},{9,10},{10,... | collective-permute-start | bytes 1572872 | tf_op jit(solution)/shard_map/ppermute | solution.py:426
  36.9 3.1 %collective-permute-start = (bf16[160,512]{1,0:T(8,128)(2,1)S(1)}, bf16[160,512]{1,0:T(8,128)(2,1)S(1)}, u32[]{:S(2)}, u32[]{:S(2)}) collective-permute-start(bf16[160,512]{1,0:T(8,128)(2,1)S(1)} %fold.1.refs_0_), channel_id=1, source_target_pairs={{0,1},{1,0},{2,3},{3,2},{4,5},{5,4},{6,7},{7,6},{8,9},{9,8},{10,11... | collective-permute-start | bytes 491528 | tf_op jit(solution)/shard_map/ppermute | solution.py:426
  37.3 1.2 collective-permute-start.5
  38.5 12.3 %collective-permute-start.6 = (f32[8,512]{1,0:T(8,128)S(1)}, f32[8,512]{1,0:T(8,128)S(1)}, u32[]{:S(2)}, u32[]{:S(2)}) collective-permute-start(f32[8,512]{1,0:T(8,128)S(1)} %get-tuple-element.29.refs_4_), channel_id=1, source_target_pairs={{0,2},{1,3},{2,0},{3,1},{4,6},{5,7},{6,4},{7,5},{8,10},{9,11},{10,... | collective-permute-start | bytes 49160 | tf_op jit(solution)/shard_map/ppermute | solution.py:426
  40.1 12.1 %collective-permute-start.7 = (f32[8,512]{1,0:T(8,128)S(1)}, f32[8,512]{1,0:T(8,128)S(1)}, u32[]{:S(2)}, u32[]{:S(2)}) collective-permute-start(f32[8,512]{1,0:T(8,128)S(1)} %get-tuple-element.29.refs_4_), channel_id=1, source_target_pairs={{0,3},{1,2},{2,1},{3,0},{4,7},{5,6},{6,5},{7,4},{8,11},{9,10},{10,... | collective-permute-start | bytes 49160 | tf_op jit(solution)/shard_map/ppermute | solution.py:426
  50.8 49.6 %collective-permute-start.8 = (bf16[160,512]{1,0:T(8,128)(2,1)S(1)}, bf16[160,512]{1,0:T(8,128)(2,1)S(1)}, u32[]{:S(2)}, u32[]{:S(2)}) collective-permute-start(bf16[160,512]{1,0:T(8,128)(2,1)S(1)} %fold.1.refs_0_), channel_id=1, source_target_pairs={{0,2},{1,3},{2,0},{3,1},{4,6},{5,7},{6,4},{7,5},{8,10},{9,11},{10,... | collective-permute-start | bytes 491528 | tf_op jit(solution)/shard_map/ppermute | solution.py:426
  52.1 48.3 %collective-permute-start.9 = (bf16[160,512]{1,0:T(8,128)(2,1)S(1)}, bf16[160,512]{1,0:T(8,128)(2,1)S(1)}, u32[]{:S(2)}, u32[]{:S(2)}) collective-permute-start(bf16[160,512]{1,0:T(8,128)(2,1)S(1)} %fold.1.refs_0_), channel_id=1, source_target_pairs={{0,3},{1,2},{2,1},{3,0},{4,7},{5,6},{6,5},{7,4},{8,11},{9,10},{10,... | collective-permute-start | bytes 491528 | tf_op jit(solution)/shard_map/ppermute | solution.py:426
  53.6 46.9 %copy-start.7 = (f32[8192]{0:T(1024)S(1)}, f32[8192]{0:T(1024)}, u32[]{:S(2)}) copy-start(f32[8192]{0:T(1024)} %param.17) | copy-start | bytes 98308
  56.2 1.4 copy-start.9
  57.6 42.9 %collective-permute-start.10 = (f32[8,512]{1,0:T(8,128)S(1)}, f32[8,512]{1,0:T(8,128)S(1)}, u32[]{:S(2)}, u32[]{:S(2)}) collective-permute-start(f32[8,512]{1,0:T(8,128)S(1)} %get-tuple-element.31.refs_4_), channel_id=1, source_target_pairs={{0,1},{1,0},{2,3},{3,2},{4,5},{5,4},{6,7},{7,6},{8,9},{9,8},{10,11... | collective-permute-start | bytes 49160 | tf_op jit(solution)/shard_map/ppermute | solution.py:426
  57.8 42.7 %collective-permute-start.11 = (f32[8,512]{1,0:T(8,128)S(1)}, f32[8,512]{1,0:T(8,128)S(1)}, u32[]{:S(2)}, u32[]{:S(2)}) collective-permute-start(f32[8,512]{1,0:T(8,128)S(1)} %get-tuple-element.31.refs_4_), channel_id=1, source_target_pairs={{0,2},{1,3},{2,0},{3,1},{4,6},{5,7},{6,4},{7,5},{8,10},{9,11},{10,... | collective-permute-start | bytes 49160 | tf_op jit(solution)/shard_map/ppermute | solution.py:426
  59.1 41.4 %collective-permute-start.12 = (f32[8,512]{1,0:T(8,128)S(1)}, f32[8,512]{1,0:T(8,128)S(1)}, u32[]{:S(2)}, u32[]{:S(2)}) collective-permute-start(f32[8,512]{1,0:T(8,128)S(1)} %get-tuple-element.31.refs_4_), channel_id=1, source_target_pairs={{0,3},{1,2},{2,1},{3,0},{4,7},{5,6},{6,5},{7,4},{8,11},{9,10},{10,... | collective-permute-start | bytes 49160 | tf_op jit(solution)/shard_map/ppermute | solution.py:426
  100.5 1.6 copy-start.10
  134.4 48.9 %copy-start.13 = (bf16[32,512]{1,0:T(8,128)(2,1)S(1)}, bf16[32,512]{1,0:T(8,128)(2,1)}, u32[]{:S(2)}) copy-start(bf16[32,512]{1,0:T(8,128)(2,1)} %param.18) | copy-start | bytes 98308
  137.3 16.0 %all-to-all-start.1 = ((bf16[8,64,512]{2,1,0:T(8,128)(2,1)}), bf16[8,64,512]{2,1,0:T(8,128)(2,1)S(1)}, u32[]{:S(2)}, u32[]{:S(2)}) async-start(bf16[8,64,512]{2,1,0:T(8,128)(2,1)} %bitcast.3), calls=%async_computation.1 | async-start | bytes 1048576 | tf_op jit(solution)/shard_map/all_to_all | solution.py:75
  153.4 26.7 %collective-permute-start.16 = (f32[32,512]{1,0:T(8,128)S(1)}, f32[32,512]{1,0:T(8,128)S(1)}, u32[]{:S(2)}, u32[]{:S(2)}) collective-permute-start(f32[32,512]{1,0:T(8,128)S(1)} %get-tuple-element.42), channel_id=1, source_target_pairs={{0,0},{1,64},{2,128},{3,192},{4,4},{5,68},{6,132},{7,196},{8,8},{9... | collective-permute-start | bytes 196616 | tf_op jit(solution)/shard_map/ppermute | solution.py:91
  176.5 6.7 %collective-permute-start.17 = (f32[32,512]{1,0:T(8,128)S(1)}, f32[32,512]{1,0:T(8,128)S(1)}, u32[]{:S(2)}, u32[]{:S(2)}) collective-permute-start(f32[32,512]{1,0:T(8,128)S(1)} %get-tuple-element.41), channel_id=1, source_target_pairs={{0,4},{1,68},{2,132},{3,196},{4,0},{5,64},{6,128},{7,192},{8,12},{... | collective-permute-start | bytes 196616 | tf_op jit(solution)/shard_map/ppermute | solution.py:91
  184.1 1.6 copy-start.2
  187.0 3.1 %collective-permute-start.13 = (bf16[160,512]{1,0:T(8,128)(2,1)S(1)}, bf16[160,512]{1,0:T(8,128)(2,1)S(1)}, u32[]{:S(2)}, u32[]{:S(2)}) collective-permute-start(bf16[160,512]{1,0:T(8,128)(2,1)S(1)} %get-tuple-element.35), channel_id=1, source_target_pairs={{0,1},{1,0},{2,3},{3,2},{4,5},{5,4},{6,7},{7,6},{8,9},{9,8},{10,11... | collective-permute-start | bytes 491528 | tf_op jit(solution)/shard_map/ppermute | solution.py:426
  187.1 6.8 %collective-permute-start.14 = (bf16[160,512]{1,0:T(8,128)(2,1)S(1)}, bf16[160,512]{1,0:T(8,128)(2,1)S(1)}, u32[]{:S(2)}, u32[]{:S(2)}) collective-permute-start(bf16[160,512]{1,0:T(8,128)(2,1)S(1)} %get-tuple-element.36), channel_id=1, source_target_pairs={{0,2},{1,3},{2,0},{3,1},{4,6},{5,7},{6,4},{7,5},{8,10},{9,11},{10,... | collective-permute-start | bytes 491528 | tf_op jit(solution)/shard_map/ppermute | solution.py:426
  189.4 8.0 %collective-permute-start.15 = (bf16[160,512]{1,0:T(8,128)(2,1)S(1)}, bf16[160,512]{1,0:T(8,128)(2,1)S(1)}, u32[]{:S(2)}, u32[]{:S(2)}) collective-permute-start(bf16[160,512]{1,0:T(8,128)(2,1)S(1)} %get-tuple-element.37), channel_id=1, source_target_pairs={{0,3},{1,2},{2,1},{3,0},{4,7},{5,6},{6,5},{7,4},{8,11},{9,10},{10,... | collective-permute-start | bytes 491528 | tf_op jit(solution)/shard_map/ppermute | solution.py:426
Sparse Core Ops, SparseCore 0:
  100.6 51.7 all-gather.1

commit v3 on v2

--- a/solution.py
+++ b/solution.py
@@ -14,6 +14,7 @@
 OFFMAX = 32
 EPSILON = 1e-05
 VMEM_LIMIT = 20 * 1024 * 1024
+FEATURES_LIMIT = 60 * 1024 * 1024
 
 VMEM = pl.BlockSpec(memory_space=pltpu.VMEM)
 SMEM = pl.BlockSpec(memory_space=pltpu.SMEM)
@@ -45,36 +46,89 @@
     return order
 
 
-def place_weight(weight):
+def moved(values, change):
+    n = lax.axis_size("dp")
+    nz, ny, nx = sides_of(n)
+    pairs = []
+    for source in range(n):
+        z, y, x = change(source // (ny * nx), source // nx % ny, source % nx)
+        pairs.append((source, (z * ny + y) * nx + x))
+    return lax.ppermute(values, "dp", pairs)
+
+
+def placed_weight(weight):
     n, tn = lax.axis_size("dp"), lax.axis_size("tensor")
     nz, ny, nx = sides_of(n)
-    pairs = []
-    for j in range(tn):
-        for q in range(n):
-            y, z, x = q // (nz * nx), q // nx % nz, q % nx
-            pairs.append((j * n + q, ((z * ny + y) * nx + x) * tn + j))
-    return lax.ppermute(weight, ("dp", "tensor"), pairs)
-
-
-def gather_weight(weight, sides):
-    groups = groups_along(lax.axis_size("dp"), *sides)
-    if len(groups[0]) > 1:
-        weight = lax.all_gather(weight, "dp", axis=0, tiled=True, axis_index_groups=groups)
-    return weight
+    x = lax.axis_index("dp") % nx
+    both = []
+    for far in (0, nz // 2) if nz > 1 else (0,):
+        parts = []
+        for turn in range(nx):
+            pairs = []
+            for j in range(tn):
+                for q in range(n):
+                    y, z, x0 = q // (nz * nx), (q // nx % nz) ^ far, (q + turn) % nx
+                    pairs.append((j * n + q, ((z * ny + y) * nx + x0) * tn + j))
+            parts.append(lax.ppermute(weight, ("dp", "tensor"), pairs))
+        both.append(parts)
+    if nx == 1:
+        return jnp.concatenate([parts[0] for parts in both])
+    return jnp.where(
+        x == 0,
+        jnp.concatenate([part for parts in both for part in parts]),
+        jnp.concatenate([part for parts in both for part in parts[::-1]]))
+
+
+def weight_along_z(part):
+    nz = sides_of(lax.axis_size("dp"))[0]
+    return [part] + [moved(part, lambda z, y, x: (z ^ s, y, x)) for s in range(1, nz // 2)]
+
+
+def weight_once(halves):
+    if sides_of(lax.axis_size("dp"))[1] == 1:
+        return [[half] for half in halves]
+    return [[half, moved(half, lambda z, y, x: (z, y ^ first, x))] for half, (first, _) in zip(halves, EXCHANGES)]
+
+
+def weight_twice(halves):
+    if sides_of(lax.axis_size("dp"))[1] == 1:
+        return halves
+    out = []
+    for half, (first, second) in zip(halves, EXCHANGES):
+        got = dict(zip((0, first), half))
+        for s in (0, first):
+            got[s ^ second] = moved(got[s], lambda z, y, x: (z, y ^ second, x))
+        out.append([got[s] for s in range(4)])
+    return out
+
+
+KEPT = ((0, 3), (0, 1))
+SENT = ((1, 2), (3, 2))
+EXCHANGES = ((1, 3), (3, 1))
+
+
+def reduce_along_y(kept, sent):
+    ny = sides_of(lax.axis_size("dp"))[1]
+    halves = []
+    for keep, send, (first, second) in zip(kept, sent, EXCHANGES):
+        if ny > 1:
+            got = moved(send, lambda z, y, x: (z, y ^ first, x))
+            own = keep[0] + got[0].astype(F32)
+            other = (keep[1] + got[1].astype(F32)).astype(BF16)
+            halves.append((own, moved(other, lambda z, y, x: (z, y ^ second, x))))
+        else:
+            halves.append((keep[0], None))
+    halves = [own if got is None else own + got.astype(F32) for own, got in halves]
+    return jnp.concatenate(halves)
 
 
 def reduce_grad(grad):
     n, tn = lax.axis_size("dp"), lax.axis_size("tensor")
     nz, ny, nx = sides_of(n)
-    columns = grad.shape[1]
-    for side in (1, 0):
-        count = sides_of(n)[side]
-        if count > 1:
-            if grad.dtype != BF16:
-                grad = grad.astype(BF16)
-            grad = lax.all_to_all(grad, "dp", 0, 0, tiled=True, axis_index_groups=groups_along(n, side))
-            grad = jnp.sum(grad.reshape(count, -1, columns).astype(F32), axis=0)
-    grad = grad.astype(F32)
+    columns = grad.shape[-1]
+    if nz > 1:
+        grad = lax.all_to_all(grad.astype(BF16), "dp", 0, 0, tiled=True, axis_index_groups=groups_along(n, 0))
+        grad = jnp.sum(grad.reshape(nz, -1, columns).astype(F32), axis=0)
     rows = grad.shape[0] // nx
     order = block_order(n, tn)
     x = lax.axis_index("dp") % nx
@@ -161,7 +215,7 @@
         ],
         out_specs=[pl.BlockSpec((block, piece), lambda b: (b, 0))] * tn,
         out_shape=[jax.ShapeDtypeStruct((rows, piece), BF16)] * tn,
-        compiler_params=pltpu.CompilerParams(vmem_limit_bytes=VMEM_LIMIT),
+        compiler_params=pltpu.CompilerParams(vmem_limit_bytes=FEATURES_LIMIT),
         cost_estimate=pl.CostEstimate(flops=10 * rows * width, bytes_accessed=6 * rows * width, transcendentals=0),
         name="features",
     )(place, low, mid, gain)
@@ -299,17 +353,22 @@
     )(place, gain, high, *parts, *squares)
 
 
-def grads(place, gain, merged, folds, squares, width, order):
+def grads(place, gain, merged, folds, squares, width, ny, tn):
     pack, piece = merged.shape
-    tn = len(squares)
     rows = pack // tn
     vw = folds[0].shape[1]
-    blocks = order.reshape(-1)
-    size = piece // blocks.size
+    chunk = piece // (2 * ny)
+    kept, sent = (KEPT, SENT) if ny > 1 else (((0,), (0,)), ((), ()))
+    steps = [(h, s, True) for h in range(2) for s in kept[h]] + [(h, s, False) for h in range(2) for s in sent[h]]
+    steps.sort(key=lambda step: step[2])
+    size = chunk // (2 * tn) if ny > 1 else chunk
 
     def kernel(place_ref, gain_ref, merged_ref, *refs):
-        fold_refs, square_refs, (grad_ref, hidden_ref, fold_ref) = refs[:tn], refs[tn:2 * tn], refs[2 * tn:]
-        j = place_ref[0]
+        fold_refs, square_refs, refs = refs[:tn], refs[tn:2 * tn], refs[2 * tn:]
+        keep_refs, refs = refs[:2], refs[2:]
+        send_refs, refs = refs[:2 if ny > 1 else 0], refs[2 if ny > 1 else 0:]
+        hidden_ref, fold_ref = refs
+        j, y = place_ref[0], place_ref[1]
         squares = square_refs[0][...]
         for s in range(1, tn):
             squares = squares + square_refs[s][...]
@@ -326,52 +385,99 @@
             at = pl.ds(pl.multiple_of((j ^ s) * rows, rows), rows + OFFMAX)
             fold_ref[at, :] = fold_ref[at, :] + fold_refs[s][...].astype(F32)
         folded = fold_ref[OFFMAX:, :].astype(BF16)
-        chunk = max(256, size)
-        for c in range(0, piece, chunk):
+        for h, s, keep in steps:
+            at = pl.ds(pl.multiple_of(h * ny * chunk + (y ^ s) * chunk, chunk), chunk)
             part = lax.dot_general(
-                hidden_ref[:, c:c + chunk], folded, (((0,), (0,)), ((), ())), preferred_element_type=F32).astype(BF16)
-            for q in range(c // size, (c + chunk) // size):
-                to = int(np.argmax(blocks == q)) * size
-                grad_ref[to:to + size, :] = part[q * size - c:(q + 1) * size - c, :]
-
-    return pl.pallas_call(
+                hidden_ref[:, at], folded, (((0,), (0,)), ((), ())), preferred_element_type=F32)
+            if size < chunk:
+                part = jnp.concatenate(
+                    [part[(x * tn + t) * size:(x * tn + t + 1) * size] for t in range(tn) for x in range(2)], axis=0)
+            if keep:
+                keep_refs[h][kept[h].index(s)] = part
+            else:
+                send_refs[h][sent[h].index(s)] = part.astype(BF16)
+
+    out_shape = [jax.ShapeDtypeStruct((len(kept[h]), chunk, vw), F32) for h in range(2)]
+    if ny > 1:
+        out_shape += [jax.ShapeDtypeStruct((len(sent[h]), chunk, vw), BF16) for h in range(2)]
+    out_shape += [jax.ShapeDtypeStruct((pack, piece), BF16)]
+    out = pl.pallas_call(
         kernel,
         in_specs=[SMEM] + [VMEM] * (2 + 2 * tn),
-        out_specs=[VMEM] * 2,
-        out_shape=[jax.ShapeDtypeStruct((piece, vw), BF16), jax.ShapeDtypeStruct((pack, piece), BF16)],
+        out_specs=[VMEM] * len(out_shape),
+        out_shape=out_shape,
         scratch_shapes=[pltpu.VMEM((pack + OFFMAX, vw), F32)],
         compiler_params=pltpu.CompilerParams(vmem_limit_bytes=VMEM_LIMIT),
         cost_estimate=pl.CostEstimate(flops=2 * pack * piece * vw, bytes_accessed=8 * pack * piece, transcendentals=0),
         name="grads",
     )(place, gain, merged, *folds, *squares)
-
-
-def project(place, hidden, weight, tn):
+    return out[:2], out[2:-1] if ny > 1 else (None, None), out[-1]
+
+
+def stacked(place, parts, nz):
+    rows, vw = parts[0].shape
+    half = rows // 2
+
+    def kernel(place_ref, *refs):
+        part_refs, out_refs = refs[:-2], refs[-2:]
+        z = place_ref[2]
+        if nz == 1:
+            for h in range(2):
+                out_refs[h][...] = part_refs[0][h * half:(h + 1) * half, :]
+            return
+        for h in range(2):
+            @pl.when((z >= nz // 2) == (h == 1))
+            def _(h=h):
+                for s, ref in enumerate(part_refs):
+                    at = pl.ds(pl.multiple_of(((z ^ s) & (nz // 2 - 1)) * half, half), half)
+                    out_refs[h][at, :] = ref[0:half, :]
+                    out_refs[1 - h][at, :] = ref[half:rows, :]
+
+    return pl.pallas_call(
+        kernel,
+        in_specs=[SMEM] + [VMEM] * len(parts),
+        out_specs=[VMEM] * 2,
+        out_shape=[jax.ShapeDtypeStruct((half * len(parts), vw), BF16)] * 2,
+        compiler_params=pltpu.CompilerParams(vmem_limit_bytes=VMEM_LIMIT),
+        cost_estimate=pl.CostEstimate(flops=0, bytes_accessed=4 * len(parts) * rows * vw, transcendentals=0),
+        name="stacked",
+    )(place, *parts)
+
+
+def project(place, hidden, weights, tn):
     pack, piece = hidden.shape
     rows = pack // tn
-    vw = weight.shape[1]
-
-    def kernel(place_ref, hidden_ref, weight_ref, *refs):
-        value_refs, total_ref = refs[:tn], refs[tn]
-        j = place_ref[0]
+    part, vw = weights[0][0].shape
+    count = len(weights[0])
+
+    def kernel(place_ref, hidden_ref, *refs):
+        weight_refs, value_refs, total_ref = refs[:2 * count], refs[2 * count:-1], refs[-1]
+        j, y = place_ref[0], place_ref[1]
         total_ref[0:OFFMAX, :] = jnp.zeros((OFFMAX, vw), F32)
-        for c in range(0, pack, 256):
-            total_ref[OFFMAX + c:OFFMAX + c + 256, :] = jnp.dot(
-                hidden_ref[c:c + 256, :], weight_ref[...], preferred_element_type=F32)
+        block = 128
+        for c in range(0, pack, block):
+            total = None
+            for h in range(2):
+                for s in range(count):
+                    at = pl.ds(pl.multiple_of((y ^ s) * 2 * part + h * part, part), part)
+                    term = jnp.dot(
+                        hidden_ref[c:c + block, at], weight_refs[h * count + s][...], preferred_element_type=F32)
+                    total = term if total is None else total + term
+            total_ref[OFFMAX + c:OFFMAX + c + block, :] = total
         for s in range(tn):
             at = pl.ds(pl.multiple_of((j ^ s) * rows, rows), rows + OFFMAX)
             value_refs[s][...] = total_ref[at, :].astype(value_refs[s].dtype)
 
     return pl.pallas_call(
         kernel,
-        in_specs=[SMEM] + [VMEM] * 2,
+        in_specs=[SMEM] + [VMEM] * (1 + 2 * count),
         out_specs=[VMEM] * tn,
         out_shape=[jax.ShapeDtypeStruct((rows + OFFMAX, vw), F32 if s == 0 else BF16) for s in range(tn)],
         scratch_shapes=[pltpu.VMEM((pack + OFFMAX, vw), F32)],
         compiler_params=pltpu.CompilerParams(vmem_limit_bytes=VMEM_LIMIT),
         cost_estimate=pl.CostEstimate(flops=2 * pack * piece * vw, bytes_accessed=4 * pack * piece, transcendentals=0),
         name="project",
-    )(place, hidden, weight)
+    )(place, hidden, *weights[0], *weights[1])
 
 
 def spread(place, lengths, offsets, parts):
@@ -415,8 +521,10 @@
     n = lax.axis_size("dp")
     tn = lax.axis_size("tensor")
     j = lax.axis_index("tensor")
-    flat = lax.axis_index("dp") * tn + j
-    place = j.reshape(1).astype(jnp.int32)
+    i = lax.axis_index("dp")
+    flat = i * tn + j
+    nz, ny, nx = sides_of(n)
+    place = jnp.stack([j, i // nx % ny, i // (ny * nx)]).astype(jnp.int32)
     width = low_feature.shape[1]
     piece = width // tn
     pack = target_queries.shape[0]
@@ -425,27 +533,29 @@
     def swapped(values, s):
         return lax.ppermute(values, "tensor", [(a, a ^ s) for a in range(tn)])
 
-    own_weight = place_weight(draft_weight)
-    low_feature, _ = lax.optimization_barrier((low_feature, own_weight))
-    sent = features(place, low_feature, mid_feature, merging_gain, tn)
+    own_weight = placed_weight(draft_weight)
+    first_place, _ = lax.optimization_barrier((place, own_weight))
+    sent = features(first_place, low_feature, mid_feature, merging_gain, tn)
     parts = [sent[0]] + [swapped(sent[s], s) for s in range(1, tn)]
-    some_weight = gather_weight(own_weight, (0, 2))
 
     high, squares = attend(doc_lengths, target_queries, target_keys, target_values)
-    squares = [squares] + [swapped(squares, s) for s in range(1, tn)]
-    cotangent, _ = lax.optimization_barrier((cotangent, high))
+    own_weight, cotangent, _ = lax.optimization_barrier((own_weight, cotangent, high))
+    halves = stacked(place, weight_along_z(own_weight), nz)
     folded = fold(place, doc_lengths, step_offsets, cotangent)
     folds = [folded] + [swapped(folded, s) for s in range(1, tn)]
-    gain, _ = lax.optimization_barrier((merging_gain, folds[1]))
-    merged, squares = merge(place, gain, high, parts, squares, width)
-    some_weight, _ = lax.optimization_barrier((some_weight, merged))
-    weight = gather_weight(some_weight, (1,))
+    squares, _, _ = lax.optimization_barrier((squares, halves[0], folds[1]))
     squares = [squares] + [swapped(squares, s) for s in range(1, tn)]
-    grad, hidden = grads(
-        place, draft_gain.reshape(1, width), merged, folds, squares, width, block_order(n, tn))
+    merged, squares = merge(place, merging_gain, high, parts, squares, width)
+    squares = [squares] + [swapped(squares, s) for s in range(1, tn)]
+    kept, cut, hidden = grads(place, draft_gain.reshape(1, width), merged, folds, squares, width, ny, tn)
+    halves, hidden = lax.optimization_barrier((halves, hidden))
+    halves = weight_once(halves)
+    grad = reduce_along_y(kept, cut)
+    halves, grad = lax.optimization_barrier((halves, grad))
+    weights = weight_twice(halves)
     weight_grad = reduce_grad(grad)
 
-    values = project(place, hidden, weight, tn)
+    values = project(place, hidden, weights, tn)
     values = [values[0]] + [swapped(values[s], s) for s in range(1, tn)]
     draft_values = spread(place, doc_lengths, step_offsets, values)
 

time: 207 us -> 155 us (0.75)
  the two profiles are of different devices: /device:TPU:1 before, /device:TPU:32 now
where the time goes in v3:
time: 155 us; the launch traced here: 154 us
  starting transfers between devices  61.6 us (40%)
  waiting for transfers between devices  59.8 us (39%)
  Pallas kernels  25.8 us (17%)
  other arithmetic  4.33 us (3%)
  local copies, waits for them, and re-layouts  1.73 us (1%)
    ppermute x13, waiting for transfers between devices, moved(): return lax.ppermute(values, 'dp', pairs)  43.2 us
    ppermute x4, starting transfers between devices, placed_weight(): parts.append(lax.ppermute(weight, ('dp', 'tensor'), pairs))  22.3 us
    ppermute x13, starting transfers between devices, moved(): return lax.ppermute(values, 'dp', pairs)  17 us
    pallas_call x1, Pallas kernels, attend(): pl.pallas_call(functools.partial(attend_kernel, window), grid=(pack // bl...  8.44 us
    ppermute x15, starting transfers between devices, swapped(): return lax.ppermute(values, 'tensor', [(a, a ^ s) for a in range(tn)])  8.17 us
    ppermute x2, waiting for transfers between devices, reduce_grad(): part = lax.ppermute(part, ('dp', 'tensor'), pairs)  8.15 us
    all_to_all x1, starting transfers between devices, reduce_grad(): lax.all_to_all(grad.astype(BF16), 'dp', 0, 0, tiled=True, axis_index_grou...  7.32 us
    ppermute x15, waiting for transfers between devices, swapped(): return lax.ppermute(values, 'tensor', [(a, a ^ s) for a in range(tn)])  7.09 us
  transfers between devices with their start and end apart: 35, of which 19 were waited for; matrix products, arithmetic and copies ran while one was open for 2% of the time, Pallas kernels for 12%

profile of v3, /device:TPU:32, one launch (start us, length us, event | category | flops | bytes accessed | tf_op | source)
XLA Modules:
  0.0 154.1 jit_solution(9867172173040605590)
XLA Ops:
  0.6 8.5 %collective-permute-start.2 = (bf16[32,512]{1,0:T(8,128)(2,1)}, bf16[32,512]{1,0:T(8,128)(2,1)S(1)}, u32[]{:S(2)}, u32[]{:S(2)}) collective-permute-start(bf16[32,512]{1,0:T(8,128)(2,1)} %param.18), channel_id=1, source_target_pairs={{0,128},{1,132},{2,160},{3,164},{4,192},{5,196},{6,224},{7,228},{8... | collective-permute-start | bytes 98312 | tf_op jit(solution)/shard_map/ppermute | solution.py:72
  9.2 2.9 %collective-permute-start.1 = (bf16[32,512]{1,0:T(8,128)(2,1)}, bf16[32,512]{1,0:T(8,128)(2,1)S(1)}, u32[]{:S(2)}, u32[]{:S(2)}) collective-permute-start(bf16[32,512]{1,0:T(8,128)(2,1)} %param.18), channel_id=1, source_target_pairs={{0,4},{1,0},{2,36},{3,32},{4,68},{5,64},{6,100},{7,96},{8,132},{9,... | collective-permute-start | bytes 98312 | tf_op jit(solution)/shard_map/ppermute | solution.py:72
  12.0 1.9 %collective-permute-start = (bf16[32,512]{1,0:T(8,128)(2,1)}, bf16[32,512]{1,0:T(8,128)(2,1)S(1)}, u32[]{:S(2)}, u32[]{:S(2)}) collective-permute-start(bf16[32,512]{1,0:T(8,128)(2,1)} %param.18), channel_id=1, source_target_pairs={{0,0},{1,4},{2,32},{3,36},{4,64},{5,68},{6,96},{7,100},{8,128},{9,... | collective-permute-start | bytes 98312 | tf_op jit(solution)/shard_map/ppermute | solution.py:72
  14.0 8.9 %collective-permute-start.3 = (bf16[32,512]{1,0:T(8,128)(2,1)}, bf16[32,512]{1,0:T(8,128)(2,1)S(1)}, u32[]{:S(2)}, u32[]{:S(2)}) collective-permute-start(bf16[32,512]{1,0:T(8,128)(2,1)} %param.18), channel_id=1, source_target_pairs={{0,132},{1,128},{2,164},{3,160},{4,196},{5,192},{6,228},{7,224},{8... | collective-permute-start | bytes 98312 | tf_op jit(solution)/shard_map/ppermute | solution.py:72
  23.5 1.3 collective-permute-done.3
  24.9 5.0 %features.1 = (bf16[128,2048]{1,0:T(8,128)(2,1)}, bf16[128,2048]{1,0:T(8,128)(2,1)}, bf16[128,2048]{1,0:T(8,128)(2,1)}, bf16[128,2048]{1,0:T(8,128)(2,1)}) custom-call(s32[3]{0:T(128)} %pad_add_fusion.place_ref, bf16[128,8192]{1,0:T(8,128)(2,1)} %low_ref.1, bf16[128,8192]{1,0:T(8,128)(2,1)} %mid_ref.1, f32[3,8192]{1,0:T(4,128)} %gain_ref.3), custom_call_target="tpu_custom_call" | custom-call | flops 10485760 | bytes 6291456 | tf_op jit(solution)/shard_map/features/pallas_call | solution.py:207
  30.0 1.8 %collective-permute-start.9 = (bf16[128,2048]{1,0:T(8,128)(2,1)}, bf16[128,2048]{1,0:T(8,128)(2,1)S(1)}, u32[]{:S(2)}, u32[]{:S(2)}) collective-permute-start(bf16[128,2048]{1,0:T(8,128)(2,1)} %get-tuple-element.42), channel_id=1, source_target_pairs={{0,3},{1,2},{2,1},{3,0},{4,7},{5,6},{6,5},{7,4},{8,11},{9,10},{10,... | collective-permute-start | bytes 1572872 | tf_op jit(solution)/shard_map/ppermute | solution.py:534
  31.9 8.4 %attend.1 = (bf16[512,2048]{1,0:T(8,128)(2,1)S(1)}, f32[8,512]{1,0:T(8,128)S(1)}) custom-call(s32[1,8]{1,0:T(1,128)S(1)} %copy-done.6, bf16[512,2048]{1,0:T(8,128)(2,1)S(1)} %copy-done.9, bf16[512,256]{1,0:T(8,128)(2,1)S(1)} %copy-done.10, bf16[512,256]{1,0:T(8,128)(2,1)S(1)} %copy-done.11), custom_call_target="tpu_custom_call" | custom-call | flops 1610612736 | bytes 4194304 | tf_op jit(solution)/shard_map/attend/pallas_call | solution.py:258
  40.3 2.6 %collective-permute-start.5 = (bf16[128,512]{1,0:T(8,128)(2,1)S(1)}, bf16[128,512]{1,0:T(8,128)(2,1)S(1)}, u32[]{:S(2)}, u32[]{:S(2)}) collective-permute-start(bf16[128,512]{1,0:T(8,128)(2,1)S(1)} %maximum_select_fusion.refs_0_), channel_id=1, source_target_pairs={{0,64},{4,68},{8,72},{12,76},{16,80},{20,84},{24,88},{28,92},{32,9... | collective-permute-start | bytes 393224 | tf_op jit(solution)/shard_map/ppermute | solution.py:56
  42.9 0.9 fold.1.refs_0_
  43.8 8.3 %collective-permute-done.6.refs_3_ = bf16[128,512]{1,0:T(8,128)(2,1)S(1)} collective-permute-done((bf16[128,512]{1,0:T(8,128)(2,1)S(1)}, bf16[128,512]{1,0:T(8,128)(2,1)S(1)}, u32[]{:S(2)}, u32[]{:S(2)}) %collective-permute-start.6) | collective-permute-done | bytes 131104 | tf_op jit(solution)/shard_map/ppermute | solution.py:56
  52.3 3.7 %collective-permute-start.4 = (bf16[128,512]{1,0:T(8,128)(2,1)S(1)}, bf16[128,512]{1,0:T(8,128)(2,1)S(1)}, u32[]{:S(2)}, u32[]{:S(2)}) collective-permute-start(bf16[128,512]{1,0:T(8,128)(2,1)S(1)} %maximum_select_fusion.refs_0_), channel_id=1, source_target_pairs={{0,32},{4,36},{8,40},{12,44},{16,48},{20,52},{24,56},{28,60},{32,0... | collective-permute-start | bytes 393224 | tf_op jit(solution)/shard_map/ppermute | solution.py:56
  56.0 3.4 %collective-permute-done.4.refs_1_ = bf16[128,512]{1,0:T(8,128)(2,1)S(1)} collective-permute-done((bf16[128,512]{1,0:T(8,128)(2,1)S(1)}, bf16[128,512]{1,0:T(8,128)(2,1)S(1)}, u32[]{:S(2)}, u32[]{:S(2)}) %collective-permute-start.4) | collective-permute-done | bytes 131104 | tf_op jit(solution)/shard_map/ppermute | solution.py:56
  60.1 0.8 collective-permute-start.12
  60.8 2.4 %collective-permute-done.13.refs_7_ = f32[8,512]{1,0:T(8,128)S(1)} collective-permute-done((f32[8,512]{1,0:T(8,128)S(1)}, f32[8,512]{1,0:T(8,128)S(1)}, u32[]{:S(2)}, u32[]{:S(2)}) %collective-permute-start.13) | collective-permute-done | bytes 16416 | tf_op jit(solution)/shard_map/ppermute | solution.py:534
  64.4 1.0 collective-permute-start.14
  65.4 3.1 %merge.1 = (bf16[512,2048]{1,0:T(8,128)(2,1)S(1)}, f32[8,512]{1,0:T(8,128)S(1)}) custom-call(s32[3]{0:T(128)S(1)} %copy-done.5, f32[3,8192]{1,0:T(4,128)S(1)} %copy-done.1, bf16[512,2048]{1,0:T(8,128)(2,1)S(1)} %get-tuple-element.34.high_ref, bf16[128,2048]{1,0:T(8,128)(2,1)S(1)} %copy-done, bf16[128,2048]{1,0:T(8,128)(2,1)S(1)} %collective-permute-done.7.refs_1_, ...), custom_call_target="tpu_custom_call" | custom-call | flops 8388608 | bytes 6291456 | tf_op jit(solution)/shard_map/merge/pallas_call | solution.py:342
  68.6 0.7 collective-permute-start.18
  69.3 1.4 collective-permute-start.17
  70.6 3.3 %collective-permute-done.14.refs_2_ = bf16[160,512]{1,0:T(8,128)(2,1)S(1)} collective-permute-done((bf16[160,512]{1,0:T(8,128)(2,1)S(1)}, bf16[160,512]{1,0:T(8,128)(2,1)S(1)}, u32[]{:S(2)}, u32[]{:S(2)}) %collective-permute-start.14) | collective-permute-done | bytes 163872 | tf_op jit(solution)/shard_map/ppermute | solution.py:534
  74.6 2.8 %grads.1 = (f32[2,256,512]{2,1,0:T(8,128)S(1)}, f32[2,256,512]{2,1,0:T(8,128)S(1)}, bf16[2,256,512]{2,1,0:T(8,128)(2,1)S(1)}, bf16[2,256,512]{2,1,0:T(8,128)(2,1)S(1)}, bf16[512,2048]{1,0:T(8,128)(2,1)S(1)}) custom-call(s32[3]{0:T(128)S(1)} %copy-done.5, f32[1,8192]{1,0:T(1,128)S(1)} %bitcast.13, bf16[512,2048]{1,0:T(8,128)(2,1)S(1)} %get-tuple-element.46.merged_ref, ...), custom_call_target="tpu_custom_call" | custom-call | flops 1073741824 | bytes 8388608 | tf_op jit(solution)/shard_map/grads/pallas_call | solution.py:404
  77.5 2.6 %collective-permute-start.21 = (bf16[2,256,512]{2,1,0:T(8,128)(2,1)S(1)}, bf16[2,256,512]{2,1,0:T(8,128)(2,1)S(1)}, u32[]{:S(2)}, u32[]{:S(2)}) collective-permute-start(bf16[2,256,512]{2,1,0:T(8,128)(2,1)S(1)} %get-tuple-element.53), channel_id=1, source_target_pairs={{0,8},{4,12},{8,0},{12,4},{16,24},{20,28},{24,16},{28,20},{32,40},... | collective-permute-start | bytes 1572872 | tf_op jit(solution)/shard_map/ppermute | solution.py:56
  80.0 11.9 %collective-permute-done.21 = bf16[2,256,512]{2,1,0:T(8,128)(2,1)S(1)} collective-permute-done((bf16[2,256,512]{2,1,0:T(8,128)(2,1)S(1)}, bf16[2,256,512]{2,1,0:T(8,128)(2,1)S(1)}, u32[]{:S(2)}, u32[]{:S(2)}) %collective-permute-start.21) | collective-permute-done | bytes 524320 | tf_op jit(solution)/shard_map/ppermute | solution.py:56
  92.1 2.5 %collective-permute-done.23 = bf16[2,256,512]{2,1,0:T(8,128)(2,1)S(1)} collective-permute-done((bf16[2,256,512]{2,1,0:T(8,128)(2,1)S(1)}, bf16[2,256,512]{2,1,0:T(8,128)(2,1)S(1)}, u32[]{:S(2)}, u32[]{:S(2)}) %collective-permute-start.23) | collective-permute-done | bytes 524320 | tf_op jit(solution)/shard_map/ppermute | solution.py:56
  94.7 2.0 %collective-permute-start.19 = (bf16[256,512]{1,0:T(8,128)(2,1)S(1)}, bf16[256,512]{1,0:T(8,128)(2,1)S(1)}, u32[]{:S(2)}, u32[]{:S(2)}) collective-permute-start(bf16[256,512]{1,0:T(8,128)(2,1)S(1)} %get-tuple-element.56.refs_0_), channel_id=1, source_target_pairs={{0,8},{4,12},{8,0},{12,4},{16,24},{20,28},{24,16},{28,20},{32,40},... | collective-permute-start | bytes 786440 | tf_op jit(solution)/shard_map/ppermute | solution.py:56
  96.8 0.7 collective-permute-start.20
  97.5 5.0 %collective-permute-done.22 = bf16[256,512]{1,0:T(8,128)(2,1)S(1)} collective-permute-done((bf16[256,512]{1,0:T(8,128)(2,1)S(1)}, bf16[256,512]{1,0:T(8,128)(2,1)S(1)}, u32[]{:S(2)}, u32[]{:S(2)}) %collective-permute-start.22) | collective-permute-done | bytes 262176 | tf_op jit(solution)/shard_map/ppermute | solution.py:56
  102.6 1.3 collective-permute-done.24
  104.1 0.9 pad_maximum_fusion
  104.9 2.2 %collective-permute-done.19.refs_1_ = bf16[256,512]{1,0:T(8,128)(2,1)S(1)} collective-permute-done((bf16[256,512]{1,0:T(8,128)(2,1)S(1)}, bf16[256,512]{1,0:T(8,128)(2,1)S(1)}, u32[]{:S(2)}, u32[]{:S(2)}) %collective-permute-start.19) | collective-permute-done | bytes 262176 | tf_op jit(solution)/shard_map/ppermute | solution.py:56
  107.1 7.3 %all-to-all-start = ((bf16[8,64,512]{2,1,0:T(8,128)(2,1)}), bf16[8,64,512]{2,1,0:T(8,128)(2,1)}, u32[]{:S(2)}, u32[]{:S(2)}) async-start(bf16[8,64,512]{2,1,0:T(8,128)(2,1)} %bitcast.14), calls=%async_computation | async-start | bytes 1048576 | tf_op jit(solution)/shard_map/all_to_all | solution.py:130
  114.5 2.1 %collective-permute-start.26 = (bf16[256,512]{1,0:T(8,128)(2,1)S(1)}, bf16[256,512]{1,0:T(8,128)(2,1)S(1)}, u32[]{:S(2)}, u32[]{:S(2)}) collective-permute-start(bf16[256,512]{1,0:T(8,128)(2,1)S(1)} %get-tuple-element.56.refs_0_), channel_id=1, source_target_pairs={{0,24},{4,28},{8,16},{12,20},{16,8},{20,12},{24,0},{28,4},{32,56},... | collective-permute-start | bytes 786440 | tf_op jit(solution)/shard_map/ppermute | solution.py:56
  116.6 1.1 collective-permute-start.25
  117.7 2.0 %collective-permute-start.28 = (bf16[256,512]{1,0:T(8,128)(2,1)S(1)}, bf16[256,512]{1,0:T(8,128)(2,1)}, u32[]{:S(2)}, u32[]{:S(2)}) collective-permute-start(bf16[256,512]{1,0:T(8,128)(2,1)S(1)} %collective-permute-done.20.refs_7_), channel_id=1, source_target_pairs={{0,8},{4,12},{8,0},{12,4},{16,24},{20,28},{24,16},{28,20},{32,40},... | collective-permute-start | bytes 786440 | tf_op jit(solution)/shard_map/ppermute | solution.py:56
  119.7 4.8 %collective-permute-done.26.refs_3_ = bf16[256,512]{1,0:T(8,128)(2,1)S(1)} collective-permute-done((bf16[256,512]{1,0:T(8,128)(2,1)S(1)}, bf16[256,512]{1,0:T(8,128)(2,1)S(1)}, u32[]{:S(2)}, u32[]{:S(2)}) %collective-permute-start.26) | collective-permute-done | bytes 262176 | tf_op jit(solution)/shard_map/ppermute | solution.py:56
  124.5 0.7 copy-done.3
  125.2 2.2 %collective-permute-done.25.refs_2_ = bf16[256,512]{1,0:T(8,128)(2,1)} collective-permute-done((bf16[256,512]{1,0:T(8,128)(2,1)S(1)}, bf16[256,512]{1,0:T(8,128)(2,1)}, u32[]{:S(2)}, u32[]{:S(2)}) %collective-permute-start.25) | collective-permute-done | bytes 262176 | tf_op jit(solution)/shard_map/ppermute | solution.py:56
  127.4 1.5 collective-permute-done.28.refs_6_
  128.9 0.9 copy-done.4
  129.8 3.2 %project.1 = (f32[160,512]{1,0:T(8,128)S(1)}, bf16[160,512]{1,0:T(8,128)(2,1)}, bf16[160,512]{1,0:T(8,128)(2,1)}, bf16[160,512]{1,0:T(8,128)(2,1)}) custom-call(s32[3]{0:T(128)S(1)} %copy-done.5, bf16[512,2048]{1,0:T(8,128)(2,1)S(1)} %get-tuple-element.49.hidden_ref, bf16[256,512]{1,0:T(8,128)(2,1)S(1)} %get-tuple-element.56.refs_0_, ...), custom_call_target="tpu_custom_call" | custom-call | flops 1073741824 | bytes 4194304 | tf_op jit(solution)/shard_map/project/pallas_call | solution.py:471
  133.8 1.2 collective-permute-start.31
  134.9 1.1 convert_reduce_fusion
  136.1 2.5 %collective-permute-start.33 = (f32[32,512]{1,0:T(8,128)S(1)}, f32[32,512]{1,0:T(8,128)S(1)}, u32[]{:S(2)}, u32[]{:S(2)}) collective-permute-start(f32[32,512]{1,0:T(8,128)S(1)} %get-tuple-element.67), channel_id=1, source_target_pairs={{0,4},{1,68},{2,132},{3,196},{4,0},{5,64},{6,128},{7,192},{8,12},{... | collective-permute-start | bytes 196616 | tf_op jit(solution)/shard_map/ppermute | solution.py:145
  138.6 4.3 %collective-permute-start.32 = (f32[32,512]{1,0:T(8,128)S(1)}, f32[32,512]{1,0:T(8,128)S(1)}, u32[]{:S(2)}, u32[]{:S(2)}) collective-permute-start(f32[32,512]{1,0:T(8,128)S(1)} %get-tuple-element.68), channel_id=1, source_target_pairs={{0,0},{1,64},{2,128},{3,192},{4,4},{5,68},{6,132},{7,196},{8,8},{9... | collective-permute-start | bytes 196616 | tf_op jit(solution)/shard_map/ppermute | solution.py:145
  142.9 1.7 %spread.1 = bf16[3,128,512]{2,1,0:T(8,128)(2,1)} custom-call(s32[3]{0:T(128)S(1)} %copy-done.5, s32[1,8]{1,0:T(1,128)S(1)} %copy-done.6, s32[3]{0:T(128)S(1)} %copy-done.7, f32[160,512]{1,0:T(8,128)S(1)} %get-tuple-element.60.refs_0_, bf16[160,512]{1,0:T(8,128)(2,1)S(1)} %collective-permute-done.29.refs_1_, ...), custom_call_target="tpu_custom_call" | custom-call | flops 62914560 | bytes 1572864 | tf_op jit(solution)/shard_map/spread/pallas_call | solution.py:497
  144.6 6.3 %collective-permute-done.33 = f32[32,512]{1,0:T(8,128)S(1)} collective-permute-done((f32[32,512]{1,0:T(8,128)S(1)}, f32[32,512]{1,0:T(8,128)S(1)}, u32[]{:S(2)}, u32[]{:S(2)}) %collective-permute-start.33) | collective-permute-done | bytes 65568 | tf_op jit(solution)/shard_map/ppermute | solution.py:145
  150.9 1.8 %collective-permute-done.32 = f32[32,512]{1,0:T(8,128)S(1)} collective-permute-done((f32[32,512]{1,0:T(8,128)S(1)}, f32[32,512]{1,0:T(8,128)S(1)}, u32[]{:S(2)}, u32[]{:S(2)}) %collective-permute-start.32) | collective-permute-done | bytes 65568 | tf_op jit(solution)/shard_map/ppermute | solution.py:145
  152.8 0.7 multiply_reduce_fusion
  (67 shorter events, 5.5 us)
Async XLA Ops:
  0.6 22.9 %collective-permute-start.2 = (bf16[32,512]{1,0:T(8,128)(2,1)}, bf16[32,512]{1,0:T(8,128)(2,1)S(1)}, u32[]{:S(2)}, u32[]{:S(2)}) collective-permute-start(bf16[32,512]{1,0:T(8,128)(2,1)} %param.18), channel_id=1, source_target_pairs={{0,128},{1,132},{2,160},{3,164},{4,192},{5,196},{6,224},{7,228},{8... | collective-permute-start | bytes 98312 | tf_op jit(solution)/shard_map/ppermute | solution.py:72
  9.2 14.3 %collective-permute-start.1 = (bf16[32,512]{1,0:T(8,128)(2,1)}, bf16[32,512]{1,0:T(8,128)(2,1)S(1)}, u32[]{:S(2)}, u32[]{:S(2)}) collective-permute-start(bf16[32,512]{1,0:T(8,128)(2,1)} %param.18), channel_id=1, source_target_pairs={{0,4},{1,0},{2,36},{3,32},{4,68},{5,64},{6,100},{7,96},{8,132},{9,... | collective-permute-start | bytes 98312 | tf_op jit(solution)/shard_map/ppermute | solution.py:72
  12.0 11.4 %collective-permute-start = (bf16[32,512]{1,0:T(8,128)(2,1)}, bf16[32,512]{1,0:T(8,128)(2,1)S(1)}, u32[]{:S(2)}, u32[]{:S(2)}) collective-permute-start(bf16[32,512]{1,0:T(8,128)(2,1)} %param.18), channel_id=1, source_target_pairs={{0,0},{1,4},{2,32},{3,36},{4,64},{5,68},{6,96},{7,100},{8,128},{9,... | collective-permute-start | bytes 98312 | tf_op jit(solution)/shard_map/ppermute | solution.py:72
  14.0 10.8 %collective-permute-start.3 = (bf16[32,512]{1,0:T(8,128)(2,1)}, bf16[32,512]{1,0:T(8,128)(2,1)S(1)}, u32[]{:S(2)}, u32[]{:S(2)}) collective-permute-start(bf16[32,512]{1,0:T(8,128)(2,1)} %param.18), channel_id=1, source_target_pairs={{0,132},{1,128},{2,164},{3,160},{4,196},{5,192},{6,228},{7,224},{8... | collective-permute-start | bytes 98312 | tf_op jit(solution)/shard_map/ppermute | solution.py:72
  24.8 7.0 %copy-start.6 = (s32[1,8]{1,0:T(1,128)S(1)}, s32[1,8]{1,0:T(1,128)}, u32[]{:S(2)}) copy-start(s32[1,8]{1,0:T(1,128)} %lengths_ref.5) | copy-start | bytes 100
  24.8 7.0 %copy-start.9 = (bf16[512,2048]{1,0:T(8,128)(2,1)S(1)}, bf16[512,2048]{1,0:T(8,128)(2,1)}, u32[]{:S(2)}) copy-start(bf16[512,2048]{1,0:T(8,128)(2,1)} %query_ref.1) | copy-start | bytes 6291460
  24.9 7.0 %copy-start.10 = (bf16[512,256]{1,0:T(8,128)(2,1)S(1)}, bf16[512,256]{1,0:T(8,128)(2,1)}, u32[]{:S(2)}) copy-start(bf16[512,256]{1,0:T(8,128)(2,1)} %key_ref.1) | copy-start | bytes 786436
  24.9 7.0 %copy-start.11 = (bf16[512,256]{1,0:T(8,128)(2,1)S(1)}, bf16[512,256]{1,0:T(8,128)(2,1)}, u32[]{:S(2)}) copy-start(bf16[512,256]{1,0:T(8,128)(2,1)} %value_ref.1) | copy-start | bytes 786436
  29.8 35.5 %collective-permute-start.7 = (bf16[128,2048]{1,0:T(8,128)(2,1)}, bf16[128,2048]{1,0:T(8,128)(2,1)S(1)}, u32[]{:S(2)}, u32[]{:S(2)}) collective-permute-start(bf16[128,2048]{1,0:T(8,128)(2,1)} %get-tuple-element.40), channel_id=1, source_target_pairs={{0,1},{1,0},{2,3},{3,2},{4,5},{5,4},{6,7},{7,6},{8,9},{9,8},{10,11... | collective-permute-start | bytes 1572872 | tf_op jit(solution)/shard_map/ppermute | solution.py:534
  29.9 35.5 %collective-permute-start.8 = (bf16[128,2048]{1,0:T(8,128)(2,1)}, bf16[128,2048]{1,0:T(8,128)(2,1)S(1)}, u32[]{:S(2)}, u32[]{:S(2)}) collective-permute-start(bf16[128,2048]{1,0:T(8,128)(2,1)} %get-tuple-element.41), channel_id=1, source_target_pairs={{0,2},{1,3},{2,0},{3,1},{4,6},{5,7},{6,4},{7,5},{8,10},{9,11},{10,... | collective-permute-start | bytes 1572872 | tf_op jit(solution)/shard_map/ppermute | solution.py:534
  30.0 13.0 %copy-start.2 = (bf16[3,128,512]{2,1,0:T(8,128)(2,1)S(1)}, bf16[3,128,512]{2,1,0:T(8,128)(2,1)}, u32[]{:S(2)}) copy-start(bf16[3,128,512]{2,1,0:T(8,128)(2,1)} %cotangent_ref) | copy-start | bytes 1179652
  30.0 12.9 %copy-start.5 = (s32[3]{0:T(128)S(1)}, s32[3]{0:T(128)}, u32[]{:S(2)}) copy-start(s32[3]{0:T(128)} %pad_add_fusion.place_ref) | copy-start | bytes 40
  30.0 12.9 %copy-start.7 = (s32[3]{0:T(128)S(1)}, s32[3]{0:T(128)}, u32[]{:S(2)}) copy-start(s32[3]{0:T(128)} %offsets_ref.3) | copy-start | bytes 40
  30.0 35.4 %copy-start = (bf16[128,2048]{1,0:T(8,128)(2,1)S(1)}, bf16[128,2048]{1,0:T(8,128)(2,1)}, u32[]{:S(2)}) copy-start(bf16[128,2048]{1,0:T(8,128)(2,1)} %get-tuple-element.39.refs_0_) | copy-start | bytes 1572868
  30.0 35.4 %copy-start.1 = (f32[3,8192]{1,0:T(4,128)S(1)}, f32[3,8192]{1,0:T(4,128)}, u32[]{:S(2)}) copy-start(f32[3,8192]{1,0:T(4,128)} %gain_ref.3) | copy-start | bytes 294916
  30.0 35.3 %collective-permute-start.9 = (bf16[128,2048]{1,0:T(8,128)(2,1)}, bf16[128,2048]{1,0:T(8,128)(2,1)S(1)}, u32[]{:S(2)}, u32[]{:S(2)}) collective-permute-start(bf16[128,2048]{1,0:T(8,128)(2,1)} %get-tuple-element.42), channel_id=1, source_target_pairs={{0,3},{1,2},{2,1},{3,0},{4,7},{5,6},{6,5},{7,4},{8,11},{9,10},{10,... | collective-permute-start | bytes 1572872 | tf_op jit(solution)/shard_map/ppermute | solution.py:534
  40.3 11.8 %collective-permute-start.6 = (bf16[128,512]{1,0:T(8,128)(2,1)S(1)}, bf16[128,512]{1,0:T(8,128)(2,1)S(1)}, u32[]{:S(2)}, u32[]{:S(2)}) collective-permute-start(bf16[128,512]{1,0:T(8,128)(2,1)S(1)} %maximum_select_fusion.refs_0_), channel_id=1, source_target_pairs={{0,96},{4,100},{8,104},{12,108},{16,112},{20,116},{24,120},{28,124... | collective-permute-start | bytes 393224 | tf_op jit(solution)/shard_map/ppermute | solution.py:56
  40.3 12.0 %collective-permute-start.5 = (bf16[128,512]{1,0:T(8,128)(2,1)S(1)}, bf16[128,512]{1,0:T(8,128)(2,1)S(1)}, u32[]{:S(2)}, u32[]{:S(2)}) collective-permute-start(bf16[128,512]{1,0:T(8,128)(2,1)S(1)} %maximum_select_fusion.refs_0_), channel_id=1, source_target_pairs={{0,64},{4,68},{8,72},{12,76},{16,80},{20,84},{24,88},{28,92},{32,9... | collective-permute-start | bytes 393224 | tf_op jit(solution)/shard_map/ppermute | solution.py:56
  52.1 7.8 %collective-permute-start.10 = (bf16[160,512]{1,0:T(8,128)(2,1)S(1)}, bf16[160,512]{1,0:T(8,128)(2,1)S(1)}, u32[]{:S(2)}, u32[]{:S(2)}) collective-permute-start(bf16[160,512]{1,0:T(8,128)(2,1)S(1)} %fold.1.refs_0_), channel_id=1, source_target_pairs={{0,1},{1,0},{2,3},{3,2},{4,5},{5,4},{6,7},{7,6},{8,9},{9,8},{10,11... | collective-permute-start | bytes 491528 | tf_op jit(solution)/shard_map/ppermute | solution.py:534
  52.3 7.0 %collective-permute-start.4 = (bf16[128,512]{1,0:T(8,128)(2,1)S(1)}, bf16[128,512]{1,0:T(8,128)(2,1)S(1)}, u32[]{:S(2)}, u32[]{:S(2)}) collective-permute-start(bf16[128,512]{1,0:T(8,128)(2,1)S(1)} %maximum_select_fusion.refs_0_), channel_id=1, source_target_pairs={{0,32},{4,36},{8,40},{12,44},{16,48},{20,52},{24,56},{28,60},{32,0... | collective-permute-start | bytes 393224 | tf_op jit(solution)/shard_map/ppermute | solution.py:56
  60.0 3.3 %collective-permute-start.13 = (f32[8,512]{1,0:T(8,128)S(1)}, f32[8,512]{1,0:T(8,128)S(1)}, u32[]{:S(2)}, u32[]{:S(2)}) collective-permute-start(f32[8,512]{1,0:T(8,128)S(1)} %get-tuple-element.45.refs_4_), channel_id=1, source_target_pairs={{0,3},{1,2},{2,1},{3,0},{4,7},{5,6},{6,5},{7,4},{8,11},{9,10},{10,... | collective-permute-start | bytes 49160 | tf_op jit(solution)/shard_map/ppermute | solution.py:534
  60.1 3.8 %collective-permute-start.12 = (f32[8,512]{1,0:T(8,128)S(1)}, f32[8,512]{1,0:T(8,128)S(1)}, u32[]{:S(2)}, u32[]{:S(2)}) collective-permute-start(f32[8,512]{1,0:T(8,128)S(1)} %get-tuple-element.45.refs_4_), channel_id=1, source_target_pairs={{0,2},{1,3},{2,0},{3,1},{4,6},{5,7},{6,4},{7,5},{8,10},{9,11},{10,... | collective-permute-start | bytes 49160 | tf_op jit(solution)/shard_map/ppermute | solution.py:534
  63.2 1.2 collective-permute-start.11
  63.9 6.7 %collective-permute-start.15 = (bf16[160,512]{1,0:T(8,128)(2,1)S(1)}, bf16[160,512]{1,0:T(8,128)(2,1)S(1)}, u32[]{:S(2)}, u32[]{:S(2)}) collective-permute-start(bf16[160,512]{1,0:T(8,128)(2,1)S(1)} %fold.1.refs_0_), channel_id=1, source_target_pairs={{0,3},{1,2},{2,1},{3,0},{4,7},{5,6},{6,5},{7,4},{8,11},{9,10},{10,... | collective-permute-start | bytes 491528 | tf_op jit(solution)/shard_map/ppermute | solution.py:534
  64.4 9.5 %collective-permute-start.14 = (bf16[160,512]{1,0:T(8,128)(2,1)S(1)}, bf16[160,512]{1,0:T(8,128)(2,1)S(1)}, u32[]{:S(2)}, u32[]{:S(2)}) collective-permute-start(bf16[160,512]{1,0:T(8,128)(2,1)S(1)} %fold.1.refs_0_), channel_id=1, source_target_pairs={{0,2},{1,3},{2,0},{3,1},{4,6},{5,7},{6,4},{7,5},{8,10},{9,11},{10,... | collective-permute-start | bytes 491528 | tf_op jit(solution)/shard_map/ppermute | solution.py:534
  65.4 9.2 %copy-start.8 = (f32[8192]{0:T(1024)S(1)}, f32[8192]{0:T(1024)}, u32[]{:S(2)}) copy-start(f32[8192]{0:T(1024)} %param.17) | copy-start | bytes 98308
  68.6 5.7 %collective-permute-start.18 = (f32[8,512]{1,0:T(8,128)S(1)}, f32[8,512]{1,0:T(8,128)S(1)}, u32[]{:S(2)}, u32[]{:S(2)}) collective-permute-start(f32[8,512]{1,0:T(8,128)S(1)} %get-tuple-element.47.refs_4_), channel_id=1, source_target_pairs={{0,3},{1,2},{2,1},{3,0},{4,7},{5,6},{6,5},{7,4},{8,11},{9,10},{10,... | collective-permute-start | bytes 49160 | tf_op jit(solution)/shard_map/ppermute | solution.py:534
  69.3 5.3 %collective-permute-start.17 = (f32[8,512]{1,0:T(8,128)S(1)}, f32[8,512]{1,0:T(8,128)S(1)}, u32[]{:S(2)}, u32[]{:S(2)}) collective-permute-start(f32[8,512]{1,0:T(8,128)S(1)} %get-tuple-element.47.refs_4_), channel_id=1, source_target_pairs={{0,2},{1,3},{2,0},{3,1},{4,6},{5,7},{6,4},{7,5},{8,10},{9,11},{10,... | collective-permute-start | bytes 49160 | tf_op jit(solution)/shard_map/ppermute | solution.py:534
  70.6 4.0 %collective-permute-start.16 = (f32[8,512]{1,0:T(8,128)S(1)}, f32[8,512]{1,0:T(8,128)S(1)}, u32[]{:S(2)}, u32[]{:S(2)}) collective-permute-start(f32[8,512]{1,0:T(8,128)S(1)} %get-tuple-element.47.refs_4_), channel_id=1, source_target_pairs={{0,1},{1,0},{2,3},{3,2},{4,5},{5,4},{6,7},{7,6},{8,9},{9,8},{10,11... | collective-permute-start | bytes 49160 | tf_op jit(solution)/shard_map/ppermute | solution.py:534
  77.5 14.4 %collective-permute-start.21 = (bf16[2,256,512]{2,1,0:T(8,128)(2,1)S(1)}, bf16[2,256,512]{2,1,0:T(8,128)(2,1)S(1)}, u32[]{:S(2)}, u32[]{:S(2)}) collective-permute-start(bf16[2,256,512]{2,1,0:T(8,128)(2,1)S(1)} %get-tuple-element.53), channel_id=1, source_target_pairs={{0,8},{4,12},{8,0},{12,4},{16,24},{20,28},{24,16},{28,20},{32,40},... | collective-permute-start | bytes 1572872 | tf_op jit(solution)/shard_map/ppermute | solution.py:56
  80.0 14.5 %collective-permute-start.23 = (bf16[2,256,512]{2,1,0:T(8,128)(2,1)S(1)}, bf16[2,256,512]{2,1,0:T(8,128)(2,1)S(1)}, u32[]{:S(2)}, u32[]{:S(2)}) collective-permute-start(bf16[2,256,512]{2,1,0:T(8,128)(2,1)S(1)} %get-tuple-element.55), channel_id=1, source_target_pairs={{0,24},{4,28},{8,16},{12,20},{16,8},{20,12},{24,0},{28,4},{32,56},... | collective-permute-start | bytes 1572872 | tf_op jit(solution)/shard_map/ppermute | solution.py:56
  92.0 10.5 %collective-permute-start.22 = (bf16[256,512]{1,0:T(8,128)(2,1)S(1)}, bf16[256,512]{1,0:T(8,128)(2,1)S(1)}, u32[]{:S(2)}, u32[]{:S(2)}) collective-permute-start(bf16[256,512]{1,0:T(8,128)(2,1)S(1)} %fusion), channel_id=1, source_target_pairs={{0,24},{4,28},{8,16},{12,20},{16,8},{20,12},{24,0},{28,4},{32,56},... | collective-permute-start | bytes 786440 | tf_op jit(solution)/shard_map/ppermute | solution.py:56
  94.6 9.3 %collective-permute-start.24 = (bf16[256,512]{1,0:T(8,128)(2,1)S(1)}, bf16[256,512]{1,0:T(8,128)(2,1)S(1)}, u32[]{:S(2)}, u32[]{:S(2)}) collective-permute-start(bf16[256,512]{1,0:T(8,128)(2,1)S(1)} %fusion.1), channel_id=1, source_target_pairs={{0,8},{4,12},{8,0},{12,4},{16,24},{20,28},{24,16},{28,20},{32,40},... | collective-permute-start | bytes 786440 | tf_op jit(solution)/shard_map/ppermute | solution.py:56
  94.7 12.4 %collective-permute-start.19 = (bf16[256,512]{1,0:T(8,128)(2,1)S(1)}, bf16[256,512]{1,0:T(8,128)(2,1)S(1)}, u32[]{:S(2)}, u32[]{:S(2)}) collective-permute-start(bf16[256,512]{1,0:T(8,128)(2,1)S(1)} %get-tuple-element.56.refs_0_), channel_id=1, source_target_pairs={{0,8},{4,12},{8,0},{12,4},{16,24},{20,28},{24,16},{28,20},{32,40},... | collective-permute-start | bytes 786440 | tf_op jit(solution)/shard_map/ppermute | solution.py:56
  96.8 10.4 %collective-permute-start.20 = (bf16[256,512]{1,0:T(8,128)(2,1)S(1)}, bf16[256,512]{1,0:T(8,128)(2,1)S(1)}, u32[]{:S(2)}, u32[]{:S(2)}) collective-permute-start(bf16[256,512]{1,0:T(8,128)(2,1)S(1)} %get-tuple-element.58.refs_4_), channel_id=1, source_target_pairs={{0,24},{4,28},{8,16},{12,20},{16,8},{20,12},{24,0},{28,4},{32,56},... | collective-permute-start | bytes 786440 | tf_op jit(solution)/shard_map/ppermute | solution.py:56
  107.1 27.8 %all-to-all-start = ((bf16[8,64,512]{2,1,0:T(8,128)(2,1)}), bf16[8,64,512]{2,1,0:T(8,128)(2,1)}, u32[]{:S(2)}, u32[]{:S(2)}) async-start(bf16[8,64,512]{2,1,0:T(8,128)(2,1)} %bitcast.14), calls=%async_computation | async-start | bytes 1048576 | tf_op jit(solution)/shard_map/all_to_all | solution.py:130
  114.5 10.0 %collective-permute-start.26 = (bf16[256,512]{1,0:T(8,128)(2,1)S(1)}, bf16[256,512]{1,0:T(8,128)(2,1)S(1)}, u32[]{:S(2)}, u32[]{:S(2)}) collective-permute-start(bf16[256,512]{1,0:T(8,128)(2,1)S(1)} %get-tuple-element.56.refs_0_), channel_id=1, source_target_pairs={{0,24},{4,28},{8,16},{12,20},{16,8},{20,12},{24,0},{28,4},{32,56},... | collective-permute-start | bytes 786440 | tf_op jit(solution)/shard_map/ppermute | solution.py:56
  116.6 10.8 %collective-permute-start.25 = (bf16[256,512]{1,0:T(8,128)(2,1)S(1)}, bf16[256,512]{1,0:T(8,128)(2,1)}, u32[]{:S(2)}, u32[]{:S(2)}) collective-permute-start(bf16[256,512]{1,0:T(8,128)(2,1)S(1)} %collective-permute-done.19.refs_1_), channel_id=1, source_target_pairs={{0,24},{4,28},{8,16},{12,20},{16,8},{20,12},{24,0},{28,4},{32,56},... | collective-permute-start | bytes 786440 | tf_op jit(solution)/shard_map/ppermute | solution.py:56
  117.7 9.7 %collective-permute-start.27 = (bf16[256,512]{1,0:T(8,128)(2,1)S(1)}, bf16[256,512]{1,0:T(8,128)(2,1)}, u32[]{:S(2)}, u32[]{:S(2)}) collective-permute-start(bf16[256,512]{1,0:T(8,128)(2,1)S(1)} %get-tuple-element.58.refs_4_), channel_id=1, source_target_pairs={{0,8},{4,12},{8,0},{12,4},{16,24},{20,28},{24,16},{28,20},{32,40},... | collective-permute-start | bytes 786440 | tf_op jit(solution)/shard_map/ppermute | solution.py:56
  117.7 11.2 %collective-permute-start.28 = (bf16[256,512]{1,0:T(8,128)(2,1)S(1)}, bf16[256,512]{1,0:T(8,128)(2,1)}, u32[]{:S(2)}, u32[]{:S(2)}) collective-permute-start(bf16[256,512]{1,0:T(8,128)(2,1)S(1)} %collective-permute-done.20.refs_7_), channel_id=1, source_target_pairs={{0,8},{4,12},{8,0},{12,4},{16,24},{20,28},{24,16},{28,20},{32,40},... | collective-permute-start | bytes 786440 | tf_op jit(solution)/shard_map/ppermute | solution.py:56
  124.5 0.7 copy-start.3
  128.9 1.0 copy-start.4
  133.1 19.7 %copy-start.12 = (bf16[32,512]{1,0:T(8,128)(2,1)S(1)}, bf16[32,512]{1,0:T(8,128)(2,1)}, u32[]{:S(2)}) copy-start(bf16[32,512]{1,0:T(8,128)(2,1)} %param.18) | copy-start | bytes 98308
  133.1 9.8 %collective-permute-start.29 = (bf16[160,512]{1,0:T(8,128)(2,1)}, bf16[160,512]{1,0:T(8,128)(2,1)S(1)}, u32[]{:S(2)}, u32[]{:S(2)}) collective-permute-start(bf16[160,512]{1,0:T(8,128)(2,1)} %get-tuple-element.61), channel_id=1, source_target_pairs={{0,1},{1,0},{2,3},{3,2},{4,5},{5,4},{6,7},{7,6},{8,9},{9,8},{10,11... | collective-permute-start | bytes 491528 | tf_op jit(solution)/shard_map/ppermute | solution.py:534
  133.1 9.8 %collective-permute-start.30 = (bf16[160,512]{1,0:T(8,128)(2,1)}, bf16[160,512]{1,0:T(8,128)(2,1)S(1)}, u32[]{:S(2)}, u32[]{:S(2)}) collective-permute-start(bf16[160,512]{1,0:T(8,128)(2,1)} %get-tuple-element.62), channel_id=1, source_target_pairs={{0,2},{1,3},{2,0},{3,1},{4,6},{5,7},{6,4},{7,5},{8,10},{9,11},{10,... | collective-permute-start | bytes 491528 | tf_op jit(solution)/shard_map/ppermute | solution.py:534
  133.8 9.2 %collective-permute-start.31 = (bf16[160,512]{1,0:T(8,128)(2,1)}, bf16[160,512]{1,0:T(8,128)(2,1)S(1)}, u32[]{:S(2)}, u32[]{:S(2)}) collective-permute-start(bf16[160,512]{1,0:T(8,128)(2,1)} %get-tuple-element.63), channel_id=1, source_target_pairs={{0,3},{1,2},{2,1},{3,0},{4,7},{5,6},{6,5},{7,4},{8,11},{9,10},{10,... | collective-permute-start | bytes 491528 | tf_op jit(solution)/shard_map/ppermute | solution.py:534
  136.1 14.9 %collective-permute-start.33 = (f32[32,512]{1,0:T(8,128)S(1)}, f32[32,512]{1,0:T(8,128)S(1)}, u32[]{:S(2)}, u32[]{:S(2)}) collective-permute-start(f32[32,512]{1,0:T(8,128)S(1)} %get-tuple-element.67), channel_id=1, source_target_pairs={{0,4},{1,68},{2,132},{3,196},{4,0},{5,64},{6,128},{7,192},{8,12},{... | collective-permute-start | bytes 196616 | tf_op jit(solution)/shard_map/ppermute | solution.py:145
  138.6 14.2 %collective-permute-start.32 = (f32[32,512]{1,0:T(8,128)S(1)}, f32[32,512]{1,0:T(8,128)S(1)}, u32[]{:S(2)}, u32[]{:S(2)}) collective-permute-start(f32[32,512]{1,0:T(8,128)S(1)} %get-tuple-element.68), channel_id=1, source_target_pairs={{0,0},{1,64},{2,128},{3,192},{4,4},{5,68},{6,132},{7,196},{8,8},{9... | collective-permute-start | bytes 196616 | tf_op jit(solution)/shard_map/ppermute | solution.py:145

commit v4 on v3

--- a/solution.py
+++ b/solution.py
@@ -56,50 +56,62 @@
     return lax.ppermute(values, "dp", pairs)
 
 
-def placed_weight(weight):
+def joined(own, got, own_first):
+    return jnp.where(own_first, jnp.concatenate([own, got]), jnp.concatenate([got, own]))
+
+
+def weight_of_chip(weight):
+    tn, j = lax.axis_size("tensor"), lax.axis_index("tensor")
+    return joined(weight, lax.ppermute(weight, "tensor", [(a, a ^ 1) for a in range(tn)]), j % 2 == 0)
+
+
+def weight_of_place(weight):
+    n, tn = lax.axis_size("dp"), lax.axis_size("tensor")
+    nx = sides_of(n)[2]
+    j, x = lax.axis_index("tensor"), lax.axis_index("dp") % nx
+    weight = joined(weight, lax.ppermute(weight, "tensor", [(a, a ^ 2) for a in range(tn)]), j < 2)
+    if nx > 1:
+        weight = joined(weight, moved(weight, lambda z, y, x: (z, y, x ^ 1)), x == 0)
+    return weight
+
+
+def weight_along_z(weight):
     n, tn = lax.axis_size("dp"), lax.axis_size("tensor")
     nz, ny, nx = sides_of(n)
-    x = lax.axis_index("dp") % nx
-    both = []
-    for far in (0, nz // 2) if nz > 1 else (0,):
-        parts = []
-        for turn in range(nx):
-            pairs = []
-            for j in range(tn):
-                for q in range(n):
-                    y, z, x0 = q // (nz * nx), (q // nx % nz) ^ far, (q + turn) % nx
-                    pairs.append((j * n + q, ((z * ny + y) * nx + x0) * tn + j))
-            parts.append(lax.ppermute(weight, ("dp", "tensor"), pairs))
-        both.append(parts)
-    if nx == 1:
-        return jnp.concatenate([parts[0] for parts in both])
-    return jnp.where(
-        x == 0,
-        jnp.concatenate([part for parts in both for part in parts]),
-        jnp.concatenate([part for parts in both for part in parts[::-1]]))
-
-
-def weight_along_z(part):
-    nz = sides_of(lax.axis_size("dp"))[0]
-    return [part] + [moved(part, lambda z, y, x: (z ^ s, y, x)) for s in range(1, nz // 2)]
-
-
-def weight_once(halves):
-    if sides_of(lax.axis_size("dp"))[1] == 1:
-        return [[half] for half in halves]
-    return [[half, moved(half, lambda z, y, x: (z, y ^ first, x))] for half, (first, _) in zip(halves, EXCHANGES)]
-
-
-def weight_twice(halves):
-    if sides_of(lax.axis_size("dp"))[1] == 1:
-        return halves
+    if nz == 1:
+        half = weight.shape[0] // (2 * tn)
+        j = lax.axis_index("tensor")
+        return [lax.dynamic_slice_in_dim(weight, (2 * j + h) * half, half) for h in range(2)]
     out = []
-    for half, (first, second) in zip(halves, EXCHANGES):
-        got = dict(zip((0, first), half))
-        for s in (0, first):
-            got[s ^ second] = moved(got[s], lambda z, y, x: (z, y ^ second, x))
-        out.append([got[s] for s in range(4)])
+    for m in range(2):
+        pairs = []
+        for z in range(nz):
+            for rest in range(ny * nx):
+                for t in range(tn):
+                    to = tn * ((z % 2) ^ m) + t
+                    pairs.append(((z * ny * nx + rest) * tn + t, (to * ny * nx + rest) * tn + z // 2))
+        out.append(lax.ppermute(weight, ("dp", "tensor"), pairs))
     return out
+
+
+def weight_once(parts):
+    nz, ny, _ = sides_of(lax.axis_size("dp"))
+    if ny == 1:
+        return [[part] for part in parts]
+    half = nz // 2
+    return [
+        [part, moved(part, lambda z, y, x: (z, y ^ EXCHANGES[z // half ^ m][0], x))]
+        for m, part in enumerate(parts)]
+
+
+def weight_twice(parts):
+    nz, ny, _ = sides_of(lax.axis_size("dp"))
+    if ny == 1:
+        return parts
+    half = nz // 2
+    return [
+        part + [moved(chunk, lambda z, y, x: (z, y ^ EXCHANGES[z // half ^ m][1], x)) for chunk in part]
+        for m, part in enumerate(parts)]
 
 
 KEPT = ((0, 3), (0, 1))
@@ -107,19 +119,19 @@
 EXCHANGES = ((1, 3), (3, 1))
 
 
-def reduce_along_y(kept, sent):
-    ny = sides_of(lax.axis_size("dp"))[1]
-    halves = []
-    for keep, send, (first, second) in zip(kept, sent, EXCHANGES):
-        if ny > 1:
-            got = moved(send, lambda z, y, x: (z, y ^ first, x))
-            own = keep[0] + got[0].astype(F32)
-            other = (keep[1] + got[1].astype(F32)).astype(BF16)
-            halves.append((own, moved(other, lambda z, y, x: (z, y ^ second, x))))
-        else:
-            halves.append((keep[0], None))
-    halves = [own if got is None else own + got.astype(F32) for own, got in halves]
-    return jnp.concatenate(halves)
+def reduce_once(kept, sent):
+    if sides_of(lax.axis_size("dp"))[1] == 1:
+        return [(keep[0], None) for keep in kept]
+    got = [moved(send, lambda z, y, x: (z, y ^ first, x)) for send, (first, _) in zip(sent, EXCHANGES)]
+    got = lax.optimization_barrier(got)
+    return [(keep[0] + part[0].astype(F32), (keep[1] + part[1].astype(F32)).astype(BF16)) for keep, part in zip(kept, got)]
+
+
+def reduce_twice(halves):
+    if sides_of(lax.axis_size("dp"))[1] == 1:
+        return jnp.concatenate([own for own, _ in halves])
+    got = [moved(other, lambda z, y, x: (z, y ^ second, x)) for (_, other), (_, second) in zip(halves, EXCHANGES)]
+    return jnp.concatenate([own + part.astype(F32) for (own, _), part in zip(halves, got)])
 
 
 def reduce_grad(grad):
@@ -202,7 +214,7 @@
 
 def features(place, low, mid, gain, tn):
     rows, width = low.shape
-    block = 32
+    block = 16
     piece = width // tn
     return pl.pallas_call(
         functools.partial(features_kernel, tn),
@@ -311,13 +323,13 @@
 
 
 def merge_kernel(width, tn, place_ref, gain_ref, high_ref, *refs):
-    parts, square_refs, out_ref, out_square_ref = refs[:tn], refs[tn:2 * tn], refs[2 * tn], refs[2 * tn + 1]
+    parts, square_refs, out_ref, out_square_ref = refs[:tn], refs[tn:-2], refs[-2], refs[-1]
     j = place_ref[0]
     rows = parts[0].shape[0]
     piece = high_ref.shape[1]
     squares = square_refs[0][...]
-    for s in range(1, tn):
-        squares = squares + square_refs[s][...]
+    for ref in square_refs[1:]:
+        squares = squares + ref[...]
     scales = lax.rsqrt(squares / width + EPSILON)
     for b in range(tn):
         out_square_ref[:, b * rows:(b + 1) * rows] = scales[:, b * rows:(b + 1) * rows]
@@ -341,7 +353,7 @@
     tn = len(parts)
     return pl.pallas_call(
         functools.partial(merge_kernel, width, tn),
-        in_specs=[SMEM] + [VMEM] * (2 + 2 * tn),
+        in_specs=[SMEM] + [VMEM] * (2 + tn + len(squares)),
         out_specs=[VMEM, VMEM],
         out_shape=[
             jax.ShapeDtypeStruct((pack, piece), BF16),
@@ -414,36 +426,6 @@
     return out[:2], out[2:-1] if ny > 1 else (None, None), out[-1]
 
 
-def stacked(place, parts, nz):
-    rows, vw = parts[0].shape
-    half = rows // 2
-
-    def kernel(place_ref, *refs):
-        part_refs, out_refs = refs[:-2], refs[-2:]
-        z = place_ref[2]
-        if nz == 1:
-            for h in range(2):
-                out_refs[h][...] = part_refs[0][h * half:(h + 1) * half, :]
-            return
-        for h in range(2):
-            @pl.when((z >= nz // 2) == (h == 1))
-            def _(h=h):
-                for s, ref in enumerate(part_refs):
-                    at = pl.ds(pl.multiple_of(((z ^ s) & (nz // 2 - 1)) * half, half), half)
-                    out_refs[h][at, :] = ref[0:half, :]
-                    out_refs[1 - h][at, :] = ref[half:rows, :]
-
-    return pl.pallas_call(
-        kernel,
-        in_specs=[SMEM] + [VMEM] * len(parts),
-        out_specs=[VMEM] * 2,
-        out_shape=[jax.ShapeDtypeStruct((half * len(parts), vw), BF16)] * 2,
-        compiler_params=pltpu.CompilerParams(vmem_limit_bytes=VMEM_LIMIT),
-        cost_estimate=pl.CostEstimate(flops=0, bytes_accessed=4 * len(parts) * rows * vw, transcendentals=0),
-        name="stacked",
-    )(place, *parts)
-
-
 def project(place, hidden, weights, tn):
     pack, piece = hidden.shape
     rows = pack // tn
@@ -452,16 +434,17 @@
 
     def kernel(place_ref, hidden_ref, *refs):
         weight_refs, value_refs, total_ref = refs[:2 * count], refs[2 * count:-1], refs[-1]
-        j, y = place_ref[0], place_ref[1]
+        j, y, half = place_ref[0], place_ref[1], place_ref[2]
         total_ref[0:OFFMAX, :] = jnp.zeros((OFFMAX, vw), F32)
         block = 128
         for c in range(0, pack, block):
             total = None
-            for h in range(2):
-                for s in range(count):
-                    at = pl.ds(pl.multiple_of((y ^ s) * 2 * part + h * part, part), part)
+            for m in range(2):
+                h = half ^ m
+                for s, at in enumerate((0, 1 + 2 * h, 3 - 2 * h, 2)[:count]):
+                    at = pl.ds(pl.multiple_of(h * count * part + (y ^ at) * part, part), part)
                     term = jnp.dot(
-                        hidden_ref[c:c + block, at], weight_refs[h * count + s][...], preferred_element_type=F32)
+                        hidden_ref[c:c + block, at], weight_refs[m * count + s][...], preferred_element_type=F32)
                     total = term if total is None else total + term
             total_ref[OFFMAX + c:OFFMAX + c + block, :] = total
         for s in range(tn):
@@ -524,7 +507,7 @@
     i = lax.axis_index("dp")
     flat = i * tn + j
     nz, ny, nx = sides_of(n)
-    place = jnp.stack([j, i // nx % ny, i // (ny * nx)]).astype(jnp.int32)
+    place = jnp.stack([j, i // nx % ny, i // (ny * nx) // max(1, nz // 2)]).astype(jnp.int32)
     width = low_feature.shape[1]
     piece = width // tn
     pack = target_queries.shape[0]
@@ -533,27 +516,28 @@
     def swapped(values, s):
         return lax.ppermute(values, "tensor", [(a, a ^ s) for a in range(tn)])
 
-    own_weight = placed_weight(draft_weight)
-    first_place, _ = lax.optimization_barrier((place, own_weight))
-    sent = features(first_place, low_feature, mid_feature, merging_gain, tn)
+    sent = features(place, low_feature, mid_feature, merging_gain, tn)
     parts = [sent[0]] + [swapped(sent[s], s) for s in range(1, tn)]
 
     high, squares = attend(doc_lengths, target_queries, target_keys, target_values)
-    own_weight, cotangent, _ = lax.optimization_barrier((own_weight, cotangent, high))
-    halves = stacked(place, weight_along_z(own_weight), nz)
+    own_weight, cotangent, high = lax.optimization_barrier((draft_weight, cotangent, high))
+    squares = squares + swapped(squares, 1)
+    own_weight = weight_of_chip(own_weight)
+    squares, own_weight = lax.optimization_barrier((squares, own_weight))
+    squares = [squares, swapped(squares, 2)]
     folded = fold(place, doc_lengths, step_offsets, cotangent)
-    folds = [folded] + [swapped(folded, s) for s in range(1, tn)]
-    squares, _, _ = lax.optimization_barrier((squares, halves[0], folds[1]))
+    across, beside = swapped(folded, 2), swapped(folded, 1)
+    merged, squares = merge(place, merging_gain, high, parts, squares, width)
+    across, merged = lax.optimization_barrier((across, merged))
+    folds = [folded, beside, across, swapped(across, 1)]
     squares = [squares] + [swapped(squares, s) for s in range(1, tn)]
-    merged, squares = merge(place, merging_gain, high, parts, squares, width)
-    squares = [squares] + [swapped(squares, s) for s in range(1, tn)]
+    weights = weight_once(weight_along_z(weight_of_place(own_weight)))
     kept, cut, hidden = grads(place, draft_gain.reshape(1, width), merged, folds, squares, width, ny, tn)
-    halves, hidden = lax.optimization_barrier((halves, hidden))
-    halves = weight_once(halves)
-    grad = reduce_along_y(kept, cut)
-    halves, grad = lax.optimization_barrier((halves, grad))
-    weights = weight_twice(halves)
-    weight_grad = reduce_grad(grad)
+    halves = reduce_once(kept, cut)
+    weights, own = lax.optimization_barrier((weights, [half[0] for half in halves]))
+    halves = [(mine, other) for mine, (_, other) in zip(own, halves)]
+    weight_grad = reduce_grad(reduce_twice(halves))
+    weights = weight_twice(weights)
 
     values = project(place, hidden, weights, tn)
     values = [values[0]] + [swapped(values[s], s) for s in range(1, tn)]

time: 155 us -> 154 us (level)
  waiting for transfers between devices: 59.8 us -> 50.6 us
  local copies, waits for them, and re-layouts: 1.73 us -> 8.91 us
  starting transfers between devices: 61.6 us -> 56.8 us
  other arithmetic: 4.33 us -> 8.36 us
  Pallas kernels: 25.8 us -> 28.2 us
    ppermute x13 -> x11, waiting for transfers between devices: 43.2 us -> 18.1 us  [moved(): return lax.ppermute(values, 'dp', pairs)]
    ppermute x4, starting transfers between devices: 22.3 us -> 9.48 us  [the longest x2 7.83 us: weight_along_z(): out.append(lax.ppermute(weight, ('dp', 'tensor'), pairs))]
    ppermute x15 -> x14, waiting for transfers between devices: 7.09 us -> 16.4 us  [swapped(): return lax.ppermute(values, 'tensor', [(a, a ^ s) for a in range(tn)])]
    unnamed x26 -> x46, local copies, waits for them, and re-layouts: 1.72 us -> 8.89 us
    all_to_all x1, starting transfers between devices: 7.32 us -> 14.3 us  [reduce_grad(): lax.all_to_all(grad.astype(BF16), 'dp', 0, 0, tiled=True, axis_index_grou...]
    ppermute x4, waiting for transfers between devices: 1.32 us -> 7.84 us  [the longest x2 7.84 us: weight_along_z(): out.append(lax.ppermute(weight, ('dp', 'tensor'), pairs))]
    ppermute x15 -> x14, starting transfers between devices: 8.17 us -> 11.6 us  [swapped(): return lax.ppermute(values, 'tensor', [(a, a ^ s) for a in range(tn)])]
    convert_element_type x2, other arithmetic: 0.16 us -> 2.67 us  [reduce_once(): (keep[1] + part[1].astype(F32)).astype(BF16)]
  transfers between devices with their start and end apart: 35 -> 32, of which waited for: 19 -> 15; matrix products, arithmetic and copies ran while one was open for 2% -> 4% of each run, Pallas kernels for 12% -> 14%
where the time goes in v4:
time: 154 us
  starting transfers between devices  56.8 us (37%)
  waiting for transfers between devices  50.6 us (33%)
  Pallas kernels  28.2 us (18%)
  local copies, waits for them, and re-layouts  8.91 us (6%)
  other arithmetic  8.36 us (5%)
    ppermute x11, waiting for transfers between devices, moved(): return lax.ppermute(values, 'dp', pairs)  18.1 us
    ppermute x14, waiting for transfers between devices, swapped(): return lax.ppermute(values, 'tensor', [(a, a ^ s) for a in range(tn)])  16.4 us
    ppermute x11, starting transfers between devices, moved(): return lax.ppermute(values, 'dp', pairs)  15.9 us
    all_to_all x1, starting transfers between devices, reduce_grad(): lax.all_to_all(grad.astype(BF16), 'dp', 0, 0, tiled=True, axis_index_grou...  14.3 us
    ppermute x14, starting transfers between devices, swapped(): return lax.ppermute(values, 'tensor', [(a, a ^ s) for a in range(tn)])  11.6 us
    unnamed x46, local copies, waits for them, and re-layouts  8.89 us
    ppermute x2, waiting for transfers between devices, reduce_grad(): part = lax.ppermute(part, ('dp', 'tensor'), pairs)  8.21 us
    pallas_call x1, Pallas kernels, attend(): pl.pallas_call(functools.partial(attend_kernel, window), grid=(pack // bl...  8.16 us
  transfers between devices with their start and end apart: 32, of which 15 were waited for; matrix products, arithmetic and copies ran while one was open for 4% of the time, Pallas kernels for 14%

profile of v4, /device:TPU:32, one launch (start us, length us, event | category | flops | bytes accessed | tf_op | source)
XLA Modules:
  0.0 153.8 jit_solution(3822894338269431834)
XLA Ops:
  1.3 6.8 %features.1 = (bf16[128,2048]{1,0:T(8,128)(2,1)}, bf16[128,2048]{1,0:T(8,128)(2,1)}, bf16[128,2048]{1,0:T(8,128)(2,1)}, bf16[128,2048]{1,0:T(8,128)(2,1)}) custom-call(s32[3]{0:T(128)} %pad_add_fusion.place_ref, bf16[128,8192]{1,0:T(8,128)(2,1)} %low_ref.1, bf16[128,8192]{1,0:T(8,128)(2,1)} %mid_ref.1, f32[3,8192]{1,0:T(4,128)} %gain_ref.3), custom_call_target="tpu_custom_call" | custom-call | flops 10485760 | bytes 6291456 | tf_op jit(solution)/shard_map/features/pallas_call | solution.py:219
  8.2 1.6 %collective-permute-start.2 = (bf16[128,2048]{1,0:T(8,128)(2,1)}, bf16[128,2048]{1,0:T(8,128)(2,1)}, u32[]{:S(2)}, u32[]{:S(2)}) collective-permute-start(bf16[128,2048]{1,0:T(8,128)(2,1)} %get-tuple-element.40), channel_id=1, source_target_pairs={{0,2},{1,3},{2,0},{3,1},{4,6},{5,7},{6,4},{7,5},{8,10},{9,11},{10,... | collective-permute-start | bytes 1572872 | tf_op jit(solution)/shard_map/ppermute | solution.py:517
  10.2 1.6 %copy-done.15 = bf16[512,2048]{1,0:T(8,128)(2,1)S(1)} copy-done((bf16[512,2048]{1,0:T(8,128)(2,1)S(1)}, bf16[512,2048]{1,0:T(8,128)(2,1)}, u32[]{:S(2)}) %copy-start.15) | copy-done | bytes 2097176
  11.8 8.2 %attend.1 = (bf16[512,2048]{1,0:T(8,128)(2,1)S(1)}, f32[8,512]{1,0:T(8,128)S(1)}) custom-call(s32[1,8]{1,0:T(1,128)S(1)} %copy-done.12, bf16[512,2048]{1,0:T(8,128)(2,1)S(1)} %copy-done.15, bf16[512,256]{1,0:T(8,128)(2,1)S(1)} %copy-done.18, bf16[512,256]{1,0:T(8,128)(2,1)S(1)} %copy-done.19), custom_call_target="tpu_custom_call" | custom-call | flops 1610612736 | bytes 4194304 | tf_op jit(solution)/shard_map/attend/pallas_call | solution.py:270
  20.5 0.9 fold.1.refs_0_
  21.4 1.6 %collective-permute-start = (bf16[160,512]{1,0:T(8,128)(2,1)S(1)}, bf16[160,512]{1,0:T(8,128)(2,1)}, u32[]{:S(2)}, u32[]{:S(2)}) collective-permute-start(bf16[160,512]{1,0:T(8,128)(2,1)S(1)} %fold.1.refs_0_), channel_id=1, source_target_pairs={{0,2},{1,3},{2,0},{3,1},{4,6},{5,7},{6,4},{7,5},{8,10},{9,11},{10,... | collective-permute-start | bytes 491528 | tf_op jit(solution)/shard_map/ppermute | solution.py:517
  24.2 13.7 %collective-permute-done.6.refs_5_ = f32[8,512]{1,0:T(8,128)S(1)} collective-permute-done((f32[8,512]{1,0:T(8,128)S(1)}, f32[8,512]{1,0:T(8,128)S(1)}, u32[]{:S(2)}, u32[]{:S(2)}) %collective-permute-start.6) | collective-permute-done | bytes 16416 | tf_op jit(solution)/shard_map/ppermute | solution.py:517
  37.9 3.8 %merge.1 = (bf16[512,2048]{1,0:T(8,128)(2,1)S(1)}, f32[8,512]{1,0:T(8,128)S(1)}) custom-call(s32[3]{0:T(128)S(1)} %copy-done.11, f32[3,8192]{1,0:T(4,128)S(1)} %copy-done.2, bf16[512,2048]{1,0:T(8,128)(2,1)S(1)} %get-tuple-element.37.high_ref, bf16[128,2048]{1,0:T(8,128)(2,1)S(1)} %copy-done.1, bf16[128,2048]{1,0:T(8,128)(2,1)S(1)} %collective-permute-done.1.refs_1_, ...), custom_call_target="tpu_custom_call" | custom-call | flops 8388608 | bytes 6291456 | tf_op jit(solution)/shard_map/merge/pallas_call | solution.py:354
  41.7 1.4 copy-done.16
  43.6 1.5 collective-permute-start.10
  45.7 1.5 collective-permute-start.12
  47.3 1.0 collective-permute-done.11.refs_7_
  49.0 1.6 %copy-done.17 = bf16[512,2048]{1,0:T(8,128)(2,1)S(1)} copy-done((bf16[512,2048]{1,0:T(8,128)(2,1)S(1)}, bf16[512,2048]{1,0:T(8,128)(2,1)}, u32[]{:S(2)}) %copy-start.17) | copy-done | bytes 2097176
  50.6 0.9 copy-done.21
  51.5 3.6 %grads.1 = (f32[2,256,512]{2,1,0:T(8,128)S(1)}, f32[2,256,512]{2,1,0:T(8,128)S(1)}, bf16[2,256,512]{2,1,0:T(8,128)(2,1)}, bf16[2,256,512]{2,1,0:T(8,128)(2,1)}, bf16[512,2048]{1,0:T(8,128)(2,1)S(1)}) custom-call(s32[3]{0:T(128)S(1)} %copy-done.11, f32[1,8192]{1,0:T(1,128)S(1)} %bitcast.13, bf16[512,2048]{1,0:T(8,128)(2,1)S(1)} %copy-done.17, ...), custom_call_target="tpu_custom_call" | custom-call | flops 1073741824 | bytes 8388608 | tf_op jit(solution)/shard_map/grads/pallas_call | solution.py:416
  55.1 1.0 copy-done
  56.1 1.6 %collective-permute-start.18 = (bf16[2,256,512]{2,1,0:T(8,128)(2,1)}, bf16[2,256,512]{2,1,0:T(8,128)(2,1)}, u32[]{:S(2)}, u32[]{:S(2)}) collective-permute-start(bf16[2,256,512]{2,1,0:T(8,128)(2,1)} %get-tuple-element.52), channel_id=1, source_target_pairs={{0,8},{4,12},{8,0},{12,4},{16,24},{20,28},{24,16},{28,20},{32,40},... | collective-permute-start | bytes 1572872 | tf_op jit(solution)/shard_map/ppermute | solution.py:56
  57.7 2.2 %collective-permute-start.19 = (bf16[2,256,512]{2,1,0:T(8,128)(2,1)}, bf16[2,256,512]{2,1,0:T(8,128)(2,1)}, u32[]{:S(2)}, u32[]{:S(2)}) collective-permute-start(bf16[2,256,512]{2,1,0:T(8,128)(2,1)} %get-tuple-element.53), channel_id=1, source_target_pairs={{0,24},{4,28},{8,16},{12,20},{16,8},{20,12},{24,0},{28,4},{32,56},... | collective-permute-start | bytes 1572872 | tf_op jit(solution)/shard_map/ppermute | solution.py:56
  59.9 0.9 maximum_select_fusion.1
  60.8 2.8 %collective-permute-start.13 = (bf16[128,512]{1,0:T(8,128)(2,1)S(1)}, bf16[128,512]{1,0:T(8,128)(2,1)S(1)}, u32[]{:S(2)}, u32[]{:S(2)}) collective-permute-start(bf16[128,512]{1,0:T(8,128)(2,1)S(1)} %maximum_select_fusion.1), channel_id=1, source_target_pairs={{0,4},{4,0},{8,12},{12,8},{16,20},{20,16},{24,28},{28,24},{32,36},... | collective-permute-start | bytes 393224 | tf_op jit(solution)/shard_map/ppermute | solution.py:56
  63.6 3.7 %collective-permute-done.13 = bf16[128,512]{1,0:T(8,128)(2,1)S(1)} collective-permute-done((bf16[128,512]{1,0:T(8,128)(2,1)S(1)}, bf16[128,512]{1,0:T(8,128)(2,1)S(1)}, u32[]{:S(2)}, u32[]{:S(2)}) %collective-permute-start.13) | collective-permute-done | bytes 131104 | tf_op jit(solution)/shard_map/ppermute | solution.py:56
  67.5 7.7 %collective-permute-start.14 = (bf16[256,512]{1,0:T(8,128)(2,1)S(1)}, bf16[256,512]{1,0:T(8,128)(2,1)S(1)}, u32[]{:S(2)}, u32[]{:S(2)}) collective-permute-start(bf16[256,512]{1,0:T(8,128)(2,1)S(1)} %maximum_select_fusion), channel_id=1, source_target_pairs={{0,0},{1,32},{2,64},{3,96},{4,4},{5,36},{6,68},{7,100},{8,8},{9,40... | collective-permute-start | bytes 786440 | tf_op jit(solution)/shard_map/ppermute | solution.py:93
  75.3 6.6 %collective-permute-done.14.refs_0_ = bf16[256,512]{1,0:T(8,128)(2,1)S(1)} collective-permute-done((bf16[256,512]{1,0:T(8,128)(2,1)S(1)}, bf16[256,512]{1,0:T(8,128)(2,1)S(1)}, u32[]{:S(2)}, u32[]{:S(2)}) %collective-permute-start.14) | collective-permute-done | bytes 262176 | tf_op jit(solution)/shard_map/ppermute | solution.py:93
  82.6 1.2 collective-permute-done.16.refs_4_
  83.8 1.0 collective-permute-start.17
  84.9 1.5 fusion
  86.4 2.3 %collective-permute-start.27 = (bf16[256,512]{1,0:T(8,128)(2,1)S(1)}, bf16[256,512]{1,0:T(8,128)(2,1)S(1)}, u32[]{:S(2)}, u32[]{:S(2)}) collective-permute-start(bf16[256,512]{1,0:T(8,128)(2,1)S(1)} %get-tuple-element.69), channel_id=1, source_target_pairs={{0,24},{4,28},{8,16},{12,20},{16,8},{20,12},{24,0},{28,4},{32,56},... | collective-permute-start | bytes 786440 | tf_op jit(solution)/shard_map/ppermute | solution.py:56
  88.7 1.2 fusion.1
  90.2 1.2 collective-permute-done.17.refs_5_
  92.1 4.4 %collective-permute-done.27 = bf16[256,512]{1,0:T(8,128)(2,1)S(1)} collective-permute-done((bf16[256,512]{1,0:T(8,128)(2,1)S(1)}, bf16[256,512]{1,0:T(8,128)(2,1)S(1)}, u32[]{:S(2)}, u32[]{:S(2)}) %collective-permute-start.27) | collective-permute-done | bytes 262176 | tf_op jit(solution)/shard_map/ppermute | solution.py:56
  96.7 0.8 pad_maximum_fusion
  97.5 14.3 %all-to-all-start = ((bf16[8,64,512]{2,1,0:T(8,128)(2,1)}), bf16[8,64,512]{2,1,0:T(8,128)(2,1)}, u32[]{:S(2)}, u32[]{:S(2)}) async-start(bf16[8,64,512]{2,1,0:T(8,128)(2,1)} %bitcast.14), calls=%async_computation | async-start | bytes 1048576 | tf_op jit(solution)/shard_map/all_to_all | solution.py:142
  111.8 1.9 %collective-permute-start.20 = (bf16[256,512]{1,0:T(8,128)(2,1)S(1)}, bf16[256,512]{1,0:T(8,128)(2,1)}, u32[]{:S(2)}, u32[]{:S(2)}) collective-permute-start(bf16[256,512]{1,0:T(8,128)(2,1)S(1)} %collective-permute-done.14.refs_0_), channel_id=1, source_target_pairs={{0,24},{4,28},{8,16},{12,20},{16,8},{20,12},{24,0},{28,4},{32,56},... | collective-permute-start | bytes 786440 | tf_op jit(solution)/shard_map/ppermute | solution.py:56
  113.6 1.4 collective-permute-start.21
  115.0 2.0 %collective-permute-start.23 = (bf16[256,512]{1,0:T(8,128)(2,1)S(1)}, bf16[256,512]{1,0:T(8,128)(2,1)}, u32[]{:S(2)}, u32[]{:S(2)}) collective-permute-start(bf16[256,512]{1,0:T(8,128)(2,1)S(1)} %copy-done.9), channel_id=1, source_target_pairs={{0,8},{4,12},{8,0},{12,4},{16,24},{20,28},{24,16},{28,20},{32,40},... | collective-permute-start | bytes 786440 | tf_op jit(solution)/shard_map/ppermute | solution.py:56
  117.0 4.3 %collective-permute-done.20.refs_2_ = bf16[256,512]{1,0:T(8,128)(2,1)} collective-permute-done((bf16[256,512]{1,0:T(8,128)(2,1)S(1)}, bf16[256,512]{1,0:T(8,128)(2,1)}, u32[]{:S(2)}, u32[]{:S(2)}) %collective-permute-start.20) | collective-permute-done | bytes 262176 | tf_op jit(solution)/shard_map/ppermute | solution.py:56
  121.3 2.8 %collective-permute-done.21.refs_3_ = bf16[256,512]{1,0:T(8,128)(2,1)} collective-permute-done((bf16[256,512]{1,0:T(8,128)(2,1)S(1)}, bf16[256,512]{1,0:T(8,128)(2,1)}, u32[]{:S(2)}, u32[]{:S(2)}) %collective-permute-start.21) | collective-permute-done | bytes 262176 | tf_op jit(solution)/shard_map/ppermute | solution.py:56
  124.1 1.5 collective-permute-done.23.refs_7_
  125.6 0.9 copy-done.10
  126.6 3.3 %project.1 = (f32[160,512]{1,0:T(8,128)S(1)}, bf16[160,512]{1,0:T(8,128)(2,1)}, bf16[160,512]{1,0:T(8,128)(2,1)}, bf16[160,512]{1,0:T(8,128)(2,1)S(1)}) custom-call(s32[3]{0:T(128)S(1)} %copy-done.11, bf16[512,2048]{1,0:T(8,128)(2,1)S(1)} %get-tuple-element.49.hidden_ref, bf16[256,512]{1,0:T(8,128)(2,1)S(1)} %collective-permute-done.14.refs_0_, ...), custom_call_target="tpu_custom_call" | custom-call | flops 1073741824 | bytes 4194304 | tf_op jit(solution)/shard_map/project/pallas_call | solution.py:454
  129.8 4.3 %collective-permute-start.25 = (bf16[160,512]{1,0:T(8,128)(2,1)}, bf16[160,512]{1,0:T(8,128)(2,1)S(1)}, u32[]{:S(2)}, u32[]{:S(2)}) collective-permute-start(bf16[160,512]{1,0:T(8,128)(2,1)} %get-tuple-element.63), channel_id=1, source_target_pairs={{0,2},{1,3},{2,0},{3,1},{4,6},{5,7},{6,4},{7,5},{8,10},{9,11},{10,... | collective-permute-start | bytes 491528 | tf_op jit(solution)/shard_map/ppermute | solution.py:517
  134.3 1.1 convert_reduce_fusion
  135.4 2.1 %collective-permute-start.29 = (f32[32,512]{1,0:T(8,128)S(1)}, f32[32,512]{1,0:T(8,128)S(1)}, u32[]{:S(2)}, u32[]{:S(2)}) collective-permute-start(f32[32,512]{1,0:T(8,128)S(1)} %get-tuple-element.74), channel_id=1, source_target_pairs={{0,0},{1,64},{2,128},{3,192},{4,4},{5,68},{6,132},{7,196},{8,8},{9... | collective-permute-start | bytes 196616 | tf_op jit(solution)/shard_map/ppermute | solution.py:157
  137.5 3.4 %collective-permute-start.30 = (f32[32,512]{1,0:T(8,128)S(1)}, f32[32,512]{1,0:T(8,128)S(1)}, u32[]{:S(2)}, u32[]{:S(2)}) collective-permute-start(f32[32,512]{1,0:T(8,128)S(1)} %get-tuple-element.73), channel_id=1, source_target_pairs={{0,4},{1,68},{2,132},{3,196},{4,0},{5,64},{6,128},{7,192},{8,12},{... | collective-permute-start | bytes 196616 | tf_op jit(solution)/shard_map/ppermute | solution.py:157
  141.0 1.6 %collective-permute-done.26.refs_3_ = bf16[160,512]{1,0:T(8,128)(2,1)S(1)} collective-permute-done((bf16[160,512]{1,0:T(8,128)(2,1)S(1)}, bf16[160,512]{1,0:T(8,128)(2,1)S(1)}, u32[]{:S(2)}, u32[]{:S(2)}) %collective-permute-start.26) | collective-permute-done | bytes 163872 | tf_op jit(solution)/shard_map/ppermute | solution.py:517
  142.5 1.7 %spread.1 = bf16[3,128,512]{2,1,0:T(8,128)(2,1)} custom-call(s32[3]{0:T(128)S(1)} %copy-done.11, s32[1,8]{1,0:T(1,128)S(1)} %copy-done.12, s32[3]{0:T(128)S(1)} %copy-done.13, f32[160,512]{1,0:T(8,128)S(1)} %get-tuple-element.61.refs_0_, bf16[160,512]{1,0:T(8,128)(2,1)S(1)} %collective-permute-done.24.refs_1_, ...), custom_call_target="tpu_custom_call" | custom-call | flops 62914560 | bytes 1572864 | tf_op jit(solution)/shard_map/spread/pallas_call | solution.py:480
  144.2 6.6 %collective-permute-done.29 = f32[32,512]{1,0:T(8,128)S(1)} collective-permute-done((f32[32,512]{1,0:T(8,128)S(1)}, f32[32,512]{1,0:T(8,128)S(1)}, u32[]{:S(2)}, u32[]{:S(2)}) %collective-permute-start.29) | collective-permute-done | bytes 65568 | tf_op jit(solution)/shard_map/ppermute | solution.py:157
  150.8 1.6 %collective-permute-done.30 = f32[32,512]{1,0:T(8,128)S(1)} collective-permute-done((f32[32,512]{1,0:T(8,128)S(1)}, f32[32,512]{1,0:T(8,128)S(1)}, u32[]{:S(2)}, u32[]{:S(2)}) %collective-permute-start.30) | collective-permute-done | bytes 65568 | tf_op jit(solution)/shard_map/ppermute | solution.py:157
  (83 shorter events, 8.3 us)
Async XLA Ops:
  1.3 8.9 %copy-start.12 = (s32[1,8]{1,0:T(1,128)S(1)}, s32[1,8]{1,0:T(1,128)}, u32[]{:S(2)}) copy-start(s32[1,8]{1,0:T(1,128)} %lengths_ref.5) | copy-start | bytes 100
  1.3 8.9 %copy-start.18 = (bf16[512,256]{1,0:T(8,128)(2,1)S(1)}, bf16[512,256]{1,0:T(8,128)(2,1)}, u32[]{:S(2)}) copy-start(bf16[512,256]{1,0:T(8,128)(2,1)} %key_ref.1) | copy-start | bytes 786436
  1.3 8.9 %copy-start.19 = (bf16[512,256]{1,0:T(8,128)(2,1)S(1)}, bf16[512,256]{1,0:T(8,128)(2,1)}, u32[]{:S(2)}) copy-start(bf16[512,256]{1,0:T(8,128)(2,1)} %value_ref.1) | copy-start | bytes 786436
  8.1 29.7 %collective-permute-start.1 = (bf16[128,2048]{1,0:T(8,128)(2,1)}, bf16[128,2048]{1,0:T(8,128)(2,1)S(1)}, u32[]{:S(2)}, u32[]{:S(2)}) collective-permute-start(bf16[128,2048]{1,0:T(8,128)(2,1)} %get-tuple-element.39), channel_id=1, source_target_pairs={{0,1},{1,0},{2,3},{3,2},{4,5},{5,4},{6,7},{7,6},{8,9},{9,8},{10,11... | collective-permute-start | bytes 1572872 | tf_op jit(solution)/shard_map/ppermute | solution.py:517
  8.2 29.7 %collective-permute-start.2 = (bf16[128,2048]{1,0:T(8,128)(2,1)}, bf16[128,2048]{1,0:T(8,128)(2,1)}, u32[]{:S(2)}, u32[]{:S(2)}) collective-permute-start(bf16[128,2048]{1,0:T(8,128)(2,1)} %get-tuple-element.40), channel_id=1, source_target_pairs={{0,2},{1,3},{2,0},{3,1},{4,6},{5,7},{6,4},{7,5},{8,10},{9,11},{10,... | collective-permute-start | bytes 1572872 | tf_op jit(solution)/shard_map/ppermute | solution.py:517
  9.8 10.7 %copy-start.3 = (bf16[3,128,512]{2,1,0:T(8,128)(2,1)S(1)}, bf16[3,128,512]{2,1,0:T(8,128)(2,1)}, u32[]{:S(2)}) copy-start(bf16[3,128,512]{2,1,0:T(8,128)(2,1)} %cotangent_ref) | copy-start | bytes 1179652
  9.8 10.7 %copy-start.11 = (s32[3]{0:T(128)S(1)}, s32[3]{0:T(128)}, u32[]{:S(2)}) copy-start(s32[3]{0:T(128)} %pad_add_fusion.place_ref) | copy-start | bytes 40
  9.8 10.7 %copy-start.13 = (s32[3]{0:T(128)S(1)}, s32[3]{0:T(128)}, u32[]{:S(2)}) copy-start(s32[3]{0:T(128)} %offsets_ref.3) | copy-start | bytes 40
  9.8 28.1 %copy-start.1 = (bf16[128,2048]{1,0:T(8,128)(2,1)S(1)}, bf16[128,2048]{1,0:T(8,128)(2,1)}, u32[]{:S(2)}) copy-start(bf16[128,2048]{1,0:T(8,128)(2,1)} %get-tuple-element.38.refs_0_) | copy-start | bytes 1572868
  9.8 28.1 %copy-start.2 = (f32[3,8192]{1,0:T(4,128)S(1)}, f32[3,8192]{1,0:T(4,128)}, u32[]{:S(2)}) copy-start(f32[3,8192]{1,0:T(4,128)} %gain_ref.3) | copy-start | bytes 294916
  9.8 28.1 %collective-permute-start.3 = (bf16[128,2048]{1,0:T(8,128)(2,1)}, bf16[128,2048]{1,0:T(8,128)(2,1)}, u32[]{:S(2)}, u32[]{:S(2)}) collective-permute-start(bf16[128,2048]{1,0:T(8,128)(2,1)} %get-tuple-element.41), channel_id=1, source_target_pairs={{0,3},{1,2},{2,1},{3,0},{4,7},{5,6},{6,5},{7,4},{8,11},{9,10},{10,... | collective-permute-start | bytes 1572872 | tf_op jit(solution)/shard_map/ppermute | solution.py:517
  10.2 1.6 %copy-start.15 = (bf16[512,2048]{1,0:T(8,128)(2,1)S(1)}, bf16[512,2048]{1,0:T(8,128)(2,1)}, u32[]{:S(2)}) copy-start(bf16[512,2048]{1,0:T(8,128)(2,1)} %query_ref.1) | copy-start | bytes 6291460
  11.8 8.5 %copy-start.22 = (bf16[32,512]{1,0:T(8,128)(2,1)S(1)}, bf16[32,512]{1,0:T(8,128)(2,1)}, u32[]{:S(2)}) copy-start(bf16[32,512]{1,0:T(8,128)(2,1)} %param.18) | copy-start | bytes 98308
  19.9 1.5 collective-permute-start.4
  20.3 2.7 %collective-permute-start.5 = (bf16[32,512]{1,0:T(8,128)(2,1)S(1)}, bf16[32,512]{1,0:T(8,128)(2,1)S(1)}, u32[]{:S(2)}, u32[]{:S(2)}) collective-permute-start(bf16[32,512]{1,0:T(8,128)(2,1)S(1)} %copy-done.22), channel_id=1, source_target_pairs={{0,1},{1,0},{2,3},{3,2},{4,5},{5,4},{6,7},{7,6},{8,9},{9,8},{10,11... | collective-permute-start | bytes 98312 | tf_op jit(solution)/shard_map/ppermute | solution.py:65
  21.4 21.7 %collective-permute-start = (bf16[160,512]{1,0:T(8,128)(2,1)S(1)}, bf16[160,512]{1,0:T(8,128)(2,1)}, u32[]{:S(2)}, u32[]{:S(2)}) collective-permute-start(bf16[160,512]{1,0:T(8,128)(2,1)S(1)} %fold.1.refs_0_), channel_id=1, source_target_pairs={{0,2},{1,3},{2,0},{3,1},{4,6},{5,7},{6,4},{7,5},{8,10},{9,11},{10,... | collective-permute-start | bytes 491528 | tf_op jit(solution)/shard_map/ppermute | solution.py:517
  23.6 14.2 %collective-permute-start.6 = (f32[8,512]{1,0:T(8,128)S(1)}, f32[8,512]{1,0:T(8,128)S(1)}, u32[]{:S(2)}, u32[]{:S(2)}) collective-permute-start(f32[8,512]{1,0:T(8,128)S(1)} %add.68.refs_4_), channel_id=1, source_target_pairs={{0,2},{1,3},{2,0},{3,1},{4,6},{5,7},{6,4},{7,5},{8,10},{9,11},{10,... | collective-permute-start | bytes 49160 | tf_op jit(solution)/shard_map/ppermute | solution.py:517
  37.8 7.9 %collective-permute-start.7 = (bf16[160,512]{1,0:T(8,128)(2,1)S(1)}, bf16[160,512]{1,0:T(8,128)(2,1)}, u32[]{:S(2)}, u32[]{:S(2)}) collective-permute-start(bf16[160,512]{1,0:T(8,128)(2,1)S(1)} %fold.1.refs_0_), channel_id=1, source_target_pairs={{0,1},{1,0},{2,3},{3,2},{4,5},{5,4},{6,7},{7,6},{8,9},{9,8},{10,11... | collective-permute-start | bytes 491528 | tf_op jit(solution)/shard_map/ppermute | solution.py:517
  37.9 11.1 %copy-start.14 = (f32[8192]{0:T(1024)S(1)}, f32[8192]{0:T(1024)}, u32[]{:S(2)}) copy-start(f32[8192]{0:T(1024)} %param.17) | copy-start | bytes 98308
  43.1 5.2 %collective-permute-start.8 = (bf16[160,512]{1,0:T(8,128)(2,1)}, bf16[160,512]{1,0:T(8,128)(2,1)S(1)}, u32[]{:S(2)}, u32[]{:S(2)}) collective-permute-start(bf16[160,512]{1,0:T(8,128)(2,1)} %collective-permute-done.refs_2_), channel_id=1, source_target_pairs={{0,1},{1,0},{2,3},{3,2},{4,5},{5,4},{6,7},{7,6},{8,9},{9,8},{10,11... | collective-permute-start | bytes 491528 | tf_op jit(solution)/shard_map/ppermute | solution.py:517
  43.6 3.7 %collective-permute-start.10 = (f32[8,512]{1,0:T(8,128)S(1)}, f32[8,512]{1,0:T(8,128)S(1)}, u32[]{:S(2)}, u32[]{:S(2)}) collective-permute-start(f32[8,512]{1,0:T(8,128)S(1)} %get-tuple-element.48.refs_4_), channel_id=1, source_target_pairs={{0,2},{1,3},{2,0},{3,1},{4,6},{5,7},{6,4},{7,5},{8,10},{9,11},{10,... | collective-permute-start | bytes 49160 | tf_op jit(solution)/shard_map/ppermute | solution.py:517
  45.1 3.2 %collective-permute-start.11 = (f32[8,512]{1,0:T(8,128)S(1)}, f32[8,512]{1,0:T(8,128)S(1)}, u32[]{:S(2)}, u32[]{:S(2)}) collective-permute-start(f32[8,512]{1,0:T(8,128)S(1)} %get-tuple-element.48.refs_4_), channel_id=1, source_target_pairs={{0,3},{1,2},{2,1},{3,0},{4,7},{5,6},{6,5},{7,4},{8,11},{9,10},{10,... | collective-permute-start | bytes 49160 | tf_op jit(solution)/shard_map/ppermute | solution.py:517
  45.1 3.2 %collective-permute-start.9 = (f32[8,512]{1,0:T(8,128)S(1)}, f32[8,512]{1,0:T(8,128)S(1)}, u32[]{:S(2)}, u32[]{:S(2)}) collective-permute-start(f32[8,512]{1,0:T(8,128)S(1)} %get-tuple-element.48.refs_4_), channel_id=1, source_target_pairs={{0,1},{1,0},{2,3},{3,2},{4,5},{5,4},{6,7},{7,6},{8,9},{9,8},{10,11... | collective-permute-start | bytes 49160 | tf_op jit(solution)/shard_map/ppermute | solution.py:517
  45.7 14.1 %collective-permute-start.12 = (bf16[64,512]{1,0:T(8,128)(2,1)}, bf16[64,512]{1,0:T(8,128)(2,1)S(1)}, u32[]{:S(2)}, u32[]{:S(2)}) collective-permute-start(bf16[64,512]{1,0:T(8,128)(2,1)} %maximum_select_fusion.2), channel_id=1, source_target_pairs={{0,2},{1,3},{2,0},{3,1},{4,6},{5,7},{6,4},{7,5},{8,10},{9,11},{10,... | collective-permute-start | bytes 196616 | tf_op jit(solution)/shard_map/ppermute | solution.py:72
  49.0 1.6 %copy-start.17 = (bf16[512,2048]{1,0:T(8,128)(2,1)S(1)}, bf16[512,2048]{1,0:T(8,128)(2,1)}, u32[]{:S(2)}) copy-start(bf16[512,2048]{1,0:T(8,128)(2,1)} %copy-done.16) | copy-start | bytes 6291460
  56.1 28.8 %collective-permute-start.18 = (bf16[2,256,512]{2,1,0:T(8,128)(2,1)}, bf16[2,256,512]{2,1,0:T(8,128)(2,1)}, u32[]{:S(2)}, u32[]{:S(2)}) collective-permute-start(bf16[2,256,512]{2,1,0:T(8,128)(2,1)} %get-tuple-element.52), channel_id=1, source_target_pairs={{0,8},{4,12},{8,0},{12,4},{16,24},{20,28},{24,16},{28,20},{32,40},... | collective-permute-start | bytes 1572872 | tf_op jit(solution)/shard_map/ppermute | solution.py:56
  57.7 27.2 %collective-permute-start.19 = (bf16[2,256,512]{2,1,0:T(8,128)(2,1)}, bf16[2,256,512]{2,1,0:T(8,128)(2,1)}, u32[]{:S(2)}, u32[]{:S(2)}) collective-permute-start(bf16[2,256,512]{2,1,0:T(8,128)(2,1)} %get-tuple-element.53), channel_id=1, source_target_pairs={{0,24},{4,28},{8,16},{12,20},{16,8},{20,12},{24,0},{28,4},{32,56},... | collective-permute-start | bytes 1572872 | tf_op jit(solution)/shard_map/ppermute | solution.py:56
  60.8 6.6 %collective-permute-start.13 = (bf16[128,512]{1,0:T(8,128)(2,1)S(1)}, bf16[128,512]{1,0:T(8,128)(2,1)S(1)}, u32[]{:S(2)}, u32[]{:S(2)}) collective-permute-start(bf16[128,512]{1,0:T(8,128)(2,1)S(1)} %maximum_select_fusion.1), channel_id=1, source_target_pairs={{0,4},{4,0},{8,12},{12,8},{16,20},{20,16},{24,28},{28,24},{32,36},... | collective-permute-start | bytes 393224 | tf_op jit(solution)/shard_map/ppermute | solution.py:56
  67.5 14.5 %collective-permute-start.14 = (bf16[256,512]{1,0:T(8,128)(2,1)S(1)}, bf16[256,512]{1,0:T(8,128)(2,1)S(1)}, u32[]{:S(2)}, u32[]{:S(2)}) collective-permute-start(bf16[256,512]{1,0:T(8,128)(2,1)S(1)} %maximum_select_fusion), channel_id=1, source_target_pairs={{0,0},{1,32},{2,64},{3,96},{4,4},{5,36},{6,68},{7,100},{8,8},{9,40... | collective-permute-start | bytes 786440 | tf_op jit(solution)/shard_map/ppermute | solution.py:93
  75.2 8.6 %collective-permute-start.16 = (bf16[256,512]{1,0:T(8,128)(2,1)S(1)}, bf16[256,512]{1,0:T(8,128)(2,1)S(1)}, u32[]{:S(2)}, u32[]{:S(2)}) collective-permute-start(bf16[256,512]{1,0:T(8,128)(2,1)S(1)} %maximum_select_fusion), channel_id=1, source_target_pairs={{0,128},{1,160},{2,192},{3,224},{4,132},{5,164},{6,196},{7,228},{8... | collective-permute-start | bytes 786440 | tf_op jit(solution)/shard_map/ppermute | solution.py:93
  81.9 8.3 %collective-permute-start.15 = (bf16[256,512]{1,0:T(8,128)(2,1)S(1)}, bf16[256,512]{1,0:T(8,128)(2,1)S(1)}, u32[]{:S(2)}, u32[]{:S(2)}) collective-permute-start(bf16[256,512]{1,0:T(8,128)(2,1)S(1)} %collective-permute-done.14.refs_0_), channel_id=1, source_target_pairs={{0,8},{4,12},{8,0},{12,4},{16,24},{20,28},{24,16},{28,20},{32,40},... | collective-permute-start | bytes 786440 | tf_op jit(solution)/shard_map/ppermute | solution.py:56
  83.8 6.0 %copy-start.4 = (bf16[256,512]{1,0:T(8,128)(2,1)}, bf16[256,512]{1,0:T(8,128)(2,1)S(1)}, u32[]{:S(2)}) copy-start(bf16[256,512]{1,0:T(8,128)(2,1)S(1)} %collective-permute-done.16.refs_4_) | copy-start | bytes 786436
  83.8 7.6 %collective-permute-start.17 = (bf16[256,512]{1,0:T(8,128)(2,1)S(1)}, bf16[256,512]{1,0:T(8,128)(2,1)S(1)}, u32[]{:S(2)}, u32[]{:S(2)}) collective-permute-start(bf16[256,512]{1,0:T(8,128)(2,1)S(1)} %collective-permute-done.16.refs_4_), channel_id=1, source_target_pairs={{0,24},{4,28},{8,16},{12,20},{16,8},{20,12},{24,0},{28,4},{32,56},... | collective-permute-start | bytes 786440 | tf_op jit(solution)/shard_map/ppermute | solution.py:56
  86.4 10.1 %collective-permute-start.27 = (bf16[256,512]{1,0:T(8,128)(2,1)S(1)}, bf16[256,512]{1,0:T(8,128)(2,1)S(1)}, u32[]{:S(2)}, u32[]{:S(2)}) collective-permute-start(bf16[256,512]{1,0:T(8,128)(2,1)S(1)} %get-tuple-element.69), channel_id=1, source_target_pairs={{0,24},{4,28},{8,16},{12,20},{16,8},{20,12},{24,0},{28,4},{32,56},... | collective-permute-start | bytes 786440 | tf_op jit(solution)/shard_map/ppermute | solution.py:56
  89.8 6.7 %collective-permute-start.28 = (bf16[256,512]{1,0:T(8,128)(2,1)S(1)}, bf16[256,512]{1,0:T(8,128)(2,1)S(1)}, u32[]{:S(2)}, u32[]{:S(2)}) collective-permute-start(bf16[256,512]{1,0:T(8,128)(2,1)S(1)} %get-tuple-element.71), channel_id=1, source_target_pairs={{0,8},{4,12},{8,0},{12,4},{16,24},{20,28},{24,16},{28,20},{32,40},... | collective-permute-start | bytes 786440 | tf_op jit(solution)/shard_map/ppermute | solution.py:56
  92.1 21.5 %copy-start.7 = (bf16[256,512]{1,0:T(8,128)(2,1)S(1)}, bf16[256,512]{1,0:T(8,128)(2,1)}, u32[]{:S(2)}) copy-start(bf16[256,512]{1,0:T(8,128)(2,1)} %copy-done.6) | copy-start | bytes 786436
  92.1 22.9 %copy-start.5 = (bf16[256,512]{1,0:T(8,128)(2,1)S(1)}, bf16[256,512]{1,0:T(8,128)(2,1)}, u32[]{:S(2)}) copy-start(bf16[256,512]{1,0:T(8,128)(2,1)} %copy-done.4) | copy-start | bytes 786436
  96.5 18.5 %copy-start.9 = (bf16[256,512]{1,0:T(8,128)(2,1)S(1)}, bf16[256,512]{1,0:T(8,128)(2,1)}, u32[]{:S(2)}) copy-start(bf16[256,512]{1,0:T(8,128)(2,1)} %copy-done.8) | copy-start | bytes 786436
  97.5 36.8 %all-to-all-start = ((bf16[8,64,512]{2,1,0:T(8,128)(2,1)}), bf16[8,64,512]{2,1,0:T(8,128)(2,1)}, u32[]{:S(2)}, u32[]{:S(2)}) async-start(bf16[8,64,512]{2,1,0:T(8,128)(2,1)} %bitcast.14), calls=%async_computation | async-start | bytes 1048576 | tf_op jit(solution)/shard_map/all_to_all | solution.py:142
  111.8 9.6 %collective-permute-start.20 = (bf16[256,512]{1,0:T(8,128)(2,1)S(1)}, bf16[256,512]{1,0:T(8,128)(2,1)}, u32[]{:S(2)}, u32[]{:S(2)}) collective-permute-start(bf16[256,512]{1,0:T(8,128)(2,1)S(1)} %collective-permute-done.14.refs_0_), channel_id=1, source_target_pairs={{0,24},{4,28},{8,16},{12,20},{16,8},{20,12},{24,0},{28,4},{32,56},... | collective-permute-start | bytes 786440 | tf_op jit(solution)/shard_map/ppermute | solution.py:56
  113.6 10.5 %collective-permute-start.21 = (bf16[256,512]{1,0:T(8,128)(2,1)S(1)}, bf16[256,512]{1,0:T(8,128)(2,1)}, u32[]{:S(2)}, u32[]{:S(2)}) collective-permute-start(bf16[256,512]{1,0:T(8,128)(2,1)S(1)} %copy-done.7), channel_id=1, source_target_pairs={{0,24},{4,28},{8,16},{12,20},{16,8},{20,12},{24,0},{28,4},{32,56},... | collective-permute-start | bytes 786440 | tf_op jit(solution)/shard_map/ppermute | solution.py:56
  115.0 9.1 %collective-permute-start.22 = (bf16[256,512]{1,0:T(8,128)(2,1)S(1)}, bf16[256,512]{1,0:T(8,128)(2,1)}, u32[]{:S(2)}, u32[]{:S(2)}) collective-permute-start(bf16[256,512]{1,0:T(8,128)(2,1)S(1)} %copy-done.5), channel_id=1, source_target_pairs={{0,8},{4,12},{8,0},{12,4},{16,24},{20,28},{24,16},{28,20},{32,40},... | collective-permute-start | bytes 786440 | tf_op jit(solution)/shard_map/ppermute | solution.py:56
  115.0 10.6 %collective-permute-start.23 = (bf16[256,512]{1,0:T(8,128)(2,1)S(1)}, bf16[256,512]{1,0:T(8,128)(2,1)}, u32[]{:S(2)}, u32[]{:S(2)}) collective-permute-start(bf16[256,512]{1,0:T(8,128)(2,1)S(1)} %copy-done.9), channel_id=1, source_target_pairs={{0,8},{4,12},{8,0},{12,4},{16,24},{20,28},{24,16},{28,20},{32,40},... | collective-permute-start | bytes 786440 | tf_op jit(solution)/shard_map/ppermute | solution.py:56
  129.8 11.1 %collective-permute-start.24 = (bf16[160,512]{1,0:T(8,128)(2,1)}, bf16[160,512]{1,0:T(8,128)(2,1)S(1)}, u32[]{:S(2)}, u32[]{:S(2)}) collective-permute-start(bf16[160,512]{1,0:T(8,128)(2,1)} %get-tuple-element.62), channel_id=1, source_target_pairs={{0,1},{1,0},{2,3},{3,2},{4,5},{5,4},{6,7},{7,6},{8,9},{9,8},{10,11... | collective-permute-start | bytes 491528 | tf_op jit(solution)/shard_map/ppermute | solution.py:517
  129.8 11.1 %collective-permute-start.25 = (bf16[160,512]{1,0:T(8,128)(2,1)}, bf16[160,512]{1,0:T(8,128)(2,1)S(1)}, u32[]{:S(2)}, u32[]{:S(2)}) collective-permute-start(bf16[160,512]{1,0:T(8,128)(2,1)} %get-tuple-element.63), channel_id=1, source_target_pairs={{0,2},{1,3},{2,0},{3,1},{4,6},{5,7},{6,4},{7,5},{8,10},{9,11},{10,... | collective-permute-start | bytes 491528 | tf_op jit(solution)/shard_map/ppermute | solution.py:517
  134.1 8.4 %collective-permute-start.26 = (bf16[160,512]{1,0:T(8,128)(2,1)S(1)}, bf16[160,512]{1,0:T(8,128)(2,1)S(1)}, u32[]{:S(2)}, u32[]{:S(2)}) collective-permute-start(bf16[160,512]{1,0:T(8,128)(2,1)S(1)} %get-tuple-element.64), channel_id=1, source_target_pairs={{0,3},{1,2},{2,1},{3,0},{4,7},{5,6},{6,5},{7,4},{8,11},{9,10},{10,... | collective-permute-start | bytes 491528 | tf_op jit(solution)/shard_map/ppermute | solution.py:517
  135.4 15.3 %collective-permute-start.29 = (f32[32,512]{1,0:T(8,128)S(1)}, f32[32,512]{1,0:T(8,128)S(1)}, u32[]{:S(2)}, u32[]{:S(2)}) collective-permute-start(f32[32,512]{1,0:T(8,128)S(1)} %get-tuple-element.74), channel_id=1, source_target_pairs={{0,0},{1,64},{2,128},{3,192},{4,4},{5,68},{6,132},{7,196},{8,8},{9... | collective-permute-start | bytes 196616 | tf_op jit(solution)/shard_map/ppermute | solution.py:157
  137.5 14.9 %collective-permute-start.30 = (f32[32,512]{1,0:T(8,128)S(1)}, f32[32,512]{1,0:T(8,128)S(1)}, u32[]{:S(2)}, u32[]{:S(2)}) collective-permute-start(f32[32,512]{1,0:T(8,128)S(1)} %get-tuple-element.73), channel_id=1, source_target_pairs={{0,4},{1,68},{2,132},{3,196},{4,0},{5,64},{6,128},{7,192},{8,12},{... | collective-permute-start | bytes 196616 | tf_op jit(solution)/shard_map/ppermute | solution.py:157
  (7 other events, 6.9 us)

commit v5 on v4

--- a/solution.py
+++ b/solution.py
@@ -18,6 +18,7 @@
 
 VMEM = pl.BlockSpec(memory_space=pltpu.VMEM)
 SMEM = pl.BlockSpec(memory_space=pltpu.SMEM)
+HBM = pl.BlockSpec(memory_space=pltpu.HBM)
 F32 = jnp.float32
 BF16 = jnp.bfloat16
 
@@ -65,14 +66,20 @@
     return joined(weight, lax.ppermute(weight, "tensor", [(a, a ^ 1) for a in range(tn)]), j % 2 == 0)
 
 
+def weight_of_both(weight):
+    nx = sides_of(lax.axis_size("dp"))[2]
+    if nx == 1:
+        return weight
+    return joined(weight, moved(weight, lambda z, y, x: (z, y, x ^ 1)), lax.axis_index("dp") % nx == 0)
+
+
 def weight_of_place(weight):
-    n, tn = lax.axis_size("dp"), lax.axis_size("tensor")
-    nx = sides_of(n)[2]
-    j, x = lax.axis_index("tensor"), lax.axis_index("dp") % nx
-    weight = joined(weight, lax.ppermute(weight, "tensor", [(a, a ^ 2) for a in range(tn)]), j < 2)
-    if nx > 1:
-        weight = joined(weight, moved(weight, lambda z, y, x: (z, y, x ^ 1)), x == 0)
-    return weight
+    tn, j = lax.axis_size("tensor"), lax.axis_index("tensor")
+    rows, columns = weight.shape
+    weight = weight.reshape(sides_of(lax.axis_size("dp"))[2], -1, columns)
+    got = lax.ppermute(weight, "tensor", [(a, a ^ 2) for a in range(tn)])
+    weight = jnp.where(j < 2, jnp.concatenate([weight, got], 1), jnp.concatenate([got, weight], 1))
+    return weight.reshape(2 * rows, columns)
 
 
 def weight_along_z(weight):
@@ -134,14 +141,20 @@
     return jnp.concatenate([own + part.astype(F32) for (own, _), part in zip(halves, got)])
 
 
-def reduce_grad(grad):
+def reduce_along_z(grad):
+    n = lax.axis_size("dp")
+    nz = sides_of(n)[0]
+    if nz == 1:
+        return grad
+    columns = grad.shape[-1]
+    grad = lax.all_to_all(grad.astype(BF16), "dp", 0, 0, tiled=True, axis_index_groups=groups_along(n, 0))
+    return jnp.sum(grad.reshape(nz, -1, columns).astype(F32), axis=0)
+
+
+def reduce_to_owner(grad):
     n, tn = lax.axis_size("dp"), lax.axis_size("tensor")
     nz, ny, nx = sides_of(n)
-    columns = grad.shape[-1]
-    if nz > 1:
-        grad = lax.all_to_all(grad.astype(BF16), "dp", 0, 0, tiled=True, axis_index_groups=groups_along(n, 0))
-        grad = jnp.sum(grad.reshape(nz, -1, columns).astype(F32), axis=0)
-    rows = grad.shape[0] // nx
+    rows, columns = grad.shape[0] // nx, grad.shape[1]
     order = block_order(n, tn)
     x = lax.axis_index("dp") % nx
     total = None
@@ -323,7 +336,8 @@
 
 
 def merge_kernel(width, tn, place_ref, gain_ref, high_ref, *refs):
-    parts, square_refs, out_ref, out_square_ref = refs[:tn], refs[tn:-2], refs[-2], refs[-1]
+    parts, square_refs, (far_ref, out_square_ref, out_ref, sems) = refs[:tn], refs[tn:-4], refs[-4:]
+    copies = []
     j = place_ref[0]
     rows = parts[0].shape[0]
     piece = high_ref.shape[1]
@@ -345,7 +359,12 @@
             out_ref[at, cols] = merged
             merged = merged.astype(F32)
             total = total + merged * merged
+        copy = pltpu.make_async_copy(out_ref.at[at, :], far_ref.at[at, :], sems.at[s])
+        copy.start()
+        copies.append(copy)
         out_square_ref[:, at] = lane_sums(total)
+    for copy in copies:
+        copy.wait()
 
 
 def merge(place, gain, high, parts, squares, width):
@@ -354,11 +373,12 @@
     return pl.pallas_call(
         functools.partial(merge_kernel, width, tn),
         in_specs=[SMEM] + [VMEM] * (2 + tn + len(squares)),
-        out_specs=[VMEM, VMEM],
+        out_specs=[HBM, VMEM],
         out_shape=[
             jax.ShapeDtypeStruct((pack, piece), BF16),
             jax.ShapeDtypeStruct((8, pack), F32),
         ],
+        scratch_shapes=[pltpu.VMEM((pack, piece), BF16), pltpu.SemaphoreType.DMA((tn,))],
         compiler_params=pltpu.CompilerParams(vmem_limit_bytes=VMEM_LIMIT),
         cost_estimate=pl.CostEstimate(flops=8 * pack * piece, bytes_accessed=6 * pack * piece, transcendentals=0),
         name="merge",
@@ -379,7 +399,15 @@
         fold_refs, square_refs, refs = refs[:tn], refs[tn:2 * tn], refs[2 * tn:]
         keep_refs, refs = refs[:2], refs[2:]
         send_refs, refs = refs[:2 if ny > 1 else 0], refs[2 if ny > 1 else 0:]
-        hidden_ref, fold_ref = refs
+        hidden_ref, fold_ref, near_ref, near_folds, near_cut, sems = refs
+        coming = [
+            pltpu.make_async_copy(
+                merged_ref.at[b * rows:(b + 1) * rows, :], near_ref.at[b * rows:(b + 1) * rows, :], sems.at[b])
+            for b in range(tn)]
+        folds_coming = [
+            pltpu.make_async_copy(fold_refs[s], near_folds.at[s], sems.at[tn + s]) for s in range(tn)]
+        for copy in coming + folds_coming:
+            copy.start()
         j, y = place_ref[0], place_ref[1]
         squares = square_refs[0][...]
         for s in range(1, tn):
@@ -388,15 +416,18 @@
         for b in range(tn):
             at = slice(b * rows, (b + 1) * rows)
             scale = column(scales[0:1, at])
+            coming[b].wait()
             for c in range(0, piece, 128):
                 cols = slice(c, c + 128)
                 gain = gain_ref[:, pl.ds(pl.multiple_of(j * piece + c, 128), 128)]
-                hidden_ref[at, cols] = (merged_ref[at, cols].astype(F32) * scale * gain).astype(BF16)
+                hidden_ref[at, cols] = (near_ref[at, cols].astype(F32) * scale * gain).astype(BF16)
         fold_ref[...] = jnp.zeros_like(fold_ref)
         for s in range(tn):
             at = pl.ds(pl.multiple_of((j ^ s) * rows, rows), rows + OFFMAX)
-            fold_ref[at, :] = fold_ref[at, :] + fold_refs[s][...].astype(F32)
+            folds_coming[s].wait()
+            fold_ref[at, :] = fold_ref[at, :] + near_folds[s].astype(F32)
         folded = fold_ref[OFFMAX:, :].astype(BF16)
+        going = []
         for h, s, keep in steps:
             at = pl.ds(pl.multiple_of(h * ny * chunk + (y ^ s) * chunk, chunk), chunk)
             part = lax.dot_general(
@@ -407,7 +438,13 @@
             if keep:
                 keep_refs[h][kept[h].index(s)] = part
             else:
-                send_refs[h][sent[h].index(s)] = part.astype(BF16)
+                k = sent[h].index(s)
+                near_cut[h, k] = part.astype(BF16)
+                copy = pltpu.make_async_copy(near_cut.at[h, k], send_refs[h].at[k], sems.at[2 * tn + 2 * h + k])
+                copy.start()
+                going.append(copy)
+        for copy in going:
+            copy.wait()
 
     out_shape = [jax.ShapeDtypeStruct((len(kept[h]), chunk, vw), F32) for h in range(2)]
     if ny > 1:
@@ -415,10 +452,16 @@
     out_shape += [jax.ShapeDtypeStruct((pack, piece), BF16)]
     out = pl.pallas_call(
         kernel,
-        in_specs=[SMEM] + [VMEM] * (2 + 2 * tn),
-        out_specs=[VMEM] * len(out_shape),
+        in_specs=[SMEM, VMEM, HBM] + [HBM] * tn + [VMEM] * tn,
+        out_specs=[VMEM] * 2 + ([HBM] * 2 if ny > 1 else []) + [VMEM],
         out_shape=out_shape,
-        scratch_shapes=[pltpu.VMEM((pack + OFFMAX, vw), F32)],
+        scratch_shapes=[
+            pltpu.VMEM((pack + OFFMAX, vw), F32),
+            pltpu.VMEM((pack, piece), BF16),
+            pltpu.VMEM((tn, rows + OFFMAX, vw), BF16),
+            pltpu.VMEM((2, 2, chunk if ny > 1 else 16, vw), BF16),
+            pltpu.SemaphoreType.DMA((2 * tn + 4,)),
+        ],
         compiler_params=pltpu.CompilerParams(vmem_limit_bytes=VMEM_LIMIT),
         cost_estimate=pl.CostEstimate(flops=2 * pack * piece * vw, bytes_accessed=8 * pack * piece, transcendentals=0),
         name="grads",
@@ -523,22 +566,25 @@
     own_weight, cotangent, high = lax.optimization_barrier((draft_weight, cotangent, high))
     squares = squares + swapped(squares, 1)
     own_weight = weight_of_chip(own_weight)
-    squares, own_weight = lax.optimization_barrier((squares, own_weight))
-    squares = [squares, swapped(squares, 2)]
     folded = fold(place, doc_lengths, step_offsets, cotangent)
     across, beside = swapped(folded, 2), swapped(folded, 1)
+    squares, own_weight, beside, parts[1] = lax.optimization_barrier((squares, own_weight, beside, parts[1]))
+    squares = [squares, swapped(squares, 2)]
     merged, squares = merge(place, merging_gain, high, parts, squares, width)
-    across, merged = lax.optimization_barrier((across, merged))
+    own_weight = weight_of_both(own_weight)
+    across, own_weight, merged, squares = lax.optimization_barrier((across, own_weight, merged, squares))
     folds = [folded, beside, across, swapped(across, 1)]
+    own_weight = weight_of_place(own_weight)
     squares = [squares] + [swapped(squares, s) for s in range(1, tn)]
-    weights = weight_once(weight_along_z(weight_of_place(own_weight)))
+    weights = weight_once(weight_along_z(own_weight))
     kept, cut, hidden = grads(place, draft_gain.reshape(1, width), merged, folds, squares, width, ny, tn)
     halves = reduce_once(kept, cut)
     weights, own = lax.optimization_barrier((weights, [half[0] for half in halves]))
     halves = [(mine, other) for mine, (_, other) in zip(own, halves)]
-    weight_grad = reduce_grad(reduce_twice(halves))
     weights = weight_twice(weights)
-
+    grad = reduce_along_z(reduce_twice(halves))
+    hidden, grad = lax.optimization_barrier((hidden, grad))
+    weight_grad = reduce_to_owner(grad)
     values = project(place, hidden, weights, tn)
     values = [values[0]] + [swapped(values[s], s) for s in range(1, tn)]
     draft_values = spread(place, doc_lengths, step_offsets, values)

time: 154 us -> 153 us (level)
  the two profiles are of different devices: /device:TPU:32 before, /device:TPU:1 now
where the time goes in v5:
time: 153 us; the launch traced here: 152 us
  starting transfers between devices  54.8 us (36%)
  waiting for transfers between devices  54 us (35%)
  Pallas kernels  28 us (18%)
  other arithmetic  10.8 us (7%)
  local copies, waits for them, and re-layouts  3.72 us (2%)
    ppermute x14, waiting for transfers between devices, swapped(): return lax.ppermute(values, 'tensor', [(a, a ^ s) for a in range(tn)])  20.4 us
    ppermute x2, starting transfers between devices, reduce_to_owner(): part = lax.ppermute(part, ('dp', 'tensor'), pairs)  13.7 us
    ppermute x14, starting transfers between devices, swapped(): return lax.ppermute(values, 'tensor', [(a, a ^ s) for a in range(tn)])  12.3 us
    ppermute x2, waiting for transfers between devices, weight_along_z(): out.append(lax.ppermute(weight, ('dp', 'tensor'), pairs))  11.5 us
    ppermute x2, starting transfers between devices, weight_along_z(): out.append(lax.ppermute(weight, ('dp', 'tensor'), pairs))  11.1 us
    ppermute x11, starting transfers between devices, moved(): return lax.ppermute(values, 'dp', pairs)  10.9 us
    all_to_all x1, waiting for transfers between devices, reduce_along_z(): lax.all_to_all(grad.astype(BF16), 'dp', 0, 0, tiled=True, axis_index_grou...  10.9 us
    pallas_call x1, Pallas kernels, attend(): pl.pallas_call(functools.partial(attend_kernel, window), grid=(pack // bl...  8.15 us
  transfers between devices with their start and end apart: 32, of which 13 were waited for; matrix products, arithmetic and copies ran while one was open for 6% of the time, Pallas kernels for 10%

profile of v5, /device:TPU:1, one launch (start us, length us, event | category | flops | bytes accessed | tf_op | source)
XLA Modules:
  0.0 152.2 jit_solution(6210023242553101803)
XLA Ops:
  1.3 6.8 %features.1 = (bf16[128,2048]{1,0:T(8,128)(2,1)}, bf16[128,2048]{1,0:T(8,128)(2,1)}, bf16[128,2048]{1,0:T(8,128)(2,1)}, bf16[128,2048]{1,0:T(8,128)(2,1)}) custom-call(s32[3]{0:T(128)} %pad_add_fusion.place_ref, bf16[128,8192]{1,0:T(8,128)(2,1)} %low_ref.1, bf16[128,8192]{1,0:T(8,128)(2,1)} %mid_ref.1, f32[3,8192]{1,0:T(4,128)} %gain_ref.3), custom_call_target="tpu_custom_call" | custom-call | flops 10485760 | bytes 6291456 | tf_op jit(solution)/shard_map/features/pallas_call | solution.py:232
  8.1 3.3 %collective-permute-start.4 = (bf16[128,2048]{1,0:T(8,128)(2,1)}, bf16[128,2048]{1,0:T(8,128)(2,1)S(1)}, u32[]{:S(2)}, u32[]{:S(2)}) collective-permute-start(bf16[128,2048]{1,0:T(8,128)(2,1)} %get-tuple-element.45), channel_id=1, source_target_pairs={{0,1},{1,0},{2,3},{3,2},{4,5},{5,4},{6,7},{7,6},{8,9},{9,8},{10,11... | collective-permute-start | bytes 1572872 | tf_op jit(solution)/shard_map/ppermute | solution.py:560
  11.4 1.8 %collective-permute-start.7 = (bf16[128,2048]{1,0:T(8,128)(2,1)}, bf16[128,2048]{1,0:T(8,128)(2,1)}, u32[]{:S(2)}, u32[]{:S(2)}) collective-permute-start(bf16[128,2048]{1,0:T(8,128)(2,1)} %get-tuple-element.51), channel_id=1, source_target_pairs={{0,3},{1,2},{2,1},{3,0},{4,7},{5,6},{6,5},{7,4},{8,11},{9,10},{10,... | collective-permute-start | bytes 1572872 | tf_op jit(solution)/shard_map/ppermute | solution.py:560
  13.3 1.6 %copy-done.14 = bf16[512,2048]{1,0:T(8,128)(2,1)S(1)} copy-done((bf16[512,2048]{1,0:T(8,128)(2,1)S(1)}, bf16[512,2048]{1,0:T(8,128)(2,1)}, u32[]{:S(2)}) %copy-start.14) | copy-done | bytes 2097176
  14.8 8.2 %attend.1 = (bf16[512,2048]{1,0:T(8,128)(2,1)S(1)}, f32[8,512]{1,0:T(8,128)S(1)}) custom-call(s32[1,8]{1,0:T(1,128)S(1)} %copy-done.11, bf16[512,2048]{1,0:T(8,128)(2,1)S(1)} %copy-done.14, bf16[512,256]{1,0:T(8,128)(2,1)S(1)} %copy-done.15, bf16[512,256]{1,0:T(8,128)(2,1)S(1)} %copy-done.16), custom_call_target="tpu_custom_call" | custom-call | flops 1610612736 | bytes 4194304 | tf_op jit(solution)/shard_map/attend/pallas_call | solution.py:283
  23.0 0.9 fold.1.refs_0_
  24.5 0.9 collective-permute-done.1
  26.1 0.7 add.69.refs_4_
  27.4 1.0 collective-permute-start.5
  28.8 1.2 collective-permute-start.8
  29.9 7.2 %collective-permute-done.7.refs_3_ = bf16[128,2048]{1,0:T(8,128)(2,1)} collective-permute-done((bf16[128,2048]{1,0:T(8,128)(2,1)}, bf16[128,2048]{1,0:T(8,128)(2,1)}, u32[]{:S(2)}, u32[]{:S(2)}) %collective-permute-start.7) | collective-permute-done | bytes 524320 | tf_op jit(solution)/shard_map/ppermute | solution.py:560
  37.1 4.6 %collective-permute-done.8.refs_5_ = f32[8,512]{1,0:T(8,128)S(1)} collective-permute-done((f32[8,512]{1,0:T(8,128)S(1)}, f32[8,512]{1,0:T(8,128)S(1)}, u32[]{:S(2)}, u32[]{:S(2)}) %collective-permute-start.8) | collective-permute-done | bytes 16416 | tf_op jit(solution)/shard_map/ppermute | solution.py:560
  41.7 4.1 %merge.1 = (bf16[512,2048]{1,0:T(8,128)(2,1)S(1)}, f32[8,512]{1,0:T(8,128)S(1)}) custom-call(s32[3]{0:T(128)S(1)} %copy-done.10, f32[3,8192]{1,0:T(4,128)S(1)} %copy-done.2, bf16[512,2048]{1,0:T(8,128)(2,1)S(1)} %get-tuple-element.47.high_ref, bf16[128,2048]{1,0:T(8,128)(2,1)S(1)} %copy-done.1, bf16[128,2048]{1,0:T(8,128)(2,1)S(1)} %collective-permute-done.4.refs_1_, ...), custom_call_target="tpu_custom_call" | custom-call | flops 8388608 | bytes 6291456 | tf_op jit(solution)/shard_map/merge/pallas_call | solution.py:373
  45.9 1.6 %maximum_select_fusion.1 = bf16[128,512]{1,0:T(8,128)(2,1)} fusion(bf16[64,512]{1,0:T(8,128)(2,1)} %collective-permute-done.5, bf16[64,512]{1,0:T(8,128)(2,1)} %maximum_select_fusion.2, pred[]{:T(512)S(6)} %eq.13), kind=kLoop, calls=%fused_computation.11 | loop fusion | flops 589824 | bytes 262145 | tf_op jit(solution)/shard_map/jit(_where)/select_n | solution.py:61
  47.5 0.8 collective-permute-start.9
  48.4 2.1 %collective-permute-start.12 = (f32[8,512]{1,0:T(8,128)S(1)}, f32[8,512]{1,0:T(8,128)S(1)}, u32[]{:S(2)}, u32[]{:S(2)}) collective-permute-start(f32[8,512]{1,0:T(8,128)S(1)} %get-tuple-element.58.refs_4_), channel_id=1, source_target_pairs={{0,3},{1,2},{2,1},{3,0},{4,7},{5,6},{6,5},{7,4},{8,11},{9,10},{10,... | collective-permute-start | bytes 49160 | tf_op jit(solution)/shard_map/ppermute | solution.py:560
  50.9 1.2 collective-permute-done.12.refs_7_
  52.1 3.9 %grads.1 = (f32[2,256,512]{2,1,0:T(8,128)S(1)}, f32[2,256,512]{2,1,0:T(8,128)S(1)}, bf16[2,256,512]{2,1,0:T(8,128)(2,1)}, bf16[2,256,512]{2,1,0:T(8,128)(2,1)}, bf16[512,2048]{1,0:T(8,128)(2,1)S(1)}) custom-call(s32[3]{0:T(128)S(1)} %copy-done.10, f32[1,8192]{1,0:T(1,128)S(1)} %bitcast.15, bf16[512,2048]{1,0:T(8,128)(2,1)S(1)} %get-tuple-element.55.merged_ref, ...), custom_call_target="tpu_custom_call" | custom-call | flops 1073741824 | bytes 8388608 | tf_op jit(solution)/shard_map/grads/pallas_call | solution.py:453
  56.0 1.0 copy-done
  57.6 1.9 %collective-permute-start.19 = (bf16[2,256,512]{2,1,0:T(8,128)(2,1)}, bf16[2,256,512]{2,1,0:T(8,128)(2,1)}, u32[]{:S(2)}, u32[]{:S(2)}) collective-permute-start(bf16[2,256,512]{2,1,0:T(8,128)(2,1)} %get-tuple-element.63), channel_id=1, source_target_pairs={{0,24},{4,28},{8,16},{12,20},{16,8},{20,12},{24,0},{28,4},{32,56},... | collective-permute-start | bytes 1572872 | tf_op jit(solution)/shard_map/ppermute | solution.py:57
  59.8 4.1 %collective-permute-done.13 = bf16[2,64,512]{2,1,0:T(8,128)(2,1)S(1)} collective-permute-done((bf16[2,64,512]{2,1,0:T(8,128)(2,1)}, bf16[2,64,512]{2,1,0:T(8,128)(2,1)S(1)}, u32[]{:S(2)}, u32[]{:S(2)}) %collective-permute-start.13) | collective-permute-done | bytes 131104 | tf_op jit(solution)/shard_map/ppermute | solution.py:80
  63.9 1.0 maximum_select_fusion
  65.0 5.2 %collective-permute-start.14 = (bf16[256,512]{1,0:T(8,128)(2,1)S(1)}, bf16[256,512]{1,0:T(8,128)(2,1)S(1)}, u32[]{:S(2)}, u32[]{:S(2)}) collective-permute-start(bf16[256,512]{1,0:T(8,128)(2,1)S(1)} %bitcast.17), channel_id=1, source_target_pairs={{0,0},{1,32},{2,64},{3,96},{4,4},{5,36},{6,68},{7,100},{8,8},{9,40... | collective-permute-start | bytes 786440 | tf_op jit(solution)/shard_map/ppermute | solution.py:100
  70.2 5.9 %collective-permute-start.16 = (bf16[256,512]{1,0:T(8,128)(2,1)S(1)}, bf16[256,512]{1,0:T(8,128)(2,1)S(1)}, u32[]{:S(2)}, u32[]{:S(2)}) collective-permute-start(bf16[256,512]{1,0:T(8,128)(2,1)S(1)} %bitcast.18), channel_id=1, source_target_pairs={{0,128},{1,160},{2,192},{3,224},{4,132},{5,164},{6,196},{7,228},{8... | collective-permute-start | bytes 786440 | tf_op jit(solution)/shard_map/ppermute | solution.py:100
  76.1 2.7 %collective-permute-done.14.refs_0_ = bf16[256,512]{1,0:T(8,128)(2,1)S(1)} collective-permute-done((bf16[256,512]{1,0:T(8,128)(2,1)S(1)}, bf16[256,512]{1,0:T(8,128)(2,1)S(1)}, u32[]{:S(2)}, u32[]{:S(2)}) %collective-permute-start.14) | collective-permute-done | bytes 262176 | tf_op jit(solution)/shard_map/ppermute | solution.py:100
  79.2 8.8 %collective-permute-done.16.refs_4_ = bf16[256,512]{1,0:T(8,128)(2,1)S(1)} collective-permute-done((bf16[256,512]{1,0:T(8,128)(2,1)S(1)}, bf16[256,512]{1,0:T(8,128)(2,1)S(1)}, u32[]{:S(2)}, u32[]{:S(2)}) %collective-permute-start.16) | collective-permute-done | bytes 262176 | tf_op jit(solution)/shard_map/ppermute | solution.py:100
  88.0 0.8 collective-permute-start.17
  88.8 1.5 fusion
  90.3 2.0 %collective-permute-start.20 = (bf16[256,512]{1,0:T(8,128)(2,1)S(1)}, bf16[256,512]{1,0:T(8,128)(2,1)S(1)}, u32[]{:S(2)}, u32[]{:S(2)}) collective-permute-start(bf16[256,512]{1,0:T(8,128)(2,1)S(1)} %get-tuple-element.81), channel_id=1, source_target_pairs={{0,24},{4,28},{8,16},{12,20},{16,8},{20,12},{24,0},{28,4},{32,56},... | collective-permute-start | bytes 786440 | tf_op jit(solution)/shard_map/ppermute | solution.py:57
  92.2 1.2 fusion.1
  93.6 4.0 %collective-permute-done.17.refs_5_ = bf16[256,512]{1,0:T(8,128)(2,1)S(1)} collective-permute-done((bf16[256,512]{1,0:T(8,128)(2,1)S(1)}, bf16[256,512]{1,0:T(8,128)(2,1)S(1)}, u32[]{:S(2)}, u32[]{:S(2)}) %collective-permute-start.17) | collective-permute-done | bytes 262176 | tf_op jit(solution)/shard_map/ppermute | solution.py:57
  98.3 3.0 %collective-permute-done.20 = bf16[256,512]{1,0:T(8,128)(2,1)S(1)} collective-permute-done((bf16[256,512]{1,0:T(8,128)(2,1)S(1)}, bf16[256,512]{1,0:T(8,128)(2,1)S(1)}, u32[]{:S(2)}, u32[]{:S(2)}) %collective-permute-start.20) | collective-permute-done | bytes 262176 | tf_op jit(solution)/shard_map/ppermute | solution.py:57
  101.5 0.8 pad_maximum_fusion
  102.3 6.1 %all-to-all-start = ((bf16[8,64,512]{2,1,0:T(8,128)(2,1)}), bf16[8,64,512]{2,1,0:T(8,128)(2,1)}, u32[]{:S(2)}, u32[]{:S(2)}) async-start(bf16[8,64,512]{2,1,0:T(8,128)(2,1)} %bitcast.16), calls=%async_computation | async-start | bytes 1048576 | tf_op jit(solution)/shard_map/all_to_all | solution.py:150
  108.4 1.9 %collective-permute-start.22 = (bf16[256,512]{1,0:T(8,128)(2,1)S(1)}, bf16[256,512]{1,0:T(8,128)(2,1)S(1)}, u32[]{:S(2)}, u32[]{:S(2)}) collective-permute-start(bf16[256,512]{1,0:T(8,128)(2,1)S(1)} %collective-permute-done.14.refs_0_), channel_id=1, source_target_pairs={{0,24},{4,28},{8,16},{12,20},{16,8},{20,12},{24,0},{28,4},{32,56},... | collective-permute-start | bytes 786440 | tf_op jit(solution)/shard_map/ppermute | solution.py:57
  110.3 0.8 collective-permute-start.23
  111.1 1.5 collective-permute-start.25
  112.6 10.9 %all-to-all-done = bf16[8,64,512]{2,1,0:T(8,128)(2,1)} async-done(((bf16[8,64,512]{2,1,0:T(8,128)(2,1)}), bf16[8,64,512]{2,1,0:T(8,128)(2,1)}, u32[]{:S(2)}, u32[]{:S(2)}) %all-to-all-start) | async-done | bytes 524320 | tf_op jit(solution)/shard_map/all_to_all | solution.py:150
  123.5 1.1 convert_reduce_fusion
  124.6 4.9 %collective-permute-start.29 = (f32[32,512]{1,0:T(8,128)S(1)}, f32[32,512]{1,0:T(8,128)S(1)}, u32[]{:S(2)}, u32[]{:S(2)}) collective-permute-start(f32[32,512]{1,0:T(8,128)S(1)} %get-tuple-element.86), channel_id=1, source_target_pairs={{0,0},{1,64},{2,128},{3,192},{4,4},{5,68},{6,132},{7,196},{8,8},{9... | collective-permute-start | bytes 196616 | tf_op jit(solution)/shard_map/ppermute | solution.py:170
  129.6 8.8 %collective-permute-start.30 = (f32[32,512]{1,0:T(8,128)S(1)}, f32[32,512]{1,0:T(8,128)S(1)}, u32[]{:S(2)}, u32[]{:S(2)}) collective-permute-start(f32[32,512]{1,0:T(8,128)S(1)} %get-tuple-element.85), channel_id=1, source_target_pairs={{0,4},{1,68},{2,132},{3,196},{4,0},{5,64},{6,128},{7,192},{8,12},{... | collective-permute-start | bytes 196616 | tf_op jit(solution)/shard_map/ppermute | solution.py:170
  138.4 2.5 %project.1 = (f32[160,512]{1,0:T(8,128)S(1)}, bf16[160,512]{1,0:T(8,128)(2,1)S(1)}, bf16[160,512]{1,0:T(8,128)(2,1)S(1)}, bf16[160,512]{1,0:T(8,128)(2,1)S(1)}) custom-call(s32[3]{0:T(128)S(1)} %copy-done.10, bf16[512,2048]{1,0:T(8,128)(2,1)S(1)} %get-tuple-element.69.hidden_ref, bf16[256,512]{1,0:T(8,128)(2,1)S(1)} %collective-permute-done.14.refs_0_, ...), custom_call_target="tpu_custom_call" | custom-call | flops 1073741824 | bytes 4194304 | tf_op jit(solution)/shard_map/project/pallas_call | solution.py:497
  141.0 1.0 collective-permute-start.27
  142.0 1.1 collective-permute-start.28
  143.1 0.8 multiply_reduce_fusion
  144.5 2.0 %collective-permute-done.27.refs_2_ = bf16[160,512]{1,0:T(8,128)(2,1)S(1)} collective-permute-done((bf16[160,512]{1,0:T(8,128)(2,1)S(1)}, bf16[160,512]{1,0:T(8,128)(2,1)S(1)}, u32[]{:S(2)}, u32[]{:S(2)}) %collective-permute-start.27) | collective-permute-done | bytes 163872 | tf_op jit(solution)/shard_map/ppermute | solution.py:560
  146.5 4.1 %collective-permute-done.28.refs_3_ = bf16[160,512]{1,0:T(8,128)(2,1)S(1)} collective-permute-done((bf16[160,512]{1,0:T(8,128)(2,1)S(1)}, bf16[160,512]{1,0:T(8,128)(2,1)S(1)}, u32[]{:S(2)}, u32[]{:S(2)}) %collective-permute-start.28) | collective-permute-done | bytes 163872 | tf_op jit(solution)/shard_map/ppermute | solution.py:560
  150.5 1.7 %spread.1 = bf16[3,128,512]{2,1,0:T(8,128)(2,1)} custom-call(s32[3]{0:T(128)S(1)} %copy-done.10, s32[1,8]{1,0:T(1,128)S(1)} %copy-done.11, s32[3]{0:T(128)S(1)} %copy-done.12, f32[160,512]{1,0:T(8,128)S(1)} %get-tuple-element.74.refs_0_, bf16[160,512]{1,0:T(8,128)(2,1)S(1)} %collective-permute-done.26.refs_1_, ...), custom_call_target="tpu_custom_call" | custom-call | flops 62914560 | bytes 1572864 | tf_op jit(solution)/shard_map/spread/pallas_call | solution.py:523
  (75 shorter events, 6.5 us)
Async XLA Ops:
  1.3 12.0 %copy-start.11 = (s32[1,8]{1,0:T(1,128)S(1)}, s32[1,8]{1,0:T(1,128)}, u32[]{:S(2)}) copy-start(s32[1,8]{1,0:T(1,128)} %lengths_ref.5) | copy-start | bytes 100
  1.3 12.0 %copy-start.15 = (bf16[512,256]{1,0:T(8,128)(2,1)S(1)}, bf16[512,256]{1,0:T(8,128)(2,1)}, u32[]{:S(2)}) copy-start(bf16[512,256]{1,0:T(8,128)(2,1)} %key_ref.1) | copy-start | bytes 786436
  1.3 12.0 %copy-start.16 = (bf16[512,256]{1,0:T(8,128)(2,1)S(1)}, bf16[512,256]{1,0:T(8,128)(2,1)}, u32[]{:S(2)}) copy-start(bf16[512,256]{1,0:T(8,128)(2,1)} %value_ref.1) | copy-start | bytes 786436
  8.1 19.3 %collective-permute-start.4 = (bf16[128,2048]{1,0:T(8,128)(2,1)}, bf16[128,2048]{1,0:T(8,128)(2,1)S(1)}, u32[]{:S(2)}, u32[]{:S(2)}) collective-permute-start(bf16[128,2048]{1,0:T(8,128)(2,1)} %get-tuple-element.45), channel_id=1, source_target_pairs={{0,1},{1,0},{2,3},{3,2},{4,5},{5,4},{6,7},{7,6},{8,9},{9,8},{10,11... | collective-permute-start | bytes 1572872 | tf_op jit(solution)/shard_map/ppermute | solution.py:560
  11.4 18.5 %collective-permute-start.6 = (bf16[128,2048]{1,0:T(8,128)(2,1)}, bf16[128,2048]{1,0:T(8,128)(2,1)}, u32[]{:S(2)}, u32[]{:S(2)}) collective-permute-start(bf16[128,2048]{1,0:T(8,128)(2,1)} %get-tuple-element.50), channel_id=1, source_target_pairs={{0,2},{1,3},{2,0},{3,1},{4,6},{5,7},{6,4},{7,5},{8,10},{9,11},{10,... | collective-permute-start | bytes 1572872 | tf_op jit(solution)/shard_map/ppermute | solution.py:560
  11.4 11.6 %copy-start.3 = (bf16[3,128,512]{2,1,0:T(8,128)(2,1)S(1)}, bf16[3,128,512]{2,1,0:T(8,128)(2,1)}, u32[]{:S(2)}) copy-start(bf16[3,128,512]{2,1,0:T(8,128)(2,1)} %cotangent_ref) | copy-start | bytes 1179652
  11.4 11.6 %copy-start.10 = (s32[3]{0:T(128)S(1)}, s32[3]{0:T(128)}, u32[]{:S(2)}) copy-start(s32[3]{0:T(128)} %pad_add_fusion.place_ref) | copy-start | bytes 40
  11.4 11.6 %copy-start.12 = (s32[3]{0:T(128)S(1)}, s32[3]{0:T(128)}, u32[]{:S(2)}) copy-start(s32[3]{0:T(128)} %offsets_ref.3) | copy-start | bytes 40
  11.4 30.3 %copy-start.1 = (bf16[128,2048]{1,0:T(8,128)(2,1)S(1)}, bf16[128,2048]{1,0:T(8,128)(2,1)}, u32[]{:S(2)}) copy-start(bf16[128,2048]{1,0:T(8,128)(2,1)} %get-tuple-element.48.refs_0_) | copy-start | bytes 1572868
  11.4 30.3 %copy-start.2 = (f32[3,8192]{1,0:T(4,128)S(1)}, f32[3,8192]{1,0:T(4,128)}, u32[]{:S(2)}) copy-start(f32[3,8192]{1,0:T(4,128)} %gain_ref.3) | copy-start | bytes 294916
  11.4 25.7 %collective-permute-start.7 = (bf16[128,2048]{1,0:T(8,128)(2,1)}, bf16[128,2048]{1,0:T(8,128)(2,1)}, u32[]{:S(2)}, u32[]{:S(2)}) collective-permute-start(bf16[128,2048]{1,0:T(8,128)(2,1)} %get-tuple-element.51), channel_id=1, source_target_pairs={{0,3},{1,2},{2,1},{3,0},{4,7},{5,6},{6,5},{7,4},{8,11},{9,10},{10,... | collective-permute-start | bytes 1572872 | tf_op jit(solution)/shard_map/ppermute | solution.py:560
  13.2 1.6 %copy-start.14 = (bf16[512,2048]{1,0:T(8,128)(2,1)S(1)}, bf16[512,2048]{1,0:T(8,128)(2,1)}, u32[]{:S(2)}) copy-start(bf16[512,2048]{1,0:T(8,128)(2,1)} %query_ref.1) | copy-start | bytes 6291460
  14.8 10.6 %copy-start.17 = (bf16[32,512]{1,0:T(8,128)(2,1)S(1)}, bf16[32,512]{1,0:T(8,128)(2,1)}, u32[]{:S(2)}) copy-start(bf16[32,512]{1,0:T(8,128)(2,1)} %param.18) | copy-start | bytes 98308
  23.9 3.5 %collective-permute-start.3 = (bf16[160,512]{1,0:T(8,128)(2,1)S(1)}, bf16[160,512]{1,0:T(8,128)(2,1)}, u32[]{:S(2)}, u32[]{:S(2)}) collective-permute-start(bf16[160,512]{1,0:T(8,128)(2,1)S(1)} %fold.1.refs_0_), channel_id=1, source_target_pairs={{0,1},{1,0},{2,3},{3,2},{4,5},{5,4},{6,7},{7,6},{8,9},{9,8},{10,11... | collective-permute-start | bytes 491528 | tf_op jit(solution)/shard_map/ppermute | solution.py:560
  24.2 1.3 collective-permute-start.1
  25.5 1.3 collective-permute-start.2
  27.4 18.4 %collective-permute-start.5 = (bf16[64,512]{1,0:T(8,128)(2,1)}, bf16[64,512]{1,0:T(8,128)(2,1)}, u32[]{:S(2)}, u32[]{:S(2)}) collective-permute-start(bf16[64,512]{1,0:T(8,128)(2,1)} %maximum_select_fusion.2), channel_id=1, source_target_pairs={{0,4},{4,0},{8,12},{12,8},{16,20},{20,16},{24,28},{28,24},{32,36},... | collective-permute-start | bytes 196616 | tf_op jit(solution)/shard_map/ppermute | solution.py:57
  28.4 19.1 %collective-permute-start = (bf16[160,512]{1,0:T(8,128)(2,1)S(1)}, bf16[160,512]{1,0:T(8,128)(2,1)}, u32[]{:S(2)}, u32[]{:S(2)}) collective-permute-start(bf16[160,512]{1,0:T(8,128)(2,1)S(1)} %fold.1.refs_0_), channel_id=1, source_target_pairs={{0,2},{1,3},{2,0},{3,1},{4,6},{5,7},{6,4},{7,5},{8,10},{9,11},{10,... | collective-permute-start | bytes 491528 | tf_op jit(solution)/shard_map/ppermute | solution.py:560
  28.8 12.9 %collective-permute-start.8 = (f32[8,512]{1,0:T(8,128)S(1)}, f32[8,512]{1,0:T(8,128)S(1)}, u32[]{:S(2)}, u32[]{:S(2)}) collective-permute-start(f32[8,512]{1,0:T(8,128)S(1)} %add.69.refs_4_), channel_id=1, source_target_pairs={{0,2},{1,3},{2,0},{3,1},{4,6},{5,7},{6,4},{7,5},{8,10},{9,11},{10,... | collective-permute-start | bytes 49160 | tf_op jit(solution)/shard_map/ppermute | solution.py:560
  41.7 10.4 %copy-start.13 = (f32[8192]{0:T(1024)S(1)}, f32[8192]{0:T(1024)}, u32[]{:S(2)}) copy-start(f32[8192]{0:T(1024)} %param.17) | copy-start | bytes 98308
  47.5 4.6 %collective-permute-start.9 = (bf16[160,512]{1,0:T(8,128)(2,1)}, bf16[160,512]{1,0:T(8,128)(2,1)S(1)}, u32[]{:S(2)}, u32[]{:S(2)}) collective-permute-start(bf16[160,512]{1,0:T(8,128)(2,1)} %collective-permute-done.refs_2_), channel_id=1, source_target_pairs={{0,1},{1,0},{2,3},{3,2},{4,5},{5,4},{6,7},{7,6},{8,9},{9,8},{10,11... | collective-permute-start | bytes 491528 | tf_op jit(solution)/shard_map/ppermute | solution.py:560
  48.3 2.1 %collective-permute-start.10 = (f32[8,512]{1,0:T(8,128)S(1)}, f32[8,512]{1,0:T(8,128)S(1)}, u32[]{:S(2)}, u32[]{:S(2)}) collective-permute-start(f32[8,512]{1,0:T(8,128)S(1)} %get-tuple-element.58.refs_4_), channel_id=1, source_target_pairs={{0,1},{1,0},{2,3},{3,2},{4,5},{5,4},{6,7},{7,6},{8,9},{9,8},{10,11... | collective-permute-start | bytes 49160 | tf_op jit(solution)/shard_map/ppermute | solution.py:560
  48.4 2.6 %collective-permute-start.11 = (f32[8,512]{1,0:T(8,128)S(1)}, f32[8,512]{1,0:T(8,128)S(1)}, u32[]{:S(2)}, u32[]{:S(2)}) collective-permute-start(f32[8,512]{1,0:T(8,128)S(1)} %get-tuple-element.58.refs_4_), channel_id=1, source_target_pairs={{0,2},{1,3},{2,0},{3,1},{4,6},{5,7},{6,4},{7,5},{8,10},{9,11},{10,... | collective-permute-start | bytes 49160 | tf_op jit(solution)/shard_map/ppermute | solution.py:560
  48.4 3.8 %collective-permute-start.12 = (f32[8,512]{1,0:T(8,128)S(1)}, f32[8,512]{1,0:T(8,128)S(1)}, u32[]{:S(2)}, u32[]{:S(2)}) collective-permute-start(f32[8,512]{1,0:T(8,128)S(1)} %get-tuple-element.58.refs_4_), channel_id=1, source_target_pairs={{0,3},{1,2},{2,1},{3,0},{4,7},{5,6},{6,5},{7,4},{8,11},{9,10},{10,... | collective-permute-start | bytes 49160 | tf_op jit(solution)/shard_map/ppermute | solution.py:560
  57.0 31.8 %collective-permute-start.18 = (bf16[2,256,512]{2,1,0:T(8,128)(2,1)}, bf16[2,256,512]{2,1,0:T(8,128)(2,1)}, u32[]{:S(2)}, u32[]{:S(2)}) collective-permute-start(bf16[2,256,512]{2,1,0:T(8,128)(2,1)} %get-tuple-element.62), channel_id=1, source_target_pairs={{0,8},{4,12},{8,0},{12,4},{16,24},{20,28},{24,16},{28,20},{32,40},... | collective-permute-start | bytes 1572872 | tf_op jit(solution)/shard_map/ppermute | solution.py:57
  57.6 31.1 %collective-permute-start.19 = (bf16[2,256,512]{2,1,0:T(8,128)(2,1)}, bf16[2,256,512]{2,1,0:T(8,128)(2,1)}, u32[]{:S(2)}, u32[]{:S(2)}) collective-permute-start(bf16[2,256,512]{2,1,0:T(8,128)(2,1)} %get-tuple-element.63), channel_id=1, source_target_pairs={{0,24},{4,28},{8,16},{12,20},{16,8},{20,12},{24,0},{28,4},{32,56},... | collective-permute-start | bytes 1572872 | tf_op jit(solution)/shard_map/ppermute | solution.py:57
  59.5 4.4 %collective-permute-start.13 = (bf16[2,64,512]{2,1,0:T(8,128)(2,1)}, bf16[2,64,512]{2,1,0:T(8,128)(2,1)S(1)}, u32[]{:S(2)}, u32[]{:S(2)}) collective-permute-start(bf16[2,64,512]{2,1,0:T(8,128)(2,1)} %bitcast.4), channel_id=1, source_target_pairs={{0,2},{1,3},{2,0},{3,1},{4,6},{5,7},{6,4},{7,5},{8,10},{9,11},{10,... | collective-permute-start | bytes 393224 | tf_op jit(solution)/shard_map/ppermute | solution.py:80
  65.0 13.8 %collective-permute-start.14 = (bf16[256,512]{1,0:T(8,128)(2,1)S(1)}, bf16[256,512]{1,0:T(8,128)(2,1)S(1)}, u32[]{:S(2)}, u32[]{:S(2)}) collective-permute-start(bf16[256,512]{1,0:T(8,128)(2,1)S(1)} %bitcast.17), channel_id=1, source_target_pairs={{0,0},{1,32},{2,64},{3,96},{4,4},{5,36},{6,68},{7,100},{8,8},{9,40... | collective-permute-start | bytes 786440 | tf_op jit(solution)/shard_map/ppermute | solution.py:100
  70.2 17.8 %collective-permute-start.16 = (bf16[256,512]{1,0:T(8,128)(2,1)S(1)}, bf16[256,512]{1,0:T(8,128)(2,1)S(1)}, u32[]{:S(2)}, u32[]{:S(2)}) collective-permute-start(bf16[256,512]{1,0:T(8,128)(2,1)S(1)} %bitcast.18), channel_id=1, source_target_pairs={{0,128},{1,160},{2,192},{3,224},{4,132},{5,164},{6,196},{7,228},{8... | collective-permute-start | bytes 786440 | tf_op jit(solution)/shard_map/ppermute | solution.py:100
  78.8 14.8 %collective-permute-start.15 = (bf16[256,512]{1,0:T(8,128)(2,1)S(1)}, bf16[256,512]{1,0:T(8,128)(2,1)S(1)}, u32[]{:S(2)}, u32[]{:S(2)}) collective-permute-start(bf16[256,512]{1,0:T(8,128)(2,1)S(1)} %collective-permute-done.14.refs_0_), channel_id=1, source_target_pairs={{0,8},{4,12},{8,0},{12,4},{16,24},{20,28},{24,16},{28,20},{32,40},... | collective-permute-start | bytes 786440 | tf_op jit(solution)/shard_map/ppermute | solution.py:57
  88.0 5.5 %copy-start.4 = (bf16[256,512]{1,0:T(8,128)(2,1)}, bf16[256,512]{1,0:T(8,128)(2,1)S(1)}, u32[]{:S(2)}) copy-start(bf16[256,512]{1,0:T(8,128)(2,1)S(1)} %collective-permute-done.16.refs_4_) | copy-start | bytes 786436
  88.0 9.6 %collective-permute-start.17 = (bf16[256,512]{1,0:T(8,128)(2,1)S(1)}, bf16[256,512]{1,0:T(8,128)(2,1)S(1)}, u32[]{:S(2)}, u32[]{:S(2)}) collective-permute-start(bf16[256,512]{1,0:T(8,128)(2,1)S(1)} %collective-permute-done.16.refs_4_), channel_id=1, source_target_pairs={{0,24},{4,28},{8,16},{12,20},{16,8},{20,12},{24,0},{28,4},{32,56},... | collective-permute-start | bytes 786440 | tf_op jit(solution)/shard_map/ppermute | solution.py:57
  90.3 11.0 %collective-permute-start.20 = (bf16[256,512]{1,0:T(8,128)(2,1)S(1)}, bf16[256,512]{1,0:T(8,128)(2,1)S(1)}, u32[]{:S(2)}, u32[]{:S(2)}) collective-permute-start(bf16[256,512]{1,0:T(8,128)(2,1)S(1)} %get-tuple-element.81), channel_id=1, source_target_pairs={{0,24},{4,28},{8,16},{12,20},{16,8},{20,12},{24,0},{28,4},{32,56},... | collective-permute-start | bytes 786440 | tf_op jit(solution)/shard_map/ppermute | solution.py:57
  93.4 7.9 %collective-permute-start.21 = (bf16[256,512]{1,0:T(8,128)(2,1)S(1)}, bf16[256,512]{1,0:T(8,128)(2,1)S(1)}, u32[]{:S(2)}, u32[]{:S(2)}) collective-permute-start(bf16[256,512]{1,0:T(8,128)(2,1)S(1)} %get-tuple-element.83), channel_id=1, source_target_pairs={{0,8},{4,12},{8,0},{12,4},{16,24},{20,28},{24,16},{28,20},{32,40},... | collective-permute-start | bytes 786440 | tf_op jit(solution)/shard_map/ppermute | solution.py:57
  93.5 4.0 %copy-start.6 = (bf16[256,512]{1,0:T(8,128)(2,1)}, bf16[256,512]{1,0:T(8,128)(2,1)S(1)}, u32[]{:S(2)}) copy-start(bf16[256,512]{1,0:T(8,128)(2,1)S(1)} %collective-permute-done.15.refs_1_) | copy-start | bytes 786436
  98.3 12.1 %copy-start.7 = (bf16[256,512]{1,0:T(8,128)(2,1)S(1)}, bf16[256,512]{1,0:T(8,128)(2,1)}, u32[]{:S(2)}) copy-start(bf16[256,512]{1,0:T(8,128)(2,1)} %copy-done.6) | copy-start | bytes 786436
  98.3 12.8 %copy-start.5 = (bf16[256,512]{1,0:T(8,128)(2,1)S(1)}, bf16[256,512]{1,0:T(8,128)(2,1)}, u32[]{:S(2)}) copy-start(bf16[256,512]{1,0:T(8,128)(2,1)} %copy-done.4) | copy-start | bytes 786436
  101.3 9.8 %copy-start.9 = (bf16[256,512]{1,0:T(8,128)(2,1)S(1)}, bf16[256,512]{1,0:T(8,128)(2,1)}, u32[]{:S(2)}) copy-start(bf16[256,512]{1,0:T(8,128)(2,1)} %copy-done.8) | copy-start | bytes 786436
  102.3 21.2 %all-to-all-start = ((bf16[8,64,512]{2,1,0:T(8,128)(2,1)}), bf16[8,64,512]{2,1,0:T(8,128)(2,1)}, u32[]{:S(2)}, u32[]{:S(2)}) async-start(bf16[8,64,512]{2,1,0:T(8,128)(2,1)} %bitcast.16), calls=%async_computation | async-start | bytes 1048576 | tf_op jit(solution)/shard_map/all_to_all | solution.py:150
  108.4 21.1 %collective-permute-start.22 = (bf16[256,512]{1,0:T(8,128)(2,1)S(1)}, bf16[256,512]{1,0:T(8,128)(2,1)S(1)}, u32[]{:S(2)}, u32[]{:S(2)}) collective-permute-start(bf16[256,512]{1,0:T(8,128)(2,1)S(1)} %collective-permute-done.14.refs_0_), channel_id=1, source_target_pairs={{0,24},{4,28},{8,16},{12,20},{16,8},{20,12},{24,0},{28,4},{32,56},... | collective-permute-start | bytes 786440 | tf_op jit(solution)/shard_map/ppermute | solution.py:57
  110.3 28.1 %collective-permute-start.23 = (bf16[256,512]{1,0:T(8,128)(2,1)S(1)}, bf16[256,512]{1,0:T(8,128)(2,1)}, u32[]{:S(2)}, u32[]{:S(2)}) collective-permute-start(bf16[256,512]{1,0:T(8,128)(2,1)S(1)} %copy-done.7), channel_id=1, source_target_pairs={{0,24},{4,28},{8,16},{12,20},{16,8},{20,12},{24,0},{28,4},{32,56},... | collective-permute-start | bytes 786440 | tf_op jit(solution)/shard_map/ppermute | solution.py:57
  111.1 27.3 %collective-permute-start.24 = (bf16[256,512]{1,0:T(8,128)(2,1)S(1)}, bf16[256,512]{1,0:T(8,128)(2,1)}, u32[]{:S(2)}, u32[]{:S(2)}) collective-permute-start(bf16[256,512]{1,0:T(8,128)(2,1)S(1)} %copy-done.5), channel_id=1, source_target_pairs={{0,8},{4,12},{8,0},{12,4},{16,24},{20,28},{24,16},{28,20},{32,40},... | collective-permute-start | bytes 786440 | tf_op jit(solution)/shard_map/ppermute | solution.py:57
  111.1 27.3 %collective-permute-start.25 = (bf16[256,512]{1,0:T(8,128)(2,1)S(1)}, bf16[256,512]{1,0:T(8,128)(2,1)}, u32[]{:S(2)}, u32[]{:S(2)}) collective-permute-start(bf16[256,512]{1,0:T(8,128)(2,1)S(1)} %copy-done.9), channel_id=1, source_target_pairs={{0,8},{4,12},{8,0},{12,4},{16,24},{20,28},{24,16},{28,20},{32,40},... | collective-permute-start | bytes 786440 | tf_op jit(solution)/shard_map/ppermute | solution.py:57
  124.6 18.5 %collective-permute-start.29 = (f32[32,512]{1,0:T(8,128)S(1)}, f32[32,512]{1,0:T(8,128)S(1)}, u32[]{:S(2)}, u32[]{:S(2)}) collective-permute-start(f32[32,512]{1,0:T(8,128)S(1)} %get-tuple-element.86), channel_id=1, source_target_pairs={{0,0},{1,64},{2,128},{3,192},{4,4},{5,68},{6,132},{7,196},{8,8},{9... | collective-permute-start | bytes 196616 | tf_op jit(solution)/shard_map/ppermute | solution.py:170
  129.6 13.6 %collective-permute-start.30 = (f32[32,512]{1,0:T(8,128)S(1)}, f32[32,512]{1,0:T(8,128)S(1)}, u32[]{:S(2)}, u32[]{:S(2)}) collective-permute-start(f32[32,512]{1,0:T(8,128)S(1)} %get-tuple-element.85), channel_id=1, source_target_pairs={{0,4},{1,68},{2,132},{3,196},{4,0},{5,64},{6,128},{7,192},{8,12},{... | collective-permute-start | bytes 196616 | tf_op jit(solution)/shard_map/ppermute | solution.py:170
  140.9 3.6 %collective-permute-start.26 = (bf16[160,512]{1,0:T(8,128)(2,1)S(1)}, bf16[160,512]{1,0:T(8,128)(2,1)S(1)}, u32[]{:S(2)}, u32[]{:S(2)}) collective-permute-start(bf16[160,512]{1,0:T(8,128)(2,1)S(1)} %get-tuple-element.75), channel_id=1, source_target_pairs={{0,1},{1,0},{2,3},{3,2},{4,5},{5,4},{6,7},{7,6},{8,9},{9,8},{10,11... | collective-permute-start | bytes 491528 | tf_op jit(solution)/shard_map/ppermute | solution.py:560
  141.0 5.5 %collective-permute-start.27 = (bf16[160,512]{1,0:T(8,128)(2,1)S(1)}, bf16[160,512]{1,0:T(8,128)(2,1)S(1)}, u32[]{:S(2)}, u32[]{:S(2)}) collective-permute-start(bf16[160,512]{1,0:T(8,128)(2,1)S(1)} %get-tuple-element.76), channel_id=1, source_target_pairs={{0,2},{1,3},{2,0},{3,1},{4,6},{5,7},{6,4},{7,5},{8,10},{9,11},{10,... | collective-permute-start | bytes 491528 | tf_op jit(solution)/shard_map/ppermute | solution.py:560
  142.0 8.5 %collective-permute-start.28 = (bf16[160,512]{1,0:T(8,128)(2,1)S(1)}, bf16[160,512]{1,0:T(8,128)(2,1)S(1)}, u32[]{:S(2)}, u32[]{:S(2)}) collective-permute-start(bf16[160,512]{1,0:T(8,128)(2,1)S(1)} %get-tuple-element.77), channel_id=1, source_target_pairs={{0,3},{1,2},{2,1},{3,0},{4,7},{5,6},{6,5},{7,4},{8,11},{9,10},{10,... | collective-permute-start | bytes 491528 | tf_op jit(solution)/shard_map/ppermute | solution.py:560
  (3 other events, 2.3 us)

commit v6 on v5

--- a/solution.py
+++ b/solution.py
@@ -57,68 +57,44 @@
     return lax.ppermute(values, "dp", pairs)
 
 
-def joined(own, got, own_first):
-    return jnp.where(own_first, jnp.concatenate([own, got]), jnp.concatenate([got, own]))
-
-
-def weight_of_chip(weight):
-    tn, j = lax.axis_size("tensor"), lax.axis_index("tensor")
-    return joined(weight, lax.ppermute(weight, "tensor", [(a, a ^ 1) for a in range(tn)]), j % 2 == 0)
-
-
-def weight_of_both(weight):
-    nx = sides_of(lax.axis_size("dp"))[2]
-    if nx == 1:
-        return weight
-    return joined(weight, moved(weight, lambda z, y, x: (z, y, x ^ 1)), lax.axis_index("dp") % nx == 0)
-
-
-def weight_of_place(weight):
-    tn, j = lax.axis_size("tensor"), lax.axis_index("tensor")
-    rows, columns = weight.shape
-    weight = weight.reshape(sides_of(lax.axis_size("dp"))[2], -1, columns)
-    got = lax.ppermute(weight, "tensor", [(a, a ^ 2) for a in range(tn)])
-    weight = jnp.where(j < 2, jnp.concatenate([weight, got], 1), jnp.concatenate([got, weight], 1))
-    return weight.reshape(2 * rows, columns)
-
-
-def weight_along_z(weight):
+def weight_to_place(weight):
     n, tn = lax.axis_size("dp"), lax.axis_size("tensor")
     nz, ny, nx = sides_of(n)
-    if nz == 1:
-        half = weight.shape[0] // (2 * tn)
-        j = lax.axis_index("tensor")
-        return [lax.dynamic_slice_in_dim(weight, (2 * j + h) * half, half) for h in range(2)]
-    out = []
-    for m in range(2):
+    parts = []
+    for turn in range(nx):
         pairs = []
-        for z in range(nz):
-            for rest in range(ny * nx):
-                for t in range(tn):
-                    to = tn * ((z % 2) ^ m) + t
-                    pairs.append(((z * ny * nx + rest) * tn + t, (to * ny * nx + rest) * tn + z // 2))
-        out.append(lax.ppermute(weight, ("dp", "tensor"), pairs))
-    return out
-
-
-def weight_once(parts):
-    nz, ny, _ = sides_of(lax.axis_size("dp"))
-    if ny == 1:
-        return [[part] for part in parts]
-    half = nz // 2
+        for j in range(tn):
+            for q in range(n):
+                y, z, x = q // (nz * nx), q // nx % nz, q % nx ^ turn
+                pairs.append((j * n + q, ((z * ny + y) * nx + x) * tn + j))
+        parts.append(lax.ppermute(weight, ("dp", "tensor"), pairs))
+    return parts
+
+
+def weight_across(weight, far):
+    if sides_of(lax.axis_size("dp"))[0] == 1:
+        return weight
+    return jnp.concatenate([weight, moved(weight, lambda z, y, x: (z ^ far, y, x))])
+
+
+def weight_halves(weight):
+    if sides_of(lax.axis_size("dp"))[0] == 1:
+        return [weight]
+    return [weight, moved(weight, lambda z, y, x: (z ^ 1, y, x))]
+
+
+def weight_once(halves):
+    if sides_of(lax.axis_size("dp"))[1] == 1:
+        return [[half] for half in halves]
+    return [[half, moved(half, lambda z, y, x: (z, y ^ first, x))] for half, (first, _) in zip(halves, EXCHANGES)]
+
+
+def weight_twice(halves):
+    if sides_of(lax.axis_size("dp"))[1] == 1:
+        return halves
     return [
-        [part, moved(part, lambda z, y, x: (z, y ^ EXCHANGES[z // half ^ m][0], x))]
-        for m, part in enumerate(parts)]
-
-
-def weight_twice(parts):
-    nz, ny, _ = sides_of(lax.axis_size("dp"))
-    if ny == 1:
-        return parts
-    half = nz // 2
-    return [
-        part + [moved(chunk, lambda z, y, x: (z, y ^ EXCHANGES[z // half ^ m][1], x)) for chunk in part]
-        for m, part in enumerate(parts)]
+        half + [moved(part, lambda z, y, x: (z, y ^ second, x)) for part in half]
+        for half, (_, second) in zip(halves, EXCHANGES)]
 
 
 KEPT = ((0, 3), (0, 1))
@@ -170,6 +146,21 @@
         part = lax.ppermute(part, ("dp", "tensor"), pairs)
         total = part if total is None else total + part
     return total
+
+
+def held(values, after):
+    def kernel(*refs):
+        pass
+
+    return pl.pallas_call(
+        kernel,
+        in_specs=[pl.BlockSpec(memory_space=pl.ANY)] * (len(values) + 1),
+        out_specs=[pl.BlockSpec(memory_space=pl.ANY)] * len(values),
+        out_shape=[jax.ShapeDtypeStruct(value.shape, value.dtype) for value in values],
+        input_output_aliases={k: k for k in range(len(values))},
+        cost_estimate=pl.CostEstimate(flops=0, bytes_accessed=0, transcendentals=0),
+        name="held",
+    )(*values, after)
 
 
 def segment_start(places, lengths_ref):
@@ -469,41 +460,44 @@
     return out[:2], out[2:-1] if ny > 1 else (None, None), out[-1]
 
 
-def project(place, hidden, weights, tn):
+def project(place, hidden, weights, tn, nz, nx):
     pack, piece = hidden.shape
     rows = pack // tn
-    part, vw = weights[0][0].shape
-    count = len(weights[0])
+    vw = weights[0][0].shape[1]
+    parts = [
+        (part, far, near)
+        for half, near, (first, second) in zip(weights, (0, 1), EXCHANGES)
+        for part, far in zip(half, (0, first, second, first ^ second))]
+    distances = (0, 4, 2, 6) if nz > 1 else (0,)
+    size = parts[0][0].shape[0] // (len(distances) * nx)
 
     def kernel(place_ref, hidden_ref, *refs):
-        weight_refs, value_refs, total_ref = refs[:2 * count], refs[2 * count:-1], refs[-1]
-        j, y, half = place_ref[0], place_ref[1], place_ref[2]
+        weight_refs, value_refs, weight_ref, total_ref = refs[:len(parts)], refs[len(parts):-2], refs[-2], refs[-1]
+        j, y, z, x = place_ref[0], place_ref[1], place_ref[2], place_ref[3]
+        for ref, (_, far, near) in zip(weight_refs, parts):
+            for k, distance in enumerate(distances):
+                for m in range(nx):
+                    block = ((y ^ far) * nz + (z ^ distance ^ near)) * nx + (x ^ m)
+                    at = pl.ds(pl.multiple_of(block * size, size), size)
+                    weight_ref[at, :] = ref[(k * nx + m) * size:(k * nx + m + 1) * size, :]
         total_ref[0:OFFMAX, :] = jnp.zeros((OFFMAX, vw), F32)
-        block = 128
-        for c in range(0, pack, block):
-            total = None
-            for m in range(2):
-                h = half ^ m
-                for s, at in enumerate((0, 1 + 2 * h, 3 - 2 * h, 2)[:count]):
-                    at = pl.ds(pl.multiple_of(h * count * part + (y ^ at) * part, part), part)
-                    term = jnp.dot(
-                        hidden_ref[c:c + block, at], weight_refs[m * count + s][...], preferred_element_type=F32)
-                    total = term if total is None else total + term
-            total_ref[OFFMAX + c:OFFMAX + c + block, :] = total
+        for c in range(0, pack, 256):
+            total_ref[OFFMAX + c:OFFMAX + c + 256, :] = jnp.dot(
+                hidden_ref[c:c + 256, :], weight_ref[...], preferred_element_type=F32)
         for s in range(tn):
             at = pl.ds(pl.multiple_of((j ^ s) * rows, rows), rows + OFFMAX)
             value_refs[s][...] = total_ref[at, :].astype(value_refs[s].dtype)
 
     return pl.pallas_call(
         kernel,
-        in_specs=[SMEM] + [VMEM] * (1 + 2 * count),
+        in_specs=[SMEM] + [VMEM] * (1 + len(parts)),
         out_specs=[VMEM] * tn,
         out_shape=[jax.ShapeDtypeStruct((rows + OFFMAX, vw), F32 if s == 0 else BF16) for s in range(tn)],
-        scratch_shapes=[pltpu.VMEM((pack + OFFMAX, vw), F32)],
+        scratch_shapes=[pltpu.VMEM((piece, vw), BF16), pltpu.VMEM((pack + OFFMAX, vw), F32)],
         compiler_params=pltpu.CompilerParams(vmem_limit_bytes=VMEM_LIMIT),
         cost_estimate=pl.CostEstimate(flops=2 * pack * piece * vw, bytes_accessed=4 * pack * piece, transcendentals=0),
         name="project",
-    )(place, hidden, *weights[0], *weights[1])
+    )(place, hidden, *[part for part, _, _ in parts])
 
 
 def spread(place, lengths, offsets, parts):
@@ -550,7 +544,7 @@
     i = lax.axis_index("dp")
     flat = i * tn + j
     nz, ny, nx = sides_of(n)
-    place = jnp.stack([j, i // nx % ny, i // (ny * nx) // max(1, nz // 2)]).astype(jnp.int32)
+    place = jnp.stack([j, i // nx % ny, i // (ny * nx), i % nx]).astype(jnp.int32)
     width = low_feature.shape[1]
     piece = width // tn
     pack = target_queries.shape[0]
@@ -559,33 +553,40 @@
     def swapped(values, s):
         return lax.ppermute(values, "tensor", [(a, a ^ s) for a in range(tn)])
 
+    folded = fold(place, doc_lengths, step_offsets, cotangent)
+    across = swapped(folded, 2)
+    low_feature, folded = lax.optimization_barrier((low_feature, folded))
     sent = features(place, low_feature, mid_feature, merging_gain, tn)
+    across, sent = lax.optimization_barrier((across, sent))
     parts = [sent[0]] + [swapped(sent[s], s) for s in range(1, tn)]
 
     high, squares = attend(doc_lengths, target_queries, target_keys, target_values)
-    own_weight, cotangent, high = lax.optimization_barrier((draft_weight, cotangent, high))
+    own_weight, high, folded, across = lax.optimization_barrier((draft_weight, high, folded, across))
     squares = squares + swapped(squares, 1)
-    own_weight = weight_of_chip(own_weight)
-    folded = fold(place, doc_lengths, step_offsets, cotangent)
-    across, beside = swapped(folded, 2), swapped(folded, 1)
-    squares, own_weight, beside, parts[1] = lax.optimization_barrier((squares, own_weight, beside, parts[1]))
+    folds = [folded, swapped(folded, 1), across, swapped(across, 1)]
+    squares, folds, parts[1] = lax.optimization_barrier((squares, folds, parts[1]))
     squares = [squares, swapped(squares, 2)]
+    weights = weight_to_place(own_weight)
     merged, squares = merge(place, merging_gain, high, parts, squares, width)
-    own_weight = weight_of_both(own_weight)
-    across, own_weight, merged, squares = lax.optimization_barrier((across, own_weight, merged, squares))
-    folds = [folded, beside, across, swapped(across, 1)]
-    own_weight = weight_of_place(own_weight)
+    weights, merged, squares = lax.optimization_barrier((weights, merged, squares))
+    weights = weight_across(jnp.concatenate(weights), nz // 2)
     squares = [squares] + [swapped(squares, s) for s in range(1, tn)]
-    weights = weight_once(weight_along_z(own_weight))
     kept, cut, hidden = grads(place, draft_gain.reshape(1, width), merged, folds, squares, width, ny, tn)
+    weights, hidden = lax.optimization_barrier((weights, hidden))
+    weights = weight_halves(weight_across(weights, nz // 4))
     halves = reduce_once(kept, cut)
     weights, own = lax.optimization_barrier((weights, [half[0] for half in halves]))
     halves = [(mine, other) for mine, (_, other) in zip(own, halves)]
+    weights = weight_once(weights)
+    grad = reduce_twice(halves)
+    if ny > 1:
+        flat_weights = held([part for half in weights for part in half], grad)
+        weights = [list(flat_weights[:2]), list(flat_weights[2:])]
     weights = weight_twice(weights)
-    grad = reduce_along_z(reduce_twice(halves))
+    grad = reduce_along_z(grad)
     hidden, grad = lax.optimization_barrier((hidden, grad))
     weight_grad = reduce_to_owner(grad)
-    values = project(place, hidden, weights, tn)
+    values = project(place, hidden, weights, tn, nz, nx)
     values = [values[0]] + [swapped(values[s], s) for s in range(1, tn)]
     draft_values = spread(place, doc_lengths, step_offsets, values)
 

time: 153 us -> 139 us (0.908)
  starting transfers between devices: 54.8 us -> 47.6 us
  waiting for transfers between devices: 54 us -> 47.4 us
  other arithmetic: 10.8 us -> 6.26 us
  local copies, waits for them, and re-layouts: 3.72 us -> 7.65 us
    ppermute x11 -> x13, waiting for transfers between devices: 7.04 us -> 23.2 us  [moved(): return lax.ppermute(values, 'dp', pairs)]
    ppermute x4 -> x2, waiting for transfers between devices: 15.6 us -> 0.01 us  [weight_to_place(): parts.append(lax.ppermute(weight, ('dp', 'tensor'), pairs))]
    all_to_all x1, waiting for transfers between devices: 10.9 us -> 3.17 us  [reduce_along_z(): lax.all_to_all(grad.astype(BF16), 'dp', 0, 0, tiled=True, axis_index_grou...]
    ppermute x4 -> x2, starting transfers between devices: 11.6 us -> 4.13 us  [weight_to_place(): parts.append(lax.ppermute(weight, ('dp', 'tensor'), pairs))]
    unnamed x38 -> x49, local copies, waits for them, and re-layouts: 3.7 us -> 7.62 us
    select_n x3 -> x0, other arithmetic: 3.32 us -> none  [the longest x2 2.27 us: joined(): jnp.where(own_first, jnp.concatenate([own, got]), jnp.concatenate([got, o...]
    ppermute x2, starting transfers between devices: 13.7 us -> 10.5 us  [reduce_to_owner(): part = lax.ppermute(part, ('dp', 'tensor'), pairs)]
    ppermute x11 -> x13, starting transfers between devices: 10.9 us -> 13.8 us  [moved(): return lax.ppermute(values, 'dp', pairs)]
  transfers between devices with their start and end apart: 32 -> 32, of which waited for: 13 -> 15; matrix products, arithmetic and copies ran while one was open for 6% -> 4% of each run, Pallas kernels for 10% -> 15%
where the time goes in v6:
time: 139 us; the launch traced here: 138 us
  starting transfers between devices  47.6 us (34%)
  waiting for transfers between devices  47.4 us (34%)
  Pallas kernels  28.2 us (20%)
  local copies, waits for them, and re-layouts  7.65 us (6%)
  other arithmetic  6.26 us (5%)
    ppermute x13, waiting for transfers between devices, moved(): return lax.ppermute(values, 'dp', pairs)  23.2 us
    ppermute x14, waiting for transfers between devices, swapped(): return lax.ppermute(values, 'tensor', [(a, a ^ s) for a in range(tn)])  21 us
    ppermute x14, starting transfers between devices, swapped(): return lax.ppermute(values, 'tensor', [(a, a ^ s) for a in range(tn)])  15 us
    ppermute x13, starting transfers between devices, moved(): return lax.ppermute(values, 'dp', pairs)  13.8 us
    ppermute x2, starting transfers between devices, reduce_to_owner(): part = lax.ppermute(part, ('dp', 'tensor'), pairs)  10.5 us
    pallas_call x1, Pallas kernels, attend(): pl.pallas_call(functools.partial(attend_kernel, window), grid=(pack // bl...  8.59 us
    unnamed x49, local copies, waits for them, and re-layouts  7.62 us
    pallas_call x1, Pallas kernels, features(): pl.pallas_call(functools.partial(features_kernel, tn), grid=(rows // bloc...  6.74 us
  transfers between devices with their start and end apart: 32, of which 15 were waited for; matrix products, arithmetic and copies ran while one was open for 4% of the time, Pallas kernels for 15%

profile of v6, /device:TPU:1, one launch (start us, length us, event | category | flops | bytes accessed | tf_op | source)
XLA Modules:
  0.0 138.2 jit_solution(9924402153071829688)
XLA Ops:
  0.8 1.0 copy-done.10
  3.1 0.9 fold.1.refs_0_
  4.0 2.1 %collective-permute-start = (bf16[160,512]{1,0:T(8,128)(2,1)S(1)}, bf16[160,512]{1,0:T(8,128)(2,1)S(1)}, u32[]{:S(2)}, u32[]{:S(2)}) collective-permute-start(bf16[160,512]{1,0:T(8,128)(2,1)S(1)} %fold.1.refs_0_), channel_id=1, source_target_pairs={{0,2},{1,3},{2,0},{3,1},{4,6},{5,7},{6,4},{7,5},{8,10},{9,11},{10,... | collective-permute-start | bytes 491528 | tf_op jit(solution)/shard_map/ppermute | solution.py:554
  6.2 6.7 %features.1 = (bf16[128,2048]{1,0:T(8,128)(2,1)}, bf16[128,2048]{1,0:T(8,128)(2,1)}, bf16[128,2048]{1,0:T(8,128)(2,1)}, bf16[128,2048]{1,0:T(8,128)(2,1)}) custom-call(s32[4]{0:T(128)} %copy-done.11, bf16[128,8192]{1,0:T(8,128)(2,1)} %low_ref, bf16[128,8192]{1,0:T(8,128)(2,1)} %mid_ref.1, f32[3,8192]{1,0:T(4,128)} %gain_ref.3), custom_call_target="tpu_custom_call" | custom-call | flops 10485760 | bytes 6291456 | tf_op jit(solution)/shard_map/features/pallas_call | solution.py:223
  12.9 1.5 %collective-permute-start.6 = (bf16[128,2048]{1,0:T(8,128)(2,1)}, bf16[128,2048]{1,0:T(8,128)(2,1)S(1)}, u32[]{:S(2)}, u32[]{:S(2)}) collective-permute-start(bf16[128,2048]{1,0:T(8,128)(2,1)} %get-tuple-element.69), channel_id=1, source_target_pairs={{0,1},{1,0},{2,3},{3,2},{4,5},{5,4},{6,7},{7,6},{8,9},{9,8},{10,11... | collective-permute-start | bytes 1572872 | tf_op jit(solution)/shard_map/ppermute | solution.py:554
  14.4 1.6 %collective-permute-start.7 = (bf16[128,2048]{1,0:T(8,128)(2,1)}, bf16[128,2048]{1,0:T(8,128)(2,1)S(1)}, u32[]{:S(2)}, u32[]{:S(2)}) collective-permute-start(bf16[128,2048]{1,0:T(8,128)(2,1)} %get-tuple-element.71), channel_id=1, source_target_pairs={{0,2},{1,3},{2,0},{3,1},{4,6},{5,7},{6,4},{7,5},{8,10},{9,11},{10,... | collective-permute-start | bytes 1572872 | tf_op jit(solution)/shard_map/ppermute | solution.py:554
  16.2 8.6 %attend.1 = (bf16[512,2048]{1,0:T(8,128)(2,1)S(1)}, f32[8,512]{1,0:T(8,128)S(1)}) custom-call(s32[1,8]{1,0:T(1,128)S(1)} %copy-done.14, bf16[512,2048]{1,0:T(8,128)(2,1)S(1)} %copy-done.18, bf16[512,256]{1,0:T(8,128)(2,1)S(1)} %copy-done.19, bf16[512,256]{1,0:T(8,128)(2,1)S(1)} %copy-done.20), custom_call_target="tpu_custom_call" | custom-call | flops 1610612736 | bytes 4194304 | tf_op jit(solution)/shard_map/attend/pallas_call | solution.py:274
  26.4 4.0 %collective-permute-start.1 = (bf16[32,512]{1,0:T(8,128)(2,1)S(1)}, bf16[32,512]{1,0:T(8,128)(2,1)S(1)}, u32[]{:S(2)}, u32[]{:S(2)}) collective-permute-start(bf16[32,512]{1,0:T(8,128)(2,1)S(1)} %copy-done.23), channel_id=1, source_target_pairs={{0,0},{1,4},{2,32},{3,36},{4,64},{5,68},{6,96},{7,100},{8,128},{9,... | collective-permute-start | bytes 98312 | tf_op jit(solution)/shard_map/ppermute | solution.py:70
  30.6 3.2 %collective-permute-start.9 = (f32[8,512]{1,0:T(8,128)S(1)}, f32[8,512]{1,0:T(8,128)S(1)}, u32[]{:S(2)}, u32[]{:S(2)}) collective-permute-start(f32[8,512]{1,0:T(8,128)S(1)} %add.65.refs_4_), channel_id=1, source_target_pairs={{0,2},{1,3},{2,0},{3,1},{4,6},{5,7},{6,4},{7,5},{8,10},{9,11},{10,... | collective-permute-start | bytes 49160 | tf_op jit(solution)/shard_map/ppermute | solution.py:554
  33.8 9.9 %collective-permute-done.8.refs_3_ = bf16[128,2048]{1,0:T(8,128)(2,1)S(1)} collective-permute-done((bf16[128,2048]{1,0:T(8,128)(2,1)}, bf16[128,2048]{1,0:T(8,128)(2,1)S(1)}, u32[]{:S(2)}, u32[]{:S(2)}) %collective-permute-start.8) | collective-permute-done | bytes 524320 | tf_op jit(solution)/shard_map/ppermute | solution.py:554
  43.7 0.9 collective-permute-done.9.refs_5_
  44.7 3.5 %merge.1 = (bf16[512,2048]{1,0:T(8,128)(2,1)S(1)}, f32[8,512]{1,0:T(8,128)S(1)}) custom-call(s32[4]{0:T(128)S(1)} %copy-done.12, f32[3,8192]{1,0:T(4,128)S(1)} %copy-done.9, bf16[512,2048]{1,0:T(8,128)(2,1)S(1)} %get-tuple-element.64.high_ref, bf16[128,2048]{1,0:T(8,128)(2,1)S(1)} %copy-done.8, bf16[128,2048]{1,0:T(8,128)(2,1)S(1)} %collective-permute-done.6.refs_1_, ...), custom_call_target="tpu_custom_call" | custom-call | flops 8388608 | bytes 6291456 | tf_op jit(solution)/shard_map/merge/pallas_call | solution.py:364
  48.2 1.0 collective-permute-start.11
  49.1 2.2 %collective-permute-start.12 = (f32[8,512]{1,0:T(8,128)S(1)}, f32[8,512]{1,0:T(8,128)S(1)}, u32[]{:S(2)}, u32[]{:S(2)}) collective-permute-start(f32[8,512]{1,0:T(8,128)S(1)} %get-tuple-element.83.refs_4_), channel_id=1, source_target_pairs={{0,2},{1,3},{2,0},{3,1},{4,6},{5,7},{6,4},{7,5},{8,10},{9,11},{10,... | collective-permute-start | bytes 49160 | tf_op jit(solution)/shard_map/ppermute | solution.py:554
  51.6 0.9 collective-permute-done.12.refs_6_
  52.5 2.1 %collective-permute-done.13.refs_7_ = f32[8,512]{1,0:T(8,128)S(1)} collective-permute-done((f32[8,512]{1,0:T(8,128)S(1)}, f32[8,512]{1,0:T(8,128)S(1)}, u32[]{:S(2)}, u32[]{:S(2)}) %collective-permute-start.13) | collective-permute-done | bytes 16416 | tf_op jit(solution)/shard_map/ppermute | solution.py:554
  54.5 4.8 %grads.1 = (f32[2,256,512]{2,1,0:T(8,128)S(1)}, f32[2,256,512]{2,1,0:T(8,128)S(1)}, bf16[2,256,512]{2,1,0:T(8,128)(2,1)S(1)}, bf16[2,256,512]{2,1,0:T(8,128)(2,1)S(1)}, bf16[512,2048]{1,0:T(8,128)(2,1)S(1)}) custom-call(s32[4]{0:T(128)S(1)} %copy-done.12, f32[1,8192]{1,0:T(1,128)S(1)} %bitcast.14, bf16[512,2048]{1,0:T(8,128)(2,1)S(1)} %get-tuple-element.78.merged_ref, ...), custom_call_target="tpu_custom_call" | custom-call | flops 1073741824 | bytes 8388608 | tf_op jit(solution)/shard_map/grads/pallas_call | solution.py:444
  59.5 1.6 %collective-permute-start.17 = (bf16[2,256,512]{2,1,0:T(8,128)(2,1)S(1)}, bf16[2,256,512]{2,1,0:T(8,128)(2,1)S(1)}, u32[]{:S(2)}, u32[]{:S(2)}) collective-permute-start(bf16[2,256,512]{2,1,0:T(8,128)(2,1)S(1)} %get-tuple-element.89), channel_id=1, source_target_pairs={{0,24},{4,28},{8,16},{12,20},{16,8},{20,12},{24,0},{28,4},{32,56},... | collective-permute-start | bytes 1572872 | tf_op jit(solution)/shard_map/ppermute | solution.py:57
  61.1 6.5 %collective-permute-start.10 = (bf16[64,512]{1,0:T(8,128)(2,1)S(1)}, bf16[64,512]{1,0:T(8,128)(2,1)S(1)}, u32[]{:S(2)}, u32[]{:S(2)}) collective-permute-start(bf16[64,512]{1,0:T(8,128)(2,1)S(1)} %pad_maximum_fusion.2), channel_id=1, source_target_pairs={{0,128},{4,132},{8,136},{12,140},{16,144},{20,148},{24,152},{28,15... | collective-permute-start | bytes 196616 | tf_op jit(solution)/shard_map/ppermute | solution.py:57
  67.6 2.9 %collective-permute-done.10 = bf16[64,512]{1,0:T(8,128)(2,1)S(1)} collective-permute-done((bf16[64,512]{1,0:T(8,128)(2,1)S(1)}, bf16[64,512]{1,0:T(8,128)(2,1)S(1)}, u32[]{:S(2)}, u32[]{:S(2)}) %collective-permute-start.10) | collective-permute-done | bytes 65568 | tf_op jit(solution)/shard_map/ppermute | solution.py:57
  70.6 9.0 %collective-permute-done.14 = bf16[128,512]{1,0:T(8,128)(2,1)S(1)} collective-permute-done((bf16[128,512]{1,0:T(8,128)(2,1)S(1)}, bf16[128,512]{1,0:T(8,128)(2,1)S(1)}, u32[]{:S(2)}, u32[]{:S(2)}) %collective-permute-start.14) | collective-permute-done | bytes 131104 | tf_op jit(solution)/shard_map/ppermute | solution.py:57
  80.3 6.6 %collective-permute-done.15.refs_2_ = bf16[256,512]{1,0:T(8,128)(2,1)S(1)} collective-permute-done((bf16[256,512]{1,0:T(8,128)(2,1)S(1)}, bf16[256,512]{1,0:T(8,128)(2,1)S(1)}, u32[]{:S(2)}, u32[]{:S(2)}) %collective-permute-start.15) | collective-permute-done | bytes 262176 | tf_op jit(solution)/shard_map/ppermute | solution.py:57
  86.9 1.5 %collective-permute-done.18 = bf16[256,512]{1,0:T(8,128)(2,1)S(1)} collective-permute-done((bf16[256,512]{1,0:T(8,128)(2,1)S(1)}, bf16[256,512]{1,0:T(8,128)(2,1)S(1)}, u32[]{:S(2)}, u32[]{:S(2)}) %collective-permute-start.18) | collective-permute-done | bytes 262176 | tf_op jit(solution)/shard_map/ppermute | solution.py:57
  88.6 0.7 copy-done.21
  89.3 1.0 fusion.2
  90.3 4.1 %all-to-all-start = ((bf16[8,64,512]{2,1,0:T(8,128)(2,1)}), bf16[8,64,512]{2,1,0:T(8,128)(2,1)}, u32[]{:S(2)}, u32[]{:S(2)}) async-start(bf16[8,64,512]{2,1,0:T(8,128)(2,1)} %bitcast.9), calls=%async_computation | async-start | bytes 1048576 | tf_op jit(solution)/shard_map/all_to_all | solution.py:126
  94.5 0.9 collective-permute-start.21
  95.4 2.3 %pad_maximum_fusion.refs_4_ = f32[512,512]{1,0:T(8,128)} fusion(f32[256,512]{1,0:T(8,128)} %copy-done.22, f32[256,512]{1,0:T(8,128)} %copy-done.21), kind=kLoop, calls=%fused_computation | loop fusion | flops 262144 | bytes 2097152 | tf_op jit(solution)/shard_map/concatenate | solution.py:117
  97.7 2.0 %collective-permute-done.20.refs_1_ = bf16[256,512]{1,0:T(8,128)(2,1)S(1)} collective-permute-done((bf16[256,512]{1,0:T(8,128)(2,1)S(1)}, bf16[256,512]{1,0:T(8,128)(2,1)S(1)}, u32[]{:S(2)}, u32[]{:S(2)}) %collective-permute-start.20) | collective-permute-done | bytes 262176 | tf_op jit(solution)/shard_map/ppermute | solution.py:57
  99.7 1.3 collective-permute-done.21.refs_3_
  101.0 0.7 copy-done.6
  101.7 0.8 collective-permute-start.22
  102.6 1.9 %collective-permute-start.23 = (bf16[256,512]{1,0:T(8,128)(2,1)}, bf16[256,512]{1,0:T(8,128)(2,1)S(1)}, u32[]{:S(2)}, u32[]{:S(2)}) collective-permute-start(bf16[256,512]{1,0:T(8,128)(2,1)} %get-tuple-element.99.refs_1_), channel_id=1, source_target_pairs={{0,24},{4,28},{8,16},{12,20},{16,8},{20,12},{24,0},{28,4},{32,56},... | collective-permute-start | bytes 786440 | tf_op jit(solution)/shard_map/ppermute | solution.py:57
  104.4 1.5 %collective-permute-start.25 = (bf16[256,512]{1,0:T(8,128)(2,1)}, bf16[256,512]{1,0:T(8,128)(2,1)S(1)}, u32[]{:S(2)}, u32[]{:S(2)}) collective-permute-start(bf16[256,512]{1,0:T(8,128)(2,1)} %get-tuple-element.101.refs_5_), channel_id=1, source_target_pairs={{0,8},{4,12},{8,0},{12,4},{16,24},{20,28},{24,16},{28,20},{32,40},... | collective-permute-start | bytes 786440 | tf_op jit(solution)/shard_map/ppermute | solution.py:57
  105.9 3.2 %all-to-all-done = bf16[8,64,512]{2,1,0:T(8,128)(2,1)} async-done(((bf16[8,64,512]{2,1,0:T(8,128)(2,1)}), bf16[8,64,512]{2,1,0:T(8,128)(2,1)}, u32[]{:S(2)}, u32[]{:S(2)}) %all-to-all-start) | async-done | bytes 524320 | tf_op jit(solution)/shard_map/all_to_all | solution.py:126
  109.1 1.1 convert_reduce_fusion
  110.2 6.1 %collective-permute-start.29 = (f32[32,512]{1,0:T(8,128)S(1)}, f32[32,512]{1,0:T(8,128)S(1)}, u32[]{:S(2)}, u32[]{:S(2)}) collective-permute-start(f32[32,512]{1,0:T(8,128)S(1)} %get-tuple-element.114), channel_id=1, source_target_pairs={{0,0},{1,64},{2,128},{3,192},{4,4},{5,68},{6,132},{7,196},{8,8},{9... | collective-permute-start | bytes 196616 | tf_op jit(solution)/shard_map/ppermute | solution.py:146
  116.3 4.5 %collective-permute-start.30 = (f32[32,512]{1,0:T(8,128)S(1)}, f32[32,512]{1,0:T(8,128)S(1)}, u32[]{:S(2)}, u32[]{:S(2)}) collective-permute-start(f32[32,512]{1,0:T(8,128)S(1)} %get-tuple-element.113), channel_id=1, source_target_pairs={{0,4},{1,68},{2,132},{3,196},{4,0},{5,64},{6,128},{7,192},{8,12},{... | collective-permute-start | bytes 196616 | tf_op jit(solution)/shard_map/ppermute | solution.py:146
  120.8 0.9 copy-done.1
  121.7 0.9 copy-done.3
  122.7 0.9 copy-done.5
  123.6 0.9 copy-done.7
  124.6 2.0 %project.1 = (f32[160,512]{1,0:T(8,128)S(1)}, bf16[160,512]{1,0:T(8,128)(2,1)S(1)}, bf16[160,512]{1,0:T(8,128)(2,1)S(1)}, bf16[160,512]{1,0:T(8,128)(2,1)S(1)}) custom-call(s32[4]{0:T(128)S(1)} %copy-done.12, bf16[512,2048]{1,0:T(8,128)(2,1)S(1)} %get-tuple-element.95.hidden_ref, bf16[256,512]{1,0:T(8,128)(2,1)S(1)} %copy-done.1, ...), custom_call_target="tpu_custom_call" | custom-call | flops 1073741824 | bytes 4194304 | tf_op jit(solution)/shard_map/project/pallas_call | solution.py:491
  126.7 1.9 %collective-permute-start.27 = (bf16[160,512]{1,0:T(8,128)(2,1)S(1)}, bf16[160,512]{1,0:T(8,128)(2,1)S(1)}, u32[]{:S(2)}, u32[]{:S(2)}) collective-permute-start(bf16[160,512]{1,0:T(8,128)(2,1)S(1)} %get-tuple-element.104), channel_id=1, source_target_pairs={{0,2},{1,3},{2,0},{3,1},{4,6},{5,7},{6,4},{7,5},{8,10},{9,11},{10,... | collective-permute-start | bytes 491528 | tf_op jit(solution)/shard_map/ppermute | solution.py:554
  128.8 0.8 multiply_reduce_fusion
  130.2 2.6 %collective-permute-done.27.refs_2_ = bf16[160,512]{1,0:T(8,128)(2,1)S(1)} collective-permute-done((bf16[160,512]{1,0:T(8,128)(2,1)S(1)}, bf16[160,512]{1,0:T(8,128)(2,1)S(1)}, u32[]{:S(2)}, u32[]{:S(2)}) %collective-permute-start.27) | collective-permute-done | bytes 163872 | tf_op jit(solution)/shard_map/ppermute | solution.py:554
  132.8 3.7 %collective-permute-done.28.refs_3_ = bf16[160,512]{1,0:T(8,128)(2,1)S(1)} collective-permute-done((bf16[160,512]{1,0:T(8,128)(2,1)S(1)}, bf16[160,512]{1,0:T(8,128)(2,1)S(1)}, u32[]{:S(2)}, u32[]{:S(2)}) %collective-permute-start.28) | collective-permute-done | bytes 163872 | tf_op jit(solution)/shard_map/ppermute | solution.py:554
  136.5 1.7 %spread.1 = bf16[3,128,512]{2,1,0:T(8,128)(2,1)} custom-call(s32[4]{0:T(128)S(1)} %copy-done.12, s32[1,8]{1,0:T(1,128)S(1)} %copy-done.14, s32[3]{0:T(128)S(1)} %copy-done.16, f32[160,512]{1,0:T(8,128)S(1)} %get-tuple-element.102.refs_0_, bf16[160,512]{1,0:T(8,128)(2,1)S(1)} %collective-permute-done.26.refs_1_, ...), custom_call_target="tpu_custom_call" | custom-call | flops 62914560 | bytes 1572864 | tf_op jit(solution)/shard_map/spread/pallas_call | solution.py:517
  (88 shorter events, 5.8 us)
Async XLA Ops:
  0.8 1.0 copy-start.10
  3.1 3.1 %copy-start.11 = (s32[4]{0:T(128)}, s32[4]{0:T(128)S(1)}, u32[]{:S(2)}) copy-start(s32[4]{0:T(128)S(1)} %pad_add_fusion.place_ref) | copy-start | bytes 52
  4.0 12.2 %copy-start.14 = (s32[1,8]{1,0:T(1,128)S(1)}, s32[1,8]{1,0:T(1,128)}, u32[]{:S(2)}) copy-start(s32[1,8]{1,0:T(1,128)} %lengths_ref.5) | copy-start | bytes 100
  4.0 12.2 %copy-start.18 = (bf16[512,2048]{1,0:T(8,128)(2,1)S(1)}, bf16[512,2048]{1,0:T(8,128)(2,1)}, u32[]{:S(2)}) copy-start(bf16[512,2048]{1,0:T(8,128)(2,1)} %query_ref.1) | copy-start | bytes 6291460
  4.0 12.2 %copy-start.19 = (bf16[512,256]{1,0:T(8,128)(2,1)S(1)}, bf16[512,256]{1,0:T(8,128)(2,1)}, u32[]{:S(2)}) copy-start(bf16[512,256]{1,0:T(8,128)(2,1)} %key_ref.1) | copy-start | bytes 786436
  4.0 12.1 %copy-start.20 = (bf16[512,256]{1,0:T(8,128)(2,1)S(1)}, bf16[512,256]{1,0:T(8,128)(2,1)}, u32[]{:S(2)}) copy-start(bf16[512,256]{1,0:T(8,128)(2,1)} %value_ref.1) | copy-start | bytes 786436
  4.0 8.9 %collective-permute-start = (bf16[160,512]{1,0:T(8,128)(2,1)S(1)}, bf16[160,512]{1,0:T(8,128)(2,1)S(1)}, u32[]{:S(2)}, u32[]{:S(2)}) collective-permute-start(bf16[160,512]{1,0:T(8,128)(2,1)S(1)} %fold.1.refs_0_), channel_id=1, source_target_pairs={{0,2},{1,3},{2,0},{3,1},{4,6},{5,7},{6,4},{7,5},{8,10},{9,11},{10,... | collective-permute-start | bytes 491528 | tf_op jit(solution)/shard_map/ppermute | solution.py:554
  12.9 13.5 %copy-start.23 = (bf16[32,512]{1,0:T(8,128)(2,1)S(1)}, bf16[32,512]{1,0:T(8,128)(2,1)}, u32[]{:S(2)}) copy-start(bf16[32,512]{1,0:T(8,128)(2,1)} %param.18) | copy-start | bytes 98308
  12.9 31.8 %copy-start.8 = (bf16[128,2048]{1,0:T(8,128)(2,1)S(1)}, bf16[128,2048]{1,0:T(8,128)(2,1)}, u32[]{:S(2)}) copy-start(bf16[128,2048]{1,0:T(8,128)(2,1)} %get-tuple-element.65.refs_0_) | copy-start | bytes 1572868
  12.9 31.8 %copy-start.9 = (f32[3,8192]{1,0:T(4,128)S(1)}, f32[3,8192]{1,0:T(4,128)}, u32[]{:S(2)}) copy-start(f32[3,8192]{1,0:T(4,128)} %gain_ref.3) | copy-start | bytes 294916
  12.9 31.8 %copy-start.12 = (s32[4]{0:T(128)S(1)}, s32[4]{0:T(128)}, u32[]{:S(2)}) copy-start(s32[4]{0:T(128)} %copy-done.11) | copy-start | bytes 52
  12.9 17.7 %collective-permute-start.6 = (bf16[128,2048]{1,0:T(8,128)(2,1)}, bf16[128,2048]{1,0:T(8,128)(2,1)S(1)}, u32[]{:S(2)}, u32[]{:S(2)}) collective-permute-start(bf16[128,2048]{1,0:T(8,128)(2,1)} %get-tuple-element.69), channel_id=1, source_target_pairs={{0,1},{1,0},{2,3},{3,2},{4,5},{5,4},{6,7},{7,6},{8,9},{9,8},{10,11... | collective-permute-start | bytes 1572872 | tf_op jit(solution)/shard_map/ppermute | solution.py:554
  14.4 19.4 %collective-permute-start.7 = (bf16[128,2048]{1,0:T(8,128)(2,1)}, bf16[128,2048]{1,0:T(8,128)(2,1)S(1)}, u32[]{:S(2)}, u32[]{:S(2)}) collective-permute-start(bf16[128,2048]{1,0:T(8,128)(2,1)} %get-tuple-element.71), channel_id=1, source_target_pairs={{0,2},{1,3},{2,0},{3,1},{4,6},{5,7},{6,4},{7,5},{8,10},{9,11},{10,... | collective-permute-start | bytes 1572872 | tf_op jit(solution)/shard_map/ppermute | solution.py:554
  16.0 27.7 %collective-permute-start.8 = (bf16[128,2048]{1,0:T(8,128)(2,1)}, bf16[128,2048]{1,0:T(8,128)(2,1)S(1)}, u32[]{:S(2)}, u32[]{:S(2)}) collective-permute-start(bf16[128,2048]{1,0:T(8,128)(2,1)} %get-tuple-element.72), channel_id=1, source_target_pairs={{0,3},{1,2},{2,1},{3,0},{4,7},{5,6},{6,5},{7,4},{8,11},{9,10},{10,... | collective-permute-start | bytes 1572872 | tf_op jit(solution)/shard_map/ppermute | solution.py:554
  24.7 1.2 collective-permute-start.3
  25.0 1.4 %collective-permute-start.4 = (bf16[160,512]{1,0:T(8,128)(2,1)S(1)}, bf16[160,512]{1,0:T(8,128)(2,1)S(1)}, u32[]{:S(2)}, u32[]{:S(2)}) collective-permute-start(bf16[160,512]{1,0:T(8,128)(2,1)S(1)} %fold.1.refs_0_), channel_id=1, source_target_pairs={{0,1},{1,0},{2,3},{3,2},{4,5},{5,4},{6,7},{7,6},{8,9},{9,8},{10,11... | collective-permute-start | bytes 491528 | tf_op jit(solution)/shard_map/ppermute | solution.py:554
  26.0 4.5 %collective-permute-start.5 = (bf16[160,512]{1,0:T(8,128)(2,1)S(1)}, bf16[160,512]{1,0:T(8,128)(2,1)S(1)}, u32[]{:S(2)}, u32[]{:S(2)}) collective-permute-start(bf16[160,512]{1,0:T(8,128)(2,1)S(1)} %collective-permute-done.refs_2_), channel_id=1, source_target_pairs={{0,1},{1,0},{2,3},{3,2},{4,5},{5,4},{6,7},{7,6},{8,9},{9,8},{10,11... | collective-permute-start | bytes 491528 | tf_op jit(solution)/shard_map/ppermute | solution.py:554
  26.4 21.7 %collective-permute-start.1 = (bf16[32,512]{1,0:T(8,128)(2,1)S(1)}, bf16[32,512]{1,0:T(8,128)(2,1)S(1)}, u32[]{:S(2)}, u32[]{:S(2)}) collective-permute-start(bf16[32,512]{1,0:T(8,128)(2,1)S(1)} %copy-done.23), channel_id=1, source_target_pairs={{0,0},{1,4},{2,32},{3,36},{4,64},{5,68},{6,96},{7,100},{8,128},{9,... | collective-permute-start | bytes 98312 | tf_op jit(solution)/shard_map/ppermute | solution.py:70
  30.5 17.7 %collective-permute-start.2 = (bf16[32,512]{1,0:T(8,128)(2,1)S(1)}, bf16[32,512]{1,0:T(8,128)(2,1)S(1)}, u32[]{:S(2)}, u32[]{:S(2)}) collective-permute-start(bf16[32,512]{1,0:T(8,128)(2,1)S(1)} %copy-done.23), channel_id=1, source_target_pairs={{0,4},{1,0},{2,36},{3,32},{4,68},{5,64},{6,100},{7,96},{8,132},{9,... | collective-permute-start | bytes 98312 | tf_op jit(solution)/shard_map/ppermute | solution.py:70
  30.6 23.9 %copy-start.17 = (f32[8192]{0:T(1024)S(1)}, f32[8192]{0:T(1024)}, u32[]{:S(2)}) copy-start(f32[8192]{0:T(1024)} %param.17) | copy-start | bytes 98308
  30.6 14.0 %collective-permute-start.9 = (f32[8,512]{1,0:T(8,128)S(1)}, f32[8,512]{1,0:T(8,128)S(1)}, u32[]{:S(2)}, u32[]{:S(2)}) collective-permute-start(f32[8,512]{1,0:T(8,128)S(1)} %add.65.refs_4_), channel_id=1, source_target_pairs={{0,2},{1,3},{2,0},{3,1},{4,6},{5,7},{6,4},{7,5},{8,10},{9,11},{10,... | collective-permute-start | bytes 49160 | tf_op jit(solution)/shard_map/ppermute | solution.py:554
  48.2 3.4 %collective-permute-start.11 = (f32[8,512]{1,0:T(8,128)S(1)}, f32[8,512]{1,0:T(8,128)S(1)}, u32[]{:S(2)}, u32[]{:S(2)}) collective-permute-start(f32[8,512]{1,0:T(8,128)S(1)} %get-tuple-element.83.refs_4_), channel_id=1, source_target_pairs={{0,1},{1,0},{2,3},{3,2},{4,5},{5,4},{6,7},{7,6},{8,9},{9,8},{10,11... | collective-permute-start | bytes 49160 | tf_op jit(solution)/shard_map/ppermute | solution.py:554
  49.1 3.3 %collective-permute-start.12 = (f32[8,512]{1,0:T(8,128)S(1)}, f32[8,512]{1,0:T(8,128)S(1)}, u32[]{:S(2)}, u32[]{:S(2)}) collective-permute-start(f32[8,512]{1,0:T(8,128)S(1)} %get-tuple-element.83.refs_4_), channel_id=1, source_target_pairs={{0,2},{1,3},{2,0},{3,1},{4,6},{5,7},{6,4},{7,5},{8,10},{9,11},{10,... | collective-permute-start | bytes 49160 | tf_op jit(solution)/shard_map/ppermute | solution.py:554
  51.4 3.2 %collective-permute-start.13 = (f32[8,512]{1,0:T(8,128)S(1)}, f32[8,512]{1,0:T(8,128)S(1)}, u32[]{:S(2)}, u32[]{:S(2)}) collective-permute-start(f32[8,512]{1,0:T(8,128)S(1)} %get-tuple-element.83.refs_4_), channel_id=1, source_target_pairs={{0,3},{1,2},{2,1},{3,0},{4,7},{5,6},{6,5},{7,4},{8,11},{9,10},{10,... | collective-permute-start | bytes 49160 | tf_op jit(solution)/shard_map/ppermute | solution.py:554
  59.4 20.3 %collective-permute-start.16 = (bf16[2,256,512]{2,1,0:T(8,128)(2,1)S(1)}, bf16[2,256,512]{2,1,0:T(8,128)(2,1)S(1)}, u32[]{:S(2)}, u32[]{:S(2)}) collective-permute-start(bf16[2,256,512]{2,1,0:T(8,128)(2,1)S(1)} %get-tuple-element.88), channel_id=1, source_target_pairs={{0,8},{4,12},{8,0},{12,4},{16,24},{20,28},{24,16},{28,20},{32,40},... | collective-permute-start | bytes 1572872 | tf_op jit(solution)/shard_map/ppermute | solution.py:57
  59.5 20.2 %collective-permute-start.17 = (bf16[2,256,512]{2,1,0:T(8,128)(2,1)S(1)}, bf16[2,256,512]{2,1,0:T(8,128)(2,1)S(1)}, u32[]{:S(2)}, u32[]{:S(2)}) collective-permute-start(bf16[2,256,512]{2,1,0:T(8,128)(2,1)S(1)} %get-tuple-element.89), channel_id=1, source_target_pairs={{0,24},{4,28},{8,16},{12,20},{16,8},{20,12},{24,0},{28,4},{32,56},... | collective-permute-start | bytes 1572872 | tf_op jit(solution)/shard_map/ppermute | solution.py:57
  61.1 9.4 %collective-permute-start.10 = (bf16[64,512]{1,0:T(8,128)(2,1)S(1)}, bf16[64,512]{1,0:T(8,128)(2,1)S(1)}, u32[]{:S(2)}, u32[]{:S(2)}) collective-permute-start(bf16[64,512]{1,0:T(8,128)(2,1)S(1)} %pad_maximum_fusion.2), channel_id=1, source_target_pairs={{0,128},{4,132},{8,136},{12,140},{16,144},{20,148},{24,152},{28,15... | collective-permute-start | bytes 196616 | tf_op jit(solution)/shard_map/ppermute | solution.py:57
  70.5 9.1 %collective-permute-start.14 = (bf16[128,512]{1,0:T(8,128)(2,1)S(1)}, bf16[128,512]{1,0:T(8,128)(2,1)S(1)}, u32[]{:S(2)}, u32[]{:S(2)}) collective-permute-start(bf16[128,512]{1,0:T(8,128)(2,1)S(1)} %pad_maximum_fusion.1), channel_id=1, source_target_pairs={{0,64},{4,68},{8,72},{12,76},{16,80},{20,84},{24,88},{28,92},{32,9... | collective-permute-start | bytes 393224 | tf_op jit(solution)/shard_map/ppermute | solution.py:57
  79.6 14.8 %copy-start = (bf16[256,512]{1,0:T(8,128)(2,1)}, bf16[256,512]{1,0:T(8,128)(2,1)S(1)}, u32[]{:S(2)}) copy-start(bf16[256,512]{1,0:T(8,128)(2,1)S(1)} %constant_dynamic-update-slice_fusion.refs_0_) | copy-start | bytes 786436
  79.6 7.3 %collective-permute-start.15 = (bf16[256,512]{1,0:T(8,128)(2,1)S(1)}, bf16[256,512]{1,0:T(8,128)(2,1)S(1)}, u32[]{:S(2)}, u32[]{:S(2)}) collective-permute-start(bf16[256,512]{1,0:T(8,128)(2,1)S(1)} %constant_dynamic-update-slice_fusion.refs_0_), channel_id=1, source_target_pairs={{0,32},{4,36},{8,40},{12,44},{16,48},{20,52},{24,56},{28,60},{32,0... | collective-permute-start | bytes 786440 | tf_op jit(solution)/shard_map/ppermute | solution.py:57
  79.9 8.5 %collective-permute-start.18 = (bf16[256,512]{1,0:T(8,128)(2,1)S(1)}, bf16[256,512]{1,0:T(8,128)(2,1)S(1)}, u32[]{:S(2)}, u32[]{:S(2)}) collective-permute-start(bf16[256,512]{1,0:T(8,128)(2,1)S(1)} %get-tuple-element.109), channel_id=1, source_target_pairs={{0,24},{4,28},{8,16},{12,20},{16,8},{20,12},{24,0},{28,4},{32,56},... | collective-permute-start | bytes 786440 | tf_op jit(solution)/shard_map/ppermute | solution.py:57
  80.1 8.4 %collective-permute-start.19 = (bf16[256,512]{1,0:T(8,128)(2,1)S(1)}, bf16[256,512]{1,0:T(8,128)(2,1)S(1)}, u32[]{:S(2)}, u32[]{:S(2)}) collective-permute-start(bf16[256,512]{1,0:T(8,128)(2,1)S(1)} %get-tuple-element.111), channel_id=1, source_target_pairs={{0,8},{4,12},{8,0},{12,4},{16,24},{20,28},{24,16},{28,20},{32,40},... | collective-permute-start | bytes 786440 | tf_op jit(solution)/shard_map/ppermute | solution.py:57
  86.9 7.6 %copy-start.2 = (bf16[256,512]{1,0:T(8,128)(2,1)}, bf16[256,512]{1,0:T(8,128)(2,1)S(1)}, u32[]{:S(2)}) copy-start(bf16[256,512]{1,0:T(8,128)(2,1)S(1)} %collective-permute-done.15.refs_2_) | copy-start | bytes 786436
  89.3 1.0 copy-start.22
  90.3 18.8 %all-to-all-start = ((bf16[8,64,512]{2,1,0:T(8,128)(2,1)}), bf16[8,64,512]{2,1,0:T(8,128)(2,1)}, u32[]{:S(2)}, u32[]{:S(2)}) async-start(bf16[8,64,512]{2,1,0:T(8,128)(2,1)} %bitcast.9), calls=%async_computation | async-start | bytes 1048576 | tf_op jit(solution)/shard_map/all_to_all | solution.py:126
  94.4 5.3 %collective-permute-start.20 = (bf16[256,512]{1,0:T(8,128)(2,1)S(1)}, bf16[256,512]{1,0:T(8,128)(2,1)S(1)}, u32[]{:S(2)}, u32[]{:S(2)}) collective-permute-start(bf16[256,512]{1,0:T(8,128)(2,1)S(1)} %constant_dynamic-update-slice_fusion.refs_0_), channel_id=1, source_target_pairs={{0,8},{4,12},{8,0},{12,4},{16,24},{20,28},{24,16},{28,20},{32,40},... | collective-permute-start | bytes 786440 | tf_op jit(solution)/shard_map/ppermute | solution.py:57
  94.5 6.5 %collective-permute-start.21 = (bf16[256,512]{1,0:T(8,128)(2,1)S(1)}, bf16[256,512]{1,0:T(8,128)(2,1)S(1)}, u32[]{:S(2)}, u32[]{:S(2)}) collective-permute-start(bf16[256,512]{1,0:T(8,128)(2,1)S(1)} %collective-permute-done.15.refs_2_), channel_id=1, source_target_pairs={{0,24},{4,28},{8,16},{12,20},{16,8},{20,12},{24,0},{28,4},{32,56},... | collective-permute-start | bytes 786440 | tf_op jit(solution)/shard_map/ppermute | solution.py:57
  99.7 1.3 copy-start.4
  101.7 14.5 %collective-permute-start.22 = (bf16[256,512]{1,0:T(8,128)(2,1)}, bf16[256,512]{1,0:T(8,128)(2,1)S(1)}, u32[]{:S(2)}, u32[]{:S(2)}) collective-permute-start(bf16[256,512]{1,0:T(8,128)(2,1)} %get-tuple-element.98.refs_0_), channel_id=1, source_target_pairs={{0,24},{4,28},{8,16},{12,20},{16,8},{20,12},{24,0},{28,4},{32,56},... | collective-permute-start | bytes 786440 | tf_op jit(solution)/shard_map/ppermute | solution.py:57
  102.6 18.2 %collective-permute-start.23 = (bf16[256,512]{1,0:T(8,128)(2,1)}, bf16[256,512]{1,0:T(8,128)(2,1)S(1)}, u32[]{:S(2)}, u32[]{:S(2)}) collective-permute-start(bf16[256,512]{1,0:T(8,128)(2,1)} %get-tuple-element.99.refs_1_), channel_id=1, source_target_pairs={{0,24},{4,28},{8,16},{12,20},{16,8},{20,12},{24,0},{28,4},{32,56},... | collective-permute-start | bytes 786440 | tf_op jit(solution)/shard_map/ppermute | solution.py:57
  104.4 16.4 %collective-permute-start.24 = (bf16[256,512]{1,0:T(8,128)(2,1)}, bf16[256,512]{1,0:T(8,128)(2,1)S(1)}, u32[]{:S(2)}, u32[]{:S(2)}) collective-permute-start(bf16[256,512]{1,0:T(8,128)(2,1)} %get-tuple-element.100.refs_4_), channel_id=1, source_target_pairs={{0,8},{4,12},{8,0},{12,4},{16,24},{20,28},{24,16},{28,20},{32,40},... | collective-permute-start | bytes 786440 | tf_op jit(solution)/shard_map/ppermute | solution.py:57
  104.4 16.4 %collective-permute-start.25 = (bf16[256,512]{1,0:T(8,128)(2,1)}, bf16[256,512]{1,0:T(8,128)(2,1)S(1)}, u32[]{:S(2)}, u32[]{:S(2)}) collective-permute-start(bf16[256,512]{1,0:T(8,128)(2,1)} %get-tuple-element.101.refs_5_), channel_id=1, source_target_pairs={{0,8},{4,12},{8,0},{12,4},{16,24},{20,28},{24,16},{28,20},{32,40},... | collective-permute-start | bytes 786440 | tf_op jit(solution)/shard_map/ppermute | solution.py:57
  110.2 18.6 %collective-permute-start.29 = (f32[32,512]{1,0:T(8,128)S(1)}, f32[32,512]{1,0:T(8,128)S(1)}, u32[]{:S(2)}, u32[]{:S(2)}) collective-permute-start(f32[32,512]{1,0:T(8,128)S(1)} %get-tuple-element.114), channel_id=1, source_target_pairs={{0,0},{1,64},{2,128},{3,192},{4,4},{5,68},{6,132},{7,196},{8,8},{9... | collective-permute-start | bytes 196616 | tf_op jit(solution)/shard_map/ppermute | solution.py:146
  116.3 20.2 %copy-start.16 = (s32[3]{0:T(128)S(1)}, s32[3]{0:T(128)}, u32[]{:S(2)}) copy-start(s32[3]{0:T(128)} %offsets_ref.3) | copy-start | bytes 40
  116.3 12.5 %collective-permute-start.30 = (f32[32,512]{1,0:T(8,128)S(1)}, f32[32,512]{1,0:T(8,128)S(1)}, u32[]{:S(2)}, u32[]{:S(2)}) collective-permute-start(f32[32,512]{1,0:T(8,128)S(1)} %get-tuple-element.113), channel_id=1, source_target_pairs={{0,4},{1,68},{2,132},{3,196},{4,0},{5,64},{6,128},{7,192},{8,12},{... | collective-permute-start | bytes 196616 | tf_op jit(solution)/shard_map/ppermute | solution.py:146
  126.6 3.6 %collective-permute-start.26 = (bf16[160,512]{1,0:T(8,128)(2,1)S(1)}, bf16[160,512]{1,0:T(8,128)(2,1)S(1)}, u32[]{:S(2)}, u32[]{:S(2)}) collective-permute-start(bf16[160,512]{1,0:T(8,128)(2,1)S(1)} %get-tuple-element.103), channel_id=1, source_target_pairs={{0,1},{1,0},{2,3},{3,2},{4,5},{5,4},{6,7},{7,6},{8,9},{9,8},{10,11... | collective-permute-start | bytes 491528 | tf_op jit(solution)/shard_map/ppermute | solution.py:554
  126.7 6.1 %collective-permute-start.27 = (bf16[160,512]{1,0:T(8,128)(2,1)S(1)}, bf16[160,512]{1,0:T(8,128)(2,1)S(1)}, u32[]{:S(2)}, u32[]{:S(2)}) collective-permute-start(bf16[160,512]{1,0:T(8,128)(2,1)S(1)} %get-tuple-element.104), channel_id=1, source_target_pairs={{0,2},{1,3},{2,0},{3,1},{4,6},{5,7},{6,4},{7,5},{8,10},{9,11},{10,... | collective-permute-start | bytes 491528 | tf_op jit(solution)/shard_map/ppermute | solution.py:554
  128.6 8.0 %collective-permute-start.28 = (bf16[160,512]{1,0:T(8,128)(2,1)S(1)}, bf16[160,512]{1,0:T(8,128)(2,1)S(1)}, u32[]{:S(2)}, u32[]{:S(2)}) collective-permute-start(bf16[160,512]{1,0:T(8,128)(2,1)S(1)} %get-tuple-element.105), channel_id=1, source_target_pairs={{0,3},{1,2},{2,1},{3,0},{4,7},{5,6},{6,5},{7,4},{8,11},{9,10},{10,... | collective-permute-start | bytes 491528 | tf_op jit(solution)/shard_map/ppermute | solution.py:554
  (8 other events, 6.6 us)

commit v7 on v6

--- a/solution.py
+++ b/solution.py
@@ -14,7 +14,7 @@
 OFFMAX = 32
 EPSILON = 1e-05
 VMEM_LIMIT = 20 * 1024 * 1024
-FEATURES_LIMIT = 60 * 1024 * 1024
+LARGE_LIMIT = 60 * 1024 * 1024
 
 VMEM = pl.BlockSpec(memory_space=pltpu.VMEM)
 SMEM = pl.BlockSpec(memory_space=pltpu.SMEM)
@@ -112,9 +112,8 @@
 
 def reduce_twice(halves):
     if sides_of(lax.axis_size("dp"))[1] == 1:
-        return jnp.concatenate([own for own, _ in halves])
-    got = [moved(other, lambda z, y, x: (z, y ^ second, x)) for (_, other), (_, second) in zip(halves, EXCHANGES)]
-    return jnp.concatenate([own + part.astype(F32) for (own, _), part in zip(halves, got)])
+        return [jnp.zeros_like(own) for own, _ in halves]
+    return [moved(other, lambda z, y, x: (z, y ^ second, x)) for (_, other), (_, second) in zip(halves, EXCHANGES)]
 
 
 def reduce_along_z(grad):
@@ -148,26 +147,15 @@
     return total
 
 
-def held(values, after):
-    def kernel(*refs):
-        pass
-
-    return pl.pallas_call(
-        kernel,
-        in_specs=[pl.BlockSpec(memory_space=pl.ANY)] * (len(values) + 1),
-        out_specs=[pl.BlockSpec(memory_space=pl.ANY)] * len(values),
-        out_shape=[jax.ShapeDtypeStruct(value.shape, value.dtype) for value in values],
-        input_output_aliases={k: k for k in range(len(values))},
-        cost_estimate=pl.CostEstimate(flops=0, bytes_accessed=0, transcendentals=0),
-        name="held",
-    )(*values, after)
-
-
-def segment_start(places, lengths_ref):
+OFFSETS = 4
+LENGTHS = OFFSETS + STEPS
+
+
+def segment_start(places, info_ref):
     end = jnp.int32(0)
     start = jnp.zeros_like(places)
-    for s in range(lengths_ref.shape[1]):
-        end = end + lengths_ref[0, s]
+    for s in range(LENGTHS, info_ref.shape[0]):
+        end = end + info_ref[s]
         start = jnp.where(places >= end, end, start)
     return start
 
@@ -192,8 +180,8 @@
     return total
 
 
-def features_kernel(tn, place_ref, low_ref, mid_ref, gain_ref, *outs):
-    j = place_ref[0]
+def features_kernel(tn, info_ref, low_ref, mid_ref, gain_ref, *outs):
+    j = info_ref[0]
     width = low_ref.shape[1]
     piece = width // tn
     step = 1024
@@ -216,9 +204,9 @@
             out[:, c:c + 512] = value.astype(BF16)
 
 
-def features(place, low, mid, gain, tn):
+def features(info, low, mid, gain, tn):
     rows, width = low.shape
-    block = 16
+    block = 32
     piece = width // tn
     return pl.pallas_call(
         functools.partial(features_kernel, tn),
@@ -231,20 +219,20 @@
         ],
         out_specs=[pl.BlockSpec((block, piece), lambda b: (b, 0))] * tn,
         out_shape=[jax.ShapeDtypeStruct((rows, piece), BF16)] * tn,
-        compiler_params=pltpu.CompilerParams(vmem_limit_bytes=FEATURES_LIMIT),
+        compiler_params=pltpu.CompilerParams(vmem_limit_bytes=LARGE_LIMIT),
         cost_estimate=pl.CostEstimate(flops=10 * rows * width, bytes_accessed=6 * rows * width, transcendentals=0),
         name="features",
-    )(place, low, mid, gain)
-
-
-def attend_kernel(window, lengths_ref, query_ref, key_ref, value_ref, high_ref, square_ref):
+    )(info, low, mid, gain)
+
+
+def attend_kernel(window, info_ref, query_ref, key_ref, value_ref, high_ref, square_ref):
     block = query_ref.shape[0]
     pack = key_ref.shape[0]
     b = pl.program_id(0)
     first = pl.multiple_of(jnp.clip(b * block - (window - block), 0, pack - window), block)
     query_places = b * block + lax.broadcasted_iota(jnp.int32, (block, window), 0)
     key_places = first + lax.broadcasted_iota(jnp.int32, (block, window), 1)
-    allowed = (key_places <= query_places) & (key_places >= segment_start(query_places, lengths_ref))
+    allowed = (key_places <= query_places) & (key_places >= segment_start(query_places, info_ref))
     bias = jnp.where(allowed, 0.0, -1e30).astype(F32)
     group = (query_ref.shape[1] // HD) // (key_ref.shape[1] // HD)
     squares = jnp.zeros((block, HD), F32)
@@ -267,7 +255,7 @@
     square_ref[...] = lane_sums(squares)
 
 
-def attend(lengths, queries, keys, values):
+def attend(info, queries, keys, values):
     pack, width = queries.shape
     block = 128
     window = min(pack, 256 + block)
@@ -293,43 +281,48 @@
             flops=4 * pack * window * width, bytes_accessed=4 * pack * width,
             transcendentals=pack * window * width // HD),
         name="attend",
-    )(lengths, queries, keys, values)
-
-
-def chosen(place_ref, lengths_ref, offset, rows, lead):
-    target = place_ref[0] * rows + lax.broadcasted_iota(jnp.int32, (rows, rows + lead), 0)
-    source = place_ref[0] * rows - lead + lax.broadcasted_iota(jnp.int32, (rows, rows + lead), 1)
-    hit = (source == target - offset) & (source >= segment_start(target, lengths_ref))
+    )(info, queries, keys, values)
+
+
+def chosen(info_ref, step, rows, lead):
+    target = info_ref[0] * rows + lax.broadcasted_iota(jnp.int32, (rows, rows + lead), 0)
+    source = info_ref[0] * rows - lead + lax.broadcasted_iota(jnp.int32, (rows, rows + lead), 1)
+    hit = (source == target - info_ref[OFFSETS + step]) & (source >= segment_start(target, info_ref))
     return jnp.where(hit, 1.0, 0.0).astype(BF16)
 
 
-def fold_kernel(place_ref, lengths_ref, offsets_ref, cotangent_ref, out_ref):
+def fold_kernel(info_ref, cotangent_ref, out_ref, near_ref, sems):
     steps, rows, width = cotangent_ref.shape
+    coming = [pltpu.make_async_copy(cotangent_ref.at[s], near_ref.at[s], sems.at[s]) for s in range(steps)]
+    for copy in coming:
+        copy.start()
     total = None
     for s in range(steps):
-        pick = chosen(place_ref, lengths_ref, offsets_ref[s], rows, OFFMAX)
-        part = lax.dot_general(pick, cotangent_ref[s], (((0,), (0,)), ((), ())), preferred_element_type=F32)
+        pick = chosen(info_ref, s, rows, OFFMAX)
+        coming[s].wait()
+        part = lax.dot_general(pick, near_ref[s], (((0,), (0,)), ((), ())), preferred_element_type=F32)
         total = part if total is None else total + part
     out_ref[...] = total.astype(BF16)
 
 
-def fold(place, lengths, offsets, cotangent):
+def fold(info, cotangent):
     steps, rows, width = cotangent.shape
     return pl.pallas_call(
         fold_kernel,
-        in_specs=[SMEM, SMEM, SMEM, VMEM],
+        in_specs=[SMEM, HBM],
         out_specs=VMEM,
         out_shape=jax.ShapeDtypeStruct((rows + OFFMAX, width), BF16),
-        compiler_params=pltpu.CompilerParams(vmem_limit_bytes=VMEM_LIMIT),
+        scratch_shapes=[pltpu.VMEM(cotangent.shape, BF16), pltpu.SemaphoreType.DMA((steps,))],
+        compiler_params=pltpu.CompilerParams(vmem_limit_bytes=LARGE_LIMIT),
         cost_estimate=pl.CostEstimate(flops=2 * steps * rows * 160 * width, bytes_accessed=2 * steps * rows * width, transcendentals=0),
         name="fold",
-    )(place, lengths, offsets, cotangent)
-
-
-def merge_kernel(width, tn, place_ref, gain_ref, high_ref, *refs):
+    )(info, cotangent)
+
+
+def merge_kernel(width, tn, info_ref, gain_ref, high_ref, *refs):
     parts, square_refs, (far_ref, out_square_ref, out_ref, sems) = refs[:tn], refs[tn:-4], refs[-4:]
     copies = []
-    j = place_ref[0]
+    j = info_ref[0]
     rows = parts[0].shape[0]
     piece = high_ref.shape[1]
     squares = square_refs[0][...]
@@ -358,7 +351,7 @@
         copy.wait()
 
 
-def merge(place, gain, high, parts, squares, width):
+def merge(info, gain, high, parts, squares, width):
     pack, piece = high.shape
     tn = len(parts)
     return pl.pallas_call(
@@ -373,10 +366,10 @@
         compiler_params=pltpu.CompilerParams(vmem_limit_bytes=VMEM_LIMIT),
         cost_estimate=pl.CostEstimate(flops=8 * pack * piece, bytes_accessed=6 * pack * piece, transcendentals=0),
         name="merge",
-    )(place, gain, high, *parts, *squares)
-
-
-def grads(place, gain, merged, folds, squares, width, ny, tn):
+    )(info, gain, high, *parts, *squares)
+
+
+def grads(info, gain, merged, folds, squares, width, ny, tn):
     pack, piece = merged.shape
     rows = pack // tn
     vw = folds[0].shape[1]
@@ -386,7 +379,7 @@
     steps.sort(key=lambda step: step[2])
     size = chunk // (2 * tn) if ny > 1 else chunk
 
-    def kernel(place_ref, gain_ref, merged_ref, *refs):
+    def kernel(info_ref, gain_ref, merged_ref, *refs):
         fold_refs, square_refs, refs = refs[:tn], refs[tn:2 * tn], refs[2 * tn:]
         keep_refs, refs = refs[:2], refs[2:]
         send_refs, refs = refs[:2 if ny > 1 else 0], refs[2 if ny > 1 else 0:]
@@ -399,7 +392,7 @@
             pltpu.make_async_copy(fold_refs[s], near_folds.at[s], sems.at[tn + s]) for s in range(tn)]
         for copy in coming + folds_coming:
             copy.start()
-        j, y = place_ref[0], place_ref[1]
+        j, y = info_ref[0], info_ref[1]
         squares = square_refs[0][...]
         for s in range(1, tn):
             squares = squares + square_refs[s][...]
@@ -456,11 +449,11 @@
         compiler_params=pltpu.CompilerParams(vmem_limit_bytes=VMEM_LIMIT),
         cost_estimate=pl.CostEstimate(flops=2 * pack * piece * vw, bytes_accessed=8 * pack * piece, transcendentals=0),
         name="grads",
-    )(place, gain, merged, *folds, *squares)
+    )(info, gain, merged, *folds, *squares)
     return out[:2], out[2:-1] if ny > 1 else (None, None), out[-1]
 
 
-def project(place, hidden, weights, tn, nz, nx):
+def project(info, hidden, weights, tn, nz, nx):
     pack, piece = hidden.shape
     rows = pack // tn
     vw = weights[0][0].shape[1]
@@ -471,15 +464,20 @@
     distances = (0, 4, 2, 6) if nz > 1 else (0,)
     size = parts[0][0].shape[0] // (len(distances) * nx)
 
-    def kernel(place_ref, hidden_ref, *refs):
-        weight_refs, value_refs, weight_ref, total_ref = refs[:len(parts)], refs[len(parts):-2], refs[-2], refs[-1]
-        j, y, z, x = place_ref[0], place_ref[1], place_ref[2], place_ref[3]
-        for ref, (_, far, near) in zip(weight_refs, parts):
+    def kernel(info_ref, hidden_ref, *refs):
+        weight_refs, value_refs = refs[:len(parts)], refs[len(parts):-4]
+        weight_ref, total_ref, near_ref, sems = refs[-4:]
+        coming = [pltpu.make_async_copy(ref, near_ref.at[p], sems.at[p]) for p, ref in enumerate(weight_refs)]
+        for copy in coming:
+            copy.start()
+        j, y, z, x = info_ref[0], info_ref[1], info_ref[2], info_ref[3]
+        for p, (_, far, near) in enumerate(parts):
+            coming[p].wait()
             for k, distance in enumerate(distances):
                 for m in range(nx):
                     block = ((y ^ far) * nz + (z ^ distance ^ near)) * nx + (x ^ m)
                     at = pl.ds(pl.multiple_of(block * size, size), size)
-                    weight_ref[at, :] = ref[(k * nx + m) * size:(k * nx + m + 1) * size, :]
+                    weight_ref[at, :] = near_ref[p, (k * nx + m) * size:(k * nx + m + 1) * size, :]
         total_ref[0:OFFMAX, :] = jnp.zeros((OFFMAX, vw), F32)
         for c in range(0, pack, 256):
             total_ref[OFFMAX + c:OFFMAX + c + 256, :] = jnp.dot(
@@ -490,20 +488,25 @@
 
     return pl.pallas_call(
         kernel,
-        in_specs=[SMEM] + [VMEM] * (1 + len(parts)),
+        in_specs=[SMEM, VMEM] + [HBM] * len(parts),
         out_specs=[VMEM] * tn,
         out_shape=[jax.ShapeDtypeStruct((rows + OFFMAX, vw), F32 if s == 0 else BF16) for s in range(tn)],
-        scratch_shapes=[pltpu.VMEM((piece, vw), BF16), pltpu.VMEM((pack + OFFMAX, vw), F32)],
+        scratch_shapes=[
+            pltpu.VMEM((piece, vw), BF16),
+            pltpu.VMEM((pack + OFFMAX, vw), F32),
+            pltpu.VMEM((len(parts),) + parts[0][0].shape, BF16),
+            pltpu.SemaphoreType.DMA((len(parts),)),
+        ],
         compiler_params=pltpu.CompilerParams(vmem_limit_bytes=VMEM_LIMIT),
         cost_estimate=pl.CostEstimate(flops=2 * pack * piece * vw, bytes_accessed=4 * pack * piece, transcendentals=0),
         name="project",
-    )(place, hidden, *[part for part, _, _ in parts])
-
-
-def spread(place, lengths, offsets, parts):
+    )(info, hidden, *[part for part, _, _ in parts])
+
+
+def spread(info, parts):
     rows, vw = parts[0].shape[0] - OFFMAX, parts[0].shape[1]
 
-    def kernel(place_ref, lengths_ref, offsets_ref, *refs):
+    def kernel(info_ref, *refs):
         parts_refs, out_ref = refs[:-1], refs[-1]
         total = None
         for ref in parts_refs:
@@ -511,18 +514,18 @@
             total = part if total is None else total + part
         total = total.astype(BF16)
         for s in range(STEPS):
-            pick = chosen(place_ref, lengths_ref, offsets_ref[s], rows, OFFMAX)
+            pick = chosen(info_ref, s, rows, OFFMAX)
             out_ref[s] = jnp.dot(pick, total, preferred_element_type=F32).astype(BF16)
 
     return pl.pallas_call(
         kernel,
-        in_specs=[SMEM] * 3 + [VMEM] * len(parts),
+        in_specs=[SMEM] + [VMEM] * len(parts),
         out_specs=VMEM,
         out_shape=jax.ShapeDtypeStruct((STEPS, rows, vw), BF16),
         compiler_params=pltpu.CompilerParams(vmem_limit_bytes=VMEM_LIMIT),
         cost_estimate=pl.CostEstimate(flops=2 * STEPS * rows * 160 * vw, bytes_accessed=8 * STEPS * rows * vw, transcendentals=0),
         name="spread",
-    )(place, lengths, offsets, *parts)
+    )(info, *parts)
 
 
 def body(
@@ -545,6 +548,7 @@
     flat = i * tn + j
     nz, ny, nx = sides_of(n)
     place = jnp.stack([j, i // nx % ny, i // (ny * nx), i % nx]).astype(jnp.int32)
+    info = jnp.concatenate([place, step_offsets, doc_lengths.reshape(-1)])
     width = low_feature.shape[1]
     piece = width // tn
     pack = target_queries.shape[0]
@@ -553,42 +557,43 @@
     def swapped(values, s):
         return lax.ppermute(values, "tensor", [(a, a ^ s) for a in range(tn)])
 
-    folded = fold(place, doc_lengths, step_offsets, cotangent)
+    folded = fold(info, cotangent)
     across = swapped(folded, 2)
     low_feature, folded = lax.optimization_barrier((low_feature, folded))
-    sent = features(place, low_feature, mid_feature, merging_gain, tn)
+    sent = features(info, low_feature, mid_feature, merging_gain, tn)
     across, sent = lax.optimization_barrier((across, sent))
     parts = [sent[0]] + [swapped(sent[s], s) for s in range(1, tn)]
 
-    high, squares = attend(doc_lengths, target_queries, target_keys, target_values)
+    high, squares = attend(info, target_queries, target_keys, target_values)
     own_weight, high, folded, across = lax.optimization_barrier((draft_weight, high, folded, across))
     squares = squares + swapped(squares, 1)
     folds = [folded, swapped(folded, 1), across, swapped(across, 1)]
     squares, folds, parts[1] = lax.optimization_barrier((squares, folds, parts[1]))
     squares = [squares, swapped(squares, 2)]
     weights = weight_to_place(own_weight)
-    merged, squares = merge(place, merging_gain, high, parts, squares, width)
+    merged, squares = merge(info, merging_gain, high, parts, squares, width)
     weights, merged, squares = lax.optimization_barrier((weights, merged, squares))
     weights = weight_across(jnp.concatenate(weights), nz // 2)
     squares = [squares] + [swapped(squares, s) for s in range(1, tn)]
-    kept, cut, hidden = grads(place, draft_gain.reshape(1, width), merged, folds, squares, width, ny, tn)
+    kept, cut, hidden = grads(info, draft_gain.reshape(1, width), merged, folds, squares, width, ny, tn)
     weights, hidden = lax.optimization_barrier((weights, hidden))
     weights = weight_halves(weight_across(weights, nz // 4))
     halves = reduce_once(kept, cut)
     weights, own = lax.optimization_barrier((weights, [half[0] for half in halves]))
-    halves = [(mine, other) for mine, (_, other) in zip(own, halves)]
+    got = reduce_twice(halves)
     weights = weight_once(weights)
-    grad = reduce_twice(halves)
+    grad = [mine + part.astype(F32) for mine, part in zip(own, got)]
     if ny > 1:
-        flat_weights = held([part for half in weights for part in half], grad)
-        weights = [list(flat_weights[:2]), list(flat_weights[2:])]
+        grad = [half.astype(BF16) for half in grad]
+    weights, grad = lax.optimization_barrier((weights, grad))
+    grad = jnp.concatenate(grad)
     weights = weight_twice(weights)
     grad = reduce_along_z(grad)
     hidden, grad = lax.optimization_barrier((hidden, grad))
     weight_grad = reduce_to_owner(grad)
-    values = project(place, hidden, weights, tn, nz, nx)
+    values = project(info, hidden, weights, tn, nz, nx)
     values = [values[0]] + [swapped(values[s], s) for s in range(1, tn)]
-    draft_values = spread(place, doc_lengths, step_offsets, values)
+    draft_values = spread(info, values)
 
     rows = weight_grad.shape[0]
     gain = lax.dynamic_slice(draft_gain, (flat * rows,), (rows,))

time: 139 us -> 140 us (level)
  waiting for transfers between devices: 47.4 us -> 56 us
  local copies, waits for them, and re-layouts: 7.65 us -> 1.37 us
  other arithmetic: 6.26 us -> 3.8 us
    unnamed x49 -> x19, local copies, waits for them, and re-layouts: 7.62 us -> 0.06 us
    all_to_all x1, waiting for transfers between devices: 3.17 us -> 10.6 us  [reduce_along_z(): lax.all_to_all(grad.astype(BF16), 'dp', 0, 0, tiled=True, axis_index_grou...]
    pallas_call x4 -> x3, Pallas kernels: 4.57 us -> 7.54 us  [the longest x1 3.16 us: project(): pl.pallas_call(kernel, in_specs=[SMEM, VMEM] + [HBM] * len(parts), out_sp...]
    pallas_call x1, Pallas kernels: 6.74 us -> 4.78 us  [features(): pl.pallas_call(functools.partial(features_kernel, tn), grid=(rows // bloc...]
    concatenate x1, other arithmetic: 2.29 us -> 0.86 us  [body(): grad = jnp.concatenate(grad)]
  transfers between devices with their start and end apart: 32 -> 32, of which waited for: 15 -> 15; matrix products, arithmetic and copies ran while one was open for 4% -> 2% of each run, Pallas kernels for 15% -> 14%
where the time goes in v7:
time: 140 us
  waiting for transfers between devices  56 us (40%)
  starting transfers between devices  48.8 us (35%)
  Pallas kernels  29.1 us (21%)
  other arithmetic  3.8 us (3%)
    ppermute x13, waiting for transfers between devices, moved(): return lax.ppermute(values, 'dp', pairs)  24.4 us
    ppermute x14, waiting for transfers between devices, swapped(): return lax.ppermute(values, 'tensor', [(a, a ^ s) for a in range(tn)])  20.9 us
    ppermute x14, starting transfers between devices, swapped(): return lax.ppermute(values, 'tensor', [(a, a ^ s) for a in range(tn)])  15.2 us
    ppermute x13, starting transfers between devices, moved(): return lax.ppermute(values, 'dp', pairs)  14.5 us
    all_to_all x1, waiting for transfers between devices, reduce_along_z(): lax.all_to_all(grad.astype(BF16), 'dp', 0, 0, tiled=True, axis_index_grou...  10.6 us
    ppermute x2, starting transfers between devices, reduce_to_owner(): part = lax.ppermute(part, ('dp', 'tensor'), pairs)  10.3 us
    pallas_call x1, Pallas kernels, attend(): pl.pallas_call(functools.partial(attend_kernel, window), grid=(pack // bl...  8.4 us
    all_to_all x1, starting transfers between devices, reduce_along_z(): lax.all_to_all(grad.astype(BF16), 'dp', 0, 0, tiled=True, axis_index_grou...  4.88 us
  transfers between devices with their start and end apart: 32, of which 15 were waited for; matrix products, arithmetic and copies ran while one was open for 2% of the time, Pallas kernels for 14%

profile of v7, /device:TPU:1, one launch (start us, length us, event | category | flops | bytes accessed | tf_op | source)
XLA Modules:
  0.0 140.0 jit_solution(13158178287418369521)
XLA Ops:
  0.7 1.3 concatenate.16.info_ref
  1.9 2.7 %fold.1.refs_0_ = bf16[160,512]{1,0:T(8,128)(2,1)} custom-call(s32[15]{0:T(128)} %concatenate.16.info_ref, bf16[3,128,512]{2,1,0:T(8,128)(2,1)} %cotangent_ref.1), custom_call_target="tpu_custom_call" | custom-call | flops 62914560 | bytes 393216 | tf_op jit(solution)/shard_map/fold/pallas_call | solution.py:310
  4.7 2.1 %collective-permute-start = (bf16[160,512]{1,0:T(8,128)(2,1)}, bf16[160,512]{1,0:T(8,128)(2,1)S(1)}, u32[]{:S(2)}, u32[]{:S(2)}) collective-permute-start(bf16[160,512]{1,0:T(8,128)(2,1)} %fold.1.refs_0_), channel_id=1, source_target_pairs={{0,2},{1,3},{2,0},{3,1},{4,6},{5,7},{6,4},{7,5},{8,10},{9,11},{10,... | collective-permute-start | bytes 491528 | tf_op jit(solution)/shard_map/ppermute | solution.py:558
  6.8 4.8 %features.1 = (bf16[128,2048]{1,0:T(8,128)(2,1)}, bf16[128,2048]{1,0:T(8,128)(2,1)}, bf16[128,2048]{1,0:T(8,128)(2,1)}, bf16[128,2048]{1,0:T(8,128)(2,1)}) custom-call(s32[15]{0:T(128)} %concatenate.16.info_ref, bf16[128,8192]{1,0:T(8,128)(2,1)} %low_ref, bf16[128,8192]{1,0:T(8,128)(2,1)} %mid_ref.1, f32[3,8192]{1,0:T(4,128)} %gain_ref.3), custom_call_target="tpu_custom_call" | custom-call | flops 10485760 | bytes 6291456 | tf_op jit(solution)/shard_map/features/pallas_call | solution.py:211
  11.7 2.0 %collective-permute-start.6 = (bf16[128,2048]{1,0:T(8,128)(2,1)}, bf16[128,2048]{1,0:T(8,128)(2,1)S(1)}, u32[]{:S(2)}, u32[]{:S(2)}) collective-permute-start(bf16[128,2048]{1,0:T(8,128)(2,1)} %get-tuple-element.71), channel_id=1, source_target_pairs={{0,1},{1,0},{2,3},{3,2},{4,5},{5,4},{6,7},{7,6},{8,9},{9,8},{10,11... | collective-permute-start | bytes 1572872 | tf_op jit(solution)/shard_map/ppermute | solution.py:558
  13.7 1.1 collective-permute-start.7
  14.7 0.7 collective-permute-start.8
  15.4 8.4 %attend.1 = (bf16[512,2048]{1,0:T(8,128)(2,1)S(1)}, f32[8,512]{1,0:T(8,128)S(1)}) custom-call(s32[15]{0:T(128)S(1)} %copy-done.3, bf16[512,2048]{1,0:T(8,128)(2,1)S(1)} %copy-done.5, bf16[512,256]{1,0:T(8,128)(2,1)S(1)} %copy-done.6, bf16[512,256]{1,0:T(8,128)(2,1)S(1)} %copy-done.7), custom_call_target="tpu_custom_call" | custom-call | flops 1610612736 | bytes 4194304 | tf_op jit(solution)/shard_map/attend/pallas_call | solution.py:262
  24.0 0.4 collective-permute-start.4
  24.4 0.7 collective-permute-done.3
  25.4 3.8 %collective-permute-start.1 = (bf16[32,512]{1,0:T(8,128)(2,1)S(1)}, bf16[32,512]{1,0:T(8,128)(2,1)S(1)}, u32[]{:S(2)}, u32[]{:S(2)}) collective-permute-start(bf16[32,512]{1,0:T(8,128)(2,1)S(1)} %copy-done.8), channel_id=1, source_target_pairs={{0,0},{1,4},{2,32},{3,36},{4,64},{5,68},{6,96},{7,100},{8,128},{9,... | collective-permute-start | bytes 98312 | tf_op jit(solution)/shard_map/ppermute | solution.py:70
  29.3 3.0 %collective-permute-start.9 = (f32[8,512]{1,0:T(8,128)S(1)}, f32[8,512]{1,0:T(8,128)S(1)}, u32[]{:S(2)}, u32[]{:S(2)}) collective-permute-start(f32[8,512]{1,0:T(8,128)S(1)} %add.65.refs_4_), channel_id=1, source_target_pairs={{0,2},{1,3},{2,0},{3,1},{4,6},{5,7},{6,4},{7,5},{8,10},{9,11},{10,... | collective-permute-start | bytes 49160 | tf_op jit(solution)/shard_map/ppermute | solution.py:558
  32.4 10.1 %collective-permute-done.8.refs_3_ = bf16[128,2048]{1,0:T(8,128)(2,1)S(1)} collective-permute-done((bf16[128,2048]{1,0:T(8,128)(2,1)}, bf16[128,2048]{1,0:T(8,128)(2,1)S(1)}, u32[]{:S(2)}, u32[]{:S(2)}) %collective-permute-start.8) | collective-permute-done | bytes 524320 | tf_op jit(solution)/shard_map/ppermute | solution.py:558
  42.5 0.9 collective-permute-done.9.refs_5_
  43.4 3.5 %merge.1 = (bf16[512,2048]{1,0:T(8,128)(2,1)S(1)}, f32[8,512]{1,0:T(8,128)S(1)}) custom-call(s32[15]{0:T(128)S(1)} %copy-done.3, f32[3,8192]{1,0:T(4,128)S(1)} %copy-done.1, bf16[512,2048]{1,0:T(8,128)(2,1)S(1)} %get-tuple-element.66.high_ref, bf16[128,2048]{1,0:T(8,128)(2,1)S(1)} %copy-done, bf16[128,2048]{1,0:T(8,128)(2,1)S(1)} %collective-permute-done.6.refs_1_, ...), custom_call_target="tpu_custom_call" | custom-call | flops 8388608 | bytes 6291456 | tf_op jit(solution)/shard_map/merge/pallas_call | solution.py:357
  46.9 1.0 collective-permute-start.11
  47.9 2.2 %collective-permute-start.12 = (f32[8,512]{1,0:T(8,128)S(1)}, f32[8,512]{1,0:T(8,128)S(1)}, u32[]{:S(2)}, u32[]{:S(2)}) collective-permute-start(f32[8,512]{1,0:T(8,128)S(1)} %get-tuple-element.85.refs_4_), channel_id=1, source_target_pairs={{0,2},{1,3},{2,0},{3,1},{4,6},{5,7},{6,4},{7,5},{8,10},{9,11},{10,... | collective-permute-start | bytes 49160 | tf_op jit(solution)/shard_map/ppermute | solution.py:558
  50.1 0.2 collective-permute-start.13
  50.4 0.9 collective-permute-done.12.refs_6_
  51.2 2.1 %collective-permute-done.13.refs_7_ = f32[8,512]{1,0:T(8,128)S(1)} collective-permute-done((f32[8,512]{1,0:T(8,128)S(1)}, f32[8,512]{1,0:T(8,128)S(1)}, u32[]{:S(2)}, u32[]{:S(2)}) %collective-permute-start.13) | collective-permute-done | bytes 16416 | tf_op jit(solution)/shard_map/ppermute | solution.py:558
  53.3 4.9 %grads.1 = (f32[2,256,512]{2,1,0:T(8,128)S(1)}, f32[2,256,512]{2,1,0:T(8,128)S(1)}, bf16[2,256,512]{2,1,0:T(8,128)(2,1)S(1)}, bf16[2,256,512]{2,1,0:T(8,128)(2,1)S(1)}, bf16[512,2048]{1,0:T(8,128)(2,1)S(1)}) custom-call(s32[15]{0:T(128)S(1)} %copy-done.3, f32[1,8192]{1,0:T(1,128)S(1)} %bitcast.15, bf16[512,2048]{1,0:T(8,128)(2,1)S(1)} %get-tuple-element.80.merged_ref, ...), custom_call_target="tpu_custom_call" | custom-call | flops 1073741824 | bytes 8388608 | tf_op jit(solution)/shard_map/grads/pallas_call | solution.py:437
  58.3 2.2 %collective-permute-start.17 = (bf16[2,256,512]{2,1,0:T(8,128)(2,1)S(1)}, bf16[2,256,512]{2,1,0:T(8,128)(2,1)S(1)}, u32[]{:S(2)}, u32[]{:S(2)}) collective-permute-start(bf16[2,256,512]{2,1,0:T(8,128)(2,1)S(1)} %get-tuple-element.91), channel_id=1, source_target_pairs={{0,24},{4,28},{8,16},{12,20},{16,8},{20,12},{24,0},{28,4},{32,56},... | collective-permute-start | bytes 1572872 | tf_op jit(solution)/shard_map/ppermute | solution.py:57
  60.5 6.6 %collective-permute-start.10 = (bf16[64,512]{1,0:T(8,128)(2,1)S(1)}, bf16[64,512]{1,0:T(8,128)(2,1)S(1)}, u32[]{:S(2)}, u32[]{:S(2)}) collective-permute-start(bf16[64,512]{1,0:T(8,128)(2,1)S(1)} %pad_maximum_fusion.2), channel_id=1, source_target_pairs={{0,128},{4,132},{8,136},{12,140},{16,144},{20,148},{24,152},{28,15... | collective-permute-start | bytes 196616 | tf_op jit(solution)/shard_map/ppermute | solution.py:57
  67.1 3.0 %collective-permute-done.10 = bf16[64,512]{1,0:T(8,128)(2,1)S(1)} collective-permute-done((bf16[64,512]{1,0:T(8,128)(2,1)S(1)}, bf16[64,512]{1,0:T(8,128)(2,1)S(1)}, u32[]{:S(2)}, u32[]{:S(2)}) %collective-permute-start.10) | collective-permute-done | bytes 65568 | tf_op jit(solution)/shard_map/ppermute | solution.py:57
  70.1 8.7 %collective-permute-done.14 = bf16[128,512]{1,0:T(8,128)(2,1)S(1)} collective-permute-done((bf16[128,512]{1,0:T(8,128)(2,1)S(1)}, bf16[128,512]{1,0:T(8,128)(2,1)S(1)}, u32[]{:S(2)}, u32[]{:S(2)}) %collective-permute-start.14) | collective-permute-done | bytes 131104 | tf_op jit(solution)/shard_map/ppermute | solution.py:57
  79.1 0.2 collective-permute-start.21
  79.5 0.6 collective-permute-start.20
  80.1 6.2 %collective-permute-done.15.refs_4_ = bf16[256,512]{1,0:T(8,128)(2,1)S(1)} collective-permute-done((bf16[256,512]{1,0:T(8,128)(2,1)S(1)}, bf16[256,512]{1,0:T(8,128)(2,1)S(1)}, u32[]{:S(2)}, u32[]{:S(2)}) %collective-permute-start.15) | collective-permute-done | bytes 262176 | tf_op jit(solution)/shard_map/ppermute | solution.py:57
  86.3 0.5 collective-permute-start.19
  86.9 0.8 collective-permute-done.20
  87.8 5.0 %collective-permute-done.18.refs_1_ = bf16[256,512]{1,0:T(8,128)(2,1)S(1)} collective-permute-done((bf16[256,512]{1,0:T(8,128)(2,1)S(1)}, bf16[256,512]{1,0:T(8,128)(2,1)S(1)}, u32[]{:S(2)}, u32[]{:S(2)}) %collective-permute-start.18) | collective-permute-done | bytes 262176 | tf_op jit(solution)/shard_map/ppermute | solution.py:57
  92.8 0.8 collective-permute-done.19.refs_5_
  93.6 0.9 pad_maximum_fusion
  94.4 4.9 %all-to-all-start = ((bf16[8,64,512]{2,1,0:T(8,128)(2,1)}), bf16[8,64,512]{2,1,0:T(8,128)(2,1)}, u32[]{:S(2)}, u32[]{:S(2)}) async-start(bf16[8,64,512]{2,1,0:T(8,128)(2,1)} %bitcast.16), calls=%async_computation | async-start | bytes 1048576 | tf_op jit(solution)/shard_map/all_to_all | solution.py:125
  99.4 2.5 %collective-permute-start.23 = (bf16[256,512]{1,0:T(8,128)(2,1)S(1)}, bf16[256,512]{1,0:T(8,128)(2,1)}, u32[]{:S(2)}, u32[]{:S(2)}) collective-permute-start(bf16[256,512]{1,0:T(8,128)(2,1)S(1)} %collective-permute-done.18.refs_1_), channel_id=1, source_target_pairs={{0,24},{4,28},{8,16},{12,20},{16,8},{20,12},{24,0},{28,4},{32,56},... | collective-permute-start | bytes 786440 | tf_op jit(solution)/shard_map/ppermute | solution.py:57
  102.0 1.5 %collective-permute-start.25 = (bf16[256,512]{1,0:T(8,128)(2,1)S(1)}, bf16[256,512]{1,0:T(8,128)(2,1)}, u32[]{:S(2)}, u32[]{:S(2)}) collective-permute-start(bf16[256,512]{1,0:T(8,128)(2,1)S(1)} %collective-permute-done.19.refs_5_), channel_id=1, source_target_pairs={{0,8},{4,12},{8,0},{12,4},{16,24},{20,28},{24,16},{28,20},{32,40},... | collective-permute-start | bytes 786440 | tf_op jit(solution)/shard_map/ppermute | solution.py:57
  103.4 10.6 %all-to-all-done = bf16[8,64,512]{2,1,0:T(8,128)(2,1)} async-done(((bf16[8,64,512]{2,1,0:T(8,128)(2,1)}), bf16[8,64,512]{2,1,0:T(8,128)(2,1)}, u32[]{:S(2)}, u32[]{:S(2)}) %all-to-all-start) | async-done | bytes 524320 | tf_op jit(solution)/shard_map/all_to_all | solution.py:125
  114.1 1.1 convert_reduce_fusion
  115.2 5.2 %collective-permute-start.29 = (f32[32,512]{1,0:T(8,128)S(1)}, f32[32,512]{1,0:T(8,128)S(1)}, u32[]{:S(2)}, u32[]{:S(2)}) collective-permute-start(f32[32,512]{1,0:T(8,128)S(1)} %get-tuple-element.118), channel_id=1, source_target_pairs={{0,0},{1,64},{2,128},{3,192},{4,4},{5,68},{6,132},{7,196},{8,8},{9... | collective-permute-start | bytes 196616 | tf_op jit(solution)/shard_map/ppermute | solution.py:145
  120.5 5.1 %collective-permute-start.30 = (f32[32,512]{1,0:T(8,128)S(1)}, f32[32,512]{1,0:T(8,128)S(1)}, u32[]{:S(2)}, u32[]{:S(2)}) collective-permute-start(f32[32,512]{1,0:T(8,128)S(1)} %get-tuple-element.117), channel_id=1, source_target_pairs={{0,4},{1,68},{2,132},{3,196},{4,0},{5,64},{6,128},{7,192},{8,12},{... | collective-permute-start | bytes 196616 | tf_op jit(solution)/shard_map/ppermute | solution.py:145
  125.5 3.2 %project.1 = (f32[160,512]{1,0:T(8,128)S(1)}, bf16[160,512]{1,0:T(8,128)(2,1)S(1)}, bf16[160,512]{1,0:T(8,128)(2,1)S(1)}, bf16[160,512]{1,0:T(8,128)(2,1)S(1)}) custom-call(s32[15]{0:T(128)S(1)} %copy-done.3, bf16[512,2048]{1,0:T(8,128)(2,1)S(1)} %get-tuple-element.101.hidden_ref, bf16[256,512]{1,0:T(8,128)(2,1)S(1)} %constant_dynamic-update-slice_fusion.refs_0_, ...), custom_call_target="tpu_custom_call" | custom-call | flops 1073741824 | bytes 4194304 | tf_op jit(solution)/shard_map/project/pallas_call | solution.py:489
  128.8 1.2 collective-permute-start.27
  130.0 1.0 collective-permute-start.28
  130.9 0.7 multiply_reduce_fusion
  131.7 0.6 dynamic-slice_divide_fusion
  132.3 2.0 %collective-permute-done.27.refs_2_ = bf16[160,512]{1,0:T(8,128)(2,1)S(1)} collective-permute-done((bf16[160,512]{1,0:T(8,128)(2,1)S(1)}, bf16[160,512]{1,0:T(8,128)(2,1)S(1)}, u32[]{:S(2)}, u32[]{:S(2)}) %collective-permute-start.27) | collective-permute-done | bytes 163872 | tf_op jit(solution)/shard_map/ppermute | solution.py:558
  134.3 4.1 %collective-permute-done.28.refs_3_ = bf16[160,512]{1,0:T(8,128)(2,1)S(1)} collective-permute-done((bf16[160,512]{1,0:T(8,128)(2,1)S(1)}, bf16[160,512]{1,0:T(8,128)(2,1)S(1)}, u32[]{:S(2)}, u32[]{:S(2)}) %collective-permute-start.28) | collective-permute-done | bytes 163872 | tf_op jit(solution)/shard_map/ppermute | solution.py:558
  138.3 1.7 %spread.1 = bf16[3,128,512]{2,1,0:T(8,128)(2,1)} custom-call(s32[15]{0:T(128)S(1)} %copy-done.3, f32[160,512]{1,0:T(8,128)S(1)} %get-tuple-element.106.refs_0_, bf16[160,512]{1,0:T(8,128)(2,1)S(1)} %collective-permute-done.26.refs_1_, bf16[160,512]{1,0:T(8,128)(2,1)S(1)} %collective-permute-done.27.refs_2_, bf16[160,512]{1,0:T(8,128)(2,1)S(1)} %collective-permute-done.28.refs_3_), custom_call_target="tpu_custom_call" | custom-call | flops 62914560 | bytes 1572864 | tf_op jit(solution)/shard_map/spread/pallas_call | solution.py:520
  (56 shorter events, 1.8 us)
Async XLA Ops:
  4.7 10.7 %copy-start.3 = (s32[15]{0:T(128)S(1)}, s32[15]{0:T(128)}, u32[]{:S(2)}) copy-start(s32[15]{0:T(128)} %concatenate.16.info_ref) | copy-start | bytes 184
  4.7 10.7 %copy-start.5 = (bf16[512,2048]{1,0:T(8,128)(2,1)S(1)}, bf16[512,2048]{1,0:T(8,128)(2,1)}, u32[]{:S(2)}) copy-start(bf16[512,2048]{1,0:T(8,128)(2,1)} %query_ref.1) | copy-start | bytes 6291460
  4.7 10.7 %copy-start.6 = (bf16[512,256]{1,0:T(8,128)(2,1)S(1)}, bf16[512,256]{1,0:T(8,128)(2,1)}, u32[]{:S(2)}) copy-start(bf16[512,256]{1,0:T(8,128)(2,1)} %key_ref.1) | copy-start | bytes 786436
  4.7 10.7 %copy-start.7 = (bf16[512,256]{1,0:T(8,128)(2,1)S(1)}, bf16[512,256]{1,0:T(8,128)(2,1)}, u32[]{:S(2)}) copy-start(bf16[512,256]{1,0:T(8,128)(2,1)} %value_ref.1) | copy-start | bytes 786436
  4.7 6.9 %collective-permute-start = (bf16[160,512]{1,0:T(8,128)(2,1)}, bf16[160,512]{1,0:T(8,128)(2,1)S(1)}, u32[]{:S(2)}, u32[]{:S(2)}) collective-permute-start(bf16[160,512]{1,0:T(8,128)(2,1)} %fold.1.refs_0_), channel_id=1, source_target_pairs={{0,2},{1,3},{2,0},{3,1},{4,6},{5,7},{6,4},{7,5},{8,10},{9,11},{10,... | collective-permute-start | bytes 491528 | tf_op jit(solution)/shard_map/ppermute | solution.py:558
  11.6 12.4 %copy-start.2 = (bf16[160,512]{1,0:T(8,128)(2,1)S(1)}, bf16[160,512]{1,0:T(8,128)(2,1)}, u32[]{:S(2)}) copy-start(bf16[160,512]{1,0:T(8,128)(2,1)} %fold.1.refs_0_) | copy-start | bytes 491524
  11.6 13.8 %copy-start.8 = (bf16[32,512]{1,0:T(8,128)(2,1)S(1)}, bf16[32,512]{1,0:T(8,128)(2,1)}, u32[]{:S(2)}) copy-start(bf16[32,512]{1,0:T(8,128)(2,1)} %param.18) | copy-start | bytes 98308
  11.7 31.8 %copy-start = (bf16[128,2048]{1,0:T(8,128)(2,1)S(1)}, bf16[128,2048]{1,0:T(8,128)(2,1)}, u32[]{:S(2)}) copy-start(bf16[128,2048]{1,0:T(8,128)(2,1)} %get-tuple-element.67.refs_0_) | copy-start | bytes 1572868
  11.7 31.8 %copy-start.1 = (f32[3,8192]{1,0:T(4,128)S(1)}, f32[3,8192]{1,0:T(4,128)}, u32[]{:S(2)}) copy-start(f32[3,8192]{1,0:T(4,128)} %gain_ref.3) | copy-start | bytes 294916
  11.7 17.7 %collective-permute-start.6 = (bf16[128,2048]{1,0:T(8,128)(2,1)}, bf16[128,2048]{1,0:T(8,128)(2,1)S(1)}, u32[]{:S(2)}, u32[]{:S(2)}) collective-permute-start(bf16[128,2048]{1,0:T(8,128)(2,1)} %get-tuple-element.71), channel_id=1, source_target_pairs={{0,1},{1,0},{2,3},{3,2},{4,5},{5,4},{6,7},{7,6},{8,9},{9,8},{10,11... | collective-permute-start | bytes 1572872 | tf_op jit(solution)/shard_map/ppermute | solution.py:558
  13.7 18.7 %collective-permute-start.7 = (bf16[128,2048]{1,0:T(8,128)(2,1)}, bf16[128,2048]{1,0:T(8,128)(2,1)S(1)}, u32[]{:S(2)}, u32[]{:S(2)}) collective-permute-start(bf16[128,2048]{1,0:T(8,128)(2,1)} %get-tuple-element.73), channel_id=1, source_target_pairs={{0,2},{1,3},{2,0},{3,1},{4,6},{5,7},{6,4},{7,5},{8,10},{9,11},{10,... | collective-permute-start | bytes 1572872 | tf_op jit(solution)/shard_map/ppermute | solution.py:558
  14.7 27.7 %collective-permute-start.8 = (bf16[128,2048]{1,0:T(8,128)(2,1)}, bf16[128,2048]{1,0:T(8,128)(2,1)S(1)}, u32[]{:S(2)}, u32[]{:S(2)}) collective-permute-start(bf16[128,2048]{1,0:T(8,128)(2,1)} %get-tuple-element.74), channel_id=1, source_target_pairs={{0,3},{1,2},{2,1},{3,0},{4,7},{5,6},{6,5},{7,4},{8,11},{9,10},{10,... | collective-permute-start | bytes 1572872 | tf_op jit(solution)/shard_map/ppermute | solution.py:558
  23.8 1.2 collective-permute-start.3
  24.0 1.4 collective-permute-start.4
  25.0 4.2 %collective-permute-start.5 = (bf16[160,512]{1,0:T(8,128)(2,1)S(1)}, bf16[160,512]{1,0:T(8,128)(2,1)S(1)}, u32[]{:S(2)}, u32[]{:S(2)}) collective-permute-start(bf16[160,512]{1,0:T(8,128)(2,1)S(1)} %collective-permute-done.refs_2_), channel_id=1, source_target_pairs={{0,1},{1,0},{2,3},{3,2},{4,5},{5,4},{6,7},{7,6},{8,9},{9,8},{10,11... | collective-permute-start | bytes 491528 | tf_op jit(solution)/shard_map/ppermute | solution.py:558
  25.4 21.5 %collective-permute-start.1 = (bf16[32,512]{1,0:T(8,128)(2,1)S(1)}, bf16[32,512]{1,0:T(8,128)(2,1)S(1)}, u32[]{:S(2)}, u32[]{:S(2)}) collective-permute-start(bf16[32,512]{1,0:T(8,128)(2,1)S(1)} %copy-done.8), channel_id=1, source_target_pairs={{0,0},{1,4},{2,32},{3,36},{4,64},{5,68},{6,96},{7,100},{8,128},{9,... | collective-permute-start | bytes 98312 | tf_op jit(solution)/shard_map/ppermute | solution.py:70
  29.2 17.7 %collective-permute-start.2 = (bf16[32,512]{1,0:T(8,128)(2,1)S(1)}, bf16[32,512]{1,0:T(8,128)(2,1)S(1)}, u32[]{:S(2)}, u32[]{:S(2)}) collective-permute-start(bf16[32,512]{1,0:T(8,128)(2,1)S(1)} %copy-done.8), channel_id=1, source_target_pairs={{0,4},{1,0},{2,36},{3,32},{4,68},{5,64},{6,100},{7,96},{8,132},{9,... | collective-permute-start | bytes 98312 | tf_op jit(solution)/shard_map/ppermute | solution.py:70
  29.3 24.0 %copy-start.4 = (f32[8192]{0:T(1024)S(1)}, f32[8192]{0:T(1024)}, u32[]{:S(2)}) copy-start(f32[8192]{0:T(1024)} %param.17) | copy-start | bytes 98308
  29.3 14.1 %collective-permute-start.9 = (f32[8,512]{1,0:T(8,128)S(1)}, f32[8,512]{1,0:T(8,128)S(1)}, u32[]{:S(2)}, u32[]{:S(2)}) collective-permute-start(f32[8,512]{1,0:T(8,128)S(1)} %add.65.refs_4_), channel_id=1, source_target_pairs={{0,2},{1,3},{2,0},{3,1},{4,6},{5,7},{6,4},{7,5},{8,10},{9,11},{10,... | collective-permute-start | bytes 49160 | tf_op jit(solution)/shard_map/ppermute | solution.py:558
  46.9 3.4 %collective-permute-start.11 = (f32[8,512]{1,0:T(8,128)S(1)}, f32[8,512]{1,0:T(8,128)S(1)}, u32[]{:S(2)}, u32[]{:S(2)}) collective-permute-start(f32[8,512]{1,0:T(8,128)S(1)} %get-tuple-element.85.refs_4_), channel_id=1, source_target_pairs={{0,1},{1,0},{2,3},{3,2},{4,5},{5,4},{6,7},{7,6},{8,9},{9,8},{10,11... | collective-permute-start | bytes 49160 | tf_op jit(solution)/shard_map/ppermute | solution.py:558
  47.9 3.3 %collective-permute-start.12 = (f32[8,512]{1,0:T(8,128)S(1)}, f32[8,512]{1,0:T(8,128)S(1)}, u32[]{:S(2)}, u32[]{:S(2)}) collective-permute-start(f32[8,512]{1,0:T(8,128)S(1)} %get-tuple-element.85.refs_4_), channel_id=1, source_target_pairs={{0,2},{1,3},{2,0},{3,1},{4,6},{5,7},{6,4},{7,5},{8,10},{9,11},{10,... | collective-permute-start | bytes 49160 | tf_op jit(solution)/shard_map/ppermute | solution.py:558
  50.1 3.2 %collective-permute-start.13 = (f32[8,512]{1,0:T(8,128)S(1)}, f32[8,512]{1,0:T(8,128)S(1)}, u32[]{:S(2)}, u32[]{:S(2)}) collective-permute-start(f32[8,512]{1,0:T(8,128)S(1)} %get-tuple-element.85.refs_4_), channel_id=1, source_target_pairs={{0,3},{1,2},{2,1},{3,0},{4,7},{5,6},{6,5},{7,4},{8,11},{9,10},{10,... | collective-permute-start | bytes 49160 | tf_op jit(solution)/shard_map/ppermute | solution.py:558
  58.2 20.8 %collective-permute-start.16 = (bf16[2,256,512]{2,1,0:T(8,128)(2,1)S(1)}, bf16[2,256,512]{2,1,0:T(8,128)(2,1)S(1)}, u32[]{:S(2)}, u32[]{:S(2)}) collective-permute-start(bf16[2,256,512]{2,1,0:T(8,128)(2,1)S(1)} %get-tuple-element.90), channel_id=1, source_target_pairs={{0,8},{4,12},{8,0},{12,4},{16,24},{20,28},{24,16},{28,20},{32,40},... | collective-permute-start | bytes 1572872 | tf_op jit(solution)/shard_map/ppermute | solution.py:57
  58.3 20.7 %collective-permute-start.17 = (bf16[2,256,512]{2,1,0:T(8,128)(2,1)S(1)}, bf16[2,256,512]{2,1,0:T(8,128)(2,1)S(1)}, u32[]{:S(2)}, u32[]{:S(2)}) collective-permute-start(bf16[2,256,512]{2,1,0:T(8,128)(2,1)S(1)} %get-tuple-element.91), channel_id=1, source_target_pairs={{0,24},{4,28},{8,16},{12,20},{16,8},{20,12},{24,0},{28,4},{32,56},... | collective-permute-start | bytes 1572872 | tf_op jit(solution)/shard_map/ppermute | solution.py:57
  60.5 9.5 %collective-permute-start.10 = (bf16[64,512]{1,0:T(8,128)(2,1)S(1)}, bf16[64,512]{1,0:T(8,128)(2,1)S(1)}, u32[]{:S(2)}, u32[]{:S(2)}) collective-permute-start(bf16[64,512]{1,0:T(8,128)(2,1)S(1)} %pad_maximum_fusion.2), channel_id=1, source_target_pairs={{0,128},{4,132},{8,136},{12,140},{16,144},{20,148},{24,152},{28,15... | collective-permute-start | bytes 196616 | tf_op jit(solution)/shard_map/ppermute | solution.py:57
  70.0 8.8 %collective-permute-start.14 = (bf16[128,512]{1,0:T(8,128)(2,1)S(1)}, bf16[128,512]{1,0:T(8,128)(2,1)S(1)}, u32[]{:S(2)}, u32[]{:S(2)}) collective-permute-start(bf16[128,512]{1,0:T(8,128)(2,1)S(1)} %pad_maximum_fusion.1), channel_id=1, source_target_pairs={{0,64},{4,68},{8,72},{12,76},{16,80},{20,84},{24,88},{28,92},{32,9... | collective-permute-start | bytes 393224 | tf_op jit(solution)/shard_map/ppermute | solution.py:57
  78.8 7.5 %collective-permute-start.15 = (bf16[256,512]{1,0:T(8,128)(2,1)S(1)}, bf16[256,512]{1,0:T(8,128)(2,1)S(1)}, u32[]{:S(2)}, u32[]{:S(2)}) collective-permute-start(bf16[256,512]{1,0:T(8,128)(2,1)S(1)} %constant_dynamic-update-slice_fusion.refs_0_), channel_id=1, source_target_pairs={{0,32},{4,36},{8,40},{12,44},{16,48},{20,52},{24,56},{28,60},{32,0... | collective-permute-start | bytes 786440 | tf_op jit(solution)/shard_map/ppermute | solution.py:57
  79.1 7.7 %collective-permute-start.21 = (bf16[256,512]{1,0:T(8,128)(2,1)S(1)}, bf16[256,512]{1,0:T(8,128)(2,1)S(1)}, u32[]{:S(2)}, u32[]{:S(2)}) collective-permute-start(bf16[256,512]{1,0:T(8,128)(2,1)S(1)} %get-tuple-element.113), channel_id=1, source_target_pairs={{0,8},{4,12},{8,0},{12,4},{16,24},{20,28},{24,16},{28,20},{32,40},... | collective-permute-start | bytes 786440 | tf_op jit(solution)/shard_map/ppermute | solution.py:57
  79.5 8.2 %collective-permute-start.20 = (bf16[256,512]{1,0:T(8,128)(2,1)S(1)}, bf16[256,512]{1,0:T(8,128)(2,1)S(1)}, u32[]{:S(2)}, u32[]{:S(2)}) collective-permute-start(bf16[256,512]{1,0:T(8,128)(2,1)S(1)} %get-tuple-element.115), channel_id=1, source_target_pairs={{0,24},{4,28},{8,16},{12,20},{16,8},{20,12},{24,0},{28,4},{32,56},... | collective-permute-start | bytes 786440 | tf_op jit(solution)/shard_map/ppermute | solution.py:57
  86.3 6.5 %collective-permute-start.18 = (bf16[256,512]{1,0:T(8,128)(2,1)S(1)}, bf16[256,512]{1,0:T(8,128)(2,1)S(1)}, u32[]{:S(2)}, u32[]{:S(2)}) collective-permute-start(bf16[256,512]{1,0:T(8,128)(2,1)S(1)} %constant_dynamic-update-slice_fusion.refs_0_), channel_id=1, source_target_pairs={{0,8},{4,12},{8,0},{12,4},{16,24},{20,28},{24,16},{28,20},{32,40},... | collective-permute-start | bytes 786440 | tf_op jit(solution)/shard_map/ppermute | solution.py:57
  86.3 7.2 %collective-permute-start.19 = (bf16[256,512]{1,0:T(8,128)(2,1)S(1)}, bf16[256,512]{1,0:T(8,128)(2,1)S(1)}, u32[]{:S(2)}, u32[]{:S(2)}) collective-permute-start(bf16[256,512]{1,0:T(8,128)(2,1)S(1)} %collective-permute-done.15.refs_4_), channel_id=1, source_target_pairs={{0,24},{4,28},{8,16},{12,20},{16,8},{20,12},{24,0},{28,4},{32,56},... | collective-permute-start | bytes 786440 | tf_op jit(solution)/shard_map/ppermute | solution.py:57
  94.4 19.6 %all-to-all-start = ((bf16[8,64,512]{2,1,0:T(8,128)(2,1)}), bf16[8,64,512]{2,1,0:T(8,128)(2,1)}, u32[]{:S(2)}, u32[]{:S(2)}) async-start(bf16[8,64,512]{2,1,0:T(8,128)(2,1)} %bitcast.16), calls=%async_computation | async-start | bytes 1048576 | tf_op jit(solution)/shard_map/all_to_all | solution.py:125
  99.3 21.1 %collective-permute-start.22 = (bf16[256,512]{1,0:T(8,128)(2,1)S(1)}, bf16[256,512]{1,0:T(8,128)(2,1)S(1)}, u32[]{:S(2)}, u32[]{:S(2)}) collective-permute-start(bf16[256,512]{1,0:T(8,128)(2,1)S(1)} %constant_dynamic-update-slice_fusion.refs_0_), channel_id=1, source_target_pairs={{0,24},{4,28},{8,16},{12,20},{16,8},{20,12},{24,0},{28,4},{32,56},... | collective-permute-start | bytes 786440 | tf_op jit(solution)/shard_map/ppermute | solution.py:57
  99.4 26.1 %collective-permute-start.23 = (bf16[256,512]{1,0:T(8,128)(2,1)S(1)}, bf16[256,512]{1,0:T(8,128)(2,1)}, u32[]{:S(2)}, u32[]{:S(2)}) collective-permute-start(bf16[256,512]{1,0:T(8,128)(2,1)S(1)} %collective-permute-done.18.refs_1_), channel_id=1, source_target_pairs={{0,24},{4,28},{8,16},{12,20},{16,8},{20,12},{24,0},{28,4},{32,56},... | collective-permute-start | bytes 786440 | tf_op jit(solution)/shard_map/ppermute | solution.py:57
  102.0 23.5 %collective-permute-start.24 = (bf16[256,512]{1,0:T(8,128)(2,1)S(1)}, bf16[256,512]{1,0:T(8,128)(2,1)}, u32[]{:S(2)}, u32[]{:S(2)}) collective-permute-start(bf16[256,512]{1,0:T(8,128)(2,1)S(1)} %collective-permute-done.15.refs_4_), channel_id=1, source_target_pairs={{0,8},{4,12},{8,0},{12,4},{16,24},{20,28},{24,16},{28,20},{32,40},... | collective-permute-start | bytes 786440 | tf_op jit(solution)/shard_map/ppermute | solution.py:57
  102.0 23.5 %collective-permute-start.25 = (bf16[256,512]{1,0:T(8,128)(2,1)S(1)}, bf16[256,512]{1,0:T(8,128)(2,1)}, u32[]{:S(2)}, u32[]{:S(2)}) collective-permute-start(bf16[256,512]{1,0:T(8,128)(2,1)S(1)} %collective-permute-done.19.refs_5_), channel_id=1, source_target_pairs={{0,8},{4,12},{8,0},{12,4},{16,24},{20,28},{24,16},{28,20},{32,40},... | collective-permute-start | bytes 786440 | tf_op jit(solution)/shard_map/ppermute | solution.py:57
  115.2 15.7 %collective-permute-start.29 = (f32[32,512]{1,0:T(8,128)S(1)}, f32[32,512]{1,0:T(8,128)S(1)}, u32[]{:S(2)}, u32[]{:S(2)}) collective-permute-start(f32[32,512]{1,0:T(8,128)S(1)} %get-tuple-element.118), channel_id=1, source_target_pairs={{0,0},{1,64},{2,128},{3,192},{4,4},{5,68},{6,132},{7,196},{8,8},{9... | collective-permute-start | bytes 196616 | tf_op jit(solution)/shard_map/ppermute | solution.py:145
  120.5 10.5 %collective-permute-start.30 = (f32[32,512]{1,0:T(8,128)S(1)}, f32[32,512]{1,0:T(8,128)S(1)}, u32[]{:S(2)}, u32[]{:S(2)}) collective-permute-start(f32[32,512]{1,0:T(8,128)S(1)} %get-tuple-element.117), channel_id=1, source_target_pairs={{0,4},{1,68},{2,132},{3,196},{4,0},{5,64},{6,128},{7,192},{8,12},{... | collective-permute-start | bytes 196616 | tf_op jit(solution)/shard_map/ppermute | solution.py:145
  128.7 3.6 %collective-permute-start.26 = (bf16[160,512]{1,0:T(8,128)(2,1)S(1)}, bf16[160,512]{1,0:T(8,128)(2,1)S(1)}, u32[]{:S(2)}, u32[]{:S(2)}) collective-permute-start(bf16[160,512]{1,0:T(8,128)(2,1)S(1)} %get-tuple-element.107), channel_id=1, source_target_pairs={{0,1},{1,0},{2,3},{3,2},{4,5},{5,4},{6,7},{7,6},{8,9},{9,8},{10,11... | collective-permute-start | bytes 491528 | tf_op jit(solution)/shard_map/ppermute | solution.py:558
  128.8 5.5 %collective-permute-start.27 = (bf16[160,512]{1,0:T(8,128)(2,1)S(1)}, bf16[160,512]{1,0:T(8,128)(2,1)S(1)}, u32[]{:S(2)}, u32[]{:S(2)}) collective-permute-start(bf16[160,512]{1,0:T(8,128)(2,1)S(1)} %get-tuple-element.108), channel_id=1, source_target_pairs={{0,2},{1,3},{2,0},{3,1},{4,6},{5,7},{6,4},{7,5},{8,10},{9,11},{10,... | collective-permute-start | bytes 491528 | tf_op jit(solution)/shard_map/ppermute | solution.py:558
  130.0 8.4 %collective-permute-start.28 = (bf16[160,512]{1,0:T(8,128)(2,1)S(1)}, bf16[160,512]{1,0:T(8,128)(2,1)S(1)}, u32[]{:S(2)}, u32[]{:S(2)}) collective-permute-start(bf16[160,512]{1,0:T(8,128)(2,1)S(1)} %get-tuple-element.109), channel_id=1, source_target_pairs={{0,3},{1,2},{2,1},{3,0},{4,7},{5,6},{6,5},{7,4},{8,11},{9,10},{10,... | collective-permute-start | bytes 491528 | tf_op jit(solution)/shard_map/ppermute | solution.py:558

commit v8 on v7

--- a/solution.py
+++ b/solution.py
@@ -145,6 +145,21 @@
         part = lax.ppermute(part, ("dp", "tensor"), pairs)
         total = part if total is None else total + part
     return total
+
+
+def held(values, after):
+    def kernel(*refs):
+        pass
+
+    return pl.pallas_call(
+        kernel,
+        in_specs=[pl.BlockSpec(memory_space=pl.ANY)] * (len(values) + 1),
+        out_specs=[pl.BlockSpec(memory_space=pl.ANY)] * len(values),
+        out_shape=[jax.ShapeDtypeStruct(value.shape, value.dtype) for value in values],
+        input_output_aliases={k: k for k in range(len(values))},
+        cost_estimate=pl.CostEstimate(flops=0, bytes_accessed=0, transcendentals=0),
+        name="held",
+    )(*values, after)
 
 
 OFFSETS = 4
@@ -573,21 +588,23 @@
     weights = weight_to_place(own_weight)
     merged, squares = merge(info, merging_gain, high, parts, squares, width)
     weights, merged, squares = lax.optimization_barrier((weights, merged, squares))
-    weights = weight_across(jnp.concatenate(weights), nz // 2)
+    weights = jnp.concatenate(weights)
+    far_weights = moved(weights, lambda z, y, x: (z ^ nz // 2, y, x)) if nz > 1 else weights
     squares = [squares] + [swapped(squares, s) for s in range(1, tn)]
     kept, cut, hidden = grads(info, draft_gain.reshape(1, width), merged, folds, squares, width, ny, tn)
+    far_weights, cut = lax.optimization_barrier((far_weights, cut))
     weights, hidden = lax.optimization_barrier((weights, hidden))
+    if nz > 1:
+        weights = jnp.concatenate([weights, far_weights])
     weights = weight_halves(weight_across(weights, nz // 4))
     halves = reduce_once(kept, cut)
     weights, own = lax.optimization_barrier((weights, [half[0] for half in halves]))
     got = reduce_twice(halves)
-    weights = weight_once(weights)
     grad = [mine + part.astype(F32) for mine, part in zip(own, got)]
     if ny > 1:
         grad = [half.astype(BF16) for half in grad]
-    weights, grad = lax.optimization_barrier((weights, grad))
     grad = jnp.concatenate(grad)
-    weights = weight_twice(weights)
+    weights = weight_twice(weight_once(held(weights, grad)))
     grad = reduce_along_z(grad)
     hidden, grad = lax.optimization_barrier((hidden, grad))
     weight_grad = reduce_to_owner(grad)

time: 140 us -> 133 us (0.950)
  waiting for transfers between devices: 56 us -> 46.4 us
  local copies, waits for them, and re-layouts: 1.37 us -> 3.26 us
    ppermute x13, waiting for transfers between devices: 24.4 us -> 20.6 us  [moved(): return lax.ppermute(values, 'dp', pairs)]
    all_to_all x1, waiting for transfers between devices: 10.6 us -> 7.19 us  [reduce_along_z(): lax.all_to_all(grad.astype(BF16), 'dp', 0, 0, tiled=True, axis_index_grou...]
    ppermute x14, waiting for transfers between devices: 20.9 us -> 18.6 us  [swapped(): return lax.ppermute(values, 'tensor', [(a, a ^ s) for a in range(tn)])]
    unnamed x19 -> x29, local copies, waits for them, and re-layouts: 0.06 us -> 1.97 us
  transfers between devices with their start and end apart: 32 -> 32, of which waited for: 15 -> 15; matrix products, arithmetic and copies ran while one was open for 2% -> 2% of each run, Pallas kernels for 14% -> 18%
where the time goes in v8:
time: 133 us; the launch traced here: 132 us
  starting transfers between devices  48.9 us (37%)
  waiting for transfers between devices  46.4 us (35%)
  Pallas kernels  28.7 us (22%)
  other arithmetic  3.78 us (3%)
  local copies, waits for them, and re-layouts  3.26 us (2%)
    ppermute x13, waiting for transfers between devices, moved(): return lax.ppermute(values, 'dp', pairs)  20.6 us
    ppermute x14, waiting for transfers between devices, swapped(): return lax.ppermute(values, 'tensor', [(a, a ^ s) for a in range(tn)])  18.6 us
    ppermute x13, starting transfers between devices, moved(): return lax.ppermute(values, 'dp', pairs)  15.3 us
    ppermute x14, starting transfers between devices, swapped(): return lax.ppermute(values, 'tensor', [(a, a ^ s) for a in range(tn)])  15 us
    ppermute x2, starting transfers between devices, reduce_to_owner(): part = lax.ppermute(part, ('dp', 'tensor'), pairs)  10.6 us
    pallas_call x1, Pallas kernels, attend(): pl.pallas_call(functools.partial(attend_kernel, window), grid=(pack // bl...  8.17 us
    all_to_all x1, waiting for transfers between devices, reduce_along_z(): lax.all_to_all(grad.astype(BF16), 'dp', 0, 0, tiled=True, axis_index_grou...  7.19 us
    pallas_call x1, Pallas kernels, grads(): pl.pallas_call(kernel, in_specs=[SMEM, VMEM, HBM] + [HBM] * tn + [VMEM] *...  4.85 us
  transfers between devices with their start and end apart: 32, of which 15 were waited for; matrix products, arithmetic and copies ran while one was open for 2% of the time, Pallas kernels for 18%

profile of v8, /device:TPU:1, one launch (start us, length us, event | category | flops | bytes accessed | tf_op | source)
XLA Modules:
  0.0 132.1 jit_solution(11739114429105200404)
XLA Ops:
  0.7 1.3 concatenate.16.info_ref
  1.9 2.7 %fold.1.refs_0_ = bf16[160,512]{1,0:T(8,128)(2,1)} custom-call(s32[15]{0:T(128)} %concatenate.16.info_ref, bf16[3,128,512]{2,1,0:T(8,128)(2,1)} %cotangent_ref.1), custom_call_target="tpu_custom_call" | custom-call | flops 62914560 | bytes 393216 | tf_op jit(solution)/shard_map/fold/pallas_call | solution.py:325
  4.7 2.1 %collective-permute-start = (bf16[160,512]{1,0:T(8,128)(2,1)}, bf16[160,512]{1,0:T(8,128)(2,1)S(1)}, u32[]{:S(2)}, u32[]{:S(2)}) collective-permute-start(bf16[160,512]{1,0:T(8,128)(2,1)} %fold.1.refs_0_), channel_id=1, source_target_pairs={{0,2},{1,3},{2,0},{3,1},{4,6},{5,7},{6,4},{7,5},{8,10},{9,11},{10,... | collective-permute-start | bytes 491528 | tf_op jit(solution)/shard_map/ppermute | solution.py:573
  6.8 4.8 %features.1 = (bf16[128,2048]{1,0:T(8,128)(2,1)}, bf16[128,2048]{1,0:T(8,128)(2,1)}, bf16[128,2048]{1,0:T(8,128)(2,1)}, bf16[128,2048]{1,0:T(8,128)(2,1)}) custom-call(s32[15]{0:T(128)} %concatenate.16.info_ref, bf16[128,8192]{1,0:T(8,128)(2,1)} %low_ref, bf16[128,8192]{1,0:T(8,128)(2,1)} %mid_ref.1, f32[3,8192]{1,0:T(4,128)} %gain_ref.3), custom_call_target="tpu_custom_call" | custom-call | flops 10485760 | bytes 6291456 | tf_op jit(solution)/shard_map/features/pallas_call | solution.py:226
  11.7 2.0 %collective-permute-start.6 = (bf16[128,2048]{1,0:T(8,128)(2,1)}, bf16[128,2048]{1,0:T(8,128)(2,1)S(1)}, u32[]{:S(2)}, u32[]{:S(2)}) collective-permute-start(bf16[128,2048]{1,0:T(8,128)(2,1)} %get-tuple-element.70), channel_id=1, source_target_pairs={{0,1},{1,0},{2,3},{3,2},{4,5},{5,4},{6,7},{7,6},{8,9},{9,8},{10,11... | collective-permute-start | bytes 1572872 | tf_op jit(solution)/shard_map/ppermute | solution.py:573
  13.7 1.1 collective-permute-start.7
  14.7 0.7 collective-permute-start.8
  15.4 8.2 %attend.1 = (bf16[512,2048]{1,0:T(8,128)(2,1)S(1)}, f32[8,512]{1,0:T(8,128)S(1)}) custom-call(s32[15]{0:T(128)S(1)} %copy-done.7, bf16[512,2048]{1,0:T(8,128)(2,1)S(1)} %copy-done.9, bf16[512,256]{1,0:T(8,128)(2,1)S(1)} %copy-done.10, bf16[512,256]{1,0:T(8,128)(2,1)S(1)} %copy-done.11), custom_call_target="tpu_custom_call" | custom-call | flops 1610612736 | bytes 4194304 | tf_op jit(solution)/shard_map/attend/pallas_call | solution.py:277
  23.8 0.4 collective-permute-start.4
  24.1 0.7 collective-permute-done.3
  25.2 3.8 %collective-permute-start.1 = (bf16[32,512]{1,0:T(8,128)(2,1)S(1)}, bf16[32,512]{1,0:T(8,128)(2,1)S(1)}, u32[]{:S(2)}, u32[]{:S(2)}) collective-permute-start(bf16[32,512]{1,0:T(8,128)(2,1)S(1)} %copy-done.12), channel_id=1, source_target_pairs={{0,0},{1,4},{2,32},{3,36},{4,64},{5,68},{6,96},{7,100},{8,128},{9,... | collective-permute-start | bytes 98312 | tf_op jit(solution)/shard_map/ppermute | solution.py:70
  29.1 3.0 %collective-permute-start.9 = (f32[8,512]{1,0:T(8,128)S(1)}, f32[8,512]{1,0:T(8,128)S(1)}, u32[]{:S(2)}, u32[]{:S(2)}) collective-permute-start(f32[8,512]{1,0:T(8,128)S(1)} %add.65.refs_4_), channel_id=1, source_target_pairs={{0,2},{1,3},{2,0},{3,1},{4,6},{5,7},{6,4},{7,5},{8,10},{9,11},{10,... | collective-permute-start | bytes 49160 | tf_op jit(solution)/shard_map/ppermute | solution.py:573
  32.1 10.4 %collective-permute-done.8.refs_3_ = bf16[128,2048]{1,0:T(8,128)(2,1)S(1)} collective-permute-done((bf16[128,2048]{1,0:T(8,128)(2,1)}, bf16[128,2048]{1,0:T(8,128)(2,1)S(1)}, u32[]{:S(2)}, u32[]{:S(2)}) %collective-permute-start.8) | collective-permute-done | bytes 524320 | tf_op jit(solution)/shard_map/ppermute | solution.py:573
  42.5 0.9 collective-permute-done.9.refs_5_
  43.4 3.5 %merge.1 = (bf16[512,2048]{1,0:T(8,128)(2,1)S(1)}, f32[8,512]{1,0:T(8,128)S(1)}) custom-call(s32[15]{0:T(128)S(1)} %copy-done.7, f32[3,8192]{1,0:T(4,128)S(1)} %copy-done.5, bf16[512,2048]{1,0:T(8,128)(2,1)S(1)} %get-tuple-element.65.high_ref, bf16[128,2048]{1,0:T(8,128)(2,1)S(1)} %copy-done.4, bf16[128,2048]{1,0:T(8,128)(2,1)S(1)} %collective-permute-done.6.refs_1_, ...), custom_call_target="tpu_custom_call" | custom-call | flops 8388608 | bytes 6291456 | tf_op jit(solution)/shard_map/merge/pallas_call | solution.py:372
  46.9 1.0 collective-permute-start.10
  47.9 2.2 %collective-permute-start.11 = (f32[8,512]{1,0:T(8,128)S(1)}, f32[8,512]{1,0:T(8,128)S(1)}, u32[]{:S(2)}, u32[]{:S(2)}) collective-permute-start(f32[8,512]{1,0:T(8,128)S(1)} %get-tuple-element.84.refs_4_), channel_id=1, source_target_pairs={{0,2},{1,3},{2,0},{3,1},{4,6},{5,7},{6,4},{7,5},{8,10},{9,11},{10,... | collective-permute-start | bytes 49160 | tf_op jit(solution)/shard_map/ppermute | solution.py:573
  50.2 3.4 %collective-permute-start.13 = (bf16[64,512]{1,0:T(8,128)(2,1)S(1)}, bf16[64,512]{1,0:T(8,128)(2,1)S(1)}, u32[]{:S(2)}, u32[]{:S(2)}) collective-permute-start(bf16[64,512]{1,0:T(8,128)(2,1)S(1)} %constant_dynamic-update-slice_fusion), channel_id=1, source_target_pairs={{0,128},{4,132},{8,136},{12,140},{16,144},{20,148},{24,152},{28,15... | collective-permute-start | bytes 196616 | tf_op jit(solution)/shard_map/ppermute | solution.py:57
  53.6 4.8 %grads.1 = (f32[2,256,512]{2,1,0:T(8,128)S(1)}, f32[2,256,512]{2,1,0:T(8,128)S(1)}, bf16[2,256,512]{2,1,0:T(8,128)(2,1)S(1)}, bf16[2,256,512]{2,1,0:T(8,128)(2,1)S(1)}, bf16[512,2048]{1,0:T(8,128)(2,1)S(1)}) custom-call(s32[15]{0:T(128)S(1)} %copy-done.7, f32[1,8192]{1,0:T(1,128)S(1)} %bitcast.15, bf16[512,2048]{1,0:T(8,128)(2,1)S(1)} %get-tuple-element.79.merged_ref, ...), custom_call_target="tpu_custom_call" | custom-call | flops 1073741824 | bytes 8388608 | tf_op jit(solution)/shard_map/grads/pallas_call | solution.py:452
  58.5 0.9 collective-permute-done.13
  59.4 3.3 %collective-permute-start.16 = (bf16[2,256,512]{2,1,0:T(8,128)(2,1)S(1)}, bf16[2,256,512]{2,1,0:T(8,128)(2,1)S(1)}, u32[]{:S(2)}, u32[]{:S(2)}) collective-permute-start(bf16[2,256,512]{2,1,0:T(8,128)(2,1)S(1)} %get-tuple-element.92), channel_id=1, source_target_pairs={{0,8},{4,12},{8,0},{12,4},{16,24},{20,28},{24,16},{28,20},{32,40},... | collective-permute-start | bytes 1572872 | tf_op jit(solution)/shard_map/ppermute | solution.py:57
  62.6 1.5 %collective-permute-start.17 = (bf16[2,256,512]{2,1,0:T(8,128)(2,1)S(1)}, bf16[2,256,512]{2,1,0:T(8,128)(2,1)S(1)}, u32[]{:S(2)}, u32[]{:S(2)}) collective-permute-start(bf16[2,256,512]{2,1,0:T(8,128)(2,1)S(1)} %get-tuple-element.93), channel_id=1, source_target_pairs={{0,24},{4,28},{8,16},{12,20},{16,8},{20,12},{24,0},{28,4},{32,56},... | collective-permute-start | bytes 1572872 | tf_op jit(solution)/shard_map/ppermute | solution.py:57
  64.3 8.2 %collective-permute-done.14 = bf16[128,512]{1,0:T(8,128)(2,1)S(1)} collective-permute-done((bf16[128,512]{1,0:T(8,128)(2,1)S(1)}, bf16[128,512]{1,0:T(8,128)(2,1)S(1)}, u32[]{:S(2)}, u32[]{:S(2)}) %collective-permute-start.14) | collective-permute-done | bytes 131104 | tf_op jit(solution)/shard_map/ppermute | solution.py:57
  72.7 1.7 %collective-permute-done.16 = bf16[2,256,512]{2,1,0:T(8,128)(2,1)S(1)} collective-permute-done((bf16[2,256,512]{2,1,0:T(8,128)(2,1)S(1)}, bf16[2,256,512]{2,1,0:T(8,128)(2,1)S(1)}, u32[]{:S(2)}, u32[]{:S(2)}) %collective-permute-start.16) | collective-permute-done | bytes 524320 | tf_op jit(solution)/shard_map/ppermute | solution.py:57
  74.4 2.0 %collective-permute-done.17 = bf16[2,256,512]{2,1,0:T(8,128)(2,1)S(1)} collective-permute-done((bf16[2,256,512]{2,1,0:T(8,128)(2,1)S(1)}, bf16[2,256,512]{2,1,0:T(8,128)(2,1)S(1)}, u32[]{:S(2)}, u32[]{:S(2)}) %collective-permute-start.17) | collective-permute-done | bytes 524320 | tf_op jit(solution)/shard_map/ppermute | solution.py:57
  76.8 1.9 %collective-permute-start.18 = (bf16[256,512]{1,0:T(8,128)(2,1)S(1)}, bf16[256,512]{1,0:T(8,128)(2,1)S(1)}, u32[]{:S(2)}, u32[]{:S(2)}) collective-permute-start(bf16[256,512]{1,0:T(8,128)(2,1)S(1)} %get-tuple-element.111), channel_id=1, source_target_pairs={{0,24},{4,28},{8,16},{12,20},{16,8},{20,12},{24,0},{28,4},{32,56},... | collective-permute-start | bytes 786440 | tf_op jit(solution)/shard_map/ppermute | solution.py:57
  78.8 0.4 collective-permute-done.15.refs_1_
  79.1 3.5 %collective-permute-done.19 = bf16[256,512]{1,0:T(8,128)(2,1)S(1)} collective-permute-done((bf16[256,512]{1,0:T(8,128)(2,1)S(1)}, bf16[256,512]{1,0:T(8,128)(2,1)S(1)}, u32[]{:S(2)}, u32[]{:S(2)}) %collective-permute-start.19) | collective-permute-done | bytes 262176 | tf_op jit(solution)/shard_map/ppermute | solution.py:57
  82.7 1.4 %collective-permute-done.18 = bf16[256,512]{1,0:T(8,128)(2,1)S(1)} collective-permute-done((bf16[256,512]{1,0:T(8,128)(2,1)S(1)}, bf16[256,512]{1,0:T(8,128)(2,1)S(1)}, u32[]{:S(2)}, u32[]{:S(2)}) %collective-permute-start.18) | collective-permute-done | bytes 262176 | tf_op jit(solution)/shard_map/ppermute | solution.py:57
  84.2 0.9 pad_maximum_fusion.refs_2_
  85.0 4.2 %all-to-all-start = ((bf16[8,64,512]{2,1,0:T(8,128)(2,1)}), bf16[8,64,512]{2,1,0:T(8,128)(2,1)}, u32[]{:S(2)}, u32[]{:S(2)}) async-start(bf16[8,64,512]{2,1,0:T(8,128)(2,1)} %bitcast.10), calls=%async_computation | async-start | bytes 1048576 | tf_op jit(solution)/shard_map/all_to_all | solution.py:125
  89.3 2.1 %collective-permute-start.23 = (bf16[256,512]{1,0:T(8,128)(2,1)}, bf16[256,512]{1,0:T(8,128)(2,1)S(1)}, u32[]{:S(2)}, u32[]{:S(2)}) collective-permute-start(bf16[256,512]{1,0:T(8,128)(2,1)} %get-tuple-element.103.refs_4_), channel_id=1, source_target_pairs={{0,24},{4,28},{8,16},{12,20},{16,8},{20,12},{24,0},{28,4},{32,56},... | collective-permute-start | bytes 786440 | tf_op jit(solution)/shard_map/ppermute | solution.py:57
  91.4 0.7 collective-permute-start.21
  92.2 2.5 %collective-permute-done.20.refs_1_ = bf16[256,512]{1,0:T(8,128)(2,1)S(1)} collective-permute-done((bf16[256,512]{1,0:T(8,128)(2,1)}, bf16[256,512]{1,0:T(8,128)(2,1)S(1)}, u32[]{:S(2)}, u32[]{:S(2)}) %collective-permute-start.20) | collective-permute-done | bytes 262176 | tf_op jit(solution)/shard_map/ppermute | solution.py:57
  94.7 1.8 %collective-permute-start.22 = (bf16[256,512]{1,0:T(8,128)(2,1)S(1)}, bf16[256,512]{1,0:T(8,128)(2,1)S(1)}, u32[]{:S(2)}, u32[]{:S(2)}) collective-permute-start(bf16[256,512]{1,0:T(8,128)(2,1)S(1)} %collective-permute-done.20.refs_1_), channel_id=1, source_target_pairs={{0,24},{4,28},{8,16},{12,20},{16,8},{20,12},{24,0},{28,4},{32,56},... | collective-permute-start | bytes 786440 | tf_op jit(solution)/shard_map/ppermute | solution.py:57
  96.5 7.2 %all-to-all-done = bf16[8,64,512]{2,1,0:T(8,128)(2,1)} async-done(((bf16[8,64,512]{2,1,0:T(8,128)(2,1)}), bf16[8,64,512]{2,1,0:T(8,128)(2,1)}, u32[]{:S(2)}, u32[]{:S(2)}) %all-to-all-start) | async-done | bytes 524320 | tf_op jit(solution)/shard_map/all_to_all | solution.py:125
  103.7 1.1 convert_reduce_fusion
  104.8 5.4 %collective-permute-start.29 = (f32[32,512]{1,0:T(8,128)S(1)}, f32[32,512]{1,0:T(8,128)S(1)}, u32[]{:S(2)}, u32[]{:S(2)}) collective-permute-start(f32[32,512]{1,0:T(8,128)S(1)} %get-tuple-element.116), channel_id=1, source_target_pairs={{0,0},{1,64},{2,128},{3,192},{4,4},{5,68},{6,132},{7,196},{8,8},{9... | collective-permute-start | bytes 196616 | tf_op jit(solution)/shard_map/ppermute | solution.py:145
  110.2 5.2 %collective-permute-start.30 = (f32[32,512]{1,0:T(8,128)S(1)}, f32[32,512]{1,0:T(8,128)S(1)}, u32[]{:S(2)}, u32[]{:S(2)}) collective-permute-start(f32[32,512]{1,0:T(8,128)S(1)} %get-tuple-element.115), channel_id=1, source_target_pairs={{0,4},{1,68},{2,132},{3,196},{4,0},{5,64},{6,128},{7,192},{8,12},{... | collective-permute-start | bytes 196616 | tf_op jit(solution)/shard_map/ppermute | solution.py:145
  115.5 0.9 copy-done.1
  116.4 0.9 copy-done.3
  117.3 3.0 %project.1 = (f32[160,512]{1,0:T(8,128)S(1)}, bf16[160,512]{1,0:T(8,128)(2,1)S(1)}, bf16[160,512]{1,0:T(8,128)(2,1)S(1)}, bf16[160,512]{1,0:T(8,128)(2,1)S(1)}) custom-call(s32[15]{0:T(128)S(1)} %copy-done.7, bf16[512,2048]{1,0:T(8,128)(2,1)S(1)} %get-tuple-element.99.hidden_ref, bf16[256,512]{1,0:T(8,128)(2,1)S(1)} %copy-done.1, ...), custom_call_target="tpu_custom_call" | custom-call | flops 1073741824 | bytes 4194304 | tf_op jit(solution)/shard_map/project/pallas_call | solution.py:504
  120.5 2.0 %collective-permute-start.27 = (bf16[160,512]{1,0:T(8,128)(2,1)S(1)}, bf16[160,512]{1,0:T(8,128)(2,1)S(1)}, u32[]{:S(2)}, u32[]{:S(2)}) collective-permute-start(bf16[160,512]{1,0:T(8,128)(2,1)S(1)} %get-tuple-element.106), channel_id=1, source_target_pairs={{0,2},{1,3},{2,0},{3,1},{4,6},{5,7},{6,4},{7,5},{8,10},{9,11},{10,... | collective-permute-start | bytes 491528 | tf_op jit(solution)/shard_map/ppermute | solution.py:573
  122.6 0.8 multiply_reduce_fusion
  123.4 0.6 dynamic-slice_divide_fusion
  124.0 2.9 %collective-permute-done.27.refs_2_ = bf16[160,512]{1,0:T(8,128)(2,1)S(1)} collective-permute-done((bf16[160,512]{1,0:T(8,128)(2,1)S(1)}, bf16[160,512]{1,0:T(8,128)(2,1)S(1)}, u32[]{:S(2)}, u32[]{:S(2)}) %collective-permute-start.27) | collective-permute-done | bytes 163872 | tf_op jit(solution)/shard_map/ppermute | solution.py:573
  126.9 3.6 %collective-permute-done.28.refs_3_ = bf16[160,512]{1,0:T(8,128)(2,1)S(1)} collective-permute-done((bf16[160,512]{1,0:T(8,128)(2,1)S(1)}, bf16[160,512]{1,0:T(8,128)(2,1)S(1)}, u32[]{:S(2)}, u32[]{:S(2)}) %collective-permute-start.28) | collective-permute-done | bytes 163872 | tf_op jit(solution)/shard_map/ppermute | solution.py:573
  130.4 1.7 %spread.1 = bf16[3,128,512]{2,1,0:T(8,128)(2,1)} custom-call(s32[15]{0:T(128)S(1)} %copy-done.7, f32[160,512]{1,0:T(8,128)S(1)} %get-tuple-element.104.refs_0_, bf16[160,512]{1,0:T(8,128)(2,1)S(1)} %collective-permute-done.26.refs_1_, bf16[160,512]{1,0:T(8,128)(2,1)S(1)} %collective-permute-done.27.refs_2_, bf16[160,512]{1,0:T(8,128)(2,1)S(1)} %collective-permute-done.28.refs_3_), custom_call_target="tpu_custom_call" | custom-call | flops 62914560 | bytes 1572864 | tf_op jit(solution)/shard_map/spread/pallas_call | solution.py:535
  (67 shorter events, 2.1 us)
Async XLA Ops:
  4.7 10.7 %copy-start.7 = (s32[15]{0:T(128)S(1)}, s32[15]{0:T(128)}, u32[]{:S(2)}) copy-start(s32[15]{0:T(128)} %concatenate.16.info_ref) | copy-start | bytes 184
  4.7 10.7 %copy-start.9 = (bf16[512,2048]{1,0:T(8,128)(2,1)S(1)}, bf16[512,2048]{1,0:T(8,128)(2,1)}, u32[]{:S(2)}) copy-start(bf16[512,2048]{1,0:T(8,128)(2,1)} %query_ref.1) | copy-start | bytes 6291460
  4.7 10.7 %copy-start.10 = (bf16[512,256]{1,0:T(8,128)(2,1)S(1)}, bf16[512,256]{1,0:T(8,128)(2,1)}, u32[]{:S(2)}) copy-start(bf16[512,256]{1,0:T(8,128)(2,1)} %key_ref.1) | copy-start | bytes 786436
  4.7 10.7 %copy-start.11 = (bf16[512,256]{1,0:T(8,128)(2,1)S(1)}, bf16[512,256]{1,0:T(8,128)(2,1)}, u32[]{:S(2)}) copy-start(bf16[512,256]{1,0:T(8,128)(2,1)} %value_ref.1) | copy-start | bytes 786436
  4.7 6.9 %collective-permute-start = (bf16[160,512]{1,0:T(8,128)(2,1)}, bf16[160,512]{1,0:T(8,128)(2,1)S(1)}, u32[]{:S(2)}, u32[]{:S(2)}) collective-permute-start(bf16[160,512]{1,0:T(8,128)(2,1)} %fold.1.refs_0_), channel_id=1, source_target_pairs={{0,2},{1,3},{2,0},{3,1},{4,6},{5,7},{6,4},{7,5},{8,10},{9,11},{10,... | collective-permute-start | bytes 491528 | tf_op jit(solution)/shard_map/ppermute | solution.py:573
  11.6 12.1 %copy-start.6 = (bf16[160,512]{1,0:T(8,128)(2,1)S(1)}, bf16[160,512]{1,0:T(8,128)(2,1)}, u32[]{:S(2)}) copy-start(bf16[160,512]{1,0:T(8,128)(2,1)} %fold.1.refs_0_) | copy-start | bytes 491524
  11.6 13.5 %copy-start.12 = (bf16[32,512]{1,0:T(8,128)(2,1)S(1)}, bf16[32,512]{1,0:T(8,128)(2,1)}, u32[]{:S(2)}) copy-start(bf16[32,512]{1,0:T(8,128)(2,1)} %param.18) | copy-start | bytes 98308
  11.7 31.8 %copy-start.4 = (bf16[128,2048]{1,0:T(8,128)(2,1)S(1)}, bf16[128,2048]{1,0:T(8,128)(2,1)}, u32[]{:S(2)}) copy-start(bf16[128,2048]{1,0:T(8,128)(2,1)} %get-tuple-element.66.refs_0_) | copy-start | bytes 1572868
  11.7 31.8 %copy-start.5 = (f32[3,8192]{1,0:T(4,128)S(1)}, f32[3,8192]{1,0:T(4,128)}, u32[]{:S(2)}) copy-start(f32[3,8192]{1,0:T(4,128)} %gain_ref.3) | copy-start | bytes 294916
  11.7 17.4 %collective-permute-start.6 = (bf16[128,2048]{1,0:T(8,128)(2,1)}, bf16[128,2048]{1,0:T(8,128)(2,1)S(1)}, u32[]{:S(2)}, u32[]{:S(2)}) collective-permute-start(bf16[128,2048]{1,0:T(8,128)(2,1)} %get-tuple-element.70), channel_id=1, source_target_pairs={{0,1},{1,0},{2,3},{3,2},{4,5},{5,4},{6,7},{7,6},{8,9},{9,8},{10,11... | collective-permute-start | bytes 1572872 | tf_op jit(solution)/shard_map/ppermute | solution.py:573
  13.7 18.4 %collective-permute-start.7 = (bf16[128,2048]{1,0:T(8,128)(2,1)}, bf16[128,2048]{1,0:T(8,128)(2,1)S(1)}, u32[]{:S(2)}, u32[]{:S(2)}) collective-permute-start(bf16[128,2048]{1,0:T(8,128)(2,1)} %get-tuple-element.72), channel_id=1, source_target_pairs={{0,2},{1,3},{2,0},{3,1},{4,6},{5,7},{6,4},{7,5},{8,10},{9,11},{10,... | collective-permute-start | bytes 1572872 | tf_op jit(solution)/shard_map/ppermute | solution.py:573
  14.7 27.7 %collective-permute-start.8 = (bf16[128,2048]{1,0:T(8,128)(2,1)}, bf16[128,2048]{1,0:T(8,128)(2,1)S(1)}, u32[]{:S(2)}, u32[]{:S(2)}) collective-permute-start(bf16[128,2048]{1,0:T(8,128)(2,1)} %get-tuple-element.73), channel_id=1, source_target_pairs={{0,3},{1,2},{2,1},{3,0},{4,7},{5,6},{6,5},{7,4},{8,11},{9,10},{10,... | collective-permute-start | bytes 1572872 | tf_op jit(solution)/shard_map/ppermute | solution.py:573
  23.6 1.2 collective-permute-start.3
  23.8 1.4 %collective-permute-start.4 = (bf16[160,512]{1,0:T(8,128)(2,1)S(1)}, bf16[160,512]{1,0:T(8,128)(2,1)S(1)}, u32[]{:S(2)}, u32[]{:S(2)}) collective-permute-start(bf16[160,512]{1,0:T(8,128)(2,1)S(1)} %copy-done.6), channel_id=1, source_target_pairs={{0,1},{1,0},{2,3},{3,2},{4,5},{5,4},{6,7},{7,6},{8,9},{9,8},{10,11... | collective-permute-start | bytes 491528 | tf_op jit(solution)/shard_map/ppermute | solution.py:573
  24.8 4.1 %collective-permute-start.5 = (bf16[160,512]{1,0:T(8,128)(2,1)S(1)}, bf16[160,512]{1,0:T(8,128)(2,1)S(1)}, u32[]{:S(2)}, u32[]{:S(2)}) collective-permute-start(bf16[160,512]{1,0:T(8,128)(2,1)S(1)} %collective-permute-done.refs_2_), channel_id=1, source_target_pairs={{0,1},{1,0},{2,3},{3,2},{4,5},{5,4},{6,7},{7,6},{8,9},{9,8},{10,11... | collective-permute-start | bytes 491528 | tf_op jit(solution)/shard_map/ppermute | solution.py:573
  25.2 21.7 %collective-permute-start.1 = (bf16[32,512]{1,0:T(8,128)(2,1)S(1)}, bf16[32,512]{1,0:T(8,128)(2,1)S(1)}, u32[]{:S(2)}, u32[]{:S(2)}) collective-permute-start(bf16[32,512]{1,0:T(8,128)(2,1)S(1)} %copy-done.12), channel_id=1, source_target_pairs={{0,0},{1,4},{2,32},{3,36},{4,64},{5,68},{6,96},{7,100},{8,128},{9,... | collective-permute-start | bytes 98312 | tf_op jit(solution)/shard_map/ppermute | solution.py:70
  28.9 18.0 %collective-permute-start.2 = (bf16[32,512]{1,0:T(8,128)(2,1)S(1)}, bf16[32,512]{1,0:T(8,128)(2,1)S(1)}, u32[]{:S(2)}, u32[]{:S(2)}) collective-permute-start(bf16[32,512]{1,0:T(8,128)(2,1)S(1)} %copy-done.12), channel_id=1, source_target_pairs={{0,4},{1,0},{2,36},{3,32},{4,68},{5,64},{6,100},{7,96},{8,132},{9,... | collective-permute-start | bytes 98312 | tf_op jit(solution)/shard_map/ppermute | solution.py:70
  29.1 24.5 %copy-start.8 = (f32[8192]{0:T(1024)S(1)}, f32[8192]{0:T(1024)}, u32[]{:S(2)}) copy-start(f32[8192]{0:T(1024)} %param.17) | copy-start | bytes 98308
  29.1 14.3 %collective-permute-start.9 = (f32[8,512]{1,0:T(8,128)S(1)}, f32[8,512]{1,0:T(8,128)S(1)}, u32[]{:S(2)}, u32[]{:S(2)}) collective-permute-start(f32[8,512]{1,0:T(8,128)S(1)} %add.65.refs_4_), channel_id=1, source_target_pairs={{0,2},{1,3},{2,0},{3,1},{4,6},{5,7},{6,4},{7,5},{8,10},{9,11},{10,... | collective-permute-start | bytes 49160 | tf_op jit(solution)/shard_map/ppermute | solution.py:573
  46.9 6.7 %collective-permute-start.10 = (f32[8,512]{1,0:T(8,128)S(1)}, f32[8,512]{1,0:T(8,128)S(1)}, u32[]{:S(2)}, u32[]{:S(2)}) collective-permute-start(f32[8,512]{1,0:T(8,128)S(1)} %get-tuple-element.84.refs_4_), channel_id=1, source_target_pairs={{0,1},{1,0},{2,3},{3,2},{4,5},{5,4},{6,7},{7,6},{8,9},{9,8},{10,11... | collective-permute-start | bytes 49160 | tf_op jit(solution)/shard_map/ppermute | solution.py:573
  47.9 5.7 %collective-permute-start.11 = (f32[8,512]{1,0:T(8,128)S(1)}, f32[8,512]{1,0:T(8,128)S(1)}, u32[]{:S(2)}, u32[]{:S(2)}) collective-permute-start(f32[8,512]{1,0:T(8,128)S(1)} %get-tuple-element.84.refs_4_), channel_id=1, source_target_pairs={{0,2},{1,3},{2,0},{3,1},{4,6},{5,7},{6,4},{7,5},{8,10},{9,11},{10,... | collective-permute-start | bytes 49160 | tf_op jit(solution)/shard_map/ppermute | solution.py:573
  50.1 3.5 %collective-permute-start.12 = (f32[8,512]{1,0:T(8,128)S(1)}, f32[8,512]{1,0:T(8,128)S(1)}, u32[]{:S(2)}, u32[]{:S(2)}) collective-permute-start(f32[8,512]{1,0:T(8,128)S(1)} %get-tuple-element.84.refs_4_), channel_id=1, source_target_pairs={{0,3},{1,2},{2,1},{3,0},{4,7},{5,6},{6,5},{7,4},{8,11},{9,10},{10,... | collective-permute-start | bytes 49160 | tf_op jit(solution)/shard_map/ppermute | solution.py:573
  50.2 9.2 %collective-permute-start.13 = (bf16[64,512]{1,0:T(8,128)(2,1)S(1)}, bf16[64,512]{1,0:T(8,128)(2,1)S(1)}, u32[]{:S(2)}, u32[]{:S(2)}) collective-permute-start(bf16[64,512]{1,0:T(8,128)(2,1)S(1)} %constant_dynamic-update-slice_fusion), channel_id=1, source_target_pairs={{0,128},{4,132},{8,136},{12,140},{16,144},{20,148},{24,152},{28,15... | collective-permute-start | bytes 196616 | tf_op jit(solution)/shard_map/ppermute | solution.py:57
  59.4 15.0 %collective-permute-start.16 = (bf16[2,256,512]{2,1,0:T(8,128)(2,1)S(1)}, bf16[2,256,512]{2,1,0:T(8,128)(2,1)S(1)}, u32[]{:S(2)}, u32[]{:S(2)}) collective-permute-start(bf16[2,256,512]{2,1,0:T(8,128)(2,1)S(1)} %get-tuple-element.92), channel_id=1, source_target_pairs={{0,8},{4,12},{8,0},{12,4},{16,24},{20,28},{24,16},{28,20},{32,40},... | collective-permute-start | bytes 1572872 | tf_op jit(solution)/shard_map/ppermute | solution.py:57
  62.6 13.7 %collective-permute-start.17 = (bf16[2,256,512]{2,1,0:T(8,128)(2,1)S(1)}, bf16[2,256,512]{2,1,0:T(8,128)(2,1)S(1)}, u32[]{:S(2)}, u32[]{:S(2)}) collective-permute-start(bf16[2,256,512]{2,1,0:T(8,128)(2,1)S(1)} %get-tuple-element.93), channel_id=1, source_target_pairs={{0,24},{4,28},{8,16},{12,20},{16,8},{20,12},{24,0},{28,4},{32,56},... | collective-permute-start | bytes 1572872 | tf_op jit(solution)/shard_map/ppermute | solution.py:57
  64.2 8.4 %collective-permute-start.14 = (bf16[128,512]{1,0:T(8,128)(2,1)S(1)}, bf16[128,512]{1,0:T(8,128)(2,1)S(1)}, u32[]{:S(2)}, u32[]{:S(2)}) collective-permute-start(bf16[128,512]{1,0:T(8,128)(2,1)S(1)} %pad_maximum_fusion.1), channel_id=1, source_target_pairs={{0,64},{4,68},{8,72},{12,76},{16,80},{20,84},{24,88},{28,92},{32,9... | collective-permute-start | bytes 393224 | tf_op jit(solution)/shard_map/ppermute | solution.py:57
  72.6 4.2 %copy-start = (bf16[256,512]{1,0:T(8,128)(2,1)}, bf16[256,512]{1,0:T(8,128)(2,1)S(1)}, u32[]{:S(2)}) copy-start(bf16[256,512]{1,0:T(8,128)(2,1)S(1)} %constant_dynamic-update-slice_fusion.2.refs_0_) | copy-start | bytes 786436
  72.6 6.5 %collective-permute-start.15 = (bf16[256,512]{1,0:T(8,128)(2,1)S(1)}, bf16[256,512]{1,0:T(8,128)(2,1)S(1)}, u32[]{:S(2)}, u32[]{:S(2)}) collective-permute-start(bf16[256,512]{1,0:T(8,128)(2,1)S(1)} %constant_dynamic-update-slice_fusion.2.refs_0_), channel_id=1, source_target_pairs={{0,32},{4,36},{8,40},{12,44},{16,48},{20,52},{24,56},{28,60},{32,0... | collective-permute-start | bytes 786440 | tf_op jit(solution)/shard_map/ppermute | solution.py:57
  76.5 6.1 %collective-permute-start.19 = (bf16[256,512]{1,0:T(8,128)(2,1)S(1)}, bf16[256,512]{1,0:T(8,128)(2,1)S(1)}, u32[]{:S(2)}, u32[]{:S(2)}) collective-permute-start(bf16[256,512]{1,0:T(8,128)(2,1)S(1)} %get-tuple-element.113), channel_id=1, source_target_pairs={{0,8},{4,12},{8,0},{12,4},{16,24},{20,28},{24,16},{28,20},{32,40},... | collective-permute-start | bytes 786440 | tf_op jit(solution)/shard_map/ppermute | solution.py:57
  76.8 7.3 %collective-permute-start.18 = (bf16[256,512]{1,0:T(8,128)(2,1)S(1)}, bf16[256,512]{1,0:T(8,128)(2,1)S(1)}, u32[]{:S(2)}, u32[]{:S(2)}) collective-permute-start(bf16[256,512]{1,0:T(8,128)(2,1)S(1)} %get-tuple-element.111), channel_id=1, source_target_pairs={{0,24},{4,28},{8,16},{12,20},{16,8},{20,12},{24,0},{28,4},{32,56},... | collective-permute-start | bytes 786440 | tf_op jit(solution)/shard_map/ppermute | solution.py:57
  79.1 5.9 %copy-start.2 = (bf16[256,512]{1,0:T(8,128)(2,1)}, bf16[256,512]{1,0:T(8,128)(2,1)S(1)}, u32[]{:S(2)}) copy-start(bf16[256,512]{1,0:T(8,128)(2,1)S(1)} %collective-permute-done.15.refs_1_) | copy-start | bytes 786436
  85.0 18.6 %all-to-all-start = ((bf16[8,64,512]{2,1,0:T(8,128)(2,1)}), bf16[8,64,512]{2,1,0:T(8,128)(2,1)}, u32[]{:S(2)}, u32[]{:S(2)}) async-start(bf16[8,64,512]{2,1,0:T(8,128)(2,1)} %bitcast.10), calls=%async_computation | async-start | bytes 1048576 | tf_op jit(solution)/shard_map/all_to_all | solution.py:125
  89.2 5.5 %collective-permute-start.20 = (bf16[256,512]{1,0:T(8,128)(2,1)}, bf16[256,512]{1,0:T(8,128)(2,1)S(1)}, u32[]{:S(2)}, u32[]{:S(2)}) collective-permute-start(bf16[256,512]{1,0:T(8,128)(2,1)} %get-tuple-element.102.refs_0_), channel_id=1, source_target_pairs={{0,8},{4,12},{8,0},{12,4},{16,24},{20,28},{24,16},{28,20},{32,40},... | collective-permute-start | bytes 786440 | tf_op jit(solution)/shard_map/ppermute | solution.py:57
  89.3 7.2 %collective-permute-start.23 = (bf16[256,512]{1,0:T(8,128)(2,1)}, bf16[256,512]{1,0:T(8,128)(2,1)S(1)}, u32[]{:S(2)}, u32[]{:S(2)}) collective-permute-start(bf16[256,512]{1,0:T(8,128)(2,1)} %get-tuple-element.103.refs_4_), channel_id=1, source_target_pairs={{0,24},{4,28},{8,16},{12,20},{16,8},{20,12},{24,0},{28,4},{32,56},... | collective-permute-start | bytes 786440 | tf_op jit(solution)/shard_map/ppermute | solution.py:57
  91.4 18.8 %collective-permute-start.21 = (bf16[256,512]{1,0:T(8,128)(2,1)}, bf16[256,512]{1,0:T(8,128)(2,1)S(1)}, u32[]{:S(2)}, u32[]{:S(2)}) collective-permute-start(bf16[256,512]{1,0:T(8,128)(2,1)} %get-tuple-element.102.refs_0_), channel_id=1, source_target_pairs={{0,24},{4,28},{8,16},{12,20},{16,8},{20,12},{24,0},{28,4},{32,56},... | collective-permute-start | bytes 786440 | tf_op jit(solution)/shard_map/ppermute | solution.py:57
  92.1 23.4 %collective-permute-start.24 = (bf16[256,512]{1,0:T(8,128)(2,1)}, bf16[256,512]{1,0:T(8,128)(2,1)S(1)}, u32[]{:S(2)}, u32[]{:S(2)}) collective-permute-start(bf16[256,512]{1,0:T(8,128)(2,1)} %get-tuple-element.103.refs_4_), channel_id=1, source_target_pairs={{0,8},{4,12},{8,0},{12,4},{16,24},{20,28},{24,16},{28,20},{32,40},... | collective-permute-start | bytes 786440 | tf_op jit(solution)/shard_map/ppermute | solution.py:57
  94.7 20.7 %collective-permute-start.22 = (bf16[256,512]{1,0:T(8,128)(2,1)S(1)}, bf16[256,512]{1,0:T(8,128)(2,1)S(1)}, u32[]{:S(2)}, u32[]{:S(2)}) collective-permute-start(bf16[256,512]{1,0:T(8,128)(2,1)S(1)} %collective-permute-done.20.refs_1_), channel_id=1, source_target_pairs={{0,24},{4,28},{8,16},{12,20},{16,8},{20,12},{24,0},{28,4},{32,56},... | collective-permute-start | bytes 786440 | tf_op jit(solution)/shard_map/ppermute | solution.py:57
  96.5 19.0 %collective-permute-start.25 = (bf16[256,512]{1,0:T(8,128)(2,1)S(1)}, bf16[256,512]{1,0:T(8,128)(2,1)}, u32[]{:S(2)}, u32[]{:S(2)}) collective-permute-start(bf16[256,512]{1,0:T(8,128)(2,1)S(1)} %collective-permute-done.23.refs_5_), channel_id=1, source_target_pairs={{0,8},{4,12},{8,0},{12,4},{16,24},{20,28},{24,16},{28,20},{32,40},... | collective-permute-start | bytes 786440 | tf_op jit(solution)/shard_map/ppermute | solution.py:57
  104.8 17.8 %collective-permute-start.29 = (f32[32,512]{1,0:T(8,128)S(1)}, f32[32,512]{1,0:T(8,128)S(1)}, u32[]{:S(2)}, u32[]{:S(2)}) collective-permute-start(f32[32,512]{1,0:T(8,128)S(1)} %get-tuple-element.116), channel_id=1, source_target_pairs={{0,0},{1,64},{2,128},{3,192},{4,4},{5,68},{6,132},{7,196},{8,8},{9... | collective-permute-start | bytes 196616 | tf_op jit(solution)/shard_map/ppermute | solution.py:145
  110.2 12.4 %collective-permute-start.30 = (f32[32,512]{1,0:T(8,128)S(1)}, f32[32,512]{1,0:T(8,128)S(1)}, u32[]{:S(2)}, u32[]{:S(2)}) collective-permute-start(f32[32,512]{1,0:T(8,128)S(1)} %get-tuple-element.115), channel_id=1, source_target_pairs={{0,4},{1,68},{2,132},{3,196},{4,0},{5,64},{6,128},{7,192},{8,12},{... | collective-permute-start | bytes 196616 | tf_op jit(solution)/shard_map/ppermute | solution.py:145
  115.4 1.0 copy-start.1
  116.4 0.9 copy-start.3
  120.4 3.6 %collective-permute-start.26 = (bf16[160,512]{1,0:T(8,128)(2,1)S(1)}, bf16[160,512]{1,0:T(8,128)(2,1)S(1)}, u32[]{:S(2)}, u32[]{:S(2)}) collective-permute-start(bf16[160,512]{1,0:T(8,128)(2,1)S(1)} %get-tuple-element.105), channel_id=1, source_target_pairs={{0,1},{1,0},{2,3},{3,2},{4,5},{5,4},{6,7},{7,6},{8,9},{9,8},{10,11... | collective-permute-start | bytes 491528 | tf_op jit(solution)/shard_map/ppermute | solution.py:573
  120.5 6.4 %collective-permute-start.27 = (bf16[160,512]{1,0:T(8,128)(2,1)S(1)}, bf16[160,512]{1,0:T(8,128)(2,1)S(1)}, u32[]{:S(2)}, u32[]{:S(2)}) collective-permute-start(bf16[160,512]{1,0:T(8,128)(2,1)S(1)} %get-tuple-element.106), channel_id=1, source_target_pairs={{0,2},{1,3},{2,0},{3,1},{4,6},{5,7},{6,4},{7,5},{8,10},{9,11},{10,... | collective-permute-start | bytes 491528 | tf_op jit(solution)/shard_map/ppermute | solution.py:573
  122.5 8.0 %collective-permute-start.28 = (bf16[160,512]{1,0:T(8,128)(2,1)S(1)}, bf16[160,512]{1,0:T(8,128)(2,1)S(1)}, u32[]{:S(2)}, u32[]{:S(2)}) collective-permute-start(bf16[160,512]{1,0:T(8,128)(2,1)S(1)} %get-tuple-element.107), channel_id=1, source_target_pairs={{0,3},{1,2},{2,1},{3,0},{4,7},{5,6},{6,5},{7,4},{8,11},{9,10},{10,... | collective-permute-start | bytes 491528 | tf_op jit(solution)/shard_map/ppermute | solution.py:573

commit v9 on v8

--- a/solution.py
+++ b/solution.py
@@ -60,13 +60,13 @@
 def weight_to_place(weight):
     n, tn = lax.axis_size("dp"), lax.axis_size("tensor")
     nz, ny, nx = sides_of(n)
+    order = block_order(n, tn)
     parts = []
     for turn in range(nx):
         pairs = []
         for j in range(tn):
-            for q in range(n):
-                y, z, x = q // (nz * nx), q // nx % nz, q % nx ^ turn
-                pairs.append((j * n + q, ((z * ny + y) * nx + x) * tn + j))
+            for y, z, x in np.ndindex(ny, nz, nx):
+                pairs.append((j * n + int(order[y, z, x ^ turn]), ((z * ny + y) * nx + x) * tn + j))
         parts.append(lax.ppermute(weight, ("dp", "tensor"), pairs))
     return parts
 
@@ -468,7 +468,7 @@
     return out[:2], out[2:-1] if ny > 1 else (None, None), out[-1]
 
 
-def project(info, hidden, weights, tn, nz, nx):
+def project(info, hidden, weights, tn, nz, ny, nx):
     pack, piece = hidden.shape
     rows = pack // tn
     vw = weights[0][0].shape[1]
@@ -490,7 +490,11 @@
             coming[p].wait()
             for k, distance in enumerate(distances):
                 for m in range(nx):
-                    block = ((y ^ far) * nz + (z ^ distance ^ near)) * nx + (x ^ m)
+                    y_at, z_at, x_at = y ^ far, z ^ distance ^ near, x ^ m
+                    if nz == 2 * tn:
+                        block = (((z_at // tn) * ny + y_at) * nx + x_at) * tn + z_at % tn
+                    else:
+                        block = (y_at * nz + z_at) * nx + x_at
                     at = pl.ds(pl.multiple_of(block * size, size), size)
                     weight_ref[at, :] = near_ref[p, (k * nx + m) * size:(k * nx + m + 1) * size, :]
         total_ref[0:OFFMAX, :] = jnp.zeros((OFFMAX, vw), F32)
@@ -606,9 +610,9 @@
     grad = jnp.concatenate(grad)
     weights = weight_twice(weight_once(held(weights, grad)))
     grad = reduce_along_z(grad)
-    hidden, grad = lax.optimization_barrier((hidden, grad))
+    values = project(info, hidden, weights, tn, nz, ny, nx)
+    values, grad = lax.optimization_barrier((values, grad))
     weight_grad = reduce_to_owner(grad)
-    values = project(info, hidden, weights, tn, nz, nx)
     values = [values[0]] + [swapped(values[s], s) for s in range(1, tn)]
     draft_values = spread(info, values)
 

time: 133 us -> 137 us (1.030)
  starting transfers between devices: 48.9 us -> 57.8 us
  waiting for transfers between devices: 46.4 us -> 37.9 us
  local copies, waits for them, and re-layouts: 3.26 us -> 6.93 us
    ppermute x14, waiting for transfers between devices: 18.6 us -> 10 us  [swapped(): return lax.ppermute(values, 'tensor', [(a, a ^ s) for a in range(tn)])]
    all_to_all x1, waiting for transfers between devices: 7.19 us -> 0.01 us  [reduce_along_z(): lax.all_to_all(grad.astype(BF16), 'dp', 0, 0, tiled=True, axis_index_grou...]
    ppermute x2, starting transfers between devices: 3.87 us -> 11 us  [weight_to_place(): parts.append(lax.ppermute(weight, ('dp', 'tensor'), pairs))]
    ppermute x13, waiting for transfers between devices: 20.6 us -> 27.6 us  [moved(): return lax.ppermute(values, 'dp', pairs)]
    unnamed x29 -> x39, local copies, waits for them, and re-layouts: 1.97 us -> 5.62 us
    ppermute x14, starting transfers between devices: 15 us -> 11.9 us  [swapped(): return lax.ppermute(values, 'tensor', [(a, a ^ s) for a in range(tn)])]
    ppermute x13, starting transfers between devices: 15.3 us -> 18.2 us  [moved(): return lax.ppermute(values, 'dp', pairs)]
    ppermute x2, starting transfers between devices: 10.6 us -> 12.5 us  [reduce_to_owner(): part = lax.ppermute(part, ('dp', 'tensor'), pairs)]
  transfers between devices with their start and end apart: 32 -> 32, of which waited for: 15 -> 16; matrix products, arithmetic and copies ran while one was open for 2% -> 1% of each run, Pallas kernels for 18% -> 18%
where the time goes in v9:
time: 137 us; the launch traced here: 136 us
  starting transfers between devices  57.8 us (42%)
  waiting for transfers between devices  37.9 us (28%)
  Pallas kernels  28.7 us (21%)
  local copies, waits for them, and re-layouts  6.93 us (5%)
  other arithmetic  3.76 us (3%)
    ppermute x13, waiting for transfers between devices, moved(): return lax.ppermute(values, 'dp', pairs)  27.6 us
    ppermute x13, starting transfers between devices, moved(): return lax.ppermute(values, 'dp', pairs)  18.2 us
    ppermute x2, starting transfers between devices, reduce_to_owner(): part = lax.ppermute(part, ('dp', 'tensor'), pairs)  12.5 us
    ppermute x14, starting transfers between devices, swapped(): return lax.ppermute(values, 'tensor', [(a, a ^ s) for a in range(tn)])  11.9 us
    ppermute x2, starting transfers between devices, weight_to_place(): parts.append(lax.ppermute(weight, ('dp', 'tensor'), pairs))  11 us
    ppermute x14, waiting for transfers between devices, swapped(): return lax.ppermute(values, 'tensor', [(a, a ^ s) for a in range(tn)])  10 us
    pallas_call x1, Pallas kernels, attend(): pl.pallas_call(functools.partial(attend_kernel, window), grid=(pack // bl...  8.18 us
    unnamed x39, local copies, waits for them, and re-layouts  5.62 us
  transfers between devices with their start and end apart: 32, of which 16 were waited for; matrix products, arithmetic and copies ran while one was open for 1% of the time, Pallas kernels for 18%

profile of v9, /device:TPU:1, one launch (start us, length us, event | category | flops | bytes accessed | tf_op | source)
XLA Modules:
  0.0 136.1 jit_solution(7905074992860768348)
XLA Ops:
  0.7 1.3 concatenate.16.info_ref
  2.0 2.7 %fold.1.refs_0_ = bf16[160,512]{1,0:T(8,128)(2,1)} custom-call(s32[15]{0:T(128)} %concatenate.16.info_ref, bf16[3,128,512]{2,1,0:T(8,128)(2,1)} %cotangent_ref.1), custom_call_target="tpu_custom_call" | custom-call | flops 62914560 | bytes 393216 | tf_op jit(solution)/shard_map/fold/pallas_call | solution.py:325
  4.7 2.1 %collective-permute-start = (bf16[160,512]{1,0:T(8,128)(2,1)}, bf16[160,512]{1,0:T(8,128)(2,1)S(1)}, u32[]{:S(2)}, u32[]{:S(2)}) collective-permute-start(bf16[160,512]{1,0:T(8,128)(2,1)} %fold.1.refs_0_), channel_id=1, source_target_pairs={{0,2},{1,3},{2,0},{3,1},{4,6},{5,7},{6,4},{7,5},{8,10},{9,11},{10,... | collective-permute-start | bytes 491528 | tf_op jit(solution)/shard_map/ppermute | solution.py:577
  6.9 4.8 %features.1 = (bf16[128,2048]{1,0:T(8,128)(2,1)}, bf16[128,2048]{1,0:T(8,128)(2,1)}, bf16[128,2048]{1,0:T(8,128)(2,1)}, bf16[128,2048]{1,0:T(8,128)(2,1)}) custom-call(s32[15]{0:T(128)} %concatenate.16.info_ref, bf16[128,8192]{1,0:T(8,128)(2,1)} %low_ref, bf16[128,8192]{1,0:T(8,128)(2,1)} %mid_ref.1, f32[3,8192]{1,0:T(4,128)} %gain_ref.3), custom_call_target="tpu_custom_call" | custom-call | flops 10485760 | bytes 6291456 | tf_op jit(solution)/shard_map/features/pallas_call | solution.py:226
  11.7 2.0 %collective-permute-start.6 = (bf16[128,2048]{1,0:T(8,128)(2,1)}, bf16[128,2048]{1,0:T(8,128)(2,1)S(1)}, u32[]{:S(2)}, u32[]{:S(2)}) collective-permute-start(bf16[128,2048]{1,0:T(8,128)(2,1)} %get-tuple-element.73), channel_id=1, source_target_pairs={{0,1},{1,0},{2,3},{3,2},{4,5},{5,4},{6,7},{7,6},{8,9},{9,8},{10,11... | collective-permute-start | bytes 1572872 | tf_op jit(solution)/shard_map/ppermute | solution.py:577
  13.7 1.1 collective-permute-start.7
  15.4 8.2 %attend.1 = (bf16[512,2048]{1,0:T(8,128)(2,1)S(1)}, f32[8,512]{1,0:T(8,128)S(1)}) custom-call(s32[15]{0:T(128)S(1)} %copy-done.9, bf16[512,2048]{1,0:T(8,128)(2,1)S(1)} %copy-done.11, bf16[512,256]{1,0:T(8,128)(2,1)S(1)} %copy-done.12, bf16[512,256]{1,0:T(8,128)(2,1)S(1)} %copy-done.13), custom_call_target="tpu_custom_call" | custom-call | flops 1610612736 | bytes 4194304 | tf_op jit(solution)/shard_map/attend/pallas_call | solution.py:277
  24.1 0.7 collective-permute-done.3
  25.2 2.8 %collective-permute-start.1 = (bf16[32,512]{1,0:T(8,128)(2,1)S(1)}, bf16[32,512]{1,0:T(8,128)(2,1)S(1)}, u32[]{:S(2)}, u32[]{:S(2)}) collective-permute-start(bf16[32,512]{1,0:T(8,128)(2,1)S(1)} %copy-done.17), channel_id=1, source_target_pairs={{0,0},{4,4},{1,32},{5,36},{2,64},{6,68},{3,96},{7,100},{32,128},{3... | collective-permute-start | bytes 98312 | tf_op jit(solution)/shard_map/ppermute | solution.py:70
  28.0 8.2 %collective-permute-start.2 = (bf16[32,512]{1,0:T(8,128)(2,1)S(1)}, bf16[32,512]{1,0:T(8,128)(2,1)S(1)}, u32[]{:S(2)}, u32[]{:S(2)}) collective-permute-start(bf16[32,512]{1,0:T(8,128)(2,1)S(1)} %copy-done.17), channel_id=1, source_target_pairs={{4,0},{0,4},{5,32},{1,36},{6,64},{2,68},{7,96},{3,100},{36,128},{3... | collective-permute-start | bytes 98312 | tf_op jit(solution)/shard_map/ppermute | solution.py:70
  36.4 2.4 %collective-permute-done.8.refs_3_ = bf16[128,2048]{1,0:T(8,128)(2,1)S(1)} collective-permute-done((bf16[128,2048]{1,0:T(8,128)(2,1)}, bf16[128,2048]{1,0:T(8,128)(2,1)S(1)}, u32[]{:S(2)}, u32[]{:S(2)}) %collective-permute-start.8) | collective-permute-done | bytes 524320 | tf_op jit(solution)/shard_map/ppermute | solution.py:577
  39.4 3.5 %merge.1 = (bf16[512,2048]{1,0:T(8,128)(2,1)S(1)}, f32[8,512]{1,0:T(8,128)S(1)}) custom-call(s32[15]{0:T(128)S(1)} %copy-done.9, f32[3,8192]{1,0:T(4,128)S(1)} %copy-done.5, bf16[512,2048]{1,0:T(8,128)(2,1)S(1)} %get-tuple-element.68.high_ref, bf16[128,2048]{1,0:T(8,128)(2,1)S(1)} %copy-done.4, bf16[128,2048]{1,0:T(8,128)(2,1)S(1)} %collective-permute-done.6.refs_1_, ...), custom_call_target="tpu_custom_call" | custom-call | flops 8388608 | bytes 6291456 | tf_op jit(solution)/shard_map/merge/pallas_call | solution.py:372
  42.9 0.8 collective-permute-start.10
  43.7 2.2 %collective-permute-start.11 = (f32[8,512]{1,0:T(8,128)S(1)}, f32[8,512]{1,0:T(8,128)S(1)}, u32[]{:S(2)}, u32[]{:S(2)}) collective-permute-start(f32[8,512]{1,0:T(8,128)S(1)} %get-tuple-element.87.refs_4_), channel_id=1, source_target_pairs={{0,2},{1,3},{2,0},{3,1},{4,6},{5,7},{6,4},{7,5},{8,10},{9,11},{10,... | collective-permute-start | bytes 49160 | tf_op jit(solution)/shard_map/ppermute | solution.py:577
  46.0 6.2 %collective-permute-start.13 = (bf16[64,512]{1,0:T(8,128)(2,1)S(1)}, bf16[64,512]{1,0:T(8,128)(2,1)S(1)}, u32[]{:S(2)}, u32[]{:S(2)}) collective-permute-start(bf16[64,512]{1,0:T(8,128)(2,1)S(1)} %constant_dynamic-update-slice_fusion), channel_id=1, source_target_pairs={{0,128},{4,132},{8,136},{12,140},{16,144},{20,148},{24,152},{28,15... | collective-permute-start | bytes 196616 | tf_op jit(solution)/shard_map/ppermute | solution.py:57
  52.2 4.8 %grads.1 = (f32[2,256,512]{2,1,0:T(8,128)S(1)}, f32[2,256,512]{2,1,0:T(8,128)S(1)}, bf16[2,256,512]{2,1,0:T(8,128)(2,1)S(1)}, bf16[2,256,512]{2,1,0:T(8,128)(2,1)S(1)}, bf16[512,2048]{1,0:T(8,128)(2,1)S(1)}) custom-call(s32[15]{0:T(128)S(1)} %copy-done.9, f32[1,8192]{1,0:T(1,128)S(1)} %bitcast.15, bf16[512,2048]{1,0:T(8,128)(2,1)S(1)} %get-tuple-element.82.merged_ref, ...), custom_call_target="tpu_custom_call" | custom-call | flops 1073741824 | bytes 8388608 | tf_op jit(solution)/shard_map/grads/pallas_call | solution.py:452
  57.1 1.4 %collective-permute-start.16 = (bf16[2,256,512]{2,1,0:T(8,128)(2,1)S(1)}, bf16[2,256,512]{2,1,0:T(8,128)(2,1)S(1)}, u32[]{:S(2)}, u32[]{:S(2)}) collective-permute-start(bf16[2,256,512]{2,1,0:T(8,128)(2,1)S(1)} %get-tuple-element.95), channel_id=1, source_target_pairs={{0,8},{4,12},{8,0},{12,4},{16,24},{20,28},{24,16},{28,20},{32,40},... | collective-permute-start | bytes 1572872 | tf_op jit(solution)/shard_map/ppermute | solution.py:57
  58.4 1.9 %collective-permute-start.17 = (bf16[2,256,512]{2,1,0:T(8,128)(2,1)S(1)}, bf16[2,256,512]{2,1,0:T(8,128)(2,1)S(1)}, u32[]{:S(2)}, u32[]{:S(2)}) collective-permute-start(bf16[2,256,512]{2,1,0:T(8,128)(2,1)S(1)} %get-tuple-element.96), channel_id=1, source_target_pairs={{0,24},{4,28},{8,16},{12,20},{16,8},{20,12},{24,0},{28,4},{32,56},... | collective-permute-start | bytes 1572872 | tf_op jit(solution)/shard_map/ppermute | solution.py:57
  60.4 1.6 %collective-permute-start.14 = (bf16[128,512]{1,0:T(8,128)(2,1)S(1)}, bf16[128,512]{1,0:T(8,128)(2,1)S(1)}, u32[]{:S(2)}, u32[]{:S(2)}) collective-permute-start(bf16[128,512]{1,0:T(8,128)(2,1)S(1)} %pad_maximum_fusion.1), channel_id=1, source_target_pairs={{0,64},{4,68},{8,72},{12,76},{16,80},{20,84},{24,88},{28,92},{32,9... | collective-permute-start | bytes 393224 | tf_op jit(solution)/shard_map/ppermute | solution.py:57
  62.0 7.0 %collective-permute-done.14 = bf16[128,512]{1,0:T(8,128)(2,1)S(1)} collective-permute-done((bf16[128,512]{1,0:T(8,128)(2,1)S(1)}, bf16[128,512]{1,0:T(8,128)(2,1)S(1)}, u32[]{:S(2)}, u32[]{:S(2)}) %collective-permute-start.14) | collective-permute-done | bytes 131104 | tf_op jit(solution)/shard_map/ppermute | solution.py:57
  69.2 0.8 collective-permute-done.16
  70.0 2.2 %collective-permute-done.17 = bf16[2,256,512]{2,1,0:T(8,128)(2,1)S(1)} collective-permute-done((bf16[2,256,512]{2,1,0:T(8,128)(2,1)S(1)}, bf16[2,256,512]{2,1,0:T(8,128)(2,1)S(1)}, u32[]{:S(2)}, u32[]{:S(2)}) %collective-permute-start.17) | collective-permute-done | bytes 524320 | tf_op jit(solution)/shard_map/ppermute | solution.py:57
  72.6 2.0 %collective-permute-start.18 = (bf16[256,512]{1,0:T(8,128)(2,1)S(1)}, bf16[256,512]{1,0:T(8,128)(2,1)S(1)}, u32[]{:S(2)}, u32[]{:S(2)}) collective-permute-start(bf16[256,512]{1,0:T(8,128)(2,1)S(1)} %get-tuple-element.117), channel_id=1, source_target_pairs={{0,24},{4,28},{8,16},{12,20},{16,8},{20,12},{24,0},{28,4},{32,56},... | collective-permute-start | bytes 786440 | tf_op jit(solution)/shard_map/ppermute | solution.py:57
  74.6 1.4 %collective-permute-done.15.refs_1_ = bf16[256,512]{1,0:T(8,128)(2,1)S(1)} collective-permute-done((bf16[256,512]{1,0:T(8,128)(2,1)S(1)}, bf16[256,512]{1,0:T(8,128)(2,1)S(1)}, u32[]{:S(2)}, u32[]{:S(2)}) %collective-permute-start.15) | collective-permute-done | bytes 262176 | tf_op jit(solution)/shard_map/ppermute | solution.py:57
  76.0 2.4 %collective-permute-done.19 = bf16[256,512]{1,0:T(8,128)(2,1)S(1)} collective-permute-done((bf16[256,512]{1,0:T(8,128)(2,1)S(1)}, bf16[256,512]{1,0:T(8,128)(2,1)S(1)}, u32[]{:S(2)}, u32[]{:S(2)}) %collective-permute-start.19) | collective-permute-done | bytes 262176 | tf_op jit(solution)/shard_map/ppermute | solution.py:57
  78.5 1.4 %collective-permute-done.18 = bf16[256,512]{1,0:T(8,128)(2,1)S(1)} collective-permute-done((bf16[256,512]{1,0:T(8,128)(2,1)S(1)}, bf16[256,512]{1,0:T(8,128)(2,1)S(1)}, u32[]{:S(2)}, u32[]{:S(2)}) %collective-permute-start.18) | collective-permute-done | bytes 262176 | tf_op jit(solution)/shard_map/ppermute | solution.py:57
  79.9 0.8 pad_maximum_fusion.refs_2_
  80.8 4.1 %all-to-all-start = ((bf16[8,64,512]{2,1,0:T(8,128)(2,1)}), bf16[8,64,512]{2,1,0:T(8,128)(2,1)}, u32[]{:S(2)}, u32[]{:S(2)}) async-start(bf16[8,64,512]{2,1,0:T(8,128)(2,1)} %bitcast.10), calls=%async_computation | async-start | bytes 1048576 | tf_op jit(solution)/shard_map/all_to_all | solution.py:125
  85.0 2.0 %collective-permute-start.23 = (bf16[256,512]{1,0:T(8,128)(2,1)}, bf16[256,512]{1,0:T(8,128)(2,1)S(1)}, u32[]{:S(2)}, u32[]{:S(2)}) collective-permute-start(bf16[256,512]{1,0:T(8,128)(2,1)} %get-tuple-element.105.refs_4_), channel_id=1, source_target_pairs={{0,24},{4,28},{8,16},{12,20},{16,8},{20,12},{24,0},{28,4},{32,56},... | collective-permute-start | bytes 786440 | tf_op jit(solution)/shard_map/ppermute | solution.py:57
  87.0 0.8 collective-permute-start.21
  88.0 2.5 %collective-permute-done.20.refs_1_ = bf16[256,512]{1,0:T(8,128)(2,1)S(1)} collective-permute-done((bf16[256,512]{1,0:T(8,128)(2,1)}, bf16[256,512]{1,0:T(8,128)(2,1)S(1)}, u32[]{:S(2)}, u32[]{:S(2)}) %collective-permute-start.20) | collective-permute-done | bytes 262176 | tf_op jit(solution)/shard_map/ppermute | solution.py:57
  90.5 1.9 %collective-permute-start.22 = (bf16[256,512]{1,0:T(8,128)(2,1)S(1)}, bf16[256,512]{1,0:T(8,128)(2,1)S(1)}, u32[]{:S(2)}, u32[]{:S(2)}) collective-permute-start(bf16[256,512]{1,0:T(8,128)(2,1)S(1)} %collective-permute-done.20.refs_1_), channel_id=1, source_target_pairs={{0,24},{4,28},{8,16},{12,20},{16,8},{20,12},{24,0},{28,4},{32,56},... | collective-permute-start | bytes 786440 | tf_op jit(solution)/shard_map/ppermute | solution.py:57
  92.3 4.2 %collective-permute-done.21.refs_2_ = bf16[256,512]{1,0:T(8,128)(2,1)S(1)} collective-permute-done((bf16[256,512]{1,0:T(8,128)(2,1)}, bf16[256,512]{1,0:T(8,128)(2,1)S(1)}, u32[]{:S(2)}, u32[]{:S(2)}) %collective-permute-start.21) | collective-permute-done | bytes 262176 | tf_op jit(solution)/shard_map/ppermute | solution.py:57
  96.6 5.6 %collective-permute-done.22.refs_3_ = bf16[256,512]{1,0:T(8,128)(2,1)S(1)} collective-permute-done((bf16[256,512]{1,0:T(8,128)(2,1)S(1)}, bf16[256,512]{1,0:T(8,128)(2,1)S(1)}, u32[]{:S(2)}, u32[]{:S(2)}) %collective-permute-start.22) | collective-permute-done | bytes 262176 | tf_op jit(solution)/shard_map/ppermute | solution.py:57
  102.2 0.7 copy-done.6
  102.9 0.9 copy-done.1
  103.9 0.9 copy-done.3
  104.8 0.9 copy-done.7
  105.8 3.0 %project.1 = (f32[160,512]{1,0:T(8,128)S(1)}, bf16[160,512]{1,0:T(8,128)(2,1)S(1)}, bf16[160,512]{1,0:T(8,128)(2,1)S(1)}, bf16[160,512]{1,0:T(8,128)(2,1)S(1)}) custom-call(s32[15]{0:T(128)S(1)} %copy-done.9, bf16[512,2048]{1,0:T(8,128)(2,1)S(1)} %get-tuple-element.89.hidden_ref, bf16[256,512]{1,0:T(8,128)(2,1)S(1)} %copy-done.1, ...), custom_call_target="tpu_custom_call" | custom-call | flops 1073741824 | bytes 4194304 | tf_op jit(solution)/shard_map/project/pallas_call | solution.py:508
  109.5 0.7 copy-done.15
  110.8 1.1 convert_reduce_fusion
  112.0 8.2 %collective-permute-start.29 = (f32[32,512]{1,0:T(8,128)S(1)}, f32[32,512]{1,0:T(8,128)S(1)}, u32[]{:S(2)}, u32[]{:S(2)}) collective-permute-start(f32[32,512]{1,0:T(8,128)S(1)} %get-tuple-element.122), channel_id=1, source_target_pairs={{0,0},{1,64},{2,128},{3,192},{4,4},{5,68},{6,132},{7,196},{8,8},{9... | collective-permute-start | bytes 196616 | tf_op jit(solution)/shard_map/ppermute | solution.py:145
  120.2 4.4 %collective-permute-start.30 = (f32[32,512]{1,0:T(8,128)S(1)}, f32[32,512]{1,0:T(8,128)S(1)}, u32[]{:S(2)}, u32[]{:S(2)}) collective-permute-start(f32[32,512]{1,0:T(8,128)S(1)} %get-tuple-element.121), channel_id=1, source_target_pairs={{0,4},{1,68},{2,132},{3,196},{4,0},{5,64},{6,128},{7,192},{8,12},{... | collective-permute-start | bytes 196616 | tf_op jit(solution)/shard_map/ppermute | solution.py:145
  124.5 1.7 %collective-permute-start.27 = (bf16[160,512]{1,0:T(8,128)(2,1)}, bf16[160,512]{1,0:T(8,128)(2,1)S(1)}, u32[]{:S(2)}, u32[]{:S(2)}) collective-permute-start(bf16[160,512]{1,0:T(8,128)(2,1)} %copy-done.15), channel_id=1, source_target_pairs={{0,2},{1,3},{2,0},{3,1},{4,6},{5,7},{6,4},{7,5},{8,10},{9,11},{10,... | collective-permute-start | bytes 491528 | tf_op jit(solution)/shard_map/ppermute | solution.py:577
  127.0 0.7 multiply_reduce_fusion
  128.4 2.2 %collective-permute-done.27.refs_2_ = bf16[160,512]{1,0:T(8,128)(2,1)S(1)} collective-permute-done((bf16[160,512]{1,0:T(8,128)(2,1)}, bf16[160,512]{1,0:T(8,128)(2,1)S(1)}, u32[]{:S(2)}, u32[]{:S(2)}) %collective-permute-start.27) | collective-permute-done | bytes 163872 | tf_op jit(solution)/shard_map/ppermute | solution.py:577
  130.6 3.9 %collective-permute-done.28.refs_3_ = bf16[160,512]{1,0:T(8,128)(2,1)S(1)} collective-permute-done((bf16[160,512]{1,0:T(8,128)(2,1)}, bf16[160,512]{1,0:T(8,128)(2,1)S(1)}, u32[]{:S(2)}, u32[]{:S(2)}) %collective-permute-start.28) | collective-permute-done | bytes 163872 | tf_op jit(solution)/shard_map/ppermute | solution.py:577
  134.4 1.7 %spread.1 = bf16[3,128,512]{2,1,0:T(8,128)(2,1)} custom-call(s32[15]{0:T(128)S(1)} %copy-done.9, f32[160,512]{1,0:T(8,128)S(1)} %get-tuple-element.110.refs_0_, bf16[160,512]{1,0:T(8,128)(2,1)S(1)} %collective-permute-done.26.refs_1_, bf16[160,512]{1,0:T(8,128)(2,1)S(1)} %collective-permute-done.27.refs_2_, bf16[160,512]{1,0:T(8,128)(2,1)S(1)} %collective-permute-done.28.refs_3_), custom_call_target="tpu_custom_call" | custom-call | flops 62914560 | bytes 1572864 | tf_op jit(solution)/shard_map/spread/pallas_call | solution.py:539
  (77 shorter events, 6.0 us)
Async XLA Ops:
  4.7 10.7 %copy-start.9 = (s32[15]{0:T(128)S(1)}, s32[15]{0:T(128)}, u32[]{:S(2)}) copy-start(s32[15]{0:T(128)} %concatenate.16.info_ref) | copy-start | bytes 184
  4.7 10.7 %copy-start.11 = (bf16[512,2048]{1,0:T(8,128)(2,1)S(1)}, bf16[512,2048]{1,0:T(8,128)(2,1)}, u32[]{:S(2)}) copy-start(bf16[512,2048]{1,0:T(8,128)(2,1)} %query_ref.1) | copy-start | bytes 6291460
  4.7 10.7 %copy-start.12 = (bf16[512,256]{1,0:T(8,128)(2,1)S(1)}, bf16[512,256]{1,0:T(8,128)(2,1)}, u32[]{:S(2)}) copy-start(bf16[512,256]{1,0:T(8,128)(2,1)} %key_ref.1) | copy-start | bytes 786436
  4.7 10.7 %copy-start.13 = (bf16[512,256]{1,0:T(8,128)(2,1)S(1)}, bf16[512,256]{1,0:T(8,128)(2,1)}, u32[]{:S(2)}) copy-start(bf16[512,256]{1,0:T(8,128)(2,1)} %value_ref.1) | copy-start | bytes 786436
  4.7 6.9 %collective-permute-start = (bf16[160,512]{1,0:T(8,128)(2,1)}, bf16[160,512]{1,0:T(8,128)(2,1)S(1)}, u32[]{:S(2)}, u32[]{:S(2)}) collective-permute-start(bf16[160,512]{1,0:T(8,128)(2,1)} %fold.1.refs_0_), channel_id=1, source_target_pairs={{0,2},{1,3},{2,0},{3,1},{4,6},{5,7},{6,4},{7,5},{8,10},{9,11},{10,... | collective-permute-start | bytes 491528 | tf_op jit(solution)/shard_map/ppermute | solution.py:577
  11.7 12.1 %copy-start.8 = (bf16[160,512]{1,0:T(8,128)(2,1)S(1)}, bf16[160,512]{1,0:T(8,128)(2,1)}, u32[]{:S(2)}) copy-start(bf16[160,512]{1,0:T(8,128)(2,1)} %fold.1.refs_0_) | copy-start | bytes 491524
  11.7 13.5 %copy-start.17 = (bf16[32,512]{1,0:T(8,128)(2,1)S(1)}, bf16[32,512]{1,0:T(8,128)(2,1)}, u32[]{:S(2)}) copy-start(bf16[32,512]{1,0:T(8,128)(2,1)} %param.18) | copy-start | bytes 98308
  11.7 27.7 %copy-start.4 = (bf16[128,2048]{1,0:T(8,128)(2,1)S(1)}, bf16[128,2048]{1,0:T(8,128)(2,1)}, u32[]{:S(2)}) copy-start(bf16[128,2048]{1,0:T(8,128)(2,1)} %get-tuple-element.69.refs_0_) | copy-start | bytes 1572868
  11.7 27.7 %copy-start.5 = (f32[3,8192]{1,0:T(4,128)S(1)}, f32[3,8192]{1,0:T(4,128)}, u32[]{:S(2)}) copy-start(f32[3,8192]{1,0:T(4,128)} %gain_ref.3) | copy-start | bytes 294916
  11.7 24.5 %collective-permute-start.6 = (bf16[128,2048]{1,0:T(8,128)(2,1)}, bf16[128,2048]{1,0:T(8,128)(2,1)S(1)}, u32[]{:S(2)}, u32[]{:S(2)}) collective-permute-start(bf16[128,2048]{1,0:T(8,128)(2,1)} %get-tuple-element.73), channel_id=1, source_target_pairs={{0,1},{1,0},{2,3},{3,2},{4,5},{5,4},{6,7},{7,6},{8,9},{9,8},{10,11... | collective-permute-start | bytes 1572872 | tf_op jit(solution)/shard_map/ppermute | solution.py:577
  13.7 22.7 %collective-permute-start.7 = (bf16[128,2048]{1,0:T(8,128)(2,1)}, bf16[128,2048]{1,0:T(8,128)(2,1)S(1)}, u32[]{:S(2)}, u32[]{:S(2)}) collective-permute-start(bf16[128,2048]{1,0:T(8,128)(2,1)} %get-tuple-element.75), channel_id=1, source_target_pairs={{0,2},{1,3},{2,0},{3,1},{4,6},{5,7},{6,4},{7,5},{8,10},{9,11},{10,... | collective-permute-start | bytes 1572872 | tf_op jit(solution)/shard_map/ppermute | solution.py:577
  14.8 24.0 %collective-permute-start.8 = (bf16[128,2048]{1,0:T(8,128)(2,1)}, bf16[128,2048]{1,0:T(8,128)(2,1)S(1)}, u32[]{:S(2)}, u32[]{:S(2)}) collective-permute-start(bf16[128,2048]{1,0:T(8,128)(2,1)} %get-tuple-element.76), channel_id=1, source_target_pairs={{0,3},{1,2},{2,1},{3,0},{4,7},{5,6},{6,5},{7,4},{8,11},{9,10},{10,... | collective-permute-start | bytes 1572872 | tf_op jit(solution)/shard_map/ppermute | solution.py:577
  23.6 1.2 collective-permute-start.3
  23.8 1.4 %collective-permute-start.4 = (bf16[160,512]{1,0:T(8,128)(2,1)S(1)}, bf16[160,512]{1,0:T(8,128)(2,1)S(1)}, u32[]{:S(2)}, u32[]{:S(2)}) collective-permute-start(bf16[160,512]{1,0:T(8,128)(2,1)S(1)} %copy-done.8), channel_id=1, source_target_pairs={{0,1},{1,0},{2,3},{3,2},{4,5},{5,4},{6,7},{7,6},{8,9},{9,8},{10,11... | collective-permute-start | bytes 491528 | tf_op jit(solution)/shard_map/ppermute | solution.py:577
  24.8 3.2 %collective-permute-start.5 = (bf16[160,512]{1,0:T(8,128)(2,1)S(1)}, bf16[160,512]{1,0:T(8,128)(2,1)S(1)}, u32[]{:S(2)}, u32[]{:S(2)}) collective-permute-start(bf16[160,512]{1,0:T(8,128)(2,1)S(1)} %collective-permute-done.refs_2_), channel_id=1, source_target_pairs={{0,1},{1,0},{2,3},{3,2},{4,5},{5,4},{6,7},{7,6},{8,9},{9,8},{10,11... | collective-permute-start | bytes 491528 | tf_op jit(solution)/shard_map/ppermute | solution.py:577
  25.2 17.7 %collective-permute-start.1 = (bf16[32,512]{1,0:T(8,128)(2,1)S(1)}, bf16[32,512]{1,0:T(8,128)(2,1)S(1)}, u32[]{:S(2)}, u32[]{:S(2)}) collective-permute-start(bf16[32,512]{1,0:T(8,128)(2,1)S(1)} %copy-done.17), channel_id=1, source_target_pairs={{0,0},{4,4},{1,32},{5,36},{2,64},{6,68},{3,96},{7,100},{32,128},{3... | collective-permute-start | bytes 98312 | tf_op jit(solution)/shard_map/ppermute | solution.py:70
  28.0 14.9 %collective-permute-start.2 = (bf16[32,512]{1,0:T(8,128)(2,1)S(1)}, bf16[32,512]{1,0:T(8,128)(2,1)S(1)}, u32[]{:S(2)}, u32[]{:S(2)}) collective-permute-start(bf16[32,512]{1,0:T(8,128)(2,1)S(1)} %copy-done.17), channel_id=1, source_target_pairs={{4,0},{0,4},{5,32},{1,36},{6,64},{2,68},{7,96},{3,100},{36,128},{3... | collective-permute-start | bytes 98312 | tf_op jit(solution)/shard_map/ppermute | solution.py:70
  36.2 15.9 %copy-start.10 = (f32[8192]{0:T(1024)S(1)}, f32[8192]{0:T(1024)}, u32[]{:S(2)}) copy-start(f32[8192]{0:T(1024)} %param.17) | copy-start | bytes 98308
  36.3 3.2 %collective-permute-start.9 = (f32[8,512]{1,0:T(8,128)S(1)}, f32[8,512]{1,0:T(8,128)S(1)}, u32[]{:S(2)}, u32[]{:S(2)}) collective-permute-start(f32[8,512]{1,0:T(8,128)S(1)} %add.65.refs_4_), channel_id=1, source_target_pairs={{0,2},{1,3},{2,0},{3,1},{4,6},{5,7},{6,4},{7,5},{8,10},{9,11},{10,... | collective-permute-start | bytes 49160 | tf_op jit(solution)/shard_map/ppermute | solution.py:577
  42.9 9.3 %collective-permute-start.10 = (f32[8,512]{1,0:T(8,128)S(1)}, f32[8,512]{1,0:T(8,128)S(1)}, u32[]{:S(2)}, u32[]{:S(2)}) collective-permute-start(f32[8,512]{1,0:T(8,128)S(1)} %get-tuple-element.87.refs_4_), channel_id=1, source_target_pairs={{0,1},{1,0},{2,3},{3,2},{4,5},{5,4},{6,7},{7,6},{8,9},{9,8},{10,11... | collective-permute-start | bytes 49160 | tf_op jit(solution)/shard_map/ppermute | solution.py:577
  43.7 8.5 %collective-permute-start.11 = (f32[8,512]{1,0:T(8,128)S(1)}, f32[8,512]{1,0:T(8,128)S(1)}, u32[]{:S(2)}, u32[]{:S(2)}) collective-permute-start(f32[8,512]{1,0:T(8,128)S(1)} %get-tuple-element.87.refs_4_), channel_id=1, source_target_pairs={{0,2},{1,3},{2,0},{3,1},{4,6},{5,7},{6,4},{7,5},{8,10},{9,11},{10,... | collective-permute-start | bytes 49160 | tf_op jit(solution)/shard_map/ppermute | solution.py:577
  45.9 6.3 %collective-permute-start.12 = (f32[8,512]{1,0:T(8,128)S(1)}, f32[8,512]{1,0:T(8,128)S(1)}, u32[]{:S(2)}, u32[]{:S(2)}) collective-permute-start(f32[8,512]{1,0:T(8,128)S(1)} %get-tuple-element.87.refs_4_), channel_id=1, source_target_pairs={{0,3},{1,2},{2,1},{3,0},{4,7},{5,6},{6,5},{7,4},{8,11},{9,10},{10,... | collective-permute-start | bytes 49160 | tf_op jit(solution)/shard_map/ppermute | solution.py:577
  46.0 11.1 %collective-permute-start.13 = (bf16[64,512]{1,0:T(8,128)(2,1)S(1)}, bf16[64,512]{1,0:T(8,128)(2,1)S(1)}, u32[]{:S(2)}, u32[]{:S(2)}) collective-permute-start(bf16[64,512]{1,0:T(8,128)(2,1)S(1)} %constant_dynamic-update-slice_fusion), channel_id=1, source_target_pairs={{0,128},{4,132},{8,136},{12,140},{16,144},{20,148},{24,152},{28,15... | collective-permute-start | bytes 196616 | tf_op jit(solution)/shard_map/ppermute | solution.py:57
  57.1 12.9 %collective-permute-start.16 = (bf16[2,256,512]{2,1,0:T(8,128)(2,1)S(1)}, bf16[2,256,512]{2,1,0:T(8,128)(2,1)S(1)}, u32[]{:S(2)}, u32[]{:S(2)}) collective-permute-start(bf16[2,256,512]{2,1,0:T(8,128)(2,1)S(1)} %get-tuple-element.95), channel_id=1, source_target_pairs={{0,8},{4,12},{8,0},{12,4},{16,24},{20,28},{24,16},{28,20},{32,40},... | collective-permute-start | bytes 1572872 | tf_op jit(solution)/shard_map/ppermute | solution.py:57
  58.4 13.7 %collective-permute-start.17 = (bf16[2,256,512]{2,1,0:T(8,128)(2,1)S(1)}, bf16[2,256,512]{2,1,0:T(8,128)(2,1)S(1)}, u32[]{:S(2)}, u32[]{:S(2)}) collective-permute-start(bf16[2,256,512]{2,1,0:T(8,128)(2,1)S(1)} %get-tuple-element.96), channel_id=1, source_target_pairs={{0,24},{4,28},{8,16},{12,20},{16,8},{20,12},{24,0},{28,4},{32,56},... | collective-permute-start | bytes 1572872 | tf_op jit(solution)/shard_map/ppermute | solution.py:57
  60.4 8.7 %collective-permute-start.14 = (bf16[128,512]{1,0:T(8,128)(2,1)S(1)}, bf16[128,512]{1,0:T(8,128)(2,1)S(1)}, u32[]{:S(2)}, u32[]{:S(2)}) collective-permute-start(bf16[128,512]{1,0:T(8,128)(2,1)S(1)} %pad_maximum_fusion.1), channel_id=1, source_target_pairs={{0,64},{4,68},{8,72},{12,76},{16,80},{20,84},{24,88},{28,92},{32,9... | collective-permute-start | bytes 393224 | tf_op jit(solution)/shard_map/ppermute | solution.py:57
  69.1 3.5 %copy-start = (bf16[256,512]{1,0:T(8,128)(2,1)}, bf16[256,512]{1,0:T(8,128)(2,1)S(1)}, u32[]{:S(2)}) copy-start(bf16[256,512]{1,0:T(8,128)(2,1)S(1)} %constant_dynamic-update-slice_fusion.2.refs_0_) | copy-start | bytes 786436
  69.1 6.9 %collective-permute-start.15 = (bf16[256,512]{1,0:T(8,128)(2,1)S(1)}, bf16[256,512]{1,0:T(8,128)(2,1)S(1)}, u32[]{:S(2)}, u32[]{:S(2)}) collective-permute-start(bf16[256,512]{1,0:T(8,128)(2,1)S(1)} %constant_dynamic-update-slice_fusion.2.refs_0_), channel_id=1, source_target_pairs={{0,32},{4,36},{8,40},{12,44},{16,48},{20,52},{24,56},{28,60},{32,0... | collective-permute-start | bytes 786440 | tf_op jit(solution)/shard_map/ppermute | solution.py:57
  72.3 6.1 %collective-permute-start.19 = (bf16[256,512]{1,0:T(8,128)(2,1)S(1)}, bf16[256,512]{1,0:T(8,128)(2,1)S(1)}, u32[]{:S(2)}, u32[]{:S(2)}) collective-permute-start(bf16[256,512]{1,0:T(8,128)(2,1)S(1)} %get-tuple-element.119), channel_id=1, source_target_pairs={{0,8},{4,12},{8,0},{12,4},{16,24},{20,28},{24,16},{28,20},{32,40},... | collective-permute-start | bytes 786440 | tf_op jit(solution)/shard_map/ppermute | solution.py:57
  72.6 7.3 %collective-permute-start.18 = (bf16[256,512]{1,0:T(8,128)(2,1)S(1)}, bf16[256,512]{1,0:T(8,128)(2,1)S(1)}, u32[]{:S(2)}, u32[]{:S(2)}) collective-permute-start(bf16[256,512]{1,0:T(8,128)(2,1)S(1)} %get-tuple-element.117), channel_id=1, source_target_pairs={{0,24},{4,28},{8,16},{12,20},{16,8},{20,12},{24,0},{28,4},{32,56},... | collective-permute-start | bytes 786440 | tf_op jit(solution)/shard_map/ppermute | solution.py:57
  76.0 4.8 %copy-start.2 = (bf16[256,512]{1,0:T(8,128)(2,1)}, bf16[256,512]{1,0:T(8,128)(2,1)S(1)}, u32[]{:S(2)}) copy-start(bf16[256,512]{1,0:T(8,128)(2,1)S(1)} %collective-permute-done.15.refs_1_) | copy-start | bytes 786436
  80.8 30.0 %all-to-all-start = ((bf16[8,64,512]{2,1,0:T(8,128)(2,1)}), bf16[8,64,512]{2,1,0:T(8,128)(2,1)}, u32[]{:S(2)}, u32[]{:S(2)}) async-start(bf16[8,64,512]{2,1,0:T(8,128)(2,1)} %bitcast.10), calls=%async_computation | async-start | bytes 1048576 | tf_op jit(solution)/shard_map/all_to_all | solution.py:125
  84.9 5.5 %collective-permute-start.20 = (bf16[256,512]{1,0:T(8,128)(2,1)}, bf16[256,512]{1,0:T(8,128)(2,1)S(1)}, u32[]{:S(2)}, u32[]{:S(2)}) collective-permute-start(bf16[256,512]{1,0:T(8,128)(2,1)} %get-tuple-element.104.refs_0_), channel_id=1, source_target_pairs={{0,8},{4,12},{8,0},{12,4},{16,24},{20,28},{24,16},{28,20},{32,40},... | collective-permute-start | bytes 786440 | tf_op jit(solution)/shard_map/ppermute | solution.py:57
  85.0 7.3 %collective-permute-start.23 = (bf16[256,512]{1,0:T(8,128)(2,1)}, bf16[256,512]{1,0:T(8,128)(2,1)S(1)}, u32[]{:S(2)}, u32[]{:S(2)}) collective-permute-start(bf16[256,512]{1,0:T(8,128)(2,1)} %get-tuple-element.105.refs_4_), channel_id=1, source_target_pairs={{0,24},{4,28},{8,16},{12,20},{16,8},{20,12},{24,0},{28,4},{32,56},... | collective-permute-start | bytes 786440 | tf_op jit(solution)/shard_map/ppermute | solution.py:57
  87.0 9.6 %collective-permute-start.21 = (bf16[256,512]{1,0:T(8,128)(2,1)}, bf16[256,512]{1,0:T(8,128)(2,1)S(1)}, u32[]{:S(2)}, u32[]{:S(2)}) collective-permute-start(bf16[256,512]{1,0:T(8,128)(2,1)} %get-tuple-element.104.refs_0_), channel_id=1, source_target_pairs={{0,24},{4,28},{8,16},{12,20},{16,8},{20,12},{24,0},{28,4},{32,56},... | collective-permute-start | bytes 786440 | tf_op jit(solution)/shard_map/ppermute | solution.py:57
  87.8 8.8 %collective-permute-start.24 = (bf16[256,512]{1,0:T(8,128)(2,1)}, bf16[256,512]{1,0:T(8,128)(2,1)S(1)}, u32[]{:S(2)}, u32[]{:S(2)}) collective-permute-start(bf16[256,512]{1,0:T(8,128)(2,1)} %get-tuple-element.105.refs_4_), channel_id=1, source_target_pairs={{0,8},{4,12},{8,0},{12,4},{16,24},{20,28},{24,16},{28,20},{32,40},... | collective-permute-start | bytes 786440 | tf_op jit(solution)/shard_map/ppermute | solution.py:57
  90.5 11.7 %collective-permute-start.22 = (bf16[256,512]{1,0:T(8,128)(2,1)S(1)}, bf16[256,512]{1,0:T(8,128)(2,1)S(1)}, u32[]{:S(2)}, u32[]{:S(2)}) collective-permute-start(bf16[256,512]{1,0:T(8,128)(2,1)S(1)} %collective-permute-done.20.refs_1_), channel_id=1, source_target_pairs={{0,24},{4,28},{8,16},{12,20},{16,8},{20,12},{24,0},{28,4},{32,56},... | collective-permute-start | bytes 786440 | tf_op jit(solution)/shard_map/ppermute | solution.py:57
  92.3 10.6 %collective-permute-start.25 = (bf16[256,512]{1,0:T(8,128)(2,1)S(1)}, bf16[256,512]{1,0:T(8,128)(2,1)}, u32[]{:S(2)}, u32[]{:S(2)}) collective-permute-start(bf16[256,512]{1,0:T(8,128)(2,1)S(1)} %collective-permute-done.23.refs_5_), channel_id=1, source_target_pairs={{0,8},{4,12},{8,0},{12,4},{16,24},{20,28},{24,16},{28,20},{32,40},... | collective-permute-start | bytes 786440 | tf_op jit(solution)/shard_map/ppermute | solution.py:57
  102.2 0.7 copy-start.6
  102.9 1.0 copy-start.1
  103.9 0.9 copy-start.3
  104.8 0.9 copy-start.7
  109.5 0.7 copy-start.15
  112.0 14.7 %collective-permute-start.29 = (f32[32,512]{1,0:T(8,128)S(1)}, f32[32,512]{1,0:T(8,128)S(1)}, u32[]{:S(2)}, u32[]{:S(2)}) collective-permute-start(f32[32,512]{1,0:T(8,128)S(1)} %get-tuple-element.122), channel_id=1, source_target_pairs={{0,0},{1,64},{2,128},{3,192},{4,4},{5,68},{6,132},{7,196},{8,8},{9... | collective-permute-start | bytes 196616 | tf_op jit(solution)/shard_map/ppermute | solution.py:145
  120.2 6.9 %collective-permute-start.30 = (f32[32,512]{1,0:T(8,128)S(1)}, f32[32,512]{1,0:T(8,128)S(1)}, u32[]{:S(2)}, u32[]{:S(2)}) collective-permute-start(f32[32,512]{1,0:T(8,128)S(1)} %get-tuple-element.121), channel_id=1, source_target_pairs={{0,4},{1,68},{2,132},{3,196},{4,0},{5,64},{6,128},{7,192},{8,12},{... | collective-permute-start | bytes 196616 | tf_op jit(solution)/shard_map/ppermute | solution.py:145
  124.5 3.9 %collective-permute-start.26 = (bf16[160,512]{1,0:T(8,128)(2,1)}, bf16[160,512]{1,0:T(8,128)(2,1)S(1)}, u32[]{:S(2)}, u32[]{:S(2)}) collective-permute-start(bf16[160,512]{1,0:T(8,128)(2,1)} %copy-done.16), channel_id=1, source_target_pairs={{0,1},{1,0},{2,3},{3,2},{4,5},{5,4},{6,7},{7,6},{8,9},{9,8},{10,11... | collective-permute-start | bytes 491528 | tf_op jit(solution)/shard_map/ppermute | solution.py:577
  124.5 6.1 %collective-permute-start.27 = (bf16[160,512]{1,0:T(8,128)(2,1)}, bf16[160,512]{1,0:T(8,128)(2,1)S(1)}, u32[]{:S(2)}, u32[]{:S(2)}) collective-permute-start(bf16[160,512]{1,0:T(8,128)(2,1)} %copy-done.15), channel_id=1, source_target_pairs={{0,2},{1,3},{2,0},{3,1},{4,6},{5,7},{6,4},{7,5},{8,10},{9,11},{10,... | collective-permute-start | bytes 491528 | tf_op jit(solution)/shard_map/ppermute | solution.py:577
  126.3 8.2 %collective-permute-start.28 = (bf16[160,512]{1,0:T(8,128)(2,1)}, bf16[160,512]{1,0:T(8,128)(2,1)S(1)}, u32[]{:S(2)}, u32[]{:S(2)}) collective-permute-start(bf16[160,512]{1,0:T(8,128)(2,1)} %copy-done.14), channel_id=1, source_target_pairs={{0,3},{1,2},{2,1},{3,0},{4,7},{5,6},{6,5},{7,4},{8,11},{9,10},{10,... | collective-permute-start | bytes 491528 | tf_op jit(solution)/shard_map/ppermute | solution.py:577
  (2 other events, 1.3 us)

commit v10 on v9

--- a/solution.py
+++ b/solution.py
@@ -507,7 +507,7 @@
 
     return pl.pallas_call(
         kernel,
-        in_specs=[SMEM, VMEM] + [HBM] * len(parts),
+        in_specs=[SMEM, VMEM] + [pl.BlockSpec(memory_space=pl.ANY)] * len(parts),
         out_specs=[VMEM] * tn,
         out_shape=[jax.ShapeDtypeStruct((rows + OFFMAX, vw), F32 if s == 0 else BF16) for s in range(tn)],
         scratch_shapes=[
@@ -566,8 +566,11 @@
     i = lax.axis_index("dp")
     flat = i * tn + j
     nz, ny, nx = sides_of(n)
-    place = jnp.stack([j, i // nx % ny, i // (ny * nx), i % nx]).astype(jnp.int32)
-    info = jnp.concatenate([place, step_offsets, doc_lengths.reshape(-1)])
+    lengths = doc_lengths.reshape(-1)
+    count = LENGTHS + lengths.size
+    info = jnp.pad(step_offsets, (OFFSETS, lengths.size)) + jnp.pad(lengths, (LENGTHS, 0))
+    for at, value in enumerate((j, i // nx % ny, i // (ny * nx), i % nx)):
+        info = jnp.where(lax.iota(jnp.int32, count) == at, value.astype(jnp.int32), info)
     width = low_feature.shape[1]
     piece = width // tn
     pack = target_queries.shape[0]
@@ -610,9 +613,9 @@
     grad = jnp.concatenate(grad)
     weights = weight_twice(weight_once(held(weights, grad)))
     grad = reduce_along_z(grad)
+    hidden, grad = lax.optimization_barrier((hidden, grad))
+    weight_grad = reduce_to_owner(grad)
     values = project(info, hidden, weights, tn, nz, ny, nx)
-    values, grad = lax.optimization_barrier((values, grad))
-    weight_grad = reduce_to_owner(grad)
     values = [values[0]] + [swapped(values[s], s) for s in range(1, tn)]
     draft_values = spread(info, values)
 

time: 137 us -> 130 us (0.949)
  local copies, waits for them, and re-layouts: 6.93 us -> 2 us
  waiting for transfers between devices: 37.9 us -> 34.7 us
    ppermute x13, waiting for transfers between devices: 27.6 us -> 17.8 us  [moved(): return lax.ppermute(values, 'dp', pairs)]
    all_to_all x1, waiting for transfers between devices: 0.01 us -> 6.95 us  [reduce_along_z(): lax.all_to_all(grad.astype(BF16), 'dp', 0, 0, tiled=True, axis_index_grou...]
    unnamed x39 -> x29, local copies, waits for them, and re-layouts: 5.62 us -> 1.97 us
  transfers between devices with their start and end apart: 32 -> 32, of which waited for: 16 -> 14; matrix products, arithmetic and copies ran while one was open for 1% -> 2% of each run, Pallas kernels for 18% -> 19%
where the time goes in v10:
time: 130 us; the launch traced here: 129 us
  starting transfers between devices  57.6 us (44%)
  waiting for transfers between devices  34.7 us (27%)
  Pallas kernels  28.7 us (22%)
  other arithmetic  5.05 us (4%)
  local copies, waits for them, and re-layouts  2 us (2%)
    ppermute x13, starting transfers between devices, moved(): return lax.ppermute(values, 'dp', pairs)  18.2 us
    ppermute x13, waiting for transfers between devices, moved(): return lax.ppermute(values, 'dp', pairs)  17.8 us
    ppermute x2, starting transfers between devices, reduce_to_owner(): part = lax.ppermute(part, ('dp', 'tensor'), pairs)  12.4 us
    ppermute x14, starting transfers between devices, swapped(): return lax.ppermute(values, 'tensor', [(a, a ^ s) for a in range(tn)])  11.9 us
    ppermute x2, starting transfers between devices, weight_to_place(): parts.append(lax.ppermute(weight, ('dp', 'tensor'), pairs))  11.1 us
    ppermute x14, waiting for transfers between devices, swapped(): return lax.ppermute(values, 'tensor', [(a, a ^ s) for a in range(tn)])  9.97 us
    pallas_call x1, Pallas kernels, attend(): pl.pallas_call(functools.partial(attend_kernel, window), grid=(pack // bl...  8.17 us
    all_to_all x1, waiting for transfers between devices, reduce_along_z(): lax.all_to_all(grad.astype(BF16), 'dp', 0, 0, tiled=True, axis_index_grou...  6.95 us
  transfers between devices with their start and end apart: 32, of which 14 were waited for; matrix products, arithmetic and copies ran while one was open for 2% of the time, Pallas kernels for 19%

profile of v10, /device:TPU:1, one launch (start us, length us, event | category | flops | bytes accessed | tf_op | source)
XLA Modules:
  0.0 129.1 jit_solution(5731067030115760502)
XLA Ops:
  0.7 1.3 compare_select_fusion.3.info_ref
  1.9 2.7 %fold.1.refs_0_ = bf16[160,512]{1,0:T(8,128)(2,1)} custom-call(s32[15]{0:T(128)} %compare_select_fusion.3.info_ref, bf16[3,128,512]{2,1,0:T(8,128)(2,1)} %cotangent_ref.1), custom_call_target="tpu_custom_call" | custom-call | flops 62914560 | bytes 393216 | tf_op jit(solution)/shard_map/fold/pallas_call | solution.py:325
  4.7 2.1 %collective-permute-start = (bf16[160,512]{1,0:T(8,128)(2,1)}, bf16[160,512]{1,0:T(8,128)(2,1)S(1)}, u32[]{:S(2)}, u32[]{:S(2)}) collective-permute-start(bf16[160,512]{1,0:T(8,128)(2,1)} %fold.1.refs_0_), channel_id=1, source_target_pairs={{0,2},{1,3},{2,0},{3,1},{4,6},{5,7},{6,4},{7,5},{8,10},{9,11},{10,... | collective-permute-start | bytes 491528 | tf_op jit(solution)/shard_map/ppermute | solution.py:580
  6.8 4.8 %features.1 = (bf16[128,2048]{1,0:T(8,128)(2,1)}, bf16[128,2048]{1,0:T(8,128)(2,1)}, bf16[128,2048]{1,0:T(8,128)(2,1)}, bf16[128,2048]{1,0:T(8,128)(2,1)}) custom-call(s32[15]{0:T(128)} %compare_select_fusion.3.info_ref, bf16[128,8192]{1,0:T(8,128)(2,1)} %low_ref, bf16[128,8192]{1,0:T(8,128)(2,1)} %mid_ref.1, f32[3,8192]{1,0:T(4,128)} %gain_ref.3), custom_call_target="tpu_custom_call" | custom-call | flops 10485760 | bytes 6291456 | tf_op jit(solution)/shard_map/features/pallas_call | solution.py:226
  11.7 2.0 %collective-permute-start.6 = (bf16[128,2048]{1,0:T(8,128)(2,1)}, bf16[128,2048]{1,0:T(8,128)(2,1)S(1)}, u32[]{:S(2)}, u32[]{:S(2)}) collective-permute-start(bf16[128,2048]{1,0:T(8,128)(2,1)} %get-tuple-element.70), channel_id=1, source_target_pairs={{0,1},{1,0},{2,3},{3,2},{4,5},{5,4},{6,7},{7,6},{8,9},{9,8},{10,11... | collective-permute-start | bytes 1572872 | tf_op jit(solution)/shard_map/ppermute | solution.py:580
  13.7 1.1 collective-permute-start.7
  14.7 0.7 collective-permute-start.8
  15.4 8.2 %attend.1 = (bf16[512,2048]{1,0:T(8,128)(2,1)S(1)}, f32[8,512]{1,0:T(8,128)S(1)}) custom-call(s32[15]{0:T(128)S(1)} %copy-done.7, bf16[512,2048]{1,0:T(8,128)(2,1)S(1)} %copy-done.9, bf16[512,256]{1,0:T(8,128)(2,1)S(1)} %copy-done.10, bf16[512,256]{1,0:T(8,128)(2,1)S(1)} %copy-done.11), custom_call_target="tpu_custom_call" | custom-call | flops 1610612736 | bytes 4194304 | tf_op jit(solution)/shard_map/attend/pallas_call | solution.py:277
  24.1 0.7 collective-permute-done.3
  25.2 2.8 %collective-permute-start.1 = (bf16[32,512]{1,0:T(8,128)(2,1)S(1)}, bf16[32,512]{1,0:T(8,128)(2,1)S(1)}, u32[]{:S(2)}, u32[]{:S(2)}) collective-permute-start(bf16[32,512]{1,0:T(8,128)(2,1)S(1)} %copy-done.12), channel_id=1, source_target_pairs={{0,0},{4,4},{1,32},{5,36},{2,64},{6,68},{3,96},{7,100},{32,128},{3... | collective-permute-start | bytes 98312 | tf_op jit(solution)/shard_map/ppermute | solution.py:70
  28.0 8.2 %collective-permute-start.2 = (bf16[32,512]{1,0:T(8,128)(2,1)S(1)}, bf16[32,512]{1,0:T(8,128)(2,1)S(1)}, u32[]{:S(2)}, u32[]{:S(2)}) collective-permute-start(bf16[32,512]{1,0:T(8,128)(2,1)S(1)} %copy-done.12), channel_id=1, source_target_pairs={{4,0},{0,4},{5,32},{1,36},{6,64},{2,68},{7,96},{3,100},{36,128},{3... | collective-permute-start | bytes 98312 | tf_op jit(solution)/shard_map/ppermute | solution.py:70
  36.4 2.4 %collective-permute-done.8.refs_3_ = bf16[128,2048]{1,0:T(8,128)(2,1)S(1)} collective-permute-done((bf16[128,2048]{1,0:T(8,128)(2,1)}, bf16[128,2048]{1,0:T(8,128)(2,1)S(1)}, u32[]{:S(2)}, u32[]{:S(2)}) %collective-permute-start.8) | collective-permute-done | bytes 524320 | tf_op jit(solution)/shard_map/ppermute | solution.py:580
  38.8 0.6 collective-permute-done.9.refs_5_
  39.4 3.5 %merge.1 = (bf16[512,2048]{1,0:T(8,128)(2,1)S(1)}, f32[8,512]{1,0:T(8,128)S(1)}) custom-call(s32[15]{0:T(128)S(1)} %copy-done.7, f32[3,8192]{1,0:T(4,128)S(1)} %copy-done.5, bf16[512,2048]{1,0:T(8,128)(2,1)S(1)} %get-tuple-element.65.high_ref, bf16[128,2048]{1,0:T(8,128)(2,1)S(1)} %copy-done.4, bf16[128,2048]{1,0:T(8,128)(2,1)S(1)} %collective-permute-done.6.refs_1_, ...), custom_call_target="tpu_custom_call" | custom-call | flops 8388608 | bytes 6291456 | tf_op jit(solution)/shard_map/merge/pallas_call | solution.py:372
  42.9 0.8 collective-permute-start.10
  43.7 2.2 %collective-permute-start.11 = (f32[8,512]{1,0:T(8,128)S(1)}, f32[8,512]{1,0:T(8,128)S(1)}, u32[]{:S(2)}, u32[]{:S(2)}) collective-permute-start(f32[8,512]{1,0:T(8,128)S(1)} %get-tuple-element.84.refs_4_), channel_id=1, source_target_pairs={{0,2},{1,3},{2,0},{3,1},{4,6},{5,7},{6,4},{7,5},{8,10},{9,11},{10,... | collective-permute-start | bytes 49160 | tf_op jit(solution)/shard_map/ppermute | solution.py:580
  46.0 6.2 %collective-permute-start.13 = (bf16[64,512]{1,0:T(8,128)(2,1)S(1)}, bf16[64,512]{1,0:T(8,128)(2,1)S(1)}, u32[]{:S(2)}, u32[]{:S(2)}) collective-permute-start(bf16[64,512]{1,0:T(8,128)(2,1)S(1)} %constant_dynamic-update-slice_fusion), channel_id=1, source_target_pairs={{0,128},{4,132},{8,136},{12,140},{16,144},{20,148},{24,152},{28,15... | collective-permute-start | bytes 196616 | tf_op jit(solution)/shard_map/ppermute | solution.py:57
  52.2 4.8 %grads.1 = (f32[2,256,512]{2,1,0:T(8,128)S(1)}, f32[2,256,512]{2,1,0:T(8,128)S(1)}, bf16[2,256,512]{2,1,0:T(8,128)(2,1)S(1)}, bf16[2,256,512]{2,1,0:T(8,128)(2,1)S(1)}, bf16[512,2048]{1,0:T(8,128)(2,1)S(1)}) custom-call(s32[15]{0:T(128)S(1)} %copy-done.7, f32[1,8192]{1,0:T(1,128)S(1)} %bitcast.11, bf16[512,2048]{1,0:T(8,128)(2,1)S(1)} %get-tuple-element.79.merged_ref, ...), custom_call_target="tpu_custom_call" | custom-call | flops 1073741824 | bytes 8388608 | tf_op jit(solution)/shard_map/grads/pallas_call | solution.py:452
  57.0 1.4 %collective-permute-start.16 = (bf16[2,256,512]{2,1,0:T(8,128)(2,1)S(1)}, bf16[2,256,512]{2,1,0:T(8,128)(2,1)S(1)}, u32[]{:S(2)}, u32[]{:S(2)}) collective-permute-start(bf16[2,256,512]{2,1,0:T(8,128)(2,1)S(1)} %get-tuple-element.92), channel_id=1, source_target_pairs={{0,8},{4,12},{8,0},{12,4},{16,24},{20,28},{24,16},{28,20},{32,40},... | collective-permute-start | bytes 1572872 | tf_op jit(solution)/shard_map/ppermute | solution.py:57
  58.4 1.9 %collective-permute-start.17 = (bf16[2,256,512]{2,1,0:T(8,128)(2,1)S(1)}, bf16[2,256,512]{2,1,0:T(8,128)(2,1)S(1)}, u32[]{:S(2)}, u32[]{:S(2)}) collective-permute-start(bf16[2,256,512]{2,1,0:T(8,128)(2,1)S(1)} %get-tuple-element.93), channel_id=1, source_target_pairs={{0,24},{4,28},{8,16},{12,20},{16,8},{20,12},{24,0},{28,4},{32,56},... | collective-permute-start | bytes 1572872 | tf_op jit(solution)/shard_map/ppermute | solution.py:57
  60.4 1.6 %collective-permute-start.14 = (bf16[128,512]{1,0:T(8,128)(2,1)S(1)}, bf16[128,512]{1,0:T(8,128)(2,1)S(1)}, u32[]{:S(2)}, u32[]{:S(2)}) collective-permute-start(bf16[128,512]{1,0:T(8,128)(2,1)S(1)} %pad_maximum_fusion.1), channel_id=1, source_target_pairs={{0,64},{4,68},{8,72},{12,76},{16,80},{20,84},{24,88},{28,92},{32,9... | collective-permute-start | bytes 393224 | tf_op jit(solution)/shard_map/ppermute | solution.py:57
  62.0 7.0 %collective-permute-done.14 = bf16[128,512]{1,0:T(8,128)(2,1)S(1)} collective-permute-done((bf16[128,512]{1,0:T(8,128)(2,1)S(1)}, bf16[128,512]{1,0:T(8,128)(2,1)S(1)}, u32[]{:S(2)}, u32[]{:S(2)}) %collective-permute-start.14) | collective-permute-done | bytes 131104 | tf_op jit(solution)/shard_map/ppermute | solution.py:57
  69.2 0.8 collective-permute-done.16
  70.0 2.2 %collective-permute-done.17 = bf16[2,256,512]{2,1,0:T(8,128)(2,1)S(1)} collective-permute-done((bf16[2,256,512]{2,1,0:T(8,128)(2,1)S(1)}, bf16[2,256,512]{2,1,0:T(8,128)(2,1)S(1)}, u32[]{:S(2)}, u32[]{:S(2)}) %collective-permute-start.17) | collective-permute-done | bytes 524320 | tf_op jit(solution)/shard_map/ppermute | solution.py:57
  72.6 2.0 %collective-permute-start.18 = (bf16[256,512]{1,0:T(8,128)(2,1)S(1)}, bf16[256,512]{1,0:T(8,128)(2,1)S(1)}, u32[]{:S(2)}, u32[]{:S(2)}) collective-permute-start(bf16[256,512]{1,0:T(8,128)(2,1)S(1)} %get-tuple-element.111), channel_id=1, source_target_pairs={{0,24},{4,28},{8,16},{12,20},{16,8},{20,12},{24,0},{28,4},{32,56},... | collective-permute-start | bytes 786440 | tf_op jit(solution)/shard_map/ppermute | solution.py:57
  74.6 1.3 %collective-permute-done.15.refs_1_ = bf16[256,512]{1,0:T(8,128)(2,1)S(1)} collective-permute-done((bf16[256,512]{1,0:T(8,128)(2,1)S(1)}, bf16[256,512]{1,0:T(8,128)(2,1)S(1)}, u32[]{:S(2)}, u32[]{:S(2)}) %collective-permute-start.15) | collective-permute-done | bytes 262176 | tf_op jit(solution)/shard_map/ppermute | solution.py:57
  75.9 2.5 %collective-permute-done.19 = bf16[256,512]{1,0:T(8,128)(2,1)S(1)} collective-permute-done((bf16[256,512]{1,0:T(8,128)(2,1)S(1)}, bf16[256,512]{1,0:T(8,128)(2,1)S(1)}, u32[]{:S(2)}, u32[]{:S(2)}) %collective-permute-start.19) | collective-permute-done | bytes 262176 | tf_op jit(solution)/shard_map/ppermute | solution.py:57
  78.5 1.4 %collective-permute-done.18 = bf16[256,512]{1,0:T(8,128)(2,1)S(1)} collective-permute-done((bf16[256,512]{1,0:T(8,128)(2,1)S(1)}, bf16[256,512]{1,0:T(8,128)(2,1)S(1)}, u32[]{:S(2)}, u32[]{:S(2)}) %collective-permute-start.18) | collective-permute-done | bytes 262176 | tf_op jit(solution)/shard_map/ppermute | solution.py:57
  79.9 0.9 pad_maximum_fusion.refs_2_
  80.8 4.2 %all-to-all-start = ((bf16[8,64,512]{2,1,0:T(8,128)(2,1)}), bf16[8,64,512]{2,1,0:T(8,128)(2,1)}, u32[]{:S(2)}, u32[]{:S(2)}) async-start(bf16[8,64,512]{2,1,0:T(8,128)(2,1)} %bitcast.6), calls=%async_computation | async-start | bytes 1048576 | tf_op jit(solution)/shard_map/all_to_all | solution.py:125
  85.1 1.9 %collective-permute-start.23 = (bf16[256,512]{1,0:T(8,128)(2,1)}, bf16[256,512]{1,0:T(8,128)(2,1)S(1)}, u32[]{:S(2)}, u32[]{:S(2)}) collective-permute-start(bf16[256,512]{1,0:T(8,128)(2,1)} %get-tuple-element.103.refs_4_), channel_id=1, source_target_pairs={{0,24},{4,28},{8,16},{12,20},{16,8},{20,12},{24,0},{28,4},{32,56},... | collective-permute-start | bytes 786440 | tf_op jit(solution)/shard_map/ppermute | solution.py:57
  87.0 0.8 collective-permute-start.21
  88.0 2.5 %collective-permute-done.20.refs_1_ = bf16[256,512]{1,0:T(8,128)(2,1)S(1)} collective-permute-done((bf16[256,512]{1,0:T(8,128)(2,1)}, bf16[256,512]{1,0:T(8,128)(2,1)S(1)}, u32[]{:S(2)}, u32[]{:S(2)}) %collective-permute-start.20) | collective-permute-done | bytes 262176 | tf_op jit(solution)/shard_map/ppermute | solution.py:57
  90.5 1.8 %collective-permute-start.22 = (bf16[256,512]{1,0:T(8,128)(2,1)S(1)}, bf16[256,512]{1,0:T(8,128)(2,1)S(1)}, u32[]{:S(2)}, u32[]{:S(2)}) collective-permute-start(bf16[256,512]{1,0:T(8,128)(2,1)S(1)} %collective-permute-done.20.refs_1_), channel_id=1, source_target_pairs={{0,24},{4,28},{8,16},{12,20},{16,8},{20,12},{24,0},{28,4},{32,56},... | collective-permute-start | bytes 786440 | tf_op jit(solution)/shard_map/ppermute | solution.py:57
  92.3 6.9 %all-to-all-done = bf16[8,64,512]{2,1,0:T(8,128)(2,1)} async-done(((bf16[8,64,512]{2,1,0:T(8,128)(2,1)}), bf16[8,64,512]{2,1,0:T(8,128)(2,1)}, u32[]{:S(2)}, u32[]{:S(2)}) %all-to-all-start) | async-done | bytes 524320 | tf_op jit(solution)/shard_map/all_to_all | solution.py:125
  99.3 1.1 convert_reduce_fusion
  100.4 5.6 %collective-permute-start.29 = (f32[32,512]{1,0:T(8,128)S(1)}, f32[32,512]{1,0:T(8,128)S(1)}, u32[]{:S(2)}, u32[]{:S(2)}) collective-permute-start(f32[32,512]{1,0:T(8,128)S(1)} %get-tuple-element.116), channel_id=1, source_target_pairs={{0,0},{1,64},{2,128},{3,192},{4,4},{5,68},{6,132},{7,196},{8,8},{9... | collective-permute-start | bytes 196616 | tf_op jit(solution)/shard_map/ppermute | solution.py:145
  106.0 6.8 %collective-permute-start.30 = (f32[32,512]{1,0:T(8,128)S(1)}, f32[32,512]{1,0:T(8,128)S(1)}, u32[]{:S(2)}, u32[]{:S(2)}) collective-permute-start(f32[32,512]{1,0:T(8,128)S(1)} %get-tuple-element.115), channel_id=1, source_target_pairs={{0,4},{1,68},{2,132},{3,196},{4,0},{5,64},{6,128},{7,192},{8,12},{... | collective-permute-start | bytes 196616 | tf_op jit(solution)/shard_map/ppermute | solution.py:145
  112.8 0.9 copy-done.1
  113.8 0.9 copy-done.3
  114.7 3.0 %project.1 = (f32[160,512]{1,0:T(8,128)S(1)}, bf16[160,512]{1,0:T(8,128)(2,1)S(1)}, bf16[160,512]{1,0:T(8,128)(2,1)S(1)}, bf16[160,512]{1,0:T(8,128)(2,1)S(1)}) custom-call(s32[15]{0:T(128)S(1)} %copy-done.7, bf16[512,2048]{1,0:T(8,128)(2,1)S(1)} %get-tuple-element.99.hidden_ref, bf16[256,512]{1,0:T(8,128)(2,1)S(1)} %copy-done.1, ...), custom_call_target="tpu_custom_call" | custom-call | flops 1073741824 | bytes 4194304 | tf_op jit(solution)/shard_map/project/pallas_call | solution.py:508
  117.9 1.0 collective-permute-start.27
  118.9 1.1 collective-permute-start.28
  120.0 0.8 multiply_reduce_fusion
  120.8 0.6 dynamic-slice_divide_fusion
  121.4 2.0 %collective-permute-done.27.refs_2_ = bf16[160,512]{1,0:T(8,128)(2,1)S(1)} collective-permute-done((bf16[160,512]{1,0:T(8,128)(2,1)S(1)}, bf16[160,512]{1,0:T(8,128)(2,1)S(1)}, u32[]{:S(2)}, u32[]{:S(2)}) %collective-permute-start.27) | collective-permute-done | bytes 163872 | tf_op jit(solution)/shard_map/ppermute | solution.py:580
  123.3 4.1 %collective-permute-done.28.refs_3_ = bf16[160,512]{1,0:T(8,128)(2,1)S(1)} collective-permute-done((bf16[160,512]{1,0:T(8,128)(2,1)S(1)}, bf16[160,512]{1,0:T(8,128)(2,1)S(1)}, u32[]{:S(2)}, u32[]{:S(2)}) %collective-permute-start.28) | collective-permute-done | bytes 163872 | tf_op jit(solution)/shard_map/ppermute | solution.py:580
  127.4 1.7 %spread.1 = bf16[3,128,512]{2,1,0:T(8,128)(2,1)} custom-call(s32[15]{0:T(128)S(1)} %copy-done.7, f32[160,512]{1,0:T(8,128)S(1)} %get-tuple-element.104.refs_0_, bf16[160,512]{1,0:T(8,128)(2,1)S(1)} %collective-permute-done.26.refs_1_, bf16[160,512]{1,0:T(8,128)(2,1)S(1)} %collective-permute-done.27.refs_2_, bf16[160,512]{1,0:T(8,128)(2,1)S(1)} %collective-permute-done.28.refs_3_), custom_call_target="tpu_custom_call" | custom-call | flops 62914560 | bytes 1572864 | tf_op jit(solution)/shard_map/spread/pallas_call | solution.py:539
  (67 shorter events, 2.2 us)
Async XLA Ops:
  4.7 10.7 %copy-start.7 = (s32[15]{0:T(128)S(1)}, s32[15]{0:T(128)}, u32[]{:S(2)}) copy-start(s32[15]{0:T(128)} %compare_select_fusion.3.info_ref) | copy-start | bytes 184
  4.7 10.7 %copy-start.9 = (bf16[512,2048]{1,0:T(8,128)(2,1)S(1)}, bf16[512,2048]{1,0:T(8,128)(2,1)}, u32[]{:S(2)}) copy-start(bf16[512,2048]{1,0:T(8,128)(2,1)} %query_ref.1) | copy-start | bytes 6291460
  4.7 10.7 %copy-start.10 = (bf16[512,256]{1,0:T(8,128)(2,1)S(1)}, bf16[512,256]{1,0:T(8,128)(2,1)}, u32[]{:S(2)}) copy-start(bf16[512,256]{1,0:T(8,128)(2,1)} %key_ref.1) | copy-start | bytes 786436
  4.7 10.7 %copy-start.11 = (bf16[512,256]{1,0:T(8,128)(2,1)S(1)}, bf16[512,256]{1,0:T(8,128)(2,1)}, u32[]{:S(2)}) copy-start(bf16[512,256]{1,0:T(8,128)(2,1)} %value_ref.1) | copy-start | bytes 786436
  4.7 6.9 %collective-permute-start = (bf16[160,512]{1,0:T(8,128)(2,1)}, bf16[160,512]{1,0:T(8,128)(2,1)S(1)}, u32[]{:S(2)}, u32[]{:S(2)}) collective-permute-start(bf16[160,512]{1,0:T(8,128)(2,1)} %fold.1.refs_0_), channel_id=1, source_target_pairs={{0,2},{1,3},{2,0},{3,1},{4,6},{5,7},{6,4},{7,5},{8,10},{9,11},{10,... | collective-permute-start | bytes 491528 | tf_op jit(solution)/shard_map/ppermute | solution.py:580
  11.6 12.1 %copy-start.6 = (bf16[160,512]{1,0:T(8,128)(2,1)S(1)}, bf16[160,512]{1,0:T(8,128)(2,1)}, u32[]{:S(2)}) copy-start(bf16[160,512]{1,0:T(8,128)(2,1)} %fold.1.refs_0_) | copy-start | bytes 491524
  11.6 13.5 %copy-start.12 = (bf16[32,512]{1,0:T(8,128)(2,1)S(1)}, bf16[32,512]{1,0:T(8,128)(2,1)}, u32[]{:S(2)}) copy-start(bf16[32,512]{1,0:T(8,128)(2,1)} %param.18) | copy-start | bytes 98308
  11.7 27.7 %copy-start.4 = (bf16[128,2048]{1,0:T(8,128)(2,1)S(1)}, bf16[128,2048]{1,0:T(8,128)(2,1)}, u32[]{:S(2)}) copy-start(bf16[128,2048]{1,0:T(8,128)(2,1)} %get-tuple-element.66.refs_0_) | copy-start | bytes 1572868
  11.7 27.7 %copy-start.5 = (f32[3,8192]{1,0:T(4,128)S(1)}, f32[3,8192]{1,0:T(4,128)}, u32[]{:S(2)}) copy-start(f32[3,8192]{1,0:T(4,128)} %gain_ref.3) | copy-start | bytes 294916
  11.7 24.6 %collective-permute-start.6 = (bf16[128,2048]{1,0:T(8,128)(2,1)}, bf16[128,2048]{1,0:T(8,128)(2,1)S(1)}, u32[]{:S(2)}, u32[]{:S(2)}) collective-permute-start(bf16[128,2048]{1,0:T(8,128)(2,1)} %get-tuple-element.70), channel_id=1, source_target_pairs={{0,1},{1,0},{2,3},{3,2},{4,5},{5,4},{6,7},{7,6},{8,9},{9,8},{10,11... | collective-permute-start | bytes 1572872 | tf_op jit(solution)/shard_map/ppermute | solution.py:580
  13.7 22.7 %collective-permute-start.7 = (bf16[128,2048]{1,0:T(8,128)(2,1)}, bf16[128,2048]{1,0:T(8,128)(2,1)S(1)}, u32[]{:S(2)}, u32[]{:S(2)}) collective-permute-start(bf16[128,2048]{1,0:T(8,128)(2,1)} %get-tuple-element.72), channel_id=1, source_target_pairs={{0,2},{1,3},{2,0},{3,1},{4,6},{5,7},{6,4},{7,5},{8,10},{9,11},{10,... | collective-permute-start | bytes 1572872 | tf_op jit(solution)/shard_map/ppermute | solution.py:580
  14.7 24.1 %collective-permute-start.8 = (bf16[128,2048]{1,0:T(8,128)(2,1)}, bf16[128,2048]{1,0:T(8,128)(2,1)S(1)}, u32[]{:S(2)}, u32[]{:S(2)}) collective-permute-start(bf16[128,2048]{1,0:T(8,128)(2,1)} %get-tuple-element.73), channel_id=1, source_target_pairs={{0,3},{1,2},{2,1},{3,0},{4,7},{5,6},{6,5},{7,4},{8,11},{9,10},{10,... | collective-permute-start | bytes 1572872 | tf_op jit(solution)/shard_map/ppermute | solution.py:580
  23.6 1.2 collective-permute-start.3
  23.8 1.4 %collective-permute-start.4 = (bf16[160,512]{1,0:T(8,128)(2,1)S(1)}, bf16[160,512]{1,0:T(8,128)(2,1)S(1)}, u32[]{:S(2)}, u32[]{:S(2)}) collective-permute-start(bf16[160,512]{1,0:T(8,128)(2,1)S(1)} %copy-done.6), channel_id=1, source_target_pairs={{0,1},{1,0},{2,3},{3,2},{4,5},{5,4},{6,7},{7,6},{8,9},{9,8},{10,11... | collective-permute-start | bytes 491528 | tf_op jit(solution)/shard_map/ppermute | solution.py:580
  24.8 3.2 %collective-permute-start.5 = (bf16[160,512]{1,0:T(8,128)(2,1)S(1)}, bf16[160,512]{1,0:T(8,128)(2,1)S(1)}, u32[]{:S(2)}, u32[]{:S(2)}) collective-permute-start(bf16[160,512]{1,0:T(8,128)(2,1)S(1)} %collective-permute-done.refs_2_), channel_id=1, source_target_pairs={{0,1},{1,0},{2,3},{3,2},{4,5},{5,4},{6,7},{7,6},{8,9},{9,8},{10,11... | collective-permute-start | bytes 491528 | tf_op jit(solution)/shard_map/ppermute | solution.py:580
  25.2 17.7 %collective-permute-start.1 = (bf16[32,512]{1,0:T(8,128)(2,1)S(1)}, bf16[32,512]{1,0:T(8,128)(2,1)S(1)}, u32[]{:S(2)}, u32[]{:S(2)}) collective-permute-start(bf16[32,512]{1,0:T(8,128)(2,1)S(1)} %copy-done.12), channel_id=1, source_target_pairs={{0,0},{4,4},{1,32},{5,36},{2,64},{6,68},{3,96},{7,100},{32,128},{3... | collective-permute-start | bytes 98312 | tf_op jit(solution)/shard_map/ppermute | solution.py:70
  28.0 14.9 %collective-permute-start.2 = (bf16[32,512]{1,0:T(8,128)(2,1)S(1)}, bf16[32,512]{1,0:T(8,128)(2,1)S(1)}, u32[]{:S(2)}, u32[]{:S(2)}) collective-permute-start(bf16[32,512]{1,0:T(8,128)(2,1)S(1)} %copy-done.12), channel_id=1, source_target_pairs={{4,0},{0,4},{5,32},{1,36},{6,64},{2,68},{7,96},{3,100},{36,128},{3... | collective-permute-start | bytes 98312 | tf_op jit(solution)/shard_map/ppermute | solution.py:70
  36.2 15.9 %copy-start.8 = (f32[8192]{0:T(1024)S(1)}, f32[8192]{0:T(1024)}, u32[]{:S(2)}) copy-start(f32[8192]{0:T(1024)} %param.17) | copy-start | bytes 98308
  36.2 3.2 %collective-permute-start.9 = (f32[8,512]{1,0:T(8,128)S(1)}, f32[8,512]{1,0:T(8,128)S(1)}, u32[]{:S(2)}, u32[]{:S(2)}) collective-permute-start(f32[8,512]{1,0:T(8,128)S(1)} %add.73.refs_4_), channel_id=1, source_target_pairs={{0,2},{1,3},{2,0},{3,1},{4,6},{5,7},{6,4},{7,5},{8,10},{9,11},{10,... | collective-permute-start | bytes 49160 | tf_op jit(solution)/shard_map/ppermute | solution.py:580
  42.9 9.3 %collective-permute-start.10 = (f32[8,512]{1,0:T(8,128)S(1)}, f32[8,512]{1,0:T(8,128)S(1)}, u32[]{:S(2)}, u32[]{:S(2)}) collective-permute-start(f32[8,512]{1,0:T(8,128)S(1)} %get-tuple-element.84.refs_4_), channel_id=1, source_target_pairs={{0,1},{1,0},{2,3},{3,2},{4,5},{5,4},{6,7},{7,6},{8,9},{9,8},{10,11... | collective-permute-start | bytes 49160 | tf_op jit(solution)/shard_map/ppermute | solution.py:580
  43.7 8.5 %collective-permute-start.11 = (f32[8,512]{1,0:T(8,128)S(1)}, f32[8,512]{1,0:T(8,128)S(1)}, u32[]{:S(2)}, u32[]{:S(2)}) collective-permute-start(f32[8,512]{1,0:T(8,128)S(1)} %get-tuple-element.84.refs_4_), channel_id=1, source_target_pairs={{0,2},{1,3},{2,0},{3,1},{4,6},{5,7},{6,4},{7,5},{8,10},{9,11},{10,... | collective-permute-start | bytes 49160 | tf_op jit(solution)/shard_map/ppermute | solution.py:580
  45.9 6.3 %collective-permute-start.12 = (f32[8,512]{1,0:T(8,128)S(1)}, f32[8,512]{1,0:T(8,128)S(1)}, u32[]{:S(2)}, u32[]{:S(2)}) collective-permute-start(f32[8,512]{1,0:T(8,128)S(1)} %get-tuple-element.84.refs_4_), channel_id=1, source_target_pairs={{0,3},{1,2},{2,1},{3,0},{4,7},{5,6},{6,5},{7,4},{8,11},{9,10},{10,... | collective-permute-start | bytes 49160 | tf_op jit(solution)/shard_map/ppermute | solution.py:580
  46.0 11.1 %collective-permute-start.13 = (bf16[64,512]{1,0:T(8,128)(2,1)S(1)}, bf16[64,512]{1,0:T(8,128)(2,1)S(1)}, u32[]{:S(2)}, u32[]{:S(2)}) collective-permute-start(bf16[64,512]{1,0:T(8,128)(2,1)S(1)} %constant_dynamic-update-slice_fusion), channel_id=1, source_target_pairs={{0,128},{4,132},{8,136},{12,140},{16,144},{20,148},{24,152},{28,15... | collective-permute-start | bytes 196616 | tf_op jit(solution)/shard_map/ppermute | solution.py:57
  57.0 12.9 %collective-permute-start.16 = (bf16[2,256,512]{2,1,0:T(8,128)(2,1)S(1)}, bf16[2,256,512]{2,1,0:T(8,128)(2,1)S(1)}, u32[]{:S(2)}, u32[]{:S(2)}) collective-permute-start(bf16[2,256,512]{2,1,0:T(8,128)(2,1)S(1)} %get-tuple-element.92), channel_id=1, source_target_pairs={{0,8},{4,12},{8,0},{12,4},{16,24},{20,28},{24,16},{28,20},{32,40},... | collective-permute-start | bytes 1572872 | tf_op jit(solution)/shard_map/ppermute | solution.py:57
  58.4 13.7 %collective-permute-start.17 = (bf16[2,256,512]{2,1,0:T(8,128)(2,1)S(1)}, bf16[2,256,512]{2,1,0:T(8,128)(2,1)S(1)}, u32[]{:S(2)}, u32[]{:S(2)}) collective-permute-start(bf16[2,256,512]{2,1,0:T(8,128)(2,1)S(1)} %get-tuple-element.93), channel_id=1, source_target_pairs={{0,24},{4,28},{8,16},{12,20},{16,8},{20,12},{24,0},{28,4},{32,56},... | collective-permute-start | bytes 1572872 | tf_op jit(solution)/shard_map/ppermute | solution.py:57
  60.4 8.7 %collective-permute-start.14 = (bf16[128,512]{1,0:T(8,128)(2,1)S(1)}, bf16[128,512]{1,0:T(8,128)(2,1)S(1)}, u32[]{:S(2)}, u32[]{:S(2)}) collective-permute-start(bf16[128,512]{1,0:T(8,128)(2,1)S(1)} %pad_maximum_fusion.1), channel_id=1, source_target_pairs={{0,64},{4,68},{8,72},{12,76},{16,80},{20,84},{24,88},{28,92},{32,9... | collective-permute-start | bytes 393224 | tf_op jit(solution)/shard_map/ppermute | solution.py:57
  69.0 3.5 %copy-start = (bf16[256,512]{1,0:T(8,128)(2,1)}, bf16[256,512]{1,0:T(8,128)(2,1)S(1)}, u32[]{:S(2)}) copy-start(bf16[256,512]{1,0:T(8,128)(2,1)S(1)} %constant_dynamic-update-slice_fusion.2.refs_0_) | copy-start | bytes 786436
  69.1 6.9 %collective-permute-start.15 = (bf16[256,512]{1,0:T(8,128)(2,1)S(1)}, bf16[256,512]{1,0:T(8,128)(2,1)S(1)}, u32[]{:S(2)}, u32[]{:S(2)}) collective-permute-start(bf16[256,512]{1,0:T(8,128)(2,1)S(1)} %constant_dynamic-update-slice_fusion.2.refs_0_), channel_id=1, source_target_pairs={{0,32},{4,36},{8,40},{12,44},{16,48},{20,52},{24,56},{28,60},{32,0... | collective-permute-start | bytes 786440 | tf_op jit(solution)/shard_map/ppermute | solution.py:57
  72.3 6.1 %collective-permute-start.19 = (bf16[256,512]{1,0:T(8,128)(2,1)S(1)}, bf16[256,512]{1,0:T(8,128)(2,1)S(1)}, u32[]{:S(2)}, u32[]{:S(2)}) collective-permute-start(bf16[256,512]{1,0:T(8,128)(2,1)S(1)} %get-tuple-element.113), channel_id=1, source_target_pairs={{0,8},{4,12},{8,0},{12,4},{16,24},{20,28},{24,16},{28,20},{32,40},... | collective-permute-start | bytes 786440 | tf_op jit(solution)/shard_map/ppermute | solution.py:57
  72.6 7.3 %collective-permute-start.18 = (bf16[256,512]{1,0:T(8,128)(2,1)S(1)}, bf16[256,512]{1,0:T(8,128)(2,1)S(1)}, u32[]{:S(2)}, u32[]{:S(2)}) collective-permute-start(bf16[256,512]{1,0:T(8,128)(2,1)S(1)} %get-tuple-element.111), channel_id=1, source_target_pairs={{0,24},{4,28},{8,16},{12,20},{16,8},{20,12},{24,0},{28,4},{32,56},... | collective-permute-start | bytes 786440 | tf_op jit(solution)/shard_map/ppermute | solution.py:57
  75.9 4.9 %copy-start.2 = (bf16[256,512]{1,0:T(8,128)(2,1)}, bf16[256,512]{1,0:T(8,128)(2,1)S(1)}, u32[]{:S(2)}) copy-start(bf16[256,512]{1,0:T(8,128)(2,1)S(1)} %collective-permute-done.15.refs_1_) | copy-start | bytes 786436
  80.8 18.5 %all-to-all-start = ((bf16[8,64,512]{2,1,0:T(8,128)(2,1)}), bf16[8,64,512]{2,1,0:T(8,128)(2,1)}, u32[]{:S(2)}, u32[]{:S(2)}) async-start(bf16[8,64,512]{2,1,0:T(8,128)(2,1)} %bitcast.6), calls=%async_computation | async-start | bytes 1048576 | tf_op jit(solution)/shard_map/all_to_all | solution.py:125
  85.0 5.5 %collective-permute-start.20 = (bf16[256,512]{1,0:T(8,128)(2,1)}, bf16[256,512]{1,0:T(8,128)(2,1)S(1)}, u32[]{:S(2)}, u32[]{:S(2)}) collective-permute-start(bf16[256,512]{1,0:T(8,128)(2,1)} %get-tuple-element.102.refs_0_), channel_id=1, source_target_pairs={{0,8},{4,12},{8,0},{12,4},{16,24},{20,28},{24,16},{28,20},{32,40},... | collective-permute-start | bytes 786440 | tf_op jit(solution)/shard_map/ppermute | solution.py:57
  85.1 7.3 %collective-permute-start.23 = (bf16[256,512]{1,0:T(8,128)(2,1)}, bf16[256,512]{1,0:T(8,128)(2,1)S(1)}, u32[]{:S(2)}, u32[]{:S(2)}) collective-permute-start(bf16[256,512]{1,0:T(8,128)(2,1)} %get-tuple-element.103.refs_4_), channel_id=1, source_target_pairs={{0,24},{4,28},{8,16},{12,20},{16,8},{20,12},{24,0},{28,4},{32,56},... | collective-permute-start | bytes 786440 | tf_op jit(solution)/shard_map/ppermute | solution.py:57
  87.0 19.0 %collective-permute-start.21 = (bf16[256,512]{1,0:T(8,128)(2,1)}, bf16[256,512]{1,0:T(8,128)(2,1)S(1)}, u32[]{:S(2)}, u32[]{:S(2)}) collective-permute-start(bf16[256,512]{1,0:T(8,128)(2,1)} %get-tuple-element.102.refs_0_), channel_id=1, source_target_pairs={{0,24},{4,28},{8,16},{12,20},{16,8},{20,12},{24,0},{28,4},{32,56},... | collective-permute-start | bytes 786440 | tf_op jit(solution)/shard_map/ppermute | solution.py:57
  87.8 25.0 %collective-permute-start.24 = (bf16[256,512]{1,0:T(8,128)(2,1)}, bf16[256,512]{1,0:T(8,128)(2,1)S(1)}, u32[]{:S(2)}, u32[]{:S(2)}) collective-permute-start(bf16[256,512]{1,0:T(8,128)(2,1)} %get-tuple-element.103.refs_4_), channel_id=1, source_target_pairs={{0,8},{4,12},{8,0},{12,4},{16,24},{20,28},{24,16},{28,20},{32,40},... | collective-permute-start | bytes 786440 | tf_op jit(solution)/shard_map/ppermute | solution.py:57
  90.5 22.3 %collective-permute-start.22 = (bf16[256,512]{1,0:T(8,128)(2,1)S(1)}, bf16[256,512]{1,0:T(8,128)(2,1)S(1)}, u32[]{:S(2)}, u32[]{:S(2)}) collective-permute-start(bf16[256,512]{1,0:T(8,128)(2,1)S(1)} %collective-permute-done.20.refs_1_), channel_id=1, source_target_pairs={{0,24},{4,28},{8,16},{12,20},{16,8},{20,12},{24,0},{28,4},{32,56},... | collective-permute-start | bytes 786440 | tf_op jit(solution)/shard_map/ppermute | solution.py:57
  92.3 20.5 %collective-permute-start.25 = (bf16[256,512]{1,0:T(8,128)(2,1)S(1)}, bf16[256,512]{1,0:T(8,128)(2,1)}, u32[]{:S(2)}, u32[]{:S(2)}) collective-permute-start(bf16[256,512]{1,0:T(8,128)(2,1)S(1)} %collective-permute-done.23.refs_5_), channel_id=1, source_target_pairs={{0,8},{4,12},{8,0},{12,4},{16,24},{20,28},{24,16},{28,20},{32,40},... | collective-permute-start | bytes 786440 | tf_op jit(solution)/shard_map/ppermute | solution.py:57
  100.4 19.6 %collective-permute-start.29 = (f32[32,512]{1,0:T(8,128)S(1)}, f32[32,512]{1,0:T(8,128)S(1)}, u32[]{:S(2)}, u32[]{:S(2)}) collective-permute-start(f32[32,512]{1,0:T(8,128)S(1)} %get-tuple-element.116), channel_id=1, source_target_pairs={{0,0},{1,64},{2,128},{3,192},{4,4},{5,68},{6,132},{7,196},{8,8},{9... | collective-permute-start | bytes 196616 | tf_op jit(solution)/shard_map/ppermute | solution.py:145
  106.0 14.0 %collective-permute-start.30 = (f32[32,512]{1,0:T(8,128)S(1)}, f32[32,512]{1,0:T(8,128)S(1)}, u32[]{:S(2)}, u32[]{:S(2)}) collective-permute-start(f32[32,512]{1,0:T(8,128)S(1)} %get-tuple-element.115), channel_id=1, source_target_pairs={{0,4},{1,68},{2,132},{3,196},{4,0},{5,64},{6,128},{7,192},{8,12},{... | collective-permute-start | bytes 196616 | tf_op jit(solution)/shard_map/ppermute | solution.py:145
  112.8 1.0 copy-start.1
  113.8 0.9 copy-start.3
  117.8 3.6 %collective-permute-start.26 = (bf16[160,512]{1,0:T(8,128)(2,1)S(1)}, bf16[160,512]{1,0:T(8,128)(2,1)S(1)}, u32[]{:S(2)}, u32[]{:S(2)}) collective-permute-start(bf16[160,512]{1,0:T(8,128)(2,1)S(1)} %get-tuple-element.105), channel_id=1, source_target_pairs={{0,1},{1,0},{2,3},{3,2},{4,5},{5,4},{6,7},{7,6},{8,9},{9,8},{10,11... | collective-permute-start | bytes 491528 | tf_op jit(solution)/shard_map/ppermute | solution.py:580
  117.9 5.5 %collective-permute-start.27 = (bf16[160,512]{1,0:T(8,128)(2,1)S(1)}, bf16[160,512]{1,0:T(8,128)(2,1)S(1)}, u32[]{:S(2)}, u32[]{:S(2)}) collective-permute-start(bf16[160,512]{1,0:T(8,128)(2,1)S(1)} %get-tuple-element.106), channel_id=1, source_target_pairs={{0,2},{1,3},{2,0},{3,1},{4,6},{5,7},{6,4},{7,5},{8,10},{9,11},{10,... | collective-permute-start | bytes 491528 | tf_op jit(solution)/shard_map/ppermute | solution.py:580
  118.9 8.5 %collective-permute-start.28 = (bf16[160,512]{1,0:T(8,128)(2,1)S(1)}, bf16[160,512]{1,0:T(8,128)(2,1)S(1)}, u32[]{:S(2)}, u32[]{:S(2)}) collective-permute-start(bf16[160,512]{1,0:T(8,128)(2,1)S(1)} %get-tuple-element.107), channel_id=1, source_target_pairs={{0,3},{1,2},{2,1},{3,0},{4,7},{5,6},{6,5},{7,4},{8,11},{9,10},{10,... | collective-permute-start | bytes 491528 | tf_op jit(solution)/shard_map/ppermute | solution.py:580

commit v11 on v10

--- a/solution.py
+++ b/solution.py
@@ -126,14 +126,19 @@
     return jnp.sum(grad.reshape(nz, -1, columns).astype(F32), axis=0)
 
 
-def reduce_to_owner(grad):
+def parts_by_turn(grad):
+    nx = sides_of(lax.axis_size("dp"))[2]
+    rows, columns = grad.shape[0] // nx, grad.shape[1]
+    x = lax.axis_index("dp") % nx
+    return [lax.dynamic_slice(grad, ((x + turn) % nx * rows, 0), (rows, columns)) for turn in range(nx)]
+
+
+def reduce_to_owner(parts):
     n, tn = lax.axis_size("dp"), lax.axis_size("tensor")
     nz, ny, nx = sides_of(n)
-    rows, columns = grad.shape[0] // nx, grad.shape[1]
     order = block_order(n, tn)
-    x = lax.axis_index("dp") % nx
     total = None
-    for turn in range(nx):
+    for turn, part in enumerate(parts):
         pairs = []
         for z in range(nz):
             for y in range(ny):
@@ -141,7 +146,6 @@
                     for j in range(tn):
                         block = j * n + int(order[y, z, (x0 + turn) % nx])
                         pairs.append((((z * ny + y) * nx + x0) * tn + j, block))
-        part = lax.dynamic_slice(grad, ((x + turn) % nx * rows, 0), (rows, columns))
         part = lax.ppermute(part, ("dp", "tensor"), pairs)
         total = part if total is None else total + part
     return total
@@ -614,8 +618,10 @@
     weights = weight_twice(weight_once(held(weights, grad)))
     grad = reduce_along_z(grad)
     hidden, grad = lax.optimization_barrier((hidden, grad))
+    grad = parts_by_turn(grad)
+    values = project(info, hidden, weights, tn, nz, ny, nx)
+    values, grad[-1] = lax.optimization_barrier((values, grad[-1]))
     weight_grad = reduce_to_owner(grad)
-    values = project(info, hidden, weights, tn, nz, ny, nx)
     values = [values[0]] + [swapped(values[s], s) for s in range(1, tn)]
     draft_values = spread(info, values)
 

time: 130 us -> 136 us (1.046)
  local copies, waits for them, and re-layouts: 2 us -> 6.27 us
  waiting for transfers between devices: 34.7 us -> 36.2 us
    unnamed x29 -> x39, local copies, waits for them, and re-layouts: 1.97 us -> 5.6 us
  transfers between devices with their start and end apart: 32 -> 32, of which waited for: 14 -> 16; matrix products, arithmetic and copies ran while one was open for 2% -> 3% of each run, Pallas kernels for 19% -> 16%
where the time goes in v11:
time: 136 us; the launch traced here: 135 us
  starting transfers between devices  57.7 us (42%)
  waiting for transfers between devices  36.2 us (27%)
  Pallas kernels  28.7 us (21%)
  local copies, waits for them, and re-layouts  6.27 us (5%)
  other arithmetic  5.02 us (4%)
    ppermute x13, waiting for transfers between devices, moved(): return lax.ppermute(values, 'dp', pairs)  18.9 us
    ppermute x13, starting transfers between devices, moved(): return lax.ppermute(values, 'dp', pairs)  18.2 us
    ppermute x2, starting transfers between devices, reduce_to_owner(): part = lax.ppermute(part, ('dp', 'tensor'), pairs)  12.5 us
    ppermute x14, starting transfers between devices, swapped(): return lax.ppermute(values, 'tensor', [(a, a ^ s) for a in range(tn)])  11.9 us
    ppermute x2, starting transfers between devices, weight_to_place(): parts.append(lax.ppermute(weight, ('dp', 'tensor'), pairs))  11.1 us
    ppermute x14, waiting for transfers between devices, swapped(): return lax.ppermute(values, 'tensor', [(a, a ^ s) for a in range(tn)])  9.79 us
    pallas_call x1, Pallas kernels, attend(): pl.pallas_call(functools.partial(attend_kernel, window), grid=(pack // bl...  8.17 us
    all_to_all x1, waiting for transfers between devices, reduce_along_z(): lax.all_to_all(grad.astype(BF16), 'dp', 0, 0, tiled=True, axis_index_grou...  6.91 us
  transfers between devices with their start and end apart: 32, of which 16 were waited for; matrix products, arithmetic and copies ran while one was open for 3% of the time, Pallas kernels for 16%

profile of v11, /device:TPU:1, one launch (start us, length us, event | category | flops | bytes accessed | tf_op | source)
XLA Modules:
  0.0 134.9 jit_solution(4913747101004154229)
XLA Ops:
  0.7 1.3 compare_select_fusion.3.info_ref
  1.9 2.7 %fold.1.refs_0_ = bf16[160,512]{1,0:T(8,128)(2,1)} custom-call(s32[15]{0:T(128)} %compare_select_fusion.3.info_ref, bf16[3,128,512]{2,1,0:T(8,128)(2,1)} %cotangent_ref.1), custom_call_target="tpu_custom_call" | custom-call | flops 62914560 | bytes 393216 | tf_op jit(solution)/shard_map/fold/pallas_call | solution.py:329
  4.7 2.1 %collective-permute-start = (bf16[160,512]{1,0:T(8,128)(2,1)}, bf16[160,512]{1,0:T(8,128)(2,1)S(1)}, u32[]{:S(2)}, u32[]{:S(2)}) collective-permute-start(bf16[160,512]{1,0:T(8,128)(2,1)} %fold.1.refs_0_), channel_id=1, source_target_pairs={{0,2},{1,3},{2,0},{3,1},{4,6},{5,7},{6,4},{7,5},{8,10},{9,11},{10,... | collective-permute-start | bytes 491528 | tf_op jit(solution)/shard_map/ppermute | solution.py:584
  6.8 4.8 %features.1 = (bf16[128,2048]{1,0:T(8,128)(2,1)}, bf16[128,2048]{1,0:T(8,128)(2,1)}, bf16[128,2048]{1,0:T(8,128)(2,1)}, bf16[128,2048]{1,0:T(8,128)(2,1)}) custom-call(s32[15]{0:T(128)} %compare_select_fusion.3.info_ref, bf16[128,8192]{1,0:T(8,128)(2,1)} %low_ref, bf16[128,8192]{1,0:T(8,128)(2,1)} %mid_ref.1, f32[3,8192]{1,0:T(4,128)} %gain_ref.3), custom_call_target="tpu_custom_call" | custom-call | flops 10485760 | bytes 6291456 | tf_op jit(solution)/shard_map/features/pallas_call | solution.py:230
  11.7 2.0 %collective-permute-start.6 = (bf16[128,2048]{1,0:T(8,128)(2,1)}, bf16[128,2048]{1,0:T(8,128)(2,1)S(1)}, u32[]{:S(2)}, u32[]{:S(2)}) collective-permute-start(bf16[128,2048]{1,0:T(8,128)(2,1)} %get-tuple-element.75), channel_id=1, source_target_pairs={{0,1},{1,0},{2,3},{3,2},{4,5},{5,4},{6,7},{7,6},{8,9},{9,8},{10,11... | collective-permute-start | bytes 1572872 | tf_op jit(solution)/shard_map/ppermute | solution.py:584
  13.7 1.1 collective-permute-start.7
  15.4 8.2 %attend.1 = (bf16[512,2048]{1,0:T(8,128)(2,1)S(1)}, f32[8,512]{1,0:T(8,128)S(1)}) custom-call(s32[15]{0:T(128)S(1)} %copy-done.9, bf16[512,2048]{1,0:T(8,128)(2,1)S(1)} %copy-done.11, bf16[512,256]{1,0:T(8,128)(2,1)S(1)} %copy-done.12, bf16[512,256]{1,0:T(8,128)(2,1)S(1)} %copy-done.13), custom_call_target="tpu_custom_call" | custom-call | flops 1610612736 | bytes 4194304 | tf_op jit(solution)/shard_map/attend/pallas_call | solution.py:281
  24.1 0.7 collective-permute-done.3
  25.2 2.9 %collective-permute-start.1 = (bf16[32,512]{1,0:T(8,128)(2,1)S(1)}, bf16[32,512]{1,0:T(8,128)(2,1)S(1)}, u32[]{:S(2)}, u32[]{:S(2)}) collective-permute-start(bf16[32,512]{1,0:T(8,128)(2,1)S(1)} %copy-done.17), channel_id=1, source_target_pairs={{0,0},{4,4},{1,32},{5,36},{2,64},{6,68},{3,96},{7,100},{32,128},{3... | collective-permute-start | bytes 98312 | tf_op jit(solution)/shard_map/ppermute | solution.py:70
  28.0 8.2 %collective-permute-start.2 = (bf16[32,512]{1,0:T(8,128)(2,1)S(1)}, bf16[32,512]{1,0:T(8,128)(2,1)S(1)}, u32[]{:S(2)}, u32[]{:S(2)}) collective-permute-start(bf16[32,512]{1,0:T(8,128)(2,1)S(1)} %copy-done.17), channel_id=1, source_target_pairs={{4,0},{0,4},{5,32},{1,36},{6,64},{2,68},{7,96},{3,100},{36,128},{3... | collective-permute-start | bytes 98312 | tf_op jit(solution)/shard_map/ppermute | solution.py:70
  36.4 2.4 %collective-permute-done.8.refs_3_ = bf16[128,2048]{1,0:T(8,128)(2,1)S(1)} collective-permute-done((bf16[128,2048]{1,0:T(8,128)(2,1)}, bf16[128,2048]{1,0:T(8,128)(2,1)S(1)}, u32[]{:S(2)}, u32[]{:S(2)}) %collective-permute-start.8) | collective-permute-done | bytes 524320 | tf_op jit(solution)/shard_map/ppermute | solution.py:584
  39.4 3.5 %merge.1 = (bf16[512,2048]{1,0:T(8,128)(2,1)S(1)}, f32[8,512]{1,0:T(8,128)S(1)}) custom-call(s32[15]{0:T(128)S(1)} %copy-done.9, f32[3,8192]{1,0:T(4,128)S(1)} %copy-done.5, bf16[512,2048]{1,0:T(8,128)(2,1)S(1)} %get-tuple-element.70.high_ref, bf16[128,2048]{1,0:T(8,128)(2,1)S(1)} %copy-done.4, bf16[128,2048]{1,0:T(8,128)(2,1)S(1)} %collective-permute-done.6.refs_1_, ...), custom_call_target="tpu_custom_call" | custom-call | flops 8388608 | bytes 6291456 | tf_op jit(solution)/shard_map/merge/pallas_call | solution.py:376
  42.9 0.8 collective-permute-start.10
  43.7 2.2 %collective-permute-start.11 = (f32[8,512]{1,0:T(8,128)S(1)}, f32[8,512]{1,0:T(8,128)S(1)}, u32[]{:S(2)}, u32[]{:S(2)}) collective-permute-start(f32[8,512]{1,0:T(8,128)S(1)} %get-tuple-element.89.refs_4_), channel_id=1, source_target_pairs={{0,2},{1,3},{2,0},{3,1},{4,6},{5,7},{6,4},{7,5},{8,10},{9,11},{10,... | collective-permute-start | bytes 49160 | tf_op jit(solution)/shard_map/ppermute | solution.py:584
  46.0 6.2 %collective-permute-start.13 = (bf16[64,512]{1,0:T(8,128)(2,1)S(1)}, bf16[64,512]{1,0:T(8,128)(2,1)S(1)}, u32[]{:S(2)}, u32[]{:S(2)}) collective-permute-start(bf16[64,512]{1,0:T(8,128)(2,1)S(1)} %constant_dynamic-update-slice_fusion), channel_id=1, source_target_pairs={{0,128},{4,132},{8,136},{12,140},{16,144},{20,148},{24,152},{28,15... | collective-permute-start | bytes 196616 | tf_op jit(solution)/shard_map/ppermute | solution.py:57
  52.2 4.8 %grads.1 = (f32[2,256,512]{2,1,0:T(8,128)S(1)}, f32[2,256,512]{2,1,0:T(8,128)S(1)}, bf16[2,256,512]{2,1,0:T(8,128)(2,1)S(1)}, bf16[2,256,512]{2,1,0:T(8,128)(2,1)S(1)}, bf16[512,2048]{1,0:T(8,128)(2,1)S(1)}) custom-call(s32[15]{0:T(128)S(1)} %copy-done.9, f32[1,8192]{1,0:T(1,128)S(1)} %bitcast.11, bf16[512,2048]{1,0:T(8,128)(2,1)S(1)} %get-tuple-element.84.merged_ref, ...), custom_call_target="tpu_custom_call" | custom-call | flops 1073741824 | bytes 8388608 | tf_op jit(solution)/shard_map/grads/pallas_call | solution.py:456
  57.0 1.4 %collective-permute-start.16 = (bf16[2,256,512]{2,1,0:T(8,128)(2,1)S(1)}, bf16[2,256,512]{2,1,0:T(8,128)(2,1)S(1)}, u32[]{:S(2)}, u32[]{:S(2)}) collective-permute-start(bf16[2,256,512]{2,1,0:T(8,128)(2,1)S(1)} %get-tuple-element.97), channel_id=1, source_target_pairs={{0,8},{4,12},{8,0},{12,4},{16,24},{20,28},{24,16},{28,20},{32,40},... | collective-permute-start | bytes 1572872 | tf_op jit(solution)/shard_map/ppermute | solution.py:57
  58.4 1.9 %collective-permute-start.17 = (bf16[2,256,512]{2,1,0:T(8,128)(2,1)S(1)}, bf16[2,256,512]{2,1,0:T(8,128)(2,1)S(1)}, u32[]{:S(2)}, u32[]{:S(2)}) collective-permute-start(bf16[2,256,512]{2,1,0:T(8,128)(2,1)S(1)} %get-tuple-element.98), channel_id=1, source_target_pairs={{0,24},{4,28},{8,16},{12,20},{16,8},{20,12},{24,0},{28,4},{32,56},... | collective-permute-start | bytes 1572872 | tf_op jit(solution)/shard_map/ppermute | solution.py:57
  60.4 1.7 %collective-permute-start.14 = (bf16[128,512]{1,0:T(8,128)(2,1)S(1)}, bf16[128,512]{1,0:T(8,128)(2,1)S(1)}, u32[]{:S(2)}, u32[]{:S(2)}) collective-permute-start(bf16[128,512]{1,0:T(8,128)(2,1)S(1)} %pad_maximum_fusion.1), channel_id=1, source_target_pairs={{0,64},{4,68},{8,72},{12,76},{16,80},{20,84},{24,88},{28,92},{32,9... | collective-permute-start | bytes 393224 | tf_op jit(solution)/shard_map/ppermute | solution.py:57
  62.0 7.0 %collective-permute-done.14 = bf16[128,512]{1,0:T(8,128)(2,1)S(1)} collective-permute-done((bf16[128,512]{1,0:T(8,128)(2,1)S(1)}, bf16[128,512]{1,0:T(8,128)(2,1)S(1)}, u32[]{:S(2)}, u32[]{:S(2)}) %collective-permute-start.14) | collective-permute-done | bytes 131104 | tf_op jit(solution)/shard_map/ppermute | solution.py:57
  69.2 0.8 collective-permute-done.16
  70.0 2.2 %collective-permute-done.17 = bf16[2,256,512]{2,1,0:T(8,128)(2,1)S(1)} collective-permute-done((bf16[2,256,512]{2,1,0:T(8,128)(2,1)S(1)}, bf16[2,256,512]{2,1,0:T(8,128)(2,1)S(1)}, u32[]{:S(2)}, u32[]{:S(2)}) %collective-permute-start.17) | collective-permute-done | bytes 524320 | tf_op jit(solution)/shard_map/ppermute | solution.py:57
  72.6 2.0 %collective-permute-start.18 = (bf16[256,512]{1,0:T(8,128)(2,1)S(1)}, bf16[256,512]{1,0:T(8,128)(2,1)S(1)}, u32[]{:S(2)}, u32[]{:S(2)}) collective-permute-start(bf16[256,512]{1,0:T(8,128)(2,1)S(1)} %get-tuple-element.121), channel_id=1, source_target_pairs={{0,24},{4,28},{8,16},{12,20},{16,8},{20,12},{24,0},{28,4},{32,56},... | collective-permute-start | bytes 786440 | tf_op jit(solution)/shard_map/ppermute | solution.py:57
  74.6 1.3 collective-permute-done.15.refs_1_
  75.9 2.5 %collective-permute-done.19 = bf16[256,512]{1,0:T(8,128)(2,1)S(1)} collective-permute-done((bf16[256,512]{1,0:T(8,128)(2,1)S(1)}, bf16[256,512]{1,0:T(8,128)(2,1)S(1)}, u32[]{:S(2)}, u32[]{:S(2)}) %collective-permute-start.19) | collective-permute-done | bytes 262176 | tf_op jit(solution)/shard_map/ppermute | solution.py:57
  78.5 1.4 %collective-permute-done.18 = bf16[256,512]{1,0:T(8,128)(2,1)S(1)} collective-permute-done((bf16[256,512]{1,0:T(8,128)(2,1)S(1)}, bf16[256,512]{1,0:T(8,128)(2,1)S(1)}, u32[]{:S(2)}, u32[]{:S(2)}) %collective-permute-start.18) | collective-permute-done | bytes 262176 | tf_op jit(solution)/shard_map/ppermute | solution.py:57
  79.9 0.8 pad_maximum_fusion.refs_2_
  80.8 4.1 %all-to-all-start = ((bf16[8,64,512]{2,1,0:T(8,128)(2,1)}), bf16[8,64,512]{2,1,0:T(8,128)(2,1)}, u32[]{:S(2)}, u32[]{:S(2)}) async-start(bf16[8,64,512]{2,1,0:T(8,128)(2,1)} %bitcast.6), calls=%async_computation | async-start | bytes 1048576 | tf_op jit(solution)/shard_map/all_to_all | solution.py:125
  85.0 1.9 %collective-permute-start.23 = (bf16[256,512]{1,0:T(8,128)(2,1)}, bf16[256,512]{1,0:T(8,128)(2,1)S(1)}, u32[]{:S(2)}, u32[]{:S(2)}) collective-permute-start(bf16[256,512]{1,0:T(8,128)(2,1)} %get-tuple-element.108.refs_4_), channel_id=1, source_target_pairs={{0,24},{4,28},{8,16},{12,20},{16,8},{20,12},{24,0},{28,4},{32,56},... | collective-permute-start | bytes 786440 | tf_op jit(solution)/shard_map/ppermute | solution.py:57
  87.0 0.8 collective-permute-start.21
  88.0 2.5 %collective-permute-done.20.refs_1_ = bf16[256,512]{1,0:T(8,128)(2,1)S(1)} collective-permute-done((bf16[256,512]{1,0:T(8,128)(2,1)}, bf16[256,512]{1,0:T(8,128)(2,1)S(1)}, u32[]{:S(2)}, u32[]{:S(2)}) %collective-permute-start.20) | collective-permute-done | bytes 262176 | tf_op jit(solution)/shard_map/ppermute | solution.py:57
  90.5 1.8 %collective-permute-start.22 = (bf16[256,512]{1,0:T(8,128)(2,1)S(1)}, bf16[256,512]{1,0:T(8,128)(2,1)S(1)}, u32[]{:S(2)}, u32[]{:S(2)}) collective-permute-start(bf16[256,512]{1,0:T(8,128)(2,1)S(1)} %collective-permute-done.20.refs_1_), channel_id=1, source_target_pairs={{0,24},{4,28},{8,16},{12,20},{16,8},{20,12},{24,0},{28,4},{32,56},... | collective-permute-start | bytes 786440 | tf_op jit(solution)/shard_map/ppermute | solution.py:57
  92.3 6.9 %all-to-all-done = bf16[8,64,512]{2,1,0:T(8,128)(2,1)} async-done(((bf16[8,64,512]{2,1,0:T(8,128)(2,1)}), bf16[8,64,512]{2,1,0:T(8,128)(2,1)}, u32[]{:S(2)}, u32[]{:S(2)}) %all-to-all-start) | async-done | bytes 524320 | tf_op jit(solution)/shard_map/all_to_all | solution.py:125
  99.2 1.1 convert_reduce_fusion
  101.0 1.2 collective-permute-done.22.refs_3_
  102.2 0.7 copy-done.6
  102.9 0.9 copy-done.1
  103.9 0.9 copy-done.3
  104.8 0.9 copy-done.7
  105.8 3.0 %project.1 = (f32[160,512]{1,0:T(8,128)S(1)}, bf16[160,512]{1,0:T(8,128)(2,1)S(1)}, bf16[160,512]{1,0:T(8,128)(2,1)S(1)}, bf16[160,512]{1,0:T(8,128)(2,1)S(1)}) custom-call(s32[15]{0:T(128)S(1)} %copy-done.9, bf16[512,2048]{1,0:T(8,128)(2,1)S(1)} %get-tuple-element.104.hidden_ref, bf16[256,512]{1,0:T(8,128)(2,1)S(1)} %copy-done.1, ...), custom_call_target="tpu_custom_call" | custom-call | flops 1073741824 | bytes 4194304 | tf_op jit(solution)/shard_map/project/pallas_call | solution.py:512
  110.1 0.7 copy-done.16
  110.8 8.2 %collective-permute-start.29 = (f32[32,512]{1,0:T(8,128)}, f32[32,512]{1,0:T(8,128)S(1)}, u32[]{:S(2)}, u32[]{:S(2)}) collective-permute-start(f32[32,512]{1,0:T(8,128)} %get-tuple-element.125), channel_id=1, source_target_pairs={{0,0},{1,64},{2,128},{3,192},{4,4},{5,68},{6,132},{7,196},{8,8},{9... | collective-permute-start | bytes 196616 | tf_op jit(solution)/shard_map/ppermute | solution.py:149
  119.0 4.4 %collective-permute-start.30 = (f32[32,512]{1,0:T(8,128)}, f32[32,512]{1,0:T(8,128)S(1)}, u32[]{:S(2)}, u32[]{:S(2)}) collective-permute-start(f32[32,512]{1,0:T(8,128)} %get-tuple-element.118), channel_id=1, source_target_pairs={{0,4},{1,68},{2,132},{3,196},{4,0},{5,64},{6,128},{7,192},{8,12},{... | collective-permute-start | bytes 196616 | tf_op jit(solution)/shard_map/ppermute | solution.py:149
  123.3 1.7 %collective-permute-start.27 = (bf16[160,512]{1,0:T(8,128)(2,1)}, bf16[160,512]{1,0:T(8,128)(2,1)S(1)}, u32[]{:S(2)}, u32[]{:S(2)}) collective-permute-start(bf16[160,512]{1,0:T(8,128)(2,1)} %copy-done.15), channel_id=1, source_target_pairs={{0,2},{1,3},{2,0},{3,1},{4,6},{5,7},{6,4},{7,5},{8,10},{9,11},{10,... | collective-permute-start | bytes 491528 | tf_op jit(solution)/shard_map/ppermute | solution.py:584
  126.0 0.7 multiply_reduce_fusion
  127.4 2.0 %collective-permute-done.27.refs_2_ = bf16[160,512]{1,0:T(8,128)(2,1)S(1)} collective-permute-done((bf16[160,512]{1,0:T(8,128)(2,1)}, bf16[160,512]{1,0:T(8,128)(2,1)S(1)}, u32[]{:S(2)}, u32[]{:S(2)}) %collective-permute-start.27) | collective-permute-done | bytes 163872 | tf_op jit(solution)/shard_map/ppermute | solution.py:584
  129.4 3.9 %collective-permute-done.28.refs_3_ = bf16[160,512]{1,0:T(8,128)(2,1)S(1)} collective-permute-done((bf16[160,512]{1,0:T(8,128)(2,1)}, bf16[160,512]{1,0:T(8,128)(2,1)S(1)}, u32[]{:S(2)}, u32[]{:S(2)}) %collective-permute-start.28) | collective-permute-done | bytes 163872 | tf_op jit(solution)/shard_map/ppermute | solution.py:584
  133.2 1.7 %spread.1 = bf16[3,128,512]{2,1,0:T(8,128)(2,1)} custom-call(s32[15]{0:T(128)S(1)} %copy-done.9, f32[160,512]{1,0:T(8,128)S(1)} %get-tuple-element.114.refs_0_, bf16[160,512]{1,0:T(8,128)(2,1)S(1)} %collective-permute-done.26.refs_1_, bf16[160,512]{1,0:T(8,128)(2,1)S(1)} %collective-permute-done.27.refs_2_, bf16[160,512]{1,0:T(8,128)(2,1)S(1)} %collective-permute-done.28.refs_3_), custom_call_target="tpu_custom_call" | custom-call | flops 62914560 | bytes 1572864 | tf_op jit(solution)/shard_map/spread/pallas_call | solution.py:543
  (77 shorter events, 6.9 us)
Async XLA Ops:
  4.7 10.7 %copy-start.9 = (s32[15]{0:T(128)S(1)}, s32[15]{0:T(128)}, u32[]{:S(2)}) copy-start(s32[15]{0:T(128)} %compare_select_fusion.3.info_ref) | copy-start | bytes 184
  4.7 10.7 %copy-start.11 = (bf16[512,2048]{1,0:T(8,128)(2,1)S(1)}, bf16[512,2048]{1,0:T(8,128)(2,1)}, u32[]{:S(2)}) copy-start(bf16[512,2048]{1,0:T(8,128)(2,1)} %query_ref.1) | copy-start | bytes 6291460
  4.7 10.7 %copy-start.12 = (bf16[512,256]{1,0:T(8,128)(2,1)S(1)}, bf16[512,256]{1,0:T(8,128)(2,1)}, u32[]{:S(2)}) copy-start(bf16[512,256]{1,0:T(8,128)(2,1)} %key_ref.1) | copy-start | bytes 786436
  4.7 10.7 %copy-start.13 = (bf16[512,256]{1,0:T(8,128)(2,1)S(1)}, bf16[512,256]{1,0:T(8,128)(2,1)}, u32[]{:S(2)}) copy-start(bf16[512,256]{1,0:T(8,128)(2,1)} %value_ref.1) | copy-start | bytes 786436
  4.7 6.9 %collective-permute-start = (bf16[160,512]{1,0:T(8,128)(2,1)}, bf16[160,512]{1,0:T(8,128)(2,1)S(1)}, u32[]{:S(2)}, u32[]{:S(2)}) collective-permute-start(bf16[160,512]{1,0:T(8,128)(2,1)} %fold.1.refs_0_), channel_id=1, source_target_pairs={{0,2},{1,3},{2,0},{3,1},{4,6},{5,7},{6,4},{7,5},{8,10},{9,11},{10,... | collective-permute-start | bytes 491528 | tf_op jit(solution)/shard_map/ppermute | solution.py:584
  11.6 12.1 %copy-start.8 = (bf16[160,512]{1,0:T(8,128)(2,1)S(1)}, bf16[160,512]{1,0:T(8,128)(2,1)}, u32[]{:S(2)}) copy-start(bf16[160,512]{1,0:T(8,128)(2,1)} %fold.1.refs_0_) | copy-start | bytes 491524
  11.7 13.5 %copy-start.17 = (bf16[32,512]{1,0:T(8,128)(2,1)S(1)}, bf16[32,512]{1,0:T(8,128)(2,1)}, u32[]{:S(2)}) copy-start(bf16[32,512]{1,0:T(8,128)(2,1)} %param.18) | copy-start | bytes 98308
  11.7 27.7 %copy-start.4 = (bf16[128,2048]{1,0:T(8,128)(2,1)S(1)}, bf16[128,2048]{1,0:T(8,128)(2,1)}, u32[]{:S(2)}) copy-start(bf16[128,2048]{1,0:T(8,128)(2,1)} %get-tuple-element.71.refs_0_) | copy-start | bytes 1572868
  11.7 27.7 %copy-start.5 = (f32[3,8192]{1,0:T(4,128)S(1)}, f32[3,8192]{1,0:T(4,128)}, u32[]{:S(2)}) copy-start(f32[3,8192]{1,0:T(4,128)} %gain_ref.3) | copy-start | bytes 294916
  11.7 24.5 %collective-permute-start.6 = (bf16[128,2048]{1,0:T(8,128)(2,1)}, bf16[128,2048]{1,0:T(8,128)(2,1)S(1)}, u32[]{:S(2)}, u32[]{:S(2)}) collective-permute-start(bf16[128,2048]{1,0:T(8,128)(2,1)} %get-tuple-element.75), channel_id=1, source_target_pairs={{0,1},{1,0},{2,3},{3,2},{4,5},{5,4},{6,7},{7,6},{8,9},{9,8},{10,11... | collective-permute-start | bytes 1572872 | tf_op jit(solution)/shard_map/ppermute | solution.py:584
  13.7 22.7 %collective-permute-start.7 = (bf16[128,2048]{1,0:T(8,128)(2,1)}, bf16[128,2048]{1,0:T(8,128)(2,1)S(1)}, u32[]{:S(2)}, u32[]{:S(2)}) collective-permute-start(bf16[128,2048]{1,0:T(8,128)(2,1)} %get-tuple-element.77), channel_id=1, source_target_pairs={{0,2},{1,3},{2,0},{3,1},{4,6},{5,7},{6,4},{7,5},{8,10},{9,11},{10,... | collective-permute-start | bytes 1572872 | tf_op jit(solution)/shard_map/ppermute | solution.py:584
  14.7 24.0 %collective-permute-start.8 = (bf16[128,2048]{1,0:T(8,128)(2,1)}, bf16[128,2048]{1,0:T(8,128)(2,1)S(1)}, u32[]{:S(2)}, u32[]{:S(2)}) collective-permute-start(bf16[128,2048]{1,0:T(8,128)(2,1)} %get-tuple-element.78), channel_id=1, source_target_pairs={{0,3},{1,2},{2,1},{3,0},{4,7},{5,6},{6,5},{7,4},{8,11},{9,10},{10,... | collective-permute-start | bytes 1572872 | tf_op jit(solution)/shard_map/ppermute | solution.py:584
  23.6 1.2 collective-permute-start.3
  23.8 1.4 %collective-permute-start.4 = (bf16[160,512]{1,0:T(8,128)(2,1)S(1)}, bf16[160,512]{1,0:T(8,128)(2,1)S(1)}, u32[]{:S(2)}, u32[]{:S(2)}) collective-permute-start(bf16[160,512]{1,0:T(8,128)(2,1)S(1)} %copy-done.8), channel_id=1, source_target_pairs={{0,1},{1,0},{2,3},{3,2},{4,5},{5,4},{6,7},{7,6},{8,9},{9,8},{10,11... | collective-permute-start | bytes 491528 | tf_op jit(solution)/shard_map/ppermute | solution.py:584
  24.8 3.2 %collective-permute-start.5 = (bf16[160,512]{1,0:T(8,128)(2,1)S(1)}, bf16[160,512]{1,0:T(8,128)(2,1)S(1)}, u32[]{:S(2)}, u32[]{:S(2)}) collective-permute-start(bf16[160,512]{1,0:T(8,128)(2,1)S(1)} %collective-permute-done.refs_2_), channel_id=1, source_target_pairs={{0,1},{1,0},{2,3},{3,2},{4,5},{5,4},{6,7},{7,6},{8,9},{9,8},{10,11... | collective-permute-start | bytes 491528 | tf_op jit(solution)/shard_map/ppermute | solution.py:584
  25.2 17.7 %collective-permute-start.1 = (bf16[32,512]{1,0:T(8,128)(2,1)S(1)}, bf16[32,512]{1,0:T(8,128)(2,1)S(1)}, u32[]{:S(2)}, u32[]{:S(2)}) collective-permute-start(bf16[32,512]{1,0:T(8,128)(2,1)S(1)} %copy-done.17), channel_id=1, source_target_pairs={{0,0},{4,4},{1,32},{5,36},{2,64},{6,68},{3,96},{7,100},{32,128},{3... | collective-permute-start | bytes 98312 | tf_op jit(solution)/shard_map/ppermute | solution.py:70
  28.0 14.9 %collective-permute-start.2 = (bf16[32,512]{1,0:T(8,128)(2,1)S(1)}, bf16[32,512]{1,0:T(8,128)(2,1)S(1)}, u32[]{:S(2)}, u32[]{:S(2)}) collective-permute-start(bf16[32,512]{1,0:T(8,128)(2,1)S(1)} %copy-done.17), channel_id=1, source_target_pairs={{4,0},{0,4},{5,32},{1,36},{6,64},{2,68},{7,96},{3,100},{36,128},{3... | collective-permute-start | bytes 98312 | tf_op jit(solution)/shard_map/ppermute | solution.py:70
  36.2 15.9 %copy-start.10 = (f32[8192]{0:T(1024)S(1)}, f32[8192]{0:T(1024)}, u32[]{:S(2)}) copy-start(f32[8192]{0:T(1024)} %param.17) | copy-start | bytes 98308
  36.2 3.2 %collective-permute-start.9 = (f32[8,512]{1,0:T(8,128)S(1)}, f32[8,512]{1,0:T(8,128)S(1)}, u32[]{:S(2)}, u32[]{:S(2)}) collective-permute-start(f32[8,512]{1,0:T(8,128)S(1)} %add.73.refs_4_), channel_id=1, source_target_pairs={{0,2},{1,3},{2,0},{3,1},{4,6},{5,7},{6,4},{7,5},{8,10},{9,11},{10,... | collective-permute-start | bytes 49160 | tf_op jit(solution)/shard_map/ppermute | solution.py:584
  42.9 9.3 %collective-permute-start.10 = (f32[8,512]{1,0:T(8,128)S(1)}, f32[8,512]{1,0:T(8,128)S(1)}, u32[]{:S(2)}, u32[]{:S(2)}) collective-permute-start(f32[8,512]{1,0:T(8,128)S(1)} %get-tuple-element.89.refs_4_), channel_id=1, source_target_pairs={{0,1},{1,0},{2,3},{3,2},{4,5},{5,4},{6,7},{7,6},{8,9},{9,8},{10,11... | collective-permute-start | bytes 49160 | tf_op jit(solution)/shard_map/ppermute | solution.py:584
  43.7 8.5 %collective-permute-start.11 = (f32[8,512]{1,0:T(8,128)S(1)}, f32[8,512]{1,0:T(8,128)S(1)}, u32[]{:S(2)}, u32[]{:S(2)}) collective-permute-start(f32[8,512]{1,0:T(8,128)S(1)} %get-tuple-element.89.refs_4_), channel_id=1, source_target_pairs={{0,2},{1,3},{2,0},{3,1},{4,6},{5,7},{6,4},{7,5},{8,10},{9,11},{10,... | collective-permute-start | bytes 49160 | tf_op jit(solution)/shard_map/ppermute | solution.py:584
  45.9 6.3 %collective-permute-start.12 = (f32[8,512]{1,0:T(8,128)S(1)}, f32[8,512]{1,0:T(8,128)S(1)}, u32[]{:S(2)}, u32[]{:S(2)}) collective-permute-start(f32[8,512]{1,0:T(8,128)S(1)} %get-tuple-element.89.refs_4_), channel_id=1, source_target_pairs={{0,3},{1,2},{2,1},{3,0},{4,7},{5,6},{6,5},{7,4},{8,11},{9,10},{10,... | collective-permute-start | bytes 49160 | tf_op jit(solution)/shard_map/ppermute | solution.py:584
  46.0 11.1 %collective-permute-start.13 = (bf16[64,512]{1,0:T(8,128)(2,1)S(1)}, bf16[64,512]{1,0:T(8,128)(2,1)S(1)}, u32[]{:S(2)}, u32[]{:S(2)}) collective-permute-start(bf16[64,512]{1,0:T(8,128)(2,1)S(1)} %constant_dynamic-update-slice_fusion), channel_id=1, source_target_pairs={{0,128},{4,132},{8,136},{12,140},{16,144},{20,148},{24,152},{28,15... | collective-permute-start | bytes 196616 | tf_op jit(solution)/shard_map/ppermute | solution.py:57
  57.0 12.9 %collective-permute-start.16 = (bf16[2,256,512]{2,1,0:T(8,128)(2,1)S(1)}, bf16[2,256,512]{2,1,0:T(8,128)(2,1)S(1)}, u32[]{:S(2)}, u32[]{:S(2)}) collective-permute-start(bf16[2,256,512]{2,1,0:T(8,128)(2,1)S(1)} %get-tuple-element.97), channel_id=1, source_target_pairs={{0,8},{4,12},{8,0},{12,4},{16,24},{20,28},{24,16},{28,20},{32,40},... | collective-permute-start | bytes 1572872 | tf_op jit(solution)/shard_map/ppermute | solution.py:57
  58.4 13.7 %collective-permute-start.17 = (bf16[2,256,512]{2,1,0:T(8,128)(2,1)S(1)}, bf16[2,256,512]{2,1,0:T(8,128)(2,1)S(1)}, u32[]{:S(2)}, u32[]{:S(2)}) collective-permute-start(bf16[2,256,512]{2,1,0:T(8,128)(2,1)S(1)} %get-tuple-element.98), channel_id=1, source_target_pairs={{0,24},{4,28},{8,16},{12,20},{16,8},{20,12},{24,0},{28,4},{32,56},... | collective-permute-start | bytes 1572872 | tf_op jit(solution)/shard_map/ppermute | solution.py:57
  60.4 8.7 %collective-permute-start.14 = (bf16[128,512]{1,0:T(8,128)(2,1)S(1)}, bf16[128,512]{1,0:T(8,128)(2,1)S(1)}, u32[]{:S(2)}, u32[]{:S(2)}) collective-permute-start(bf16[128,512]{1,0:T(8,128)(2,1)S(1)} %pad_maximum_fusion.1), channel_id=1, source_target_pairs={{0,64},{4,68},{8,72},{12,76},{16,80},{20,84},{24,88},{28,92},{32,9... | collective-permute-start | bytes 393224 | tf_op jit(solution)/shard_map/ppermute | solution.py:57
  69.0 3.5 %copy-start = (bf16[256,512]{1,0:T(8,128)(2,1)}, bf16[256,512]{1,0:T(8,128)(2,1)S(1)}, u32[]{:S(2)}) copy-start(bf16[256,512]{1,0:T(8,128)(2,1)S(1)} %constant_dynamic-update-slice_fusion.2.refs_0_) | copy-start | bytes 786436
  69.1 6.9 %collective-permute-start.15 = (bf16[256,512]{1,0:T(8,128)(2,1)S(1)}, bf16[256,512]{1,0:T(8,128)(2,1)S(1)}, u32[]{:S(2)}, u32[]{:S(2)}) collective-permute-start(bf16[256,512]{1,0:T(8,128)(2,1)S(1)} %constant_dynamic-update-slice_fusion.2.refs_0_), channel_id=1, source_target_pairs={{0,32},{4,36},{8,40},{12,44},{16,48},{20,52},{24,56},{28,60},{32,0... | collective-permute-start | bytes 786440 | tf_op jit(solution)/shard_map/ppermute | solution.py:57
  72.3 6.1 %collective-permute-start.19 = (bf16[256,512]{1,0:T(8,128)(2,1)S(1)}, bf16[256,512]{1,0:T(8,128)(2,1)S(1)}, u32[]{:S(2)}, u32[]{:S(2)}) collective-permute-start(bf16[256,512]{1,0:T(8,128)(2,1)S(1)} %get-tuple-element.123), channel_id=1, source_target_pairs={{0,8},{4,12},{8,0},{12,4},{16,24},{20,28},{24,16},{28,20},{32,40},... | collective-permute-start | bytes 786440 | tf_op jit(solution)/shard_map/ppermute | solution.py:57
  72.6 7.3 %collective-permute-start.18 = (bf16[256,512]{1,0:T(8,128)(2,1)S(1)}, bf16[256,512]{1,0:T(8,128)(2,1)S(1)}, u32[]{:S(2)}, u32[]{:S(2)}) collective-permute-start(bf16[256,512]{1,0:T(8,128)(2,1)S(1)} %get-tuple-element.121), channel_id=1, source_target_pairs={{0,24},{4,28},{8,16},{12,20},{16,8},{20,12},{24,0},{28,4},{32,56},... | collective-permute-start | bytes 786440 | tf_op jit(solution)/shard_map/ppermute | solution.py:57
  75.9 4.9 %copy-start.2 = (bf16[256,512]{1,0:T(8,128)(2,1)}, bf16[256,512]{1,0:T(8,128)(2,1)S(1)}, u32[]{:S(2)}) copy-start(bf16[256,512]{1,0:T(8,128)(2,1)S(1)} %collective-permute-done.15.refs_1_) | copy-start | bytes 786436
  80.8 18.4 %all-to-all-start = ((bf16[8,64,512]{2,1,0:T(8,128)(2,1)}), bf16[8,64,512]{2,1,0:T(8,128)(2,1)}, u32[]{:S(2)}, u32[]{:S(2)}) async-start(bf16[8,64,512]{2,1,0:T(8,128)(2,1)} %bitcast.6), calls=%async_computation | async-start | bytes 1048576 | tf_op jit(solution)/shard_map/all_to_all | solution.py:125
  84.9 5.5 %collective-permute-start.20 = (bf16[256,512]{1,0:T(8,128)(2,1)}, bf16[256,512]{1,0:T(8,128)(2,1)S(1)}, u32[]{:S(2)}, u32[]{:S(2)}) collective-permute-start(bf16[256,512]{1,0:T(8,128)(2,1)} %get-tuple-element.107.refs_0_), channel_id=1, source_target_pairs={{0,8},{4,12},{8,0},{12,4},{16,24},{20,28},{24,16},{28,20},{32,40},... | collective-permute-start | bytes 786440 | tf_op jit(solution)/shard_map/ppermute | solution.py:57
  85.0 7.3 %collective-permute-start.23 = (bf16[256,512]{1,0:T(8,128)(2,1)}, bf16[256,512]{1,0:T(8,128)(2,1)S(1)}, u32[]{:S(2)}, u32[]{:S(2)}) collective-permute-start(bf16[256,512]{1,0:T(8,128)(2,1)} %get-tuple-element.108.refs_4_), channel_id=1, source_target_pairs={{0,24},{4,28},{8,16},{12,20},{16,8},{20,12},{24,0},{28,4},{32,56},... | collective-permute-start | bytes 786440 | tf_op jit(solution)/shard_map/ppermute | solution.py:57
  87.0 14.0 %collective-permute-start.21 = (bf16[256,512]{1,0:T(8,128)(2,1)}, bf16[256,512]{1,0:T(8,128)(2,1)S(1)}, u32[]{:S(2)}, u32[]{:S(2)}) collective-permute-start(bf16[256,512]{1,0:T(8,128)(2,1)} %get-tuple-element.107.refs_0_), channel_id=1, source_target_pairs={{0,24},{4,28},{8,16},{12,20},{16,8},{20,12},{24,0},{28,4},{32,56},... | collective-permute-start | bytes 786440 | tf_op jit(solution)/shard_map/ppermute | solution.py:57
  87.8 13.2 %collective-permute-start.24 = (bf16[256,512]{1,0:T(8,128)(2,1)}, bf16[256,512]{1,0:T(8,128)(2,1)S(1)}, u32[]{:S(2)}, u32[]{:S(2)}) collective-permute-start(bf16[256,512]{1,0:T(8,128)(2,1)} %get-tuple-element.108.refs_4_), channel_id=1, source_target_pairs={{0,8},{4,12},{8,0},{12,4},{16,24},{20,28},{24,16},{28,20},{32,40},... | collective-permute-start | bytes 786440 | tf_op jit(solution)/shard_map/ppermute | solution.py:57
  90.5 11.7 %collective-permute-start.22 = (bf16[256,512]{1,0:T(8,128)(2,1)S(1)}, bf16[256,512]{1,0:T(8,128)(2,1)S(1)}, u32[]{:S(2)}, u32[]{:S(2)}) collective-permute-start(bf16[256,512]{1,0:T(8,128)(2,1)S(1)} %collective-permute-done.20.refs_1_), channel_id=1, source_target_pairs={{0,24},{4,28},{8,16},{12,20},{16,8},{20,12},{24,0},{28,4},{32,56},... | collective-permute-start | bytes 786440 | tf_op jit(solution)/shard_map/ppermute | solution.py:57
  92.3 10.6 %collective-permute-start.25 = (bf16[256,512]{1,0:T(8,128)(2,1)S(1)}, bf16[256,512]{1,0:T(8,128)(2,1)}, u32[]{:S(2)}, u32[]{:S(2)}) collective-permute-start(bf16[256,512]{1,0:T(8,128)(2,1)S(1)} %collective-permute-done.23.refs_5_), channel_id=1, source_target_pairs={{0,8},{4,12},{8,0},{12,4},{16,24},{20,28},{24,16},{28,20},{32,40},... | collective-permute-start | bytes 786440 | tf_op jit(solution)/shard_map/ppermute | solution.py:57
  102.2 0.7 copy-start.6
  102.9 1.0 copy-start.1
  103.9 0.9 copy-start.3
  104.8 0.9 copy-start.7
  110.1 0.7 copy-start.16
  110.8 14.7 %collective-permute-start.29 = (f32[32,512]{1,0:T(8,128)}, f32[32,512]{1,0:T(8,128)S(1)}, u32[]{:S(2)}, u32[]{:S(2)}) collective-permute-start(f32[32,512]{1,0:T(8,128)} %get-tuple-element.125), channel_id=1, source_target_pairs={{0,0},{1,64},{2,128},{3,192},{4,4},{5,68},{6,132},{7,196},{8,8},{9... | collective-permute-start | bytes 196616 | tf_op jit(solution)/shard_map/ppermute | solution.py:149
  119.0 7.1 %collective-permute-start.30 = (f32[32,512]{1,0:T(8,128)}, f32[32,512]{1,0:T(8,128)S(1)}, u32[]{:S(2)}, u32[]{:S(2)}) collective-permute-start(f32[32,512]{1,0:T(8,128)} %get-tuple-element.118), channel_id=1, source_target_pairs={{0,4},{1,68},{2,132},{3,196},{4,0},{5,64},{6,128},{7,192},{8,12},{... | collective-permute-start | bytes 196616 | tf_op jit(solution)/shard_map/ppermute | solution.py:149
  123.3 4.1 %collective-permute-start.26 = (bf16[160,512]{1,0:T(8,128)(2,1)}, bf16[160,512]{1,0:T(8,128)(2,1)S(1)}, u32[]{:S(2)}, u32[]{:S(2)}) collective-permute-start(bf16[160,512]{1,0:T(8,128)(2,1)} %copy-done.16), channel_id=1, source_target_pairs={{0,1},{1,0},{2,3},{3,2},{4,5},{5,4},{6,7},{7,6},{8,9},{9,8},{10,11... | collective-permute-start | bytes 491528 | tf_op jit(solution)/shard_map/ppermute | solution.py:584
  123.3 6.1 %collective-permute-start.27 = (bf16[160,512]{1,0:T(8,128)(2,1)}, bf16[160,512]{1,0:T(8,128)(2,1)S(1)}, u32[]{:S(2)}, u32[]{:S(2)}) collective-permute-start(bf16[160,512]{1,0:T(8,128)(2,1)} %copy-done.15), channel_id=1, source_target_pairs={{0,2},{1,3},{2,0},{3,1},{4,6},{5,7},{6,4},{7,5},{8,10},{9,11},{10,... | collective-permute-start | bytes 491528 | tf_op jit(solution)/shard_map/ppermute | solution.py:584
  125.1 8.2 %collective-permute-start.28 = (bf16[160,512]{1,0:T(8,128)(2,1)}, bf16[160,512]{1,0:T(8,128)(2,1)S(1)}, u32[]{:S(2)}, u32[]{:S(2)}) collective-permute-start(bf16[160,512]{1,0:T(8,128)(2,1)} %copy-done.14), channel_id=1, source_target_pairs={{0,3},{1,2},{2,1},{3,0},{4,7},{5,6},{6,5},{7,4},{8,11},{9,10},{10,... | collective-permute-start | bytes 491528 | tf_op jit(solution)/shard_map/ppermute | solution.py:584
  (2 other events, 1.3 us)

commit v12 on v10

--- a/solution.py
+++ b/solution.py
@@ -613,7 +613,6 @@
     grad = jnp.concatenate(grad)
     weights = weight_twice(weight_once(held(weights, grad)))
     grad = reduce_along_z(grad)
-    hidden, grad = lax.optimization_barrier((hidden, grad))
     weight_grad = reduce_to_owner(grad)
     values = project(info, hidden, weights, tn, nz, ny, nx)
     values = [values[0]] + [swapped(values[s], s) for s in range(1, tn)]

time: 130 us -> 136 us (1.046)
  the two profiles are of different devices: /device:TPU:1 before, /device:TPU:32 now
where the time goes in v12:
time: 136 us; the launch traced here: 135 us
  starting transfers between devices  55.3 us (41%)
  waiting for transfers between devices  40.8 us (30%)
  Pallas kernels  29.4 us (22%)
  other arithmetic  5.03 us (4%)
  local copies, waits for them, and re-layouts  3.65 us (3%)
    ppermute x13, waiting for transfers between devices, moved(): return lax.ppermute(values, 'dp', pairs)  25.6 us
    ppermute x13, starting transfers between devices, moved(): return lax.ppermute(values, 'dp', pairs)  23.4 us
    ppermute x2, starting transfers between devices, weight_to_place(): parts.append(lax.ppermute(weight, ('dp', 'tensor'), pairs))  10.1 us
    ppermute x2, waiting for transfers between devices, reduce_to_owner(): part = lax.ppermute(part, ('dp', 'tensor'), pairs)  9.84 us
    ppermute x14, starting transfers between devices, swapped(): return lax.ppermute(values, 'tensor', [(a, a ^ s) for a in range(tn)])  9.56 us
    pallas_call x1, Pallas kernels, attend(): pl.pallas_call(functools.partial(attend_kernel, window), grid=(pack // bl...  8.17 us
    ppermute x2, starting transfers between devices, reduce_to_owner(): part = lax.ppermute(part, ('dp', 'tensor'), pairs)  6.81 us
    all_to_all x1, starting transfers between devices, reduce_along_z(): lax.all_to_all(grad.astype(BF16), 'dp', 0, 0, tiled=True, axis_index_grou...  5.42 us
  transfers between devices with their start and end apart: 32, of which 16 were waited for; matrix products, arithmetic and copies ran while one was open for 1% of the time, Pallas kernels for 20%

profile of v12, /device:TPU:32, one launch (start us, length us, event | category | flops | bytes accessed | tf_op | source)
XLA Modules:
  0.0 135.2 jit_solution(2385501823042690115)
XLA Ops:
  0.7 1.3 compare_select_fusion.3.info_ref
  1.9 2.7 %fold.1.refs_0_ = bf16[160,512]{1,0:T(8,128)(2,1)} custom-call(s32[15]{0:T(128)} %compare_select_fusion.3.info_ref, bf16[3,128,512]{2,1,0:T(8,128)(2,1)} %cotangent_ref.1), custom_call_target="tpu_custom_call" | custom-call | flops 62914560 | bytes 393216 | tf_op jit(solution)/shard_map/fold/pallas_call | solution.py:325
  4.7 1.6 %collective-permute-start = (bf16[160,512]{1,0:T(8,128)(2,1)}, bf16[160,512]{1,0:T(8,128)(2,1)S(1)}, u32[]{:S(2)}, u32[]{:S(2)}) collective-permute-start(bf16[160,512]{1,0:T(8,128)(2,1)} %fold.1.refs_0_), channel_id=1, source_target_pairs={{0,2},{1,3},{2,0},{3,1},{4,6},{5,7},{6,4},{7,5},{8,10},{9,11},{10,... | collective-permute-start | bytes 491528 | tf_op jit(solution)/shard_map/ppermute | solution.py:580
  6.3 4.8 %features.1 = (bf16[128,2048]{1,0:T(8,128)(2,1)}, bf16[128,2048]{1,0:T(8,128)(2,1)}, bf16[128,2048]{1,0:T(8,128)(2,1)}, bf16[128,2048]{1,0:T(8,128)(2,1)}) custom-call(s32[15]{0:T(128)} %compare_select_fusion.3.info_ref, bf16[128,8192]{1,0:T(8,128)(2,1)} %low_ref, bf16[128,8192]{1,0:T(8,128)(2,1)} %mid_ref.1, f32[3,8192]{1,0:T(4,128)} %gain_ref.3), custom_call_target="tpu_custom_call" | custom-call | flops 10485760 | bytes 6291456 | tf_op jit(solution)/shard_map/features/pallas_call | solution.py:226
  11.2 1.4 %collective-permute-start.7 = (bf16[128,2048]{1,0:T(8,128)(2,1)}, bf16[128,2048]{1,0:T(8,128)(2,1)S(1)}, u32[]{:S(2)}, u32[]{:S(2)}) collective-permute-start(bf16[128,2048]{1,0:T(8,128)(2,1)} %get-tuple-element.70), channel_id=1, source_target_pairs={{0,2},{1,3},{2,0},{3,1},{4,6},{5,7},{6,4},{7,5},{8,10},{9,11},{10,... | collective-permute-start | bytes 1572872 | tf_op jit(solution)/shard_map/ppermute | solution.py:580
  12.6 0.5 collective-permute-start.8
  13.1 8.2 %attend.1 = (bf16[512,2048]{1,0:T(8,128)(2,1)S(1)}, f32[8,512]{1,0:T(8,128)S(1)}) custom-call(s32[15]{0:T(128)S(1)} %copy-done.9, bf16[512,2048]{1,0:T(8,128)(2,1)S(1)} %copy-done.11, bf16[512,256]{1,0:T(8,128)(2,1)S(1)} %copy-done.12, bf16[512,256]{1,0:T(8,128)(2,1)S(1)} %copy-done.13), custom_call_target="tpu_custom_call" | custom-call | flops 1610612736 | bytes 4194304 | tf_op jit(solution)/shard_map/attend/pallas_call | solution.py:277
  21.8 0.7 collective-permute-done.3
  23.1 7.7 %collective-permute-start.1 = (bf16[32,512]{1,0:T(8,128)(2,1)S(1)}, bf16[32,512]{1,0:T(8,128)(2,1)S(1)}, u32[]{:S(2)}, u32[]{:S(2)}) collective-permute-start(bf16[32,512]{1,0:T(8,128)(2,1)S(1)} %copy-done.14), channel_id=1, source_target_pairs={{0,0},{4,4},{1,32},{5,36},{2,64},{6,68},{3,96},{7,100},{32,128},{3... | collective-permute-start | bytes 98312 | tf_op jit(solution)/shard_map/ppermute | solution.py:70
  30.8 2.4 %collective-permute-start.2 = (bf16[32,512]{1,0:T(8,128)(2,1)S(1)}, bf16[32,512]{1,0:T(8,128)(2,1)S(1)}, u32[]{:S(2)}, u32[]{:S(2)}) collective-permute-start(bf16[32,512]{1,0:T(8,128)(2,1)S(1)} %copy-done.14), channel_id=1, source_target_pairs={{4,0},{0,4},{5,32},{1,36},{6,64},{2,68},{7,96},{3,100},{36,128},{3... | collective-permute-start | bytes 98312 | tf_op jit(solution)/shard_map/ppermute | solution.py:70
  33.3 4.2 %collective-permute-done.8.refs_3_ = bf16[128,2048]{1,0:T(8,128)(2,1)S(1)} collective-permute-done((bf16[128,2048]{1,0:T(8,128)(2,1)}, bf16[128,2048]{1,0:T(8,128)(2,1)S(1)}, u32[]{:S(2)}, u32[]{:S(2)}) %collective-permute-start.8) | collective-permute-done | bytes 524320 | tf_op jit(solution)/shard_map/ppermute | solution.py:580
  37.6 3.5 %merge.1 = (bf16[512,2048]{1,0:T(8,128)(2,1)S(1)}, f32[8,512]{1,0:T(8,128)S(1)}) custom-call(s32[15]{0:T(128)S(1)} %copy-done.9, f32[3,8192]{1,0:T(4,128)S(1)} %copy-done.5, bf16[512,2048]{1,0:T(8,128)(2,1)S(1)} %get-tuple-element.63.high_ref, bf16[128,2048]{1,0:T(8,128)(2,1)S(1)} %copy-done.4, bf16[128,2048]{1,0:T(8,128)(2,1)S(1)} %collective-permute-done.6.refs_1_, ...), custom_call_target="tpu_custom_call" | custom-call | flops 8388608 | bytes 6291456 | tf_op jit(solution)/shard_map/merge/pallas_call | solution.py:372
  41.1 0.6 collective-permute-start.10
  41.7 2.1 %collective-permute-start.11 = (f32[8,512]{1,0:T(8,128)S(1)}, f32[8,512]{1,0:T(8,128)S(1)}, u32[]{:S(2)}, u32[]{:S(2)}) collective-permute-start(f32[8,512]{1,0:T(8,128)S(1)} %get-tuple-element.82.refs_4_), channel_id=1, source_target_pairs={{0,2},{1,3},{2,0},{3,1},{4,6},{5,7},{6,4},{7,5},{8,10},{9,11},{10,... | collective-permute-start | bytes 49160 | tf_op jit(solution)/shard_map/ppermute | solution.py:580
  43.9 6.5 %collective-permute-start.13 = (bf16[64,512]{1,0:T(8,128)(2,1)S(1)}, bf16[64,512]{1,0:T(8,128)(2,1)S(1)}, u32[]{:S(2)}, u32[]{:S(2)}) collective-permute-start(bf16[64,512]{1,0:T(8,128)(2,1)S(1)} %constant_dynamic-update-slice_fusion), channel_id=1, source_target_pairs={{0,128},{4,132},{8,136},{12,140},{16,144},{20,148},{24,152},{28,15... | collective-permute-start | bytes 196616 | tf_op jit(solution)/shard_map/ppermute | solution.py:57
  50.4 4.8 %grads.1 = (f32[2,256,512]{2,1,0:T(8,128)S(1)}, f32[2,256,512]{2,1,0:T(8,128)S(1)}, bf16[2,256,512]{2,1,0:T(8,128)(2,1)S(1)}, bf16[2,256,512]{2,1,0:T(8,128)(2,1)S(1)}, bf16[512,2048]{1,0:T(8,128)(2,1)S(1)}) custom-call(s32[15]{0:T(128)S(1)} %copy-done.9, f32[1,8192]{1,0:T(1,128)S(1)} %bitcast.11, bf16[512,2048]{1,0:T(8,128)(2,1)S(1)} %get-tuple-element.77.merged_ref, ...), custom_call_target="tpu_custom_call" | custom-call | flops 1073741824 | bytes 8388608 | tf_op jit(solution)/shard_map/grads/pallas_call | solution.py:452
  55.3 1.7 %collective-permute-start.16 = (bf16[2,256,512]{2,1,0:T(8,128)(2,1)S(1)}, bf16[2,256,512]{2,1,0:T(8,128)(2,1)S(1)}, u32[]{:S(2)}, u32[]{:S(2)}) collective-permute-start(bf16[2,256,512]{2,1,0:T(8,128)(2,1)S(1)} %get-tuple-element.90), channel_id=1, source_target_pairs={{0,8},{4,12},{8,0},{12,4},{16,24},{20,28},{24,16},{28,20},{32,40},... | collective-permute-start | bytes 1572872 | tf_op jit(solution)/shard_map/ppermute | solution.py:57
  56.9 2.2 %collective-permute-start.17 = (bf16[2,256,512]{2,1,0:T(8,128)(2,1)S(1)}, bf16[2,256,512]{2,1,0:T(8,128)(2,1)S(1)}, u32[]{:S(2)}, u32[]{:S(2)}) collective-permute-start(bf16[2,256,512]{2,1,0:T(8,128)(2,1)S(1)} %get-tuple-element.91), channel_id=1, source_target_pairs={{0,24},{4,28},{8,16},{12,20},{16,8},{20,12},{24,0},{28,4},{32,56},... | collective-permute-start | bytes 1572872 | tf_op jit(solution)/shard_map/ppermute | solution.py:57
  59.1 1.7 %collective-permute-start.14 = (bf16[128,512]{1,0:T(8,128)(2,1)S(1)}, bf16[128,512]{1,0:T(8,128)(2,1)S(1)}, u32[]{:S(2)}, u32[]{:S(2)}) collective-permute-start(bf16[128,512]{1,0:T(8,128)(2,1)S(1)} %pad_maximum_fusion.1), channel_id=1, source_target_pairs={{0,64},{4,68},{8,72},{12,76},{16,80},{20,84},{24,88},{28,92},{32,9... | collective-permute-start | bytes 393224 | tf_op jit(solution)/shard_map/ppermute | solution.py:57
  60.9 5.2 %collective-permute-done.14 = bf16[128,512]{1,0:T(8,128)(2,1)S(1)} collective-permute-done((bf16[128,512]{1,0:T(8,128)(2,1)S(1)}, bf16[128,512]{1,0:T(8,128)(2,1)S(1)}, u32[]{:S(2)}, u32[]{:S(2)}) %collective-permute-start.14) | collective-permute-done | bytes 131104 | tf_op jit(solution)/shard_map/ppermute | solution.py:57
  66.1 2.6 %collective-permute-start.15 = (bf16[256,512]{1,0:T(8,128)(2,1)S(1)}, bf16[256,512]{1,0:T(8,128)(2,1)S(1)}, u32[]{:S(2)}, u32[]{:S(2)}) collective-permute-start(bf16[256,512]{1,0:T(8,128)(2,1)S(1)} %constant_dynamic-update-slice_fusion.2.refs_0_), channel_id=1, source_target_pairs={{0,32},{4,36},{8,40},{12,44},{16,48},{20,52},{24,56},{28,60},{32,0... | collective-permute-start | bytes 786440 | tf_op jit(solution)/shard_map/ppermute | solution.py:57
  69.1 2.5 %collective-permute-done.17 = bf16[2,256,512]{2,1,0:T(8,128)(2,1)S(1)} collective-permute-done((bf16[2,256,512]{2,1,0:T(8,128)(2,1)S(1)}, bf16[2,256,512]{2,1,0:T(8,128)(2,1)S(1)}, u32[]{:S(2)}, u32[]{:S(2)}) %collective-permute-start.17) | collective-permute-done | bytes 524320 | tf_op jit(solution)/shard_map/ppermute | solution.py:57
  72.0 2.3 %collective-permute-start.18 = (bf16[256,512]{1,0:T(8,128)(2,1)S(1)}, bf16[256,512]{1,0:T(8,128)(2,1)S(1)}, u32[]{:S(2)}, u32[]{:S(2)}) collective-permute-start(bf16[256,512]{1,0:T(8,128)(2,1)S(1)} %get-tuple-element.107), channel_id=1, source_target_pairs={{0,24},{4,28},{8,16},{12,20},{16,8},{20,12},{24,0},{28,4},{32,56},... | collective-permute-start | bytes 786440 | tf_op jit(solution)/shard_map/ppermute | solution.py:57
  74.7 4.0 %collective-permute-done.19 = bf16[256,512]{1,0:T(8,128)(2,1)S(1)} collective-permute-done((bf16[256,512]{1,0:T(8,128)(2,1)S(1)}, bf16[256,512]{1,0:T(8,128)(2,1)S(1)}, u32[]{:S(2)}, u32[]{:S(2)}) %collective-permute-start.19) | collective-permute-done | bytes 262176 | tf_op jit(solution)/shard_map/ppermute | solution.py:57
  78.8 1.4 %collective-permute-done.18 = bf16[256,512]{1,0:T(8,128)(2,1)S(1)} collective-permute-done((bf16[256,512]{1,0:T(8,128)(2,1)S(1)}, bf16[256,512]{1,0:T(8,128)(2,1)S(1)}, u32[]{:S(2)}, u32[]{:S(2)}) %collective-permute-start.18) | collective-permute-done | bytes 262176 | tf_op jit(solution)/shard_map/ppermute | solution.py:57
  80.3 0.8 pad_maximum_fusion.refs_2_
  81.1 5.4 %all-to-all-start = ((bf16[8,64,512]{2,1,0:T(8,128)(2,1)}), bf16[8,64,512]{2,1,0:T(8,128)(2,1)}, u32[]{:S(2)}, u32[]{:S(2)}) async-start(bf16[8,64,512]{2,1,0:T(8,128)(2,1)} %bitcast.6), calls=%async_computation | async-start | bytes 1048576 | tf_op jit(solution)/shard_map/all_to_all | solution.py:125
  86.5 0.6 collective-permute-start.20
  87.1 2.2 %collective-permute-start.23 = (bf16[256,512]{1,0:T(8,128)(2,1)}, bf16[256,512]{1,0:T(8,128)(2,1)S(1)}, u32[]{:S(2)}, u32[]{:S(2)}) collective-permute-start(bf16[256,512]{1,0:T(8,128)(2,1)} %get-tuple-element.100.refs_4_), channel_id=1, source_target_pairs={{0,24},{4,28},{8,16},{12,20},{16,8},{20,12},{24,0},{28,4},{32,56},... | collective-permute-start | bytes 786440 | tf_op jit(solution)/shard_map/ppermute | solution.py:57
  89.3 1.1 collective-permute-start.21
  90.6 5.4 %collective-permute-done.20.refs_1_ = bf16[256,512]{1,0:T(8,128)(2,1)S(1)} collective-permute-done((bf16[256,512]{1,0:T(8,128)(2,1)}, bf16[256,512]{1,0:T(8,128)(2,1)S(1)}, u32[]{:S(2)}, u32[]{:S(2)}) %collective-permute-start.20) | collective-permute-done | bytes 262176 | tf_op jit(solution)/shard_map/ppermute | solution.py:57
  96.0 2.2 %collective-permute-start.22 = (bf16[256,512]{1,0:T(8,128)(2,1)S(1)}, bf16[256,512]{1,0:T(8,128)(2,1)S(1)}, u32[]{:S(2)}, u32[]{:S(2)}) collective-permute-start(bf16[256,512]{1,0:T(8,128)(2,1)S(1)} %collective-permute-done.20.refs_1_), channel_id=1, source_target_pairs={{0,24},{4,28},{8,16},{12,20},{16,8},{20,12},{24,0},{28,4},{32,56},... | collective-permute-start | bytes 786440 | tf_op jit(solution)/shard_map/ppermute | solution.py:57
  98.2 3.5 %collective-permute-done.21.refs_2_ = bf16[256,512]{1,0:T(8,128)(2,1)S(1)} collective-permute-done((bf16[256,512]{1,0:T(8,128)(2,1)}, bf16[256,512]{1,0:T(8,128)(2,1)S(1)}, u32[]{:S(2)}, u32[]{:S(2)}) %collective-permute-start.21) | collective-permute-done | bytes 262176 | tf_op jit(solution)/shard_map/ppermute | solution.py:57
  101.7 2.8 %collective-permute-done.22.refs_3_ = bf16[256,512]{1,0:T(8,128)(2,1)S(1)} collective-permute-done((bf16[256,512]{1,0:T(8,128)(2,1)S(1)}, bf16[256,512]{1,0:T(8,128)(2,1)S(1)}, u32[]{:S(2)}, u32[]{:S(2)}) %collective-permute-start.22) | collective-permute-done | bytes 262176 | tf_op jit(solution)/shard_map/ppermute | solution.py:57
  104.5 0.7 copy-done.6
  105.2 0.9 copy-done.1
  106.2 0.9 copy-done.3
  107.1 0.9 copy-done.7
  108.1 3.8 %project.1 = (f32[160,512]{1,0:T(8,128)S(1)}, bf16[160,512]{1,0:T(8,128)(2,1)}, bf16[160,512]{1,0:T(8,128)(2,1)}, bf16[160,512]{1,0:T(8,128)(2,1)}) custom-call(s32[15]{0:T(128)S(1)} %copy-done.9, bf16[512,2048]{1,0:T(8,128)(2,1)S(1)} %get-tuple-element.84.hidden_ref, bf16[256,512]{1,0:T(8,128)(2,1)S(1)} %copy-done.1, ...), custom_call_target="tpu_custom_call" | custom-call | flops 1073741824 | bytes 4194304 | tf_op jit(solution)/shard_map/project/pallas_call | solution.py:508
  111.9 2.2 %collective-permute-start.27 = (bf16[160,512]{1,0:T(8,128)(2,1)}, bf16[160,512]{1,0:T(8,128)(2,1)S(1)}, u32[]{:S(2)}, u32[]{:S(2)}) collective-permute-start(bf16[160,512]{1,0:T(8,128)(2,1)} %get-tuple-element.103), channel_id=1, source_target_pairs={{0,2},{1,3},{2,0},{3,1},{4,6},{5,7},{6,4},{7,5},{8,10},{9,11},{10,... | collective-permute-start | bytes 491528 | tf_op jit(solution)/shard_map/ppermute | solution.py:580
  114.2 1.1 convert_reduce_fusion
  115.3 2.3 %collective-permute-start.29 = (f32[32,512]{1,0:T(8,128)S(1)}, f32[32,512]{1,0:T(8,128)S(1)}, u32[]{:S(2)}, u32[]{:S(2)}) collective-permute-start(f32[32,512]{1,0:T(8,128)S(1)} %get-tuple-element.112), channel_id=1, source_target_pairs={{0,0},{1,64},{2,128},{3,192},{4,4},{5,68},{6,132},{7,196},{8,8},{9... | collective-permute-start | bytes 196616 | tf_op jit(solution)/shard_map/ppermute | solution.py:145
  117.6 4.5 %collective-permute-start.30 = (f32[32,512]{1,0:T(8,128)S(1)}, f32[32,512]{1,0:T(8,128)S(1)}, u32[]{:S(2)}, u32[]{:S(2)}) collective-permute-start(f32[32,512]{1,0:T(8,128)S(1)} %get-tuple-element.111), channel_id=1, source_target_pairs={{0,4},{1,68},{2,132},{3,196},{4,0},{5,64},{6,128},{7,192},{8,12},{... | collective-permute-start | bytes 196616 | tf_op jit(solution)/shard_map/ppermute | solution.py:145
  122.3 1.7 %spread.1 = bf16[3,128,512]{2,1,0:T(8,128)(2,1)} custom-call(s32[15]{0:T(128)S(1)} %copy-done.9, f32[160,512]{1,0:T(8,128)S(1)} %get-tuple-element.101.refs_0_, bf16[160,512]{1,0:T(8,128)(2,1)S(1)} %collective-permute-done.26.refs_1_, bf16[160,512]{1,0:T(8,128)(2,1)S(1)} %collective-permute-done.27.refs_2_, bf16[160,512]{1,0:T(8,128)(2,1)S(1)} %collective-permute-done.28.refs_3_), custom_call_target="tpu_custom_call" | custom-call | flops 62914560 | bytes 1572864 | tf_op jit(solution)/shard_map/spread/pallas_call | solution.py:539
  124.0 2.0 %collective-permute-done.29 = f32[32,512]{1,0:T(8,128)S(1)} collective-permute-done((f32[32,512]{1,0:T(8,128)S(1)}, f32[32,512]{1,0:T(8,128)S(1)}, u32[]{:S(2)}, u32[]{:S(2)}) %collective-permute-start.29) | collective-permute-done | bytes 65568 | tf_op jit(solution)/shard_map/ppermute | solution.py:145
  126.0 7.8 %collective-permute-done.30 = f32[32,512]{1,0:T(8,128)S(1)} collective-permute-done((f32[32,512]{1,0:T(8,128)S(1)}, f32[32,512]{1,0:T(8,128)S(1)}, u32[]{:S(2)}, u32[]{:S(2)}) %collective-permute-start.30) | collective-permute-done | bytes 65568 | tf_op jit(solution)/shard_map/ppermute | solution.py:145
  133.8 0.7 multiply_reduce_fusion
  134.6 0.6 dynamic-slice_divide_fusion
  (71 shorter events, 3.3 us)
Async XLA Ops:
  4.7 8.4 %copy-start.9 = (s32[15]{0:T(128)S(1)}, s32[15]{0:T(128)}, u32[]{:S(2)}) copy-start(s32[15]{0:T(128)} %compare_select_fusion.3.info_ref) | copy-start | bytes 184
  4.7 8.4 %copy-start.11 = (bf16[512,2048]{1,0:T(8,128)(2,1)S(1)}, bf16[512,2048]{1,0:T(8,128)(2,1)}, u32[]{:S(2)}) copy-start(bf16[512,2048]{1,0:T(8,128)(2,1)} %query_ref.1) | copy-start | bytes 6291460
  4.7 8.4 %copy-start.12 = (bf16[512,256]{1,0:T(8,128)(2,1)S(1)}, bf16[512,256]{1,0:T(8,128)(2,1)}, u32[]{:S(2)}) copy-start(bf16[512,256]{1,0:T(8,128)(2,1)} %key_ref.1) | copy-start | bytes 786436
  4.7 8.4 %copy-start.13 = (bf16[512,256]{1,0:T(8,128)(2,1)S(1)}, bf16[512,256]{1,0:T(8,128)(2,1)}, u32[]{:S(2)}) copy-start(bf16[512,256]{1,0:T(8,128)(2,1)} %value_ref.1) | copy-start | bytes 786436
  4.7 6.4 %collective-permute-start = (bf16[160,512]{1,0:T(8,128)(2,1)}, bf16[160,512]{1,0:T(8,128)(2,1)S(1)}, u32[]{:S(2)}, u32[]{:S(2)}) collective-permute-start(bf16[160,512]{1,0:T(8,128)(2,1)} %fold.1.refs_0_), channel_id=1, source_target_pairs={{0,2},{1,3},{2,0},{3,1},{4,6},{5,7},{6,4},{7,5},{8,10},{9,11},{10,... | collective-permute-start | bytes 491528 | tf_op jit(solution)/shard_map/ppermute | solution.py:580
  11.1 10.6 %copy-start.8 = (bf16[160,512]{1,0:T(8,128)(2,1)S(1)}, bf16[160,512]{1,0:T(8,128)(2,1)}, u32[]{:S(2)}) copy-start(bf16[160,512]{1,0:T(8,128)(2,1)} %fold.1.refs_0_) | copy-start | bytes 491524
  11.1 12.0 %copy-start.14 = (bf16[32,512]{1,0:T(8,128)(2,1)S(1)}, bf16[32,512]{1,0:T(8,128)(2,1)}, u32[]{:S(2)}) copy-start(bf16[32,512]{1,0:T(8,128)(2,1)} %param.18) | copy-start | bytes 98308
  11.1 26.5 %copy-start.4 = (bf16[128,2048]{1,0:T(8,128)(2,1)S(1)}, bf16[128,2048]{1,0:T(8,128)(2,1)}, u32[]{:S(2)}) copy-start(bf16[128,2048]{1,0:T(8,128)(2,1)} %get-tuple-element.64.refs_0_) | copy-start | bytes 1572868
  11.1 26.5 %copy-start.5 = (f32[3,8192]{1,0:T(4,128)S(1)}, f32[3,8192]{1,0:T(4,128)}, u32[]{:S(2)}) copy-start(f32[3,8192]{1,0:T(4,128)} %gain_ref.3) | copy-start | bytes 294916
  11.1 22.1 %collective-permute-start.6 = (bf16[128,2048]{1,0:T(8,128)(2,1)}, bf16[128,2048]{1,0:T(8,128)(2,1)S(1)}, u32[]{:S(2)}, u32[]{:S(2)}) collective-permute-start(bf16[128,2048]{1,0:T(8,128)(2,1)} %get-tuple-element.68), channel_id=1, source_target_pairs={{0,1},{1,0},{2,3},{3,2},{4,5},{5,4},{6,7},{7,6},{8,9},{9,8},{10,11... | collective-permute-start | bytes 1572872 | tf_op jit(solution)/shard_map/ppermute | solution.py:580
  11.2 22.1 %collective-permute-start.7 = (bf16[128,2048]{1,0:T(8,128)(2,1)}, bf16[128,2048]{1,0:T(8,128)(2,1)S(1)}, u32[]{:S(2)}, u32[]{:S(2)}) collective-permute-start(bf16[128,2048]{1,0:T(8,128)(2,1)} %get-tuple-element.70), channel_id=1, source_target_pairs={{0,2},{1,3},{2,0},{3,1},{4,6},{5,7},{6,4},{7,5},{8,10},{9,11},{10,... | collective-permute-start | bytes 1572872 | tf_op jit(solution)/shard_map/ppermute | solution.py:580
  12.6 24.9 %collective-permute-start.8 = (bf16[128,2048]{1,0:T(8,128)(2,1)}, bf16[128,2048]{1,0:T(8,128)(2,1)S(1)}, u32[]{:S(2)}, u32[]{:S(2)}) collective-permute-start(bf16[128,2048]{1,0:T(8,128)(2,1)} %get-tuple-element.71), channel_id=1, source_target_pairs={{0,3},{1,2},{2,1},{3,0},{4,7},{5,6},{6,5},{7,4},{8,11},{9,10},{10,... | collective-permute-start | bytes 1572872 | tf_op jit(solution)/shard_map/ppermute | solution.py:580
  21.3 1.2 collective-permute-start.3
  21.7 1.4 %collective-permute-start.4 = (bf16[160,512]{1,0:T(8,128)(2,1)S(1)}, bf16[160,512]{1,0:T(8,128)(2,1)S(1)}, u32[]{:S(2)}, u32[]{:S(2)}) collective-permute-start(bf16[160,512]{1,0:T(8,128)(2,1)S(1)} %copy-done.8), channel_id=1, source_target_pairs={{0,1},{1,0},{2,3},{3,2},{4,5},{5,4},{6,7},{7,6},{8,9},{9,8},{10,11... | collective-permute-start | bytes 491528 | tf_op jit(solution)/shard_map/ppermute | solution.py:580
  22.5 8.3 %collective-permute-start.5 = (bf16[160,512]{1,0:T(8,128)(2,1)S(1)}, bf16[160,512]{1,0:T(8,128)(2,1)S(1)}, u32[]{:S(2)}, u32[]{:S(2)}) collective-permute-start(bf16[160,512]{1,0:T(8,128)(2,1)S(1)} %collective-permute-done.refs_2_), channel_id=1, source_target_pairs={{0,1},{1,0},{2,3},{3,2},{4,5},{5,4},{6,7},{7,6},{8,9},{9,8},{10,11... | collective-permute-start | bytes 491528 | tf_op jit(solution)/shard_map/ppermute | solution.py:580
  23.1 18.0 %collective-permute-start.1 = (bf16[32,512]{1,0:T(8,128)(2,1)S(1)}, bf16[32,512]{1,0:T(8,128)(2,1)S(1)}, u32[]{:S(2)}, u32[]{:S(2)}) collective-permute-start(bf16[32,512]{1,0:T(8,128)(2,1)S(1)} %copy-done.14), channel_id=1, source_target_pairs={{0,0},{4,4},{1,32},{5,36},{2,64},{6,68},{3,96},{7,100},{32,128},{3... | collective-permute-start | bytes 98312 | tf_op jit(solution)/shard_map/ppermute | solution.py:70
  30.8 10.3 %collective-permute-start.2 = (bf16[32,512]{1,0:T(8,128)(2,1)S(1)}, bf16[32,512]{1,0:T(8,128)(2,1)S(1)}, u32[]{:S(2)}, u32[]{:S(2)}) collective-permute-start(bf16[32,512]{1,0:T(8,128)(2,1)S(1)} %copy-done.14), channel_id=1, source_target_pairs={{4,0},{0,4},{5,32},{1,36},{6,64},{2,68},{7,96},{3,100},{36,128},{3... | collective-permute-start | bytes 98312 | tf_op jit(solution)/shard_map/ppermute | solution.py:70
  33.2 17.2 %copy-start.10 = (f32[8192]{0:T(1024)S(1)}, f32[8192]{0:T(1024)}, u32[]{:S(2)}) copy-start(f32[8192]{0:T(1024)} %param.17) | copy-start | bytes 98308
  33.2 4.4 %collective-permute-start.9 = (f32[8,512]{1,0:T(8,128)S(1)}, f32[8,512]{1,0:T(8,128)S(1)}, u32[]{:S(2)}, u32[]{:S(2)}) collective-permute-start(f32[8,512]{1,0:T(8,128)S(1)} %add.73.refs_4_), channel_id=1, source_target_pairs={{0,2},{1,3},{2,0},{3,1},{4,6},{5,7},{6,4},{7,5},{8,10},{9,11},{10,... | collective-permute-start | bytes 49160 | tf_op jit(solution)/shard_map/ppermute | solution.py:580
  41.1 9.3 %collective-permute-start.10 = (f32[8,512]{1,0:T(8,128)S(1)}, f32[8,512]{1,0:T(8,128)S(1)}, u32[]{:S(2)}, u32[]{:S(2)}) collective-permute-start(f32[8,512]{1,0:T(8,128)S(1)} %get-tuple-element.82.refs_4_), channel_id=1, source_target_pairs={{0,1},{1,0},{2,3},{3,2},{4,5},{5,4},{6,7},{7,6},{8,9},{9,8},{10,11... | collective-permute-start | bytes 49160 | tf_op jit(solution)/shard_map/ppermute | solution.py:580
  41.7 8.7 %collective-permute-start.11 = (f32[8,512]{1,0:T(8,128)S(1)}, f32[8,512]{1,0:T(8,128)S(1)}, u32[]{:S(2)}, u32[]{:S(2)}) collective-permute-start(f32[8,512]{1,0:T(8,128)S(1)} %get-tuple-element.82.refs_4_), channel_id=1, source_target_pairs={{0,2},{1,3},{2,0},{3,1},{4,6},{5,7},{6,4},{7,5},{8,10},{9,11},{10,... | collective-permute-start | bytes 49160 | tf_op jit(solution)/shard_map/ppermute | solution.py:580
  43.8 6.6 %collective-permute-start.12 = (f32[8,512]{1,0:T(8,128)S(1)}, f32[8,512]{1,0:T(8,128)S(1)}, u32[]{:S(2)}, u32[]{:S(2)}) collective-permute-start(f32[8,512]{1,0:T(8,128)S(1)} %get-tuple-element.82.refs_4_), channel_id=1, source_target_pairs={{0,3},{1,2},{2,1},{3,0},{4,7},{5,6},{6,5},{7,4},{8,11},{9,10},{10,... | collective-permute-start | bytes 49160 | tf_op jit(solution)/shard_map/ppermute | solution.py:580
  43.9 11.4 %collective-permute-start.13 = (bf16[64,512]{1,0:T(8,128)(2,1)S(1)}, bf16[64,512]{1,0:T(8,128)(2,1)S(1)}, u32[]{:S(2)}, u32[]{:S(2)}) collective-permute-start(bf16[64,512]{1,0:T(8,128)(2,1)S(1)} %constant_dynamic-update-slice_fusion), channel_id=1, source_target_pairs={{0,128},{4,132},{8,136},{12,140},{16,144},{20,148},{24,152},{28,15... | collective-permute-start | bytes 196616 | tf_op jit(solution)/shard_map/ppermute | solution.py:57
  55.3 13.8 %collective-permute-start.16 = (bf16[2,256,512]{2,1,0:T(8,128)(2,1)S(1)}, bf16[2,256,512]{2,1,0:T(8,128)(2,1)S(1)}, u32[]{:S(2)}, u32[]{:S(2)}) collective-permute-start(bf16[2,256,512]{2,1,0:T(8,128)(2,1)S(1)} %get-tuple-element.90), channel_id=1, source_target_pairs={{0,8},{4,12},{8,0},{12,4},{16,24},{20,28},{24,16},{28,20},{32,40},... | collective-permute-start | bytes 1572872 | tf_op jit(solution)/shard_map/ppermute | solution.py:57
  56.9 14.6 %collective-permute-start.17 = (bf16[2,256,512]{2,1,0:T(8,128)(2,1)S(1)}, bf16[2,256,512]{2,1,0:T(8,128)(2,1)S(1)}, u32[]{:S(2)}, u32[]{:S(2)}) collective-permute-start(bf16[2,256,512]{2,1,0:T(8,128)(2,1)S(1)} %get-tuple-element.91), channel_id=1, source_target_pairs={{0,24},{4,28},{8,16},{12,20},{16,8},{20,12},{24,0},{28,4},{32,56},... | collective-permute-start | bytes 1572872 | tf_op jit(solution)/shard_map/ppermute | solution.py:57
  59.1 7.0 %collective-permute-start.14 = (bf16[128,512]{1,0:T(8,128)(2,1)S(1)}, bf16[128,512]{1,0:T(8,128)(2,1)S(1)}, u32[]{:S(2)}, u32[]{:S(2)}) collective-permute-start(bf16[128,512]{1,0:T(8,128)(2,1)S(1)} %pad_maximum_fusion.1), channel_id=1, source_target_pairs={{0,64},{4,68},{8,72},{12,76},{16,80},{20,84},{24,88},{28,92},{32,9... | collective-permute-start | bytes 393224 | tf_op jit(solution)/shard_map/ppermute | solution.py:57
  66.1 5.9 %copy-start = (bf16[256,512]{1,0:T(8,128)(2,1)}, bf16[256,512]{1,0:T(8,128)(2,1)S(1)}, u32[]{:S(2)}) copy-start(bf16[256,512]{1,0:T(8,128)(2,1)S(1)} %constant_dynamic-update-slice_fusion.2.refs_0_) | copy-start | bytes 786436
  66.1 8.6 %collective-permute-start.15 = (bf16[256,512]{1,0:T(8,128)(2,1)S(1)}, bf16[256,512]{1,0:T(8,128)(2,1)S(1)}, u32[]{:S(2)}, u32[]{:S(2)}) collective-permute-start(bf16[256,512]{1,0:T(8,128)(2,1)S(1)} %constant_dynamic-update-slice_fusion.2.refs_0_), channel_id=1, source_target_pairs={{0,32},{4,36},{8,40},{12,44},{16,48},{20,52},{24,56},{28,60},{32,0... | collective-permute-start | bytes 786440 | tf_op jit(solution)/shard_map/ppermute | solution.py:57
  71.7 7.0 %collective-permute-start.19 = (bf16[256,512]{1,0:T(8,128)(2,1)S(1)}, bf16[256,512]{1,0:T(8,128)(2,1)S(1)}, u32[]{:S(2)}, u32[]{:S(2)}) collective-permute-start(bf16[256,512]{1,0:T(8,128)(2,1)S(1)} %get-tuple-element.109), channel_id=1, source_target_pairs={{0,8},{4,12},{8,0},{12,4},{16,24},{20,28},{24,16},{28,20},{32,40},... | collective-permute-start | bytes 786440 | tf_op jit(solution)/shard_map/ppermute | solution.py:57
  72.0 8.2 %collective-permute-start.18 = (bf16[256,512]{1,0:T(8,128)(2,1)S(1)}, bf16[256,512]{1,0:T(8,128)(2,1)S(1)}, u32[]{:S(2)}, u32[]{:S(2)}) collective-permute-start(bf16[256,512]{1,0:T(8,128)(2,1)S(1)} %get-tuple-element.107), channel_id=1, source_target_pairs={{0,24},{4,28},{8,16},{12,20},{16,8},{20,12},{24,0},{28,4},{32,56},... | collective-permute-start | bytes 786440 | tf_op jit(solution)/shard_map/ppermute | solution.py:57
  74.7 6.4 %copy-start.2 = (bf16[256,512]{1,0:T(8,128)(2,1)}, bf16[256,512]{1,0:T(8,128)(2,1)S(1)}, u32[]{:S(2)}) copy-start(bf16[256,512]{1,0:T(8,128)(2,1)S(1)} %collective-permute-done.15.refs_1_) | copy-start | bytes 786436
  81.1 33.1 %all-to-all-start = ((bf16[8,64,512]{2,1,0:T(8,128)(2,1)}), bf16[8,64,512]{2,1,0:T(8,128)(2,1)}, u32[]{:S(2)}, u32[]{:S(2)}) async-start(bf16[8,64,512]{2,1,0:T(8,128)(2,1)} %bitcast.6), calls=%async_computation | async-start | bytes 1048576 | tf_op jit(solution)/shard_map/all_to_all | solution.py:125
  86.5 9.5 %collective-permute-start.20 = (bf16[256,512]{1,0:T(8,128)(2,1)}, bf16[256,512]{1,0:T(8,128)(2,1)S(1)}, u32[]{:S(2)}, u32[]{:S(2)}) collective-permute-start(bf16[256,512]{1,0:T(8,128)(2,1)} %get-tuple-element.99.refs_0_), channel_id=1, source_target_pairs={{0,8},{4,12},{8,0},{12,4},{16,24},{20,28},{24,16},{28,20},{32,40},... | collective-permute-start | bytes 786440 | tf_op jit(solution)/shard_map/ppermute | solution.py:57
  87.1 11.0 %collective-permute-start.23 = (bf16[256,512]{1,0:T(8,128)(2,1)}, bf16[256,512]{1,0:T(8,128)(2,1)S(1)}, u32[]{:S(2)}, u32[]{:S(2)}) collective-permute-start(bf16[256,512]{1,0:T(8,128)(2,1)} %get-tuple-element.100.refs_4_), channel_id=1, source_target_pairs={{0,24},{4,28},{8,16},{12,20},{16,8},{20,12},{24,0},{28,4},{32,56},... | collective-permute-start | bytes 786440 | tf_op jit(solution)/shard_map/ppermute | solution.py:57
  89.3 12.4 %collective-permute-start.21 = (bf16[256,512]{1,0:T(8,128)(2,1)}, bf16[256,512]{1,0:T(8,128)(2,1)S(1)}, u32[]{:S(2)}, u32[]{:S(2)}) collective-permute-start(bf16[256,512]{1,0:T(8,128)(2,1)} %get-tuple-element.99.refs_0_), channel_id=1, source_target_pairs={{0,24},{4,28},{8,16},{12,20},{16,8},{20,12},{24,0},{28,4},{32,56},... | collective-permute-start | bytes 786440 | tf_op jit(solution)/shard_map/ppermute | solution.py:57
  90.4 11.3 %collective-permute-start.24 = (bf16[256,512]{1,0:T(8,128)(2,1)}, bf16[256,512]{1,0:T(8,128)(2,1)S(1)}, u32[]{:S(2)}, u32[]{:S(2)}) collective-permute-start(bf16[256,512]{1,0:T(8,128)(2,1)} %get-tuple-element.100.refs_4_), channel_id=1, source_target_pairs={{0,8},{4,12},{8,0},{12,4},{16,24},{20,28},{24,16},{28,20},{32,40},... | collective-permute-start | bytes 786440 | tf_op jit(solution)/shard_map/ppermute | solution.py:57
  96.0 8.5 %collective-permute-start.22 = (bf16[256,512]{1,0:T(8,128)(2,1)S(1)}, bf16[256,512]{1,0:T(8,128)(2,1)S(1)}, u32[]{:S(2)}, u32[]{:S(2)}) collective-permute-start(bf16[256,512]{1,0:T(8,128)(2,1)S(1)} %collective-permute-done.20.refs_1_), channel_id=1, source_target_pairs={{0,24},{4,28},{8,16},{12,20},{16,8},{20,12},{24,0},{28,4},{32,56},... | collective-permute-start | bytes 786440 | tf_op jit(solution)/shard_map/ppermute | solution.py:57
  98.2 7.0 %collective-permute-start.25 = (bf16[256,512]{1,0:T(8,128)(2,1)S(1)}, bf16[256,512]{1,0:T(8,128)(2,1)}, u32[]{:S(2)}, u32[]{:S(2)}) collective-permute-start(bf16[256,512]{1,0:T(8,128)(2,1)S(1)} %collective-permute-done.23.refs_5_), channel_id=1, source_target_pairs={{0,8},{4,12},{8,0},{12,4},{16,24},{20,28},{24,16},{28,20},{32,40},... | collective-permute-start | bytes 786440 | tf_op jit(solution)/shard_map/ppermute | solution.py:57
  104.5 0.7 copy-start.6
  105.2 1.0 copy-start.1
  106.2 0.9 copy-start.3
  107.1 0.9 copy-start.7
  111.8 10.3 %collective-permute-start.26 = (bf16[160,512]{1,0:T(8,128)(2,1)}, bf16[160,512]{1,0:T(8,128)(2,1)S(1)}, u32[]{:S(2)}, u32[]{:S(2)}) collective-permute-start(bf16[160,512]{1,0:T(8,128)(2,1)} %get-tuple-element.102), channel_id=1, source_target_pairs={{0,1},{1,0},{2,3},{3,2},{4,5},{5,4},{6,7},{7,6},{8,9},{9,8},{10,11... | collective-permute-start | bytes 491528 | tf_op jit(solution)/shard_map/ppermute | solution.py:580
  111.9 10.2 %collective-permute-start.27 = (bf16[160,512]{1,0:T(8,128)(2,1)}, bf16[160,512]{1,0:T(8,128)(2,1)S(1)}, u32[]{:S(2)}, u32[]{:S(2)}) collective-permute-start(bf16[160,512]{1,0:T(8,128)(2,1)} %get-tuple-element.103), channel_id=1, source_target_pairs={{0,2},{1,3},{2,0},{3,1},{4,6},{5,7},{6,4},{7,5},{8,10},{9,11},{10,... | collective-permute-start | bytes 491528 | tf_op jit(solution)/shard_map/ppermute | solution.py:580
  114.1 8.2 %collective-permute-start.28 = (bf16[160,512]{1,0:T(8,128)(2,1)}, bf16[160,512]{1,0:T(8,128)(2,1)S(1)}, u32[]{:S(2)}, u32[]{:S(2)}) collective-permute-start(bf16[160,512]{1,0:T(8,128)(2,1)} %get-tuple-element.104), channel_id=1, source_target_pairs={{0,3},{1,2},{2,1},{3,0},{4,7},{5,6},{6,5},{7,4},{8,11},{9,10},{10,... | collective-permute-start | bytes 491528 | tf_op jit(solution)/shard_map/ppermute | solution.py:580
  115.3 10.7 %collective-permute-start.29 = (f32[32,512]{1,0:T(8,128)S(1)}, f32[32,512]{1,0:T(8,128)S(1)}, u32[]{:S(2)}, u32[]{:S(2)}) collective-permute-start(f32[32,512]{1,0:T(8,128)S(1)} %get-tuple-element.112), channel_id=1, source_target_pairs={{0,0},{1,64},{2,128},{3,192},{4,4},{5,68},{6,132},{7,196},{8,8},{9... | collective-permute-start | bytes 196616 | tf_op jit(solution)/shard_map/ppermute | solution.py:145
  117.6 16.2 %collective-permute-start.30 = (f32[32,512]{1,0:T(8,128)S(1)}, f32[32,512]{1,0:T(8,128)S(1)}, u32[]{:S(2)}, u32[]{:S(2)}) collective-permute-start(f32[32,512]{1,0:T(8,128)S(1)} %get-tuple-element.111), channel_id=1, source_target_pairs={{0,4},{1,68},{2,132},{3,196},{4,0},{5,64},{6,128},{7,192},{8,12},{... | collective-permute-start | bytes 196616 | tf_op jit(solution)/shard_map/ppermute | solution.py:145
